TPU v7x, 32 devices: a whole 2x2x4 slice. The times are simulated.
32 devices in a mesh: dp: 8 (over z, x), tensor: 4 (over y, core).
Axes of the slice: x: 2, y: 2, z: 4, core: 2. Of those that a mesh axis runs over, the one named last changes fastest.
Arguments:
- acts: bfloat16 [12288, 8192], P('dp', 'tensor'), may hold values from -60 to 60
- cotangent: bfloat16 [12288, 2048], P(('dp', 'tensor')), may hold values from -6 to 6
- master: float32 [8192, 2048], P('tensor', 'dp'), may hold values from -0.0625 to 0.0625
- first_moment: float32 [8192, 2048], P('tensor', 'dp'), may hold values from -4 to 4
- second_moment: float32 [8192, 2048], P('tensor', 'dp'), may hold values from 0.01 to 1
Outputs:
- new_master: float32 [8192, 2048], P('tensor', 'dp')
- new_first: float32 [8192, 2048], P('tensor', 'dp')
- new_second: float32 [8192, 2048], P('tensor', 'dp')
- weights: bfloat16 [8192, 2048], P('tensor')
- block_scales: float32 [64, 16], P('tensor')
All inputs are finite; a program needn't handle non-finite values.
Results may differ from a plain program's by a relative error of at most 0.02.
Values may be sent and summed in bfloat16 or wider, within the bound.
No kernel may reach another device: no remote copies, remote signals or barrier semaphores. Data moves between devices by JAX's collectives and lax.ppermute only.
A program may use at most 192 MiB of HBM per device.

v0:
```python
import math

import jax
import jax.numpy as jnp
from jax import lax
from jax.sharding import PartitionSpec as P

BLOCK = 128


def contract_rows(left, right):
    return lax.dot_general(
        left, right, (((0,), (0,)), ((), ())), preferred_element_type=jnp.float32
    )


def body(acts, cotangent, master, first_moment, second_moment):
    width_rows = acts.shape[1]
    columns = cotangent.shape[1]
    whole = lax.all_gather(cotangent, "tensor", axis=0, tiled=True)
    partial_value = contract_rows(acts, whole)
    magnitude = jnp.abs(partial_value).reshape(width_rows // BLOCK, BLOCK, columns // BLOCK, BLOCK)
    local_max = jnp.max(magnitude, axis=(1, 3))
    block_scales = lax.pmax(local_max, "dp") + 1e-06
    wide_scale = jnp.repeat(jnp.repeat(block_scales, BLOCK, axis=0), BLOCK, axis=1)
    quantized = (partial_value / wide_scale).astype(jnp.bfloat16)
    quantized = lax.optimization_barrier(quantized)
    summed = lax.psum_scatter(
        quantized.astype(jnp.float32).astype(jnp.bfloat16), "dp", scatter_dimension=1, tiled=True
    ).astype(jnp.float32)
    owned_width = summed.shape[1]
    owner = lax.axis_index("dp")
    own_scale = lax.dynamic_slice_in_dim(wide_scale, owner * owned_width, owned_width, 1)
    token_count = acts.shape[0] * lax.axis_size("dp")
    gradient = summed * own_scale / math.sqrt(token_count)
    new_first = 0.9 * first_moment + 0.1 * gradient
    new_second = 0.95 * second_moment + 0.05 * gradient * gradient
    first_hat = new_first / (1.0 - 0.9**10)
    second_hat = new_second / (1.0 - 0.95**10)
    new_master = master * (1.0 - 0.01 * 0.1) - 0.01 * first_hat / (jnp.sqrt(second_hat) + 1e-08)
    owned_weights = new_master.astype(jnp.bfloat16)
    weights = lax.all_gather(owned_weights, "dp", axis=1, tiled=True)
    return (new_master, new_first, new_second, weights, block_scales)


def solution(mesh):
    in_specs = (
        P("dp", "tensor"),
        P(("dp", "tensor"), None),
        P("tensor", "dp"),
        P("tensor", "dp"),
        P("tensor", "dp"),
    )
    out_specs = (
        P("tensor", "dp"),
        P("tensor", "dp"),
        P("tensor", "dp"),
        P("tensor", None),
        P("tensor", None),
    )
    return jax.shard_map(body, mesh=mesh, in_specs=in_specs, out_specs=out_specs, check_vma=False)
```

profile of v0, /device:TPU:0, one launch (start us, length us, event | category | flops | bytes accessed | tf_op | source)
XLA Modules:
  0.0 445.1 jit_solution(5957255818619527466)
XLA Ops:
  7.2 0.0 all-gather.3.cloned.1.call-start
  7.2 0.7 all-gather.3.cloned.1.call-update
  7.9 0.0 reduce-scatter.2.cloned.1.call-start
  7.9 50.7 %all-gather.3.cloned.1.call-done = bf16[1536,2048]{1,0:T(8,128)(2,1)} async-done(((bf16[384,2048]{1,0:T(8,128)(2,1)}), bf16[1536,2048]{1,0:T(8,128)(2,1)}) %all-gather.3.cloned.1.call-update) | async-done | bytes 6291472 | tf_op jit(solution)/shard_map/all_gather | solution.py:20
  58.7 17.5 %fusion.1 = f32[2048,2048]{1,0:T(8,128)S(1)} fusion(bf16[1536,2048]{1,0:T(8,128)(2,1)} %param.5, bf16[1536,2048]{1,0:T(8,128)(2,1)} %all-gather.3.cloned.1.call-done), kind=kOutput, calls=%fused_computation.10 | convolution fusion | flops 12884901888 | bytes 29360128 | tf_op jit(solution)/shard_map/dot_general | solution.py:12
  76.2 0.0 copy-start.1
  76.2 7.0 %abs_bitcast_fusion = f32[256,8,16,128]{3,1,2,0:T(8,128)} fusion(f32[2048,2048]{1,0:T(8,128)S(1)} %fusion.1), kind=kLoop, calls=%fused_computation.3 | loop fusion | flops 4194304 | bytes 33554432
  83.1 3.8 copy-done.1
  86.9 14.1 %copy.10 = f32[256,8,16,128]{3,2,1,0:T(8,128)} copy(f32[256,8,16,128]{3,1,2,0:T(8,128)} %abs_bitcast_fusion) | data formatting | bytes 33554432
  101.0 6.6 %bitcast_reduce_fusion = f32[16,16]{1,0:T(8,128)S(1)} fusion(f32[16,128,16,128]{3,2,1,0:T(8,128)} %bitcast.17), kind=kLoop, calls=%fused_computation.1 | loop fusion | flops 4194048 | bytes 16778240 | tf_op jit(solution)/shard_map/reduce_max | solution.py:23
  107.6 21.8 %pmax.7 = f32[16,16]{1,0:T(8,128)S(1)} all-reduce(f32[16,16]{1,0:T(8,128)S(1)} %bitcast_reduce_fusion), channel_id=1, replica_groups=mesh['dp'=8,'tensor'=4] {'dp'}, use_global_device_ids=true, to_apply=%region_1.0 | all-reduce | flops 256 | bytes 2048 | tf_op jit(solution)/shard_map/pmax | solution.py:24
  129.4 0.0 copy-start.3
  129.4 0.1 broadcast_in_dim.6
  129.5 4.6 %broadcast_in_dim.7 = f32[2048,16,128]{2,1,0:T(8,128)S(1)} broadcast(f32[2048,16]{1,0:T(8,128)S(1)} %bitcast.19), dimensions={0,1} | broadcast | bytes 16908288 | tf_op jit(solution)/shard_map/broadcast_in_dim | solution.py:25
  134.1 0.0 copy-done.3
  134.1 0.0 copy-start
  134.1 5.7 %copy-done = f32[2048,16,128]{2,1,0:T(8,128)} copy-done((f32[2048,16,128]{2,1,0:T(8,128)}, f32[2048,16,128]{2,1,0:T(8,128)S(1)}, u32[]{:S(2)}) %copy-start) | copy-done | bytes 16777240
  139.8 12.6 %divide_convert_fusion = bf16[2048,2048]{1,0:T(8,128)(2,1)} fusion(f32[2048,2048]{1,0:T(8,128)} %copy-done.1, f32[256,8,16,128]{3,2,1,0:T(8,128)S(1)} %bitcast.15), kind=kLoop, calls=%fused_computation.2 | loop fusion | flops 8388608 | bytes 41943040 | tf_op jit(solution)/shard_map/convert_element_type | solution.py:26
  152.4 0.0 reduce-scatter.2.cloned.1.call-update
  152.5 0.0 all-gather.5.cloned.1.call-start
  152.5 0.0 copy-start.2
  152.5 15.9 %copy.15 = f32[256,8,16,128]{3,1,2,0:T(8,128)} copy(f32[256,8,16,128]{3,2,1,0:T(8,128)} %bitcast.16) | data formatting | bytes 33554432
  168.4 129.9 %reduce-scatter.2.cloned.1.call-done = bf16[2048,256]{1,0:T(8,128)(2,1)} async-done(((bf16[2048,2048]{1,0:T(8,128)(2,1)}), bf16[2048,256]{1,0:T(8,128)(2,1)}) %reduce-scatter.2.cloned.1.call-update) | async-done | bytes 1048592 | tf_op jit(solution)/shard_map/reduce_scatter | solution.py:28
  298.3 0.0 copy-done.2
  298.3 7.2 %fusion = (bf16[2048,256]{1,0:T(8,128)(2,1)}, f32[2048,256]{1,0:T(8,128)}, f32[2048,256]{1,0:T(8,128)}, f32[2048,256]{1,0:T(8,128)}) fusion(f32[2048,256]{1,0:T(8,128)S(1)} %copy-done.2, f32[2048,2048]{1,0:T(8,128)} %bitcast.18, s32[]{:T(128)S(6)} %select_n.3, bf16[2048,256]{1,0:T(8,128)(2,1)} %reduce-scatter.2.cloned.1.call-done, f32[2048,256]{1,0:T(8,128)} %param.8, ...), kind=kLoop, calls=%fused_computation.9 | loop fusion | flops 8912896 | bytes 16777220 | tf_op jit(solution)/shard_map/convert_element_type | solution.py:41
  305.6 0.0 all-gather.5.cloned.1.call-update
  305.6 124.5 %all-gather.5.cloned.1.call-done = bf16[2048,2048]{1,0:T(8,128)(2,1)} async-done(((bf16[2048,256]{1,0:T(8,128)(2,1)}), bf16[2048,2048]{1,0:T(8,128)(2,1)}) %all-gather.5.cloned.1.call-update) | async-done | bytes 8388624 | tf_op jit(solution)/shard_map/all_gather | solution.py:42
  430.1 8.4 %copy.17 = bf16[2048,2048]{1,0:T(8,128)(2,1)} copy(bf16[2048,2048]{1,0:T(8,128)(2,1)} %all-gather.5.cloned.1.call-done) | data formatting | bytes 16777216
  (1 shorter events, 0.0 us)
Async XLA Ops:
  7.2 51.5 %all-gather.3.cloned.1.call-start = ((), (), s32[]{:S(2)}) async-start(), calls=%async_computation.1 | async-start | bytes 7864320 | tf_op jit(solution)/shard_map/all_gather | solution.py:20
  7.9 290.4 %reduce-scatter.2.cloned.1.call-start = ((), (), s32[]{:S(2)}) async-start(), calls=%async_computation.2 | async-start | bytes 9437184 | tf_op jit(solution)/shard_map/reduce_scatter | solution.py:28
  76.2 10.7 %copy-start.1 = (f32[2048,2048]{1,0:T(8,128)}, f32[2048,2048]{1,0:T(8,128)S(1)}, u32[]{:S(2)}) copy-start(f32[2048,2048]{1,0:T(8,128)S(1)} %fusion.1) | copy-start | bytes 50331652
  129.4 4.7 %copy-start.3 = (f32[16,16]{1,0:T(8,128)}, f32[16,16]{1,0:T(8,128)S(1)}, u32[]{:S(2)}) copy-start(f32[16,16]{1,0:T(8,128)S(1)} %broadcast_add_fusion) | copy-start | bytes 3076
  134.1 5.7 %copy-start = (f32[2048,16,128]{2,1,0:T(8,128)}, f32[2048,16,128]{2,1,0:T(8,128)S(1)}, u32[]{:S(2)}) copy-start(f32[2048,16,128]{2,1,0:T(8,128)S(1)} %broadcast_in_dim.7) | copy-start | bytes 50331652
  152.5 277.7 %all-gather.5.cloned.1.call-start = ((), (), s32[]{:S(2)}) async-start(), calls=%async_computation.3 | async-start | bytes 9437184 | tf_op jit(solution)/shard_map/all_gather | solution.py:42
  152.5 145.8 %copy-start.2 = (f32[2048,256]{1,0:T(8,128)S(1)}, f32[2048,256]{1,0:T(8,128)}, u32[]{:S(2)}) copy-start(f32[2048,256]{1,0:T(8,128)} %param.7) | copy-start | bytes 6291460
Sparse Core Ops, SparseCore 0:
  9.6 49.0 all-gather.2
  152.6 145.7 reduce-scatter.1
  305.7 124.3 all-gather.4
where the time goes:
time: 445 us
  waiting for transfers between devices  306 us (69%)
  local copies, waits for them, and re-layouts  52.6 us (12%)
  other arithmetic  33.4 us (8%)
  blocking collectives  21.8 us (5%)
  matrix products  17.5 us (4%)
  between operations  13.8 us (3%)
    reduce_scatter x1, waiting for transfers between devices, body(): lax.psum_scatter(quantized.astype(jnp.float32).astype(jnp.bfloat16), 'dp'...  130 us
    all_gather x1, waiting for transfers between devices, body(): weights = lax.all_gather(owned_weights, 'dp', axis=1, tiled=True)  125 us
    all_gather x1, waiting for transfers between devices, body(): whole = lax.all_gather(cotangent, 'tensor', axis=0, tiled=True)  50.7 us
    unnamed x11, local copies, waits for them, and re-layouts  47.9 us
    pmax x1, blocking collectives, body(): block_scales = lax.pmax(local_max, 'dp') + 1e-06  21.8 us
    dot_general x1, matrix products, contract_rows(): lax.dot_general(left, right, (((0,), (0,)), ((), ())), preferred_element_...  17.5 us
    convert_element_type x1, other arithmetic, body(): quantized = (partial_value / wide_scale).astype(jnp.bfloat16)  12.6 us
  transfers between devices with their start and end apart: 3, of which 3 were waited for; matrix products, arithmetic and copies ran while one was open for 4% of the time, Pallas kernels for 0%

commit v1 on v0

v1 whole, which is shorter than its diff:
```python
import math

import jax
import jax.numpy as jnp
from jax import lax
from jax.experimental import pallas as pl
from jax.experimental.pallas import tpu as pltpu
from jax.sharding import PartitionSpec as P

BLOCK = 128
Z = 4
F32 = jnp.float32
BF16 = jnp.bfloat16

ORDER = ((3, 2, 1, 0), (3, 2, 0, 1), (0, 1, 3, 2), (0, 1, 2, 3))
GATHER = ((0, 1, 2, 3), (1, 0, 2, 3), (2, 3, 1, 0), (3, 2, 1, 0))


def matmul_kernel(place_ref, acts_ref, *refs, parts, chunks, width):
    cot_refs, outs = refs[:parts], refs[parts : parts + chunks]
    max_ref, cot = refs[parts + chunks], refs[parts + chunks + 1]
    rows = cot_refs[0].shape[0]

    @pl.when(pl.program_id(0) == 0)
    def _():
        for k in range(parts):
            at = pl.multiple_of(place_ref[k] * rows, rows)
            cot[pl.ds(at, rows), :] = cot_refs[k][...]

    blocks = acts_ref.shape[0] // BLOCK
    for j in range(chunks):
        columns = slice(j * width, (j + 1) * width)
        acc = jnp.dot(acts_ref[...], cot[:, columns], preferred_element_type=F32)
        outs[j][...] = acc.astype(BF16)
        max_ref[0, :, columns] = jnp.max(jnp.abs(acc).reshape(blocks, BLOCK, width), axis=1)


def partial_chunks(place, acts_t, cot_parts, chunks):
    rows, tokens = acts_t.shape
    parts = len(cot_parts)
    part_rows, columns = cot_parts[0].shape
    width = columns // chunks
    step = 512
    blocks = step // BLOCK
    grid_spec = pltpu.PrefetchScalarGridSpec(
        num_scalar_prefetch=1,
        grid=(rows // step,),
        in_specs=[pl.BlockSpec((step, tokens), lambda i, p: (i, 0))]
        + [pl.BlockSpec((part_rows, columns), lambda i, p: (0, 0))] * parts,
        out_specs=[pl.BlockSpec((step, width), lambda i, p: (i, 0))] * chunks
        + [pl.BlockSpec((1, blocks, columns), lambda i, p: (i, 0, 0))],
        scratch_shapes=[pltpu.VMEM((tokens, columns), BF16)],
    )
    out = pl.pallas_call(
        lambda *refs: matmul_kernel(*refs, parts=parts, chunks=chunks, width=width),
        grid_spec=grid_spec,
        out_shape=[jax.ShapeDtypeStruct((rows, width), BF16)] * chunks
        + [jax.ShapeDtypeStruct((rows // step, blocks, columns), F32)],
        compiler_params=pltpu.CompilerParams(vmem_limit_bytes=40 * 1024 * 1024),
        cost_estimate=pl.CostEstimate(
            flops=2 * rows * tokens * columns,
            bytes_accessed=2 * (rows * tokens + tokens * columns + rows * columns),
            transcendentals=0,
        ),
        name="partials",
    )(place, acts_t, *cot_parts)
    maxima = out[chunks].reshape(rows // BLOCK, chunks, width // BLOCK, BLOCK).max(axis=3)
    return out[:chunks], maxima


def body(acts, cotangent, master, first_moment, second_moment):
    n_dp = lax.axis_size("dp")
    n_tensor = lax.axis_size("tensor")
    n_x = n_dp // Z
    owner = lax.axis_index("dp")
    z, x = owner // n_x, owner % n_x
    seat = lax.axis_index("tensor")
    rows, columns = acts.shape[1], cotangent.shape[1]
    width = columns // n_dp

    def z_perm(value, pairs):
        return lax.ppermute(value, "dp", [(a * n_x + i, b * n_x + i) for a, b in pairs for i in range(n_x)])

    def x_perm(value, by):
        return lax.ppermute(value, "dp", [(a * n_x + i, a * n_x + (i + by) % n_x) for a in range(Z) for i in range(n_x)])

    def seat_perm(value, flip):
        return lax.ppermute(value, "tensor", [(i, i ^ flip) for i in range(n_tensor)])

    def table(entries):
        return jnp.asarray(entries, jnp.int32)[z]

    order = [table([ORDER[a][i] for a in range(Z)]) for i in range(Z)]

    def column_of(slot, by):
        return (order[slot] * n_x + (x + by) % n_x) * width

    others = range(1, n_x)
    pieces = [
        [(0, by) for by in others],
        [(0, 0)] + [(1, by) for by in others],
        [(1, 0)] + [(2, by) for by in others] + [(2, 0)] + [(3, by) for by in others] + [(3, 0)],
    ]
    place = jnp.stack([seat ^ k for k in range(n_tensor)]).astype(jnp.int32)
    acts_t = lax.optimization_barrier(acts.T)

    partial, maxima, before = {}, {}, None
    for piece in pieces:
        own = jnp.concatenate(
            [lax.dynamic_slice_in_dim(cotangent, column_of(*at), width, 1) for at in piece], axis=1
        )
        if before is not None:
            own, before = lax.optimization_barrier((own, before))
        across = [own] + [seat_perm(own, k) for k in range(2, n_tensor, 2)]
        before = across[-1]
        cot_parts = [part for near in across for part in (near, seat_perm(near, 1))]
        chunks, block_max = partial_chunks(place, acts_t, cot_parts, len(piece))
        for j, at in enumerate(piece):
            partial[at] = chunks[j]
            maxima[at] = block_max[:, j]

    summed = []
    for i in range(Z):
        total = partial[i, 0].astype(F32)
        for by in others:
            total = total + x_perm(partial[i, by], by).astype(F32)
        summed.append(total)

    ends = (z == 0) | (z == Z - 1)
    first = z_perm(summed[0].astype(BF16), [(0, 1), (3, 2)])
    middle = jnp.where(ends, summed[1], summed[0] + first.astype(F32)).astype(BF16)
    up = z_perm(middle, [(0, 1), (1, 2)])
    down = z_perm(middle, [(3, 2), (2, 1)])
    up = z_perm((jnp.where(z == 1, summed[1], summed[2]) + up.astype(F32)).astype(BF16), [(0, 1), (1, 2), (2, 3)])
    down = z_perm((jnp.where(z == 2, summed[1], summed[2]) + down.astype(F32)).astype(BF16), [(3, 2), (2, 1), (1, 0)])
    total = summed[3] + up.astype(F32) + down.astype(F32)

    slots = [(i, by) for i in range(Z) for by in range(n_x)]
    scales = jnp.zeros((rows // BLOCK, columns // BLOCK), F32)
    for at in slots:
        scales = lax.dynamic_update_slice_in_dim(scales, maxima[at], column_of(*at) // BLOCK, 1)
    mine = scales
    for by in others:
        scales = jnp.maximum(scales, x_perm(mine, by))
    scales = jnp.maximum(scales, z_perm(scales, [(a, a ^ 1) for a in range(Z)]))
    scales = jnp.maximum(scales, z_perm(scales, [(a, a ^ 2) for a in range(Z)]))
    block_scales = scales + 1e-06

    gradient = total * (1.0 / math.sqrt(acts.shape[0] * n_dp))
    new_first = 0.9 * first_moment + 0.1 * gradient
    new_second = 0.95 * second_moment + 0.05 * gradient * gradient
    first_hat = new_first / (1.0 - 0.9**10)
    second_hat = new_second / (1.0 - 0.95**10)
    new_master = master * (1.0 - 0.01 * 0.1) - 0.01 * first_hat / (jnp.sqrt(second_hat) + 1e-08)
    owned = new_master.astype(BF16)

    up1 = z_perm(owned, [(0, 1), (1, 2), (2, 3)])
    down1 = z_perm(owned, [(3, 2), (2, 1), (1, 0)])
    up2 = z_perm(up1, [(1, 2), (2, 3)])
    down2 = z_perm(down1, [(2, 1), (1, 0)])
    far2 = jnp.where(z >= 2, up2, down2)
    far3 = z_perm(far2, [(2, 3), (1, 0)])
    held = [
        owned,
        jnp.where(z % 2 == 1, up1, down1),
        jnp.where(ends, far2, jnp.where(z == 1, down1, up1)),
        jnp.where(ends, far3, far2),
    ]
    weights = jnp.zeros((rows, columns), BF16)
    for i in range(Z):
        at = table([GATHER[a][i] for a in range(Z)])
        weights = lax.dynamic_update_slice_in_dim(weights, held[i], (at * n_x + x) * width, 1)
        for by in others:
            got = x_perm(held[i], by)
            weights = lax.dynamic_update_slice_in_dim(weights, got, (at * n_x + (x - by) % n_x) * width, 1)
    return (new_master, new_first, new_second, weights, block_scales)


def solution(mesh):
    in_specs = (
        P("dp", "tensor"),
        P(("dp", "tensor"), None),
        P("tensor", "dp"),
        P("tensor", "dp"),
        P("tensor", "dp"),
    )
    out_specs = (
        P("tensor", "dp"),
        P("tensor", "dp"),
        P("tensor", "dp"),
        P("tensor", None),
        P("tensor", None),
    )
    return jax.shard_map(body, mesh=mesh, in_specs=in_specs, out_specs=out_specs, check_vma=False)
```

time: 445 us -> 275 us (0.62)
  waiting for transfers between devices: 306 us -> 149 us
  starting transfers between devices: 0.12 us -> 44.3 us
  blocking collectives: 21.8 us -> 0 us
  Pallas kernels: 0 us -> 21 us
  matrix products: 17.5 us -> 0 us
  local copies, waits for them, and re-layouts: 52.6 us -> 35.5 us
  other arithmetic: 33.4 us -> 21 us
  between operations: 13.8 us -> 3.1 us
    all_gather x2 -> x0, waiting for transfers between devices: 175 us -> none  [the longest x1 125 us: body(): weights = lax.all_gather(owned_weights, 'dp', axis=1, tiled=True)]
    ppermute x0 -> x30, waiting for transfers between devices: none -> 149 us  [the longest x9 76 us: x_perm(): lax.ppermute(value, 'dp', [(a * n_x + i, a * n_x + (i + by) % n_x) for a...]
    reduce_scatter x1 -> x0, waiting for transfers between devices: 130 us -> none  [body(): lax.psum_scatter(quantized.astype(jnp.float32).astype(jnp.bfloat16), 'dp'...]
    ppermute x0 -> x30, starting transfers between devices: none -> 44.3 us  [the longest x12 28.3 us: z_perm(): lax.ppermute(value, 'dp', [(a * n_x + i, b * n_x + i) for a, b in pairs f...]
    unnamed x11 -> x33, local copies, waits for them, and re-layouts: 47.9 us -> 23 us
    pmax x1 -> x0, blocking collectives: 21.8 us -> none  [body(): block_scales = lax.pmax(local_max, 'dp') + 1e-06]
    pallas_call x0 -> x3, Pallas kernels: none -> 21 us  [partial_chunks(): pl.pallas_call(lambda *refs: matmul_kernel(*refs, parts=parts, chunks=chu...]
    dot_general x1 -> x0, matrix products: 17.5 us -> none  [contract_rows(): lax.dot_general(left, right, (((0,), (0,)), ((), ())), preferred_element_...]
  transfers between devices with their start and end apart: 3 -> 30, of which waited for: 3 -> 19; matrix products, arithmetic and copies ran while one was open for 4% -> 9% of each run, Pallas kernels for 0% -> 8%
where the time goes in v1:
time: 275 us; the launch traced here: 274 us
  waiting for transfers between devices  149 us (54%)
  starting transfers between devices  44.3 us (16%)
  local copies, waits for them, and re-layouts  35.5 us (13%)
  other arithmetic  21 us (8%)
  Pallas kernels  21 us (8%)
  between operations  3.1 us (1%)
    ppermute x9, waiting for transfers between devices, x_perm(): lax.ppermute(value, 'dp', [(a * n_x + i, a * n_x + (i + by) % n_x) for a...  76 us
    ppermute x12, waiting for transfers between devices, z_perm(): lax.ppermute(value, 'dp', [(a * n_x + i, b * n_x + i) for a, b in pairs f...  53.3 us
    ppermute x12, starting transfers between devices, z_perm(): lax.ppermute(value, 'dp', [(a * n_x + i, b * n_x + i) for a, b in pairs f...  28.3 us
    unnamed x33, local copies, waits for them, and re-layouts  23 us
    pallas_call x3, Pallas kernels, partial_chunks(): pl.pallas_call(lambda *refs: matmul_kernel(*refs, parts=parts, chunks=chu...  21 us
    ppermute x9, waiting for transfers between devices, seat_perm(): lax.ppermute(value, 'tensor', [(i, i ^ flip) for i in range(n_tensor)])  19.8 us
    dynamic_update_slice x4, other arithmetic, body(): lax.dynamic_update_slice_in_dim(weights, held[i], (at * n_x + x) * width, 1)  11.5 us
    ppermute x9, starting transfers between devices, x_perm(): lax.ppermute(value, 'dp', [(a * n_x + i, a * n_x + (i + by) % n_x) for a...  9.44 us
  transfers between devices with their start and end apart: 30, of which 19 were waited for; matrix products, arithmetic and copies ran while one was open for 9% of the time, Pallas kernels for 8%

profile of v1, /device:TPU:0, one launch (start us, length us, event | category | flops | bytes accessed | tf_op | source)
XLA Modules:
  0.0 274.2 jit_solution(8060432956145472176)
XLA Ops:
  0.7 1.2 dynamic_slice.50
  2.6 1.2 dynamic_slice.48
  4.5 1.2 dynamic_slice.56
  6.5 1.1 dynamic-slice_dynamic-update-slice_fusion.4
  7.6 0.9 dynamic-slice_dynamic-update-slice_fusion.3
  8.5 0.9 dynamic-slice_dynamic-update-slice_fusion.2
  9.5 0.9 dynamic-slice_dynamic-update-slice_fusion.1
  10.5 3.0 %collective-permute-start = (bf16[384,256]{1,0:T(8,128)(2,1)S(1)}, bf16[384,256]{1,0:T(8,128)(2,1)S(1)}, u32[]{:S(2)}, u32[]{:S(2)}) collective-permute-start(bf16[384,256]{1,0:T(8,128)(2,1)S(1)} %get-tuple-element.47.refs_2_), channel_id=1, source_target_pairs={{0,2},{1,3},{2,0},{3,1},{4,6},{5,7},{6,4},{7,5},{8,10},{9,11},{10,... | collective-permute-start | bytes 589832 | tf_op jit(solution)/shard_map/ppermute | solution.py:88
  13.6 4.9 %collective-permute-done.refs_4_ = bf16[384,256]{1,0:T(8,128)(2,1)S(1)} collective-permute-done((bf16[384,256]{1,0:T(8,128)(2,1)S(1)}, bf16[384,256]{1,0:T(8,128)(2,1)S(1)}, u32[]{:S(2)}, u32[]{:S(2)}) %collective-permute-start) | collective-permute-done | bytes 196640 | tf_op jit(solution)/shard_map/ppermute | solution.py:88
  18.5 1.7 collective-permute-start.1
  20.7 8.6 %copy.26 = bf16[1536,2048]{0,1:T(8,128)(2,1)} copy(bf16[1536,2048]{1,0:T(8,128)(2,1)} %param.13) | data formatting | bytes 12582912 | tf_op args[0]
  29.3 0.9 collective-permute-start.3
  30.3 2.8 %copy-done = bf16[1536,2048]{0,1:T(8,128)(2,1)S(1)} copy-done((bf16[1536,2048]{0,1:T(8,128)(2,1)S(1)}, bf16[1536,2048]{0,1:T(8,128)(2,1)}, u32[]{:S(2)}) %copy-start) | copy-done | bytes 6291480
  33.1 3.0 %partials.5 = (bf16[2048,256]{1,0:T(8,128)(2,1)S(1)}, f32[4,4,256]{2,1,0:T(4,128)S(1)}) custom-call(s32[4]{0:T(128)S(1)} %pad_add_fusion.refs_0_, bf16[2048,1536]{1,0:T(8,128)(2,1)S(1)} %bitcast.16, bf16[384,256]{1,0:T(8,128)(2,1)S(1)} %get-tuple-element.47.refs_2_, bf16[384,256]{1,0:T(8,128)(2,1)S(1)} %collective-permute-done.10.refs_3_, ...), custom_call_target="tpu_custom_call" | custom-call | flops 1610612736 | bytes 8126464 | tf_op jit(solution)/shard_map/partials/pallas_call | solution.py:54
  36.1 1.6 collective-permute-start.12
  38.2 15.0 %collective-permute-done.3.refs_4_ = bf16[384,1280]{1,0:T(8,128)(2,1)} collective-permute-done((bf16[384,1280]{1,0:T(8,128)(2,1)S(1)}, bf16[384,1280]{1,0:T(8,128)(2,1)}, u32[]{:S(2)}, u32[]{:S(2)}) %collective-permute-start.3) | collective-permute-done | bytes 983072 | tf_op jit(solution)/shard_map/ppermute | solution.py:88
  53.1 5.4 %partials.4 = (bf16[2048,256]{1,0:T(8,128)(2,1)S(1)}, bf16[2048,256]{1,0:T(8,128)(2,1)}, f32[4,4,512]{2,1,0:T(4,128)S(1)}) custom-call(s32[4]{0:T(128)S(1)} %pad_add_fusion.refs_0_, bf16[2048,1536]{1,0:T(8,128)(2,1)S(1)} %bitcast.17, bf16[384,512]{1,0:T(8,128)(2,1)S(1)} %pad_maximum_fusion.refs_2_, bf16[384,512]{1,0:T(8,128)(2,1)S(1)} %collective-permute-done.6.refs_3_, ...), custom_call_target="tpu_custom_call" | custom-call | flops 3221225472 | bytes 9961472 | tf_op jit(solution)/shard_map/partials/pallas_call | solution.py:54
  58.5 1.5 collective-permute-start.8
  60.4 1.0 copy-done.7
  61.3 1.3 fusion
  62.6 4.7 %collective-permute-start.13 = (bf16[2048,256]{1,0:T(8,128)(2,1)}, bf16[2048,256]{1,0:T(8,128)(2,1)}, u32[]{:S(2)}, u32[]{:S(2)}) collective-permute-start(bf16[2048,256]{1,0:T(8,128)(2,1)} %fusion), channel_id=1, source_target_pairs={{0,8},{4,12},{24,16},{28,20},{1,9},{5,13},{25,17},{29,21},{2,10},{... | collective-permute-start | bytes 3145736 | tf_op jit(solution)/shard_map/ppermute | solution.py:82
  67.3 1.2 copy-done.4
  68.5 12.6 %partials.3 = (bf16[2048,256]{1,0:T(8,128)(2,1)S(1)}, bf16[2048,256]{1,0:T(8,128)(2,1)}, bf16[2048,256]{1,0:T(8,128)(2,1)S(1)}, bf16[2048,256]{1,0:T(8,128)(2,1)...) custom-call(s32[4]{0:T(128)S(1)} %pad_add_fusion.refs_0_, bf16[2048,1536]{1,0:T(8,128)(2,1)} %bitcast.15, ...), custom_call_target="tpu_custom_call" | custom-call | flops 8053063680 | bytes 15466496 | tf_op jit(solution)/shard_map/partials/pallas_call | solution.py:54
  81.1 1.5 collective-permute-start.9
  82.6 2.2 collective-permute-done.8
  84.8 4.0 %collective-permute-done.13 = bf16[2048,256]{1,0:T(8,128)(2,1)} collective-permute-done((bf16[2048,256]{1,0:T(8,128)(2,1)}, bf16[2048,256]{1,0:T(8,128)(2,1)}, u32[]{:S(2)}, u32[]{:S(2)}) %collective-permute-start.13) | collective-permute-done | bytes 1048608 | tf_op jit(solution)/shard_map/ppermute | solution.py:82
  88.9 3.2 %select_convert_fusion = bf16[2048,256]{1,0:T(8,128)(2,1)} fusion(bf16[2048,256]{1,0:T(8,128)(2,1)} %collective-permute-done.13, bf16[2048,256]{1,0:T(8,128)(2,1)S(1)} %copy-done.8, bf16[2048,256]{1,0:T(8,128)(2,1)S(1)} %get-tuple-element.26, bf16[2048,256]{1,0:T(8,128)(2,1)} %collective-permute-done.8, bf16[2048,256]{1,0:T(8,128)(2,1)S(1)} %get-tuple-element.22, ...), kind=kLoop, calls=%fused_computation.6 | loop fusion | flops 5242880 | bytes 6291457 | tf_op jit(solution)/shard_map/convert_element_type | solution.py:131
  92.0 0.7 collective-permute-start.16
  92.8 5.9 %collective-permute-start.14 = (bf16[2048,256]{1,0:T(8,128)(2,1)}, bf16[2048,256]{1,0:T(8,128)(2,1)}, u32[]{:S(2)}, u32[]{:S(2)}) collective-permute-start(bf16[2048,256]{1,0:T(8,128)(2,1)} %select_convert_fusion), channel_id=1, source_target_pairs={{0,8},{4,12},{8,16},{12,20},{1,9},{5,13},{9,17},{13,21},{2,10},{6,... | collective-permute-start | bytes 3145736 | tf_op jit(solution)/shard_map/ppermute | solution.py:82
  99.2 8.3 %collective-permute-done.9 = bf16[2048,256]{1,0:T(8,128)(2,1)} collective-permute-done((bf16[2048,256]{1,0:T(8,128)(2,1)}, bf16[2048,256]{1,0:T(8,128)(2,1)}, u32[]{:S(2)}, u32[]{:S(2)}) %collective-permute-start.9) | collective-permute-done | bytes 1048608 | tf_op jit(solution)/shard_map/ppermute | solution.py:85
  107.5 11.8 %collective-permute-done.14 = bf16[2048,256]{1,0:T(8,128)(2,1)} collective-permute-done((bf16[2048,256]{1,0:T(8,128)(2,1)}, bf16[2048,256]{1,0:T(8,128)(2,1)}, u32[]{:S(2)}, u32[]{:S(2)}) %collective-permute-start.14) | collective-permute-done | bytes 1048608 | tf_op jit(solution)/shard_map/ppermute | solution.py:82
  119.4 4.0 %add_convert_fusion.1 = (bf16[2048,256]{1,0:T(8,128)(2,1)}, bf16[2048,256]{1,0:T(8,128)(2,1)S(1)}) fusion(bf16[2048,256]{1,0:T(8,128)(2,1)} %collective-permute-done.14, bf16[2048,256]{1,0:T(8,128)(2,1)} %collective-permute-done.9, bf16[2048,256]{1,0:T(8,128)(2,1)S(1)} %get-tuple-element.24, bf16[2048,256]{1,0:T(8,128)(2,1)} %collective-permute-done.8, ...), kind=kLoop, calls=%fused_computation.5 | loop fusion | flops 7340032 | bytes 8388610 | tf_op jit(solution)/shard_map/convert_element_type | solution.py:134
  123.4 4.4 %collective-permute-start.15 = (bf16[2048,256]{1,0:T(8,128)(2,1)}, bf16[2048,256]{1,0:T(8,128)(2,1)S(1)}, u32[]{:S(2)}, u32[]{:S(2)}) collective-permute-start(bf16[2048,256]{1,0:T(8,128)(2,1)} %get-tuple-element.43), channel_id=1, source_target_pairs={{0,8},{4,12},{8,16},{12,20},{16,24},{20,28},{1,9},{5,13},{9,17},{1... | collective-permute-start | bytes 3145736 | tf_op jit(solution)/shard_map/ppermute | solution.py:82
  127.9 1.3 collective-permute-start.17
  129.4 19.2 %collective-permute-done.15 = bf16[2048,256]{1,0:T(8,128)(2,1)S(1)} collective-permute-done((bf16[2048,256]{1,0:T(8,128)(2,1)}, bf16[2048,256]{1,0:T(8,128)(2,1)S(1)}, u32[]{:S(2)}, u32[]{:S(2)}) %collective-permute-start.15) | collective-permute-done | bytes 1048608 | tf_op jit(solution)/shard_map/ppermute | solution.py:82
  148.5 4.1 %collective-permute-done.17 = bf16[2048,256]{1,0:T(8,128)(2,1)S(1)} collective-permute-done((bf16[2048,256]{1,0:T(8,128)(2,1)S(1)}, bf16[2048,256]{1,0:T(8,128)(2,1)S(1)}, u32[]{:S(2)}, u32[]{:S(2)}) %collective-permute-start.17) | collective-permute-done | bytes 1048608 | tf_op jit(solution)/shard_map/ppermute | solution.py:82
  152.7 1.1 broadcast_in_dim.6
  153.9 0.7 copy-done.9
  155.9 6.0 %constant_dynamic-update-slice_fusion.7 = (bf16[2048,2048]{1,0:T(8,128)(2,1)S(1)}, bf16[2048,256]{1,0:T(8,128)(2,1)}, f32[2048,256]{1,0:T(8,128)}, f32[2048,256]{1,0:T(8,128)}, f32[2048,256]{1,0:T(8,128)}) fusion(bf16[2048,2048]{1,0:T(8,128)(2,1)S(1)} %broadcast_in_dim.6, s32[]{:T(128)S(6)} %select_n.232, f32[2048,256]{1,0:T(8,128)S(1)} %copy-done.9, ...), kind=kLoop, calls=%fused_computation.29 | loop fusion | flops 11534336 | bytes 18874372 | tf_op jit(solution)/shard_map/dynamic_update_slice | solution.py:172
  161.8 3.4 %copy-done.6 = bf16[2048,2048]{1,0:T(8,128)(2,1)} copy-done((bf16[2048,2048]{1,0:T(8,128)(2,1)}, bf16[2048,2048]{1,0:T(8,128)(2,1)S(1)}, u32[]{:S(2)}) %copy-start.6) | copy-done | bytes 8388632
  165.2 3.7 %collective-permute-start.19 = (bf16[2048,256]{1,0:T(8,128)(2,1)}, bf16[2048,256]{1,0:T(8,128)(2,1)S(1)}, u32[]{:S(2)}, u32[]{:S(2)}) collective-permute-start(bf16[2048,256]{1,0:T(8,128)(2,1)} %get-tuple-element.39), channel_id=1, source_target_pairs={{0,8},{4,12},{8,16},{12,20},{16,24},{20,28},{1,9},{5,13},{9,17},{1... | collective-permute-start | bytes 3145736 | tf_op jit(solution)/shard_map/ppermute | solution.py:82
  168.9 1.3 collective-permute-start.20
  170.3 16.9 %collective-permute-done.18 = bf16[2048,256]{1,0:T(8,128)(2,1)S(1)} collective-permute-done((bf16[2048,256]{1,0:T(8,128)(2,1)}, bf16[2048,256]{1,0:T(8,128)(2,1)S(1)}, u32[]{:S(2)}, u32[]{:S(2)}) %collective-permute-start.18) | collective-permute-done | bytes 1048608 | tf_op jit(solution)/shard_map/ppermute | solution.py:85
  187.2 1.0 constant_dynamic-update-slice_fusion.6
  188.2 4.0 %collective-permute-done.20 = bf16[2048,256]{1,0:T(8,128)(2,1)S(1)} collective-permute-done((bf16[2048,256]{1,0:T(8,128)(2,1)}, bf16[2048,256]{1,0:T(8,128)(2,1)S(1)}, u32[]{:S(2)}, u32[]{:S(2)}) %collective-permute-start.20) | collective-permute-done | bytes 1048608 | tf_op jit(solution)/shard_map/ppermute | solution.py:82
  192.2 1.2 constant_dynamic-update-slice_fusion.5
  193.4 1.7 collective-permute-start.21
  195.2 1.7 collective-permute-start.22
  196.8 1.5 collective-permute-start.23
  198.3 15.4 %collective-permute-done.21 = bf16[2048,256]{1,0:T(8,128)(2,1)} collective-permute-done((bf16[2048,256]{1,0:T(8,128)(2,1)S(1)}, bf16[2048,256]{1,0:T(8,128)(2,1)}, u32[]{:S(2)}, u32[]{:S(2)}) %collective-permute-start.21) | collective-permute-done | bytes 1048608 | tf_op jit(solution)/shard_map/ppermute | solution.py:85
  213.8 2.3 constant_dynamic-update-slice_fusion.4
  216.0 3.1 %collective-permute-done.23 = bf16[2048,256]{1,0:T(8,128)(2,1)} collective-permute-done((bf16[2048,256]{1,0:T(8,128)(2,1)S(1)}, bf16[2048,256]{1,0:T(8,128)(2,1)}, u32[]{:S(2)}, u32[]{:S(2)}) %collective-permute-start.23) | collective-permute-done | bytes 1048608 | tf_op jit(solution)/shard_map/ppermute | solution.py:82
  219.1 3.1 %constant_dynamic-update-slice_fusion.3 = (bf16[2048,2048]{1,0:T(8,128)(2,1)}, bf16[2048,256]{1,0:T(8,128)(2,1)}, bf16[2048,256]{1,0:T(8,128)(2,1)S(1)}) fusion(bf16[2048,2048]{1,0:T(8,128)(2,1)} %constant_dynamic-update-slice_fusion.4, s32[]{:T(128)S(6)} %select_n.244, bf16[2048,256]{1,0:T(8,128)(2,1)S(1)} %collective-permute-done.20, ...), kind=kLoop, calls=%fused_computation.25 | loop fusion | flops 1572864 | bytes 7340039 | tf_op jit(solution)/shard_map/dynamic_update_slice | solution.py:172
  222.7 1.3 collective-permute-start.25
  224.0 18.2 %collective-permute-done.24 = bf16[2048,256]{1,0:T(8,128)(2,1)S(1)} collective-permute-done((bf16[2048,256]{1,0:T(8,128)(2,1)}, bf16[2048,256]{1,0:T(8,128)(2,1)S(1)}, u32[]{:S(2)}, u32[]{:S(2)}) %collective-permute-start.24) | collective-permute-done | bytes 1048608 | tf_op jit(solution)/shard_map/ppermute | solution.py:85
  242.3 1.0 constant_dynamic-update-slice_fusion.2
  243.9 1.2 constant_dynamic-update-slice_fusion.1
  245.1 1.2 collective-permute-start.26
  249.0 0.9 collective-permute-start.27
  249.9 14.5 %collective-permute-done.27 = f32[16,16]{1,0:T(8,128)S(1)} collective-permute-done((f32[16,16]{1,0:T(8,128)S(1)}, f32[16,16]{1,0:T(8,128)S(1)}, u32[]{:S(2)}, u32[]{:S(2)}) %collective-permute-start.27) | collective-permute-done | bytes 1056 | tf_op jit(solution)/shard_map/ppermute | solution.py:85
  264.4 1.5 collective-permute-start.28
  265.8 2.2 collective-permute-done.28
  268.3 4.2 %collective-permute-done.29 = f32[16,16]{1,0:T(8,128)S(1)} collective-permute-done((f32[16,16]{1,0:T(8,128)S(1)}, f32[16,16]{1,0:T(8,128)S(1)}, u32[]{:S(2)}, u32[]{:S(2)}) %collective-permute-start.29) | collective-permute-done | bytes 1056 | tf_op jit(solution)/shard_map/ppermute | solution.py:82
  273.2 1.0 constant_dynamic-update-slice_fusion
  (70 shorter events, 8.5 us)
Async XLA Ops:
  6.5 3.9 %copy-start.12 = (bf16[384,2048]{1,0:T(8,128)(2,1)S(1)}, bf16[384,2048]{1,0:T(8,128)(2,1)}, u32[]{:S(2)}) copy-start(bf16[384,2048]{1,0:T(8,128)(2,1)} %param.14) | copy-start | bytes 4718596
  10.5 27.6 %copy-start.3 = (bf16[384,1280]{1,0:T(8,128)(2,1)}, bf16[384,1280]{1,0:T(8,128)(2,1)S(1)}, u32[]{:S(2)}) copy-start(bf16[384,1280]{1,0:T(8,128)(2,1)S(1)} %get-tuple-element.19.refs_2_) | copy-start | bytes 2949124
  10.5 7.9 %collective-permute-start = (bf16[384,256]{1,0:T(8,128)(2,1)S(1)}, bf16[384,256]{1,0:T(8,128)(2,1)S(1)}, u32[]{:S(2)}, u32[]{:S(2)}) collective-permute-start(bf16[384,256]{1,0:T(8,128)(2,1)S(1)} %get-tuple-element.47.refs_2_), channel_id=1, source_target_pairs={{0,2},{1,3},{2,0},{3,1},{4,6},{5,7},{6,4},{7,5},{8,10},{9,11},{10,... | collective-permute-start | bytes 589832 | tf_op jit(solution)/shard_map/ppermute | solution.py:88
  18.5 10.9 %collective-permute-start.1 = (bf16[384,512]{1,0:T(8,128)(2,1)S(1)}, bf16[384,512]{1,0:T(8,128)(2,1)S(1)}, u32[]{:S(2)}, u32[]{:S(2)}) collective-permute-start(bf16[384,512]{1,0:T(8,128)(2,1)S(1)} %pad_maximum_fusion.refs_2_), channel_id=1, source_target_pairs={{0,2},{1,3},{2,0},{3,1},{4,6},{5,7},{6,4},{7,5},{8,10},{9,11},{10,... | collective-permute-start | bytes 1179656 | tf_op jit(solution)/shard_map/ppermute | solution.py:88
  20.2 10.1 %collective-permute-start.10 = (bf16[384,256]{1,0:T(8,128)(2,1)S(1)}, bf16[384,256]{1,0:T(8,128)(2,1)S(1)}, u32[]{:S(2)}, u32[]{:S(2)}) collective-permute-start(bf16[384,256]{1,0:T(8,128)(2,1)S(1)} %get-tuple-element.47.refs_2_), channel_id=1, source_target_pairs={{0,1},{1,0},{2,3},{3,2},{4,5},{5,4},{6,7},{7,6},{8,9},{9,8},{10,11... | collective-permute-start | bytes 589832 | tf_op jit(solution)/shard_map/ppermute | solution.py:88
  20.2 10.1 %collective-permute-start.11 = (bf16[384,256]{1,0:T(8,128)(2,1)S(1)}, bf16[384,256]{1,0:T(8,128)(2,1)S(1)}, u32[]{:S(2)}, u32[]{:S(2)}) collective-permute-start(bf16[384,256]{1,0:T(8,128)(2,1)S(1)} %collective-permute-done.refs_4_), channel_id=1, source_target_pairs={{0,1},{1,0},{2,3},{3,2},{4,5},{5,4},{6,7},{7,6},{8,9},{9,8},{10,11... | collective-permute-start | bytes 589832 | tf_op jit(solution)/shard_map/ppermute | solution.py:88
  29.3 23.8 %collective-permute-start.3 = (bf16[384,1280]{1,0:T(8,128)(2,1)S(1)}, bf16[384,1280]{1,0:T(8,128)(2,1)}, u32[]{:S(2)}, u32[]{:S(2)}) collective-permute-start(bf16[384,1280]{1,0:T(8,128)(2,1)S(1)} %get-tuple-element.19.refs_2_), channel_id=1, source_target_pairs={{0,2},{1,3},{2,0},{3,1},{4,6},{5,7},{6,4},{7,5},{8,10},{9,11},{10,... | collective-permute-start | bytes 2949128 | tf_op jit(solution)/shard_map/ppermute | solution.py:88
  30.3 2.8 %copy-start = (bf16[1536,2048]{0,1:T(8,128)(2,1)S(1)}, bf16[1536,2048]{0,1:T(8,128)(2,1)}, u32[]{:S(2)}) copy-start(bf16[1536,2048]{0,1:T(8,128)(2,1)} %copy.26) | copy-start | bytes 18874372
  36.1 24.3 %collective-permute-start.12 = (bf16[2048,256]{1,0:T(8,128)(2,1)S(1)}, bf16[2048,256]{1,0:T(8,128)(2,1)S(1)}, u32[]{:S(2)}, u32[]{:S(2)}) collective-permute-start(bf16[2048,256]{1,0:T(8,128)(2,1)S(1)} %get-tuple-element.27), channel_id=1, source_target_pairs={{0,4},{4,0},{8,12},{12,8},{16,20},{20,16},{24,28},{28,24},{1,5},{5... | collective-permute-start | bytes 3145736 | tf_op jit(solution)/shard_map/ppermute | solution.py:85
  37.6 15.5 %collective-permute-start.6 = (bf16[384,512]{1,0:T(8,128)(2,1)S(1)}, bf16[384,512]{1,0:T(8,128)(2,1)S(1)}, u32[]{:S(2)}, u32[]{:S(2)}) collective-permute-start(bf16[384,512]{1,0:T(8,128)(2,1)S(1)} %pad_maximum_fusion.refs_2_), channel_id=1, source_target_pairs={{0,1},{1,0},{2,3},{3,2},{4,5},{5,4},{6,7},{7,6},{8,9},{9,8},{10,11... | collective-permute-start | bytes 1179656 | tf_op jit(solution)/shard_map/ppermute | solution.py:88
  37.6 15.5 %collective-permute-start.7 = (bf16[384,512]{1,0:T(8,128)(2,1)S(1)}, bf16[384,512]{1,0:T(8,128)(2,1)S(1)}, u32[]{:S(2)}, u32[]{:S(2)}) collective-permute-start(bf16[384,512]{1,0:T(8,128)(2,1)S(1)} %collective-permute-done.1.refs_4_), channel_id=1, source_target_pairs={{0,1},{1,0},{2,3},{3,2},{4,5},{5,4},{6,7},{7,6},{8,9},{9,8},{10,11... | collective-permute-start | bytes 1179656 | tf_op jit(solution)/shard_map/ppermute | solution.py:88
  38.2 29.1 %collective-permute-start.2 = (bf16[384,1280]{1,0:T(8,128)(2,1)S(1)}, bf16[384,1280]{1,0:T(8,128)(2,1)}, u32[]{:S(2)}, u32[]{:S(2)}) collective-permute-start(bf16[384,1280]{1,0:T(8,128)(2,1)S(1)} %get-tuple-element.19.refs_2_), channel_id=1, source_target_pairs={{0,1},{1,0},{2,3},{3,2},{4,5},{5,4},{6,7},{7,6},{8,9},{9,8},{10,11... | collective-permute-start | bytes 2949128 | tf_op jit(solution)/shard_map/ppermute | solution.py:88
  53.1 14.2 %collective-permute-start.4 = (bf16[384,1280]{1,0:T(8,128)(2,1)}, bf16[384,1280]{1,0:T(8,128)(2,1)}, u32[]{:S(2)}, u32[]{:S(2)}) collective-permute-start(bf16[384,1280]{1,0:T(8,128)(2,1)} %collective-permute-done.3.refs_4_), channel_id=1, source_target_pairs={{0,1},{1,0},{2,3},{3,2},{4,5},{5,4},{6,7},{7,6},{8,9},{9,8},{10,11... | collective-permute-start | bytes 2949128 | tf_op jit(solution)/shard_map/ppermute | solution.py:88
  58.5 26.3 %collective-permute-start.8 = (bf16[2048,256]{1,0:T(8,128)(2,1)}, bf16[2048,256]{1,0:T(8,128)(2,1)}, u32[]{:S(2)}, u32[]{:S(2)}) collective-permute-start(bf16[2048,256]{1,0:T(8,128)(2,1)} %get-tuple-element.23), channel_id=1, source_target_pairs={{0,4},{4,0},{8,12},{12,8},{16,20},{20,16},{24,28},{28,24},{1,5},{5... | collective-permute-start | bytes 3145736 | tf_op jit(solution)/shard_map/ppermute | solution.py:85
  60.4 1.0 copy-start.7
  62.6 26.3 %collective-permute-start.13 = (bf16[2048,256]{1,0:T(8,128)(2,1)}, bf16[2048,256]{1,0:T(8,128)(2,1)}, u32[]{:S(2)}, u32[]{:S(2)}) collective-permute-start(bf16[2048,256]{1,0:T(8,128)(2,1)} %fusion), channel_id=1, source_target_pairs={{0,8},{4,12},{24,16},{28,20},{1,9},{5,13},{25,17},{29,21},{2,10},{... | collective-permute-start | bytes 3145736 | tf_op jit(solution)/shard_map/ppermute | solution.py:82
  67.3 1.2 copy-start.4
  68.5 20.4 %copy-start.8 = (bf16[2048,256]{1,0:T(8,128)(2,1)S(1)}, bf16[2048,256]{1,0:T(8,128)(2,1)}, u32[]{:S(2)}) copy-start(bf16[2048,256]{1,0:T(8,128)(2,1)} %copy-done.7) | copy-start | bytes 3145732
  81.1 10.9 %copy-start.1 = (bf16[2048,256]{1,0:T(8,128)(2,1)}, bf16[2048,256]{1,0:T(8,128)(2,1)S(1)}, u32[]{:S(2)}) copy-start(bf16[2048,256]{1,0:T(8,128)(2,1)S(1)} %get-tuple-element.20) | copy-start | bytes 3145732
  81.1 10.9 %copy-start.5 = (bf16[2048,256]{1,0:T(8,128)(2,1)}, bf16[2048,256]{1,0:T(8,128)(2,1)S(1)}, u32[]{:S(2)}) copy-start(bf16[2048,256]{1,0:T(8,128)(2,1)S(1)} %get-tuple-element.21) | copy-start | bytes 3145732
  81.1 26.4 %collective-permute-start.9 = (bf16[2048,256]{1,0:T(8,128)(2,1)}, bf16[2048,256]{1,0:T(8,128)(2,1)}, u32[]{:S(2)}, u32[]{:S(2)}) collective-permute-start(bf16[2048,256]{1,0:T(8,128)(2,1)} %get-tuple-element.25), channel_id=1, source_target_pairs={{0,4},{4,0},{8,12},{12,8},{16,20},{20,16},{24,28},{28,24},{1,5},{5... | collective-permute-start | bytes 3145736 | tf_op jit(solution)/shard_map/ppermute | solution.py:85
  92.0 15.5 %collective-permute-start.16 = (bf16[2048,256]{1,0:T(8,128)(2,1)}, bf16[2048,256]{1,0:T(8,128)(2,1)S(1)}, u32[]{:S(2)}, u32[]{:S(2)}) collective-permute-start(bf16[2048,256]{1,0:T(8,128)(2,1)} %select_convert_fusion), channel_id=1, source_target_pairs={{24,16},{28,20},{16,8},{20,12},{25,17},{29,21},{17,9},{21,13},{26,... | collective-permute-start | bytes 3145736 | tf_op jit(solution)/shard_map/ppermute | solution.py:82
  92.8 26.6 %collective-permute-start.14 = (bf16[2048,256]{1,0:T(8,128)(2,1)}, bf16[2048,256]{1,0:T(8,128)(2,1)}, u32[]{:S(2)}, u32[]{:S(2)}) collective-permute-start(bf16[2048,256]{1,0:T(8,128)(2,1)} %select_convert_fusion), channel_id=1, source_target_pairs={{0,8},{4,12},{8,16},{12,20},{1,9},{5,13},{9,17},{13,21},{2,10},{6,... | collective-permute-start | bytes 3145736 | tf_op jit(solution)/shard_map/ppermute | solution.py:82
  98.7 30.6 %collective-permute-start.5 = (bf16[2048,256]{1,0:T(8,128)(2,1)}, bf16[2048,256]{1,0:T(8,128)(2,1)}, u32[]{:S(2)}, u32[]{:S(2)}) collective-permute-start(bf16[2048,256]{1,0:T(8,128)(2,1)} %copy-done.5), channel_id=1, source_target_pairs={{0,4},{4,0},{8,12},{12,8},{16,20},{20,16},{24,28},{28,24},{1,5},{5... | collective-permute-start | bytes 3145736 | tf_op jit(solution)/shard_map/ppermute | solution.py:85
  107.5 11.9 %copy-start.13 = (bf16[2048,256]{1,0:T(8,128)(2,1)}, bf16[2048,256]{1,0:T(8,128)(2,1)S(1)}, u32[]{:S(2)}) copy-start(bf16[2048,256]{1,0:T(8,128)(2,1)S(1)} %collective-permute-done.16) | copy-start | bytes 3145732
  123.4 25.1 %collective-permute-start.15 = (bf16[2048,256]{1,0:T(8,128)(2,1)}, bf16[2048,256]{1,0:T(8,128)(2,1)S(1)}, u32[]{:S(2)}, u32[]{:S(2)}) collective-permute-start(bf16[2048,256]{1,0:T(8,128)(2,1)} %get-tuple-element.43), channel_id=1, source_target_pairs={{0,8},{4,12},{8,16},{12,20},{16,24},{20,28},{1,9},{5,13},{9,17},{1... | collective-permute-start | bytes 3145736 | tf_op jit(solution)/shard_map/ppermute | solution.py:82
  127.9 24.8 %collective-permute-start.17 = (bf16[2048,256]{1,0:T(8,128)(2,1)S(1)}, bf16[2048,256]{1,0:T(8,128)(2,1)S(1)}, u32[]{:S(2)}, u32[]{:S(2)}) collective-permute-start(bf16[2048,256]{1,0:T(8,128)(2,1)S(1)} %get-tuple-element.44), channel_id=1, source_target_pairs={{24,16},{28,20},{16,8},{20,12},{8,0},{12,4},{25,17},{29,21},{17,9}... | collective-permute-start | bytes 3145736 | tf_op jit(solution)/shard_map/ppermute | solution.py:82
  152.7 1.2 copy-start.2
  152.7 1.9 copy-start.9
  152.7 2.5 copy-start.10
  152.7 3.2 %copy-start.11 = (f32[2048,256]{1,0:T(8,128)S(1)}, f32[2048,256]{1,0:T(8,128)}, u32[]{:S(2)}) copy-start(f32[2048,256]{1,0:T(8,128)} %param.17) | copy-start | bytes 6291460
  161.8 3.4 %copy-start.6 = (bf16[2048,2048]{1,0:T(8,128)(2,1)}, bf16[2048,2048]{1,0:T(8,128)(2,1)S(1)}, u32[]{:S(2)}) copy-start(bf16[2048,2048]{1,0:T(8,128)(2,1)S(1)} %get-tuple-element.38) | copy-start | bytes 25165828
  165.2 21.9 %collective-permute-start.18 = (bf16[2048,256]{1,0:T(8,128)(2,1)}, bf16[2048,256]{1,0:T(8,128)(2,1)S(1)}, u32[]{:S(2)}, u32[]{:S(2)}) collective-permute-start(bf16[2048,256]{1,0:T(8,128)(2,1)} %get-tuple-element.39), channel_id=1, source_target_pairs={{0,4},{4,0},{8,12},{12,8},{16,20},{20,16},{24,28},{28,24},{1,5},{5... | collective-permute-start | bytes 3145736 | tf_op jit(solution)/shard_map/ppermute | solution.py:85
  165.2 23.0 %collective-permute-start.19 = (bf16[2048,256]{1,0:T(8,128)(2,1)}, bf16[2048,256]{1,0:T(8,128)(2,1)S(1)}, u32[]{:S(2)}, u32[]{:S(2)}) collective-permute-start(bf16[2048,256]{1,0:T(8,128)(2,1)} %get-tuple-element.39), channel_id=1, source_target_pairs={{0,8},{4,12},{8,16},{12,20},{16,24},{20,28},{1,9},{5,13},{9,17},{1... | collective-permute-start | bytes 3145736 | tf_op jit(solution)/shard_map/ppermute | solution.py:82
  168.9 23.3 %collective-permute-start.20 = (bf16[2048,256]{1,0:T(8,128)(2,1)}, bf16[2048,256]{1,0:T(8,128)(2,1)S(1)}, u32[]{:S(2)}, u32[]{:S(2)}) collective-permute-start(bf16[2048,256]{1,0:T(8,128)(2,1)} %get-tuple-element.39), channel_id=1, source_target_pairs={{24,16},{28,20},{16,8},{20,12},{8,0},{12,4},{25,17},{29,21},{17,9}... | collective-permute-start | bytes 3145736 | tf_op jit(solution)/shard_map/ppermute | solution.py:82
  193.4 20.3 %collective-permute-start.21 = (bf16[2048,256]{1,0:T(8,128)(2,1)S(1)}, bf16[2048,256]{1,0:T(8,128)(2,1)}, u32[]{:S(2)}, u32[]{:S(2)}) collective-permute-start(bf16[2048,256]{1,0:T(8,128)(2,1)S(1)} %get-tuple-element.37), channel_id=1, source_target_pairs={{0,4},{4,0},{8,12},{12,8},{16,20},{20,16},{24,28},{28,24},{1,5},{5... | collective-permute-start | bytes 3145736 | tf_op jit(solution)/shard_map/ppermute | solution.py:85
  195.2 20.9 %collective-permute-start.22 = (bf16[2048,256]{1,0:T(8,128)(2,1)S(1)}, bf16[2048,256]{1,0:T(8,128)(2,1)}, u32[]{:S(2)}, u32[]{:S(2)}) collective-permute-start(bf16[2048,256]{1,0:T(8,128)(2,1)S(1)} %collective-permute-done.19), channel_id=1, source_target_pairs={{8,16},{12,20},{16,24},{20,28},{9,17},{13,21},{17,25},{21,29},{10,... | collective-permute-start | bytes 3145736 | tf_op jit(solution)/shard_map/ppermute | solution.py:82
  196.8 22.3 %collective-permute-start.23 = (bf16[2048,256]{1,0:T(8,128)(2,1)S(1)}, bf16[2048,256]{1,0:T(8,128)(2,1)}, u32[]{:S(2)}, u32[]{:S(2)}) collective-permute-start(bf16[2048,256]{1,0:T(8,128)(2,1)S(1)} %collective-permute-done.20), channel_id=1, source_target_pairs={{16,8},{20,12},{8,0},{12,4},{17,9},{21,13},{9,1},{13,5},{18,10},{2... | collective-permute-start | bytes 3145736 | tf_op jit(solution)/shard_map/ppermute | solution.py:82
  222.2 20.1 %collective-permute-start.24 = (bf16[2048,256]{1,0:T(8,128)(2,1)}, bf16[2048,256]{1,0:T(8,128)(2,1)S(1)}, u32[]{:S(2)}, u32[]{:S(2)}) collective-permute-start(bf16[2048,256]{1,0:T(8,128)(2,1)} %get-tuple-element.34), channel_id=1, source_target_pairs={{0,4},{4,0},{8,12},{12,8},{16,20},{20,16},{24,28},{28,24},{1,5},{5... | collective-permute-start | bytes 3145736 | tf_op jit(solution)/shard_map/ppermute | solution.py:85
  222.7 21.2 %collective-permute-start.25 = (bf16[2048,256]{1,0:T(8,128)(2,1)S(1)}, bf16[2048,256]{1,0:T(8,128)(2,1)S(1)}, u32[]{:S(2)}, u32[]{:S(2)}) collective-permute-start(bf16[2048,256]{1,0:T(8,128)(2,1)S(1)} %get-tuple-element.35), channel_id=1, source_target_pairs={{16,24},{20,28},{8,0},{12,4},{17,25},{21,29},{9,1},{13,5},{18,26},... | collective-permute-start | bytes 3145736 | tf_op jit(solution)/shard_map/ppermute | solution.py:82
  245.1 28.0 %collective-permute-start.26 = (bf16[2048,256]{1,0:T(8,128)(2,1)S(1)}, bf16[2048,256]{1,0:T(8,128)(2,1)S(1)}, u32[]{:S(2)}, u32[]{:S(2)}) collective-permute-start(bf16[2048,256]{1,0:T(8,128)(2,1)S(1)} %get-tuple-element.32), channel_id=1, source_target_pairs={{0,4},{4,0},{8,12},{12,8},{16,20},{20,16},{24,28},{28,24},{1,5},{5... | collective-permute-start | bytes 3145736 | tf_op jit(solution)/shard_map/ppermute | solution.py:85
  249.0 15.3 %collective-permute-start.27 = (f32[16,16]{1,0:T(8,128)S(1)}, f32[16,16]{1,0:T(8,128)S(1)}, u32[]{:S(2)}, u32[]{:S(2)}) collective-permute-start(f32[16,16]{1,0:T(8,128)S(1)} %dynamic_update_slice.63), channel_id=1, source_target_pairs={{0,4},{4,0},{8,12},{12,8},{16,20},{20,16},{24,28},{28,24},{1,5},{5... | collective-permute-start | bytes 3080 | tf_op jit(solution)/shard_map/ppermute | solution.py:85
  264.4 3.7 %collective-permute-start.28 = (f32[16,16]{1,0:T(8,128)S(1)}, f32[16,16]{1,0:T(8,128)S(1)}, u32[]{:S(2)}, u32[]{:S(2)}) collective-permute-start(f32[16,16]{1,0:T(8,128)S(1)} %max.9), channel_id=1, source_target_pairs={{0,8},{4,12},{8,0},{12,4},{16,24},{20,28},{24,16},{28,20},{1,9},{5... | collective-permute-start | bytes 3080 | tf_op jit(solution)/shard_map/ppermute | solution.py:82
  268.0 4.5 %collective-permute-start.29 = (f32[16,16]{1,0:T(8,128)S(1)}, f32[16,16]{1,0:T(8,128)S(1)}, u32[]{:S(2)}, u32[]{:S(2)}) collective-permute-start(f32[16,16]{1,0:T(8,128)S(1)} %max.10), channel_id=1, source_target_pairs={{0,16},{4,20},{8,24},{12,28},{16,0},{20,4},{24,8},{28,12},{1,17},{... | collective-permute-start | bytes 3080 | tf_op jit(solution)/shard_map/ppermute | solution.py:82

commit v2 on v0

v2 whole, which is shorter than its diff:
```python
import math

import jax
import jax.numpy as jnp
from jax import lax
from jax.experimental import pallas as pl
from jax.experimental.pallas import tpu as pltpu
from jax.sharding import PartitionSpec as P

BLOCK = 128
Z = 4
F32 = jnp.float32
BF16 = jnp.bfloat16
VMEM = pl.BlockSpec(memory_space=pltpu.VMEM)
FREE = pl.CostEstimate(flops=0, bytes_accessed=0, transcendentals=0)

INWARDS = ((0, 1), (3, 2))
OUTWARDS = ((1, 0), (2, 3))
MIDDLE = ((1, 2), (2, 1))
PAIRS = ((0, 1), (1, 0), (2, 3), (3, 2))


def owner_z(z, slot):
    low = z < 2
    if slot == 3:
        return z
    if slot == 0:
        return jnp.where(low, 3, 0)
    end = (z == 0) | (z == Z - 1)
    two, one = jnp.where(low, 2, 1), jnp.where(end, jnp.where(low, 1, 2), jnp.where(low, 0, 3))
    return two if slot == 1 else one


def call(kernel, out_shape, operands, name):
    return pl.pallas_call(
        kernel,
        out_shape=list(out_shape),
        in_specs=[VMEM] * len(operands),
        out_specs=[VMEM] * len(out_shape),
        cost_estimate=FREE,
        name=name,
    )


def arrange(cot, pieces, width, n_x):
    def kernel(cot_ref, *outs):
        owner = lax.axis_index("dp")
        z, x = owner // n_x, owner % n_x
        for piece, out in zip(pieces, outs):
            for j, (slot, by) in enumerate(piece):
                at = pl.multiple_of((owner_z(z, slot) * n_x + (x + by) % n_x) * width, width)
                out[:, j * width : (j + 1) * width] = cot_ref[:, pl.ds(at, width)]

    shapes = [jax.ShapeDtypeStruct((cot.shape[0], len(piece) * width), BF16) for piece in pieces]
    return call(kernel, shapes, [cot], "arrange")(cot)


def multiply(acts_t, group, chunks, width):
    rows, tokens = acts_t.shape
    depth, columns = group[0].shape
    step = min(rows, 512)
    blocks = step // BLOCK

    def kernel(acts_ref, *refs):
        parts, outs, top, cot = refs[: len(group)], refs[len(group) : -2], refs[-2], refs[-1]

        @pl.when(pl.program_id(0) == 0)
        def _():
            seat = lax.axis_index("tensor")
            for k, part in enumerate(parts):
                cot[pl.ds(pl.multiple_of((seat ^ k) * depth, depth), depth), :] = part[...]

        for j, out in enumerate(outs):
            here = slice(j * width, (j + 1) * width)
            acc = jnp.dot(acts_ref[...], cot[:, here], preferred_element_type=F32)
            out[...] = acc.astype(BF16)
            top[0, :, here] = jnp.max(jnp.abs(acc).reshape(blocks, BLOCK, width), axis=1)

    out = pl.pallas_call(
        kernel,
        grid=(rows // step,),
        in_specs=[pl.BlockSpec((step, tokens), lambda i: (i, 0))]
        + [pl.BlockSpec((depth, columns), lambda i: (0, 0))] * len(group),
        out_specs=[pl.BlockSpec((step, width), lambda i: (i, 0))] * chunks
        + [pl.BlockSpec((1, blocks, columns), lambda i: (i, 0, 0))],
        out_shape=[jax.ShapeDtypeStruct((rows, width), BF16)] * chunks
        + [jax.ShapeDtypeStruct((rows // step, blocks, columns), F32)],
        scratch_shapes=[pltpu.VMEM((tokens, columns), BF16)],
        compiler_params=pltpu.CompilerParams(vmem_limit_bytes=48 * 1024 * 1024),
        cost_estimate=FREE,
        name="partials",
    )(acts_t, *group)
    return out[:chunks], out[chunks]


def add(terms):
    rows, columns = terms[0].shape
    step = 64

    def kernel(*refs):
        def one(i, carry):
            here = pl.ds(pl.multiple_of(i * step, step), step)
            total = refs[0][here, :].astype(F32)
            for ref in refs[1:-1]:
                total = total + ref[here, :].astype(F32)
            refs[-1][here, :] = total.astype(BF16)
            return carry

        lax.fori_loop(0, rows // step, one, 0, unroll=4)

    return call(kernel, [jax.ShapeDtypeStruct((rows, columns), BF16)], terms, "add")(*terms)[0]


def adamw(terms, states, factor):
    rows, width = states[0].shape
    rate = 0.01 / (1.0 - 0.9**10)
    spread = 1.0 / (1.0 - 0.95**10)
    step = 64

    def kernel(*refs):
        master_ref, first_ref, second_ref, new_master_ref, new_first_ref, new_second_ref, weights_ref = refs[len(terms) :]

        def one(i, carry):
            at = pl.ds(pl.multiple_of(i * step, step), step)
            total = refs[0][at, :].astype(F32)
            for ref in refs[1 : len(terms)]:
                total = total + ref[at, :].astype(F32)
            gradient = total * factor
            new_first = 0.9 * first_ref[at, :] + 0.1 * gradient
            new_second = 0.95 * second_ref[at, :] + (0.05 * gradient) * gradient
            hat = new_second * spread
            root = hat * lax.rsqrt(hat) + 1e-08
            inverse = pl.reciprocal(root, approx=True)
            inverse = inverse * (2.0 - root * inverse)
            new_master = master_ref[at, :] * (1.0 - 0.01 * 0.1) - (rate * new_first) * inverse
            new_master_ref[at, :] = new_master
            new_first_ref[at, :] = new_first
            new_second_ref[at, :] = new_second
            weights_ref[at, :] = new_master.astype(BF16)
            return carry

        lax.fori_loop(0, rows // step, one, 0, unroll=2)

    shapes = [jax.ShapeDtypeStruct((rows, width), F32)] * 3 + [jax.ShapeDtypeStruct((rows, width), BF16)]
    return call(kernel, shapes, list(terms) + list(states), "adamw")(*terms, *states)


def blank(shape, dtype):
    return pl.pallas_call(
        lambda ref: None,
        out_specs=pl.BlockSpec(memory_space=pl.ANY),
        out_shape=jax.ShapeDtypeStruct(shape, dtype),
        cost_estimate=FREE,
        name="blank",
    )()


def after(value, *earlier):
    return lax.optimization_barrier((value, *earlier))[0] if earlier else value


def body(acts, cotangent, master, first_moment, second_moment):
    n_dp = lax.axis_size("dp")
    n_tensor = lax.axis_size("tensor")
    n_x = n_dp // Z
    owner = lax.axis_index("dp")
    z, x = owner // n_x, owner % n_x
    rows, columns = acts.shape[1], cotangent.shape[1]
    width = columns // n_dp
    high = width // BLOCK
    others = range(1, n_x)

    def z_perm(value, pairs):
        return lax.ppermute(value, "dp", [(a * n_x + i, b * n_x + i) for a, b in pairs for i in range(n_x)])

    def x_perm(value, by, where=range(Z)):
        pairs = [(a * n_x + i, a * n_x + (i + by) % n_x) for a in where for i in range(n_x)]
        return lax.ppermute(value, "dp", pairs)

    def seat_perm(value, flip):
        return lax.ppermute(value, "tensor", [(i, i ^ flip) for i in range(n_tensor)])

    pieces = [[(0, by) for by in others]]
    pieces += [[(i, 0)] + [(i + 1, by) for by in others] for i in range(Z - 1)]
    pieces[-1].append((Z - 1, 0))
    own = arrange(cotangent, pieces, width, n_x)
    partial, tops, across = {}, [], []

    def fetch(piece, *earlier):
        value = after(own[piece], *earlier)
        across.append([value] + [seat_perm(value, k) for k in range(2, n_tensor, 2)])

    def partials(piece, *earlier):
        group = [part for value in across[piece] for part in (value, seat_perm(after(value, *earlier), 1))]
        chunks, top = multiply(after(acts_t, *earlier), group, len(pieces[piece]), width)
        partial.update(zip(pieces[piece], chunks))
        tops.append(top)
        return chunks[0]

    def send_x(slot, *earlier):
        return [x_perm(after(partial[slot, by], *earlier), by) for by in others]

    fetch(0)
    acts_t = after(acts, own[0]).T
    token = partials(0, acts_t)
    got0 = send_x(0)
    fetch(1, token)
    token = partials(1, token)
    fetch(2, token)
    got1 = send_x(1, *got0)
    sum0 = add([after(partial[0, 0], token), *got0])
    far = z_perm(sum0, INWARDS)
    token = partials(2, sum0)
    fetch(3, token)
    got2 = send_x(2, *got1, token)
    sum1 = add([after(partial[1, 0], token), *got1])
    inwards = z_perm(sum1, INWARDS)
    sum0 = add([after(partial[0, 0], sum1), *got0, far])
    middle = z_perm(sum0, MIDDLE)
    token = partials(3, sum0)

    top = jnp.concatenate([after(t, token).reshape(rows // BLOCK, -1, BLOCK).max(axis=2) for t in tops], axis=1)
    column = jnp.stack(
        [(owner_z(z, i) * n_x + (x + by) % n_x) * high + h for piece in pieces for i, by in piece for h in range(high)]
    )
    here = column[None, :, None] == jnp.arange(n_dp * high)[None, None, :]
    scales = jnp.max(jnp.where(here, top[:, :, None], 0.0), axis=1)
    scales_x = [x_perm(scales, by) for by in others]

    got3 = send_x(3, *got2, scales)
    for got in scales_x:
        scales = jnp.maximum(scales, got)
    sum2 = add([after(partial[2, 0], scales), *got2, middle])
    pairs = z_perm(sum2, PAIRS)
    sum1 = add([after(partial[1, 0], sum2), *got1, inwards])
    last = z_perm(sum1, MIDDLE)
    scales_z = z_perm(after(scales, sum1), PAIRS)

    scales = jnp.maximum(scales, scales_z)
    new_master, new_first, new_second, owned = adamw(
        [after(partial[3, 0], scales), *got3, pairs, last],
        [master, first_moment, second_moment],
        1.0 / math.sqrt(acts.shape[0] * n_dp),
    )

    weights = blank((rows, columns), BF16)
    low, between = z < 2, (z == 1) | (z == 2)
    sources = [z, z ^ 1, jnp.where(low, 2, 1), jnp.where(low, 3, 0)]
    over0 = [[x_perm(owned, by)] for by in others]
    pairs, mid = z_perm(owned, PAIRS), z_perm(owned, MIDDLE)
    scales_z = z_perm(after(scales, owned), [(a, a ^ 2) for a in range(Z)])
    block_scales = jnp.maximum(scales, scales_z) + 1e-06
    over1 = [[x_perm(after(pairs, *(v for vs in over0 for v in vs)), by)] for by in others]
    outwards, mid_far = z_perm(after(mid, block_scales), OUTWARDS), z_perm(after(pairs, block_scales), MIDDLE)
    before = [v for vs in over1 for v in vs]
    over2 = [[x_perm(after(mid, *before), by, (1, 2)), x_perm(after(outwards, *before), by, (0, 3))] for by in others]
    far = z_perm(mid_far, OUTWARDS)
    before = [v for vs in over2 for v in vs]
    over3 = [[x_perm(after(mid_far, *before), by, (1, 2)), x_perm(after(far, *before), by, (0, 3))] for by in others]

    def put(weights, values, slot, by):
        value = values[0] if len(values) == 1 else jnp.where(between, *values)
        return lax.dynamic_update_slice(weights, value, (0, (sources[slot] * n_x + (x - by) % n_x) * width))

    held = [owned], [pairs], [mid, outwards], [mid_far, far]
    for slot, over in enumerate([over0, over1, over2, over3]):
        weights = put(weights, held[slot], slot, 0)
        for by in others:
            weights = put(weights, over[by - 1], slot, by)
    return (new_master, new_first, new_second, weights, block_scales)


def solution(mesh):
    in_specs = (
        P("dp", "tensor"),
        P(("dp", "tensor"), None),
        P("tensor", "dp"),
        P("tensor", "dp"),
        P("tensor", "dp"),
    )
    out_specs = (
        P("tensor", "dp"),
        P("tensor", "dp"),
        P("tensor", "dp"),
        P("tensor", None),
        P("tensor", None),
    )
    return jax.shard_map(body, mesh=mesh, in_specs=in_specs, out_specs=out_specs, check_vma=False)
```

time: 445 us -> 250 us (0.56)
  waiting for transfers between devices: 306 us -> 112 us
  starting transfers between devices: 0.12 us -> 52.9 us
  Pallas kernels: 0 us -> 52.7 us
  local copies, waits for them, and re-layouts: 52.6 us -> 23.3 us
  other arithmetic: 33.4 us -> 7.47 us
  blocking collectives: 21.8 us -> 0 us
  matrix products: 17.5 us -> 0 us
  between operations: 13.8 us -> 0.89 us
    all_gather x2 -> x0, waiting for transfers between devices: 175 us -> none  [the longest x1 125 us: body(): weights = lax.all_gather(owned_weights, 'dp', axis=1, tiled=True)]
    reduce_scatter x1 -> x0, waiting for transfers between devices: 130 us -> none  [body(): lax.psum_scatter(quantized.astype(jnp.float32).astype(jnp.bfloat16), 'dp'...]
    ppermute x0 -> x35, waiting for transfers between devices: none -> 112 us  [the longest x11 54.2 us: x_perm(): return lax.ppermute(value, 'dp', pairs)]
    ppermute x0 -> x35, starting transfers between devices: none -> 52.9 us  [the longest x12 32.6 us: z_perm(): lax.ppermute(value, 'dp', [(a * n_x + i, b * n_x + i) for a, b in pairs f...]
    pallas_call x0 -> x12, Pallas kernels: none -> 52.7 us  [the longest x4 25 us: multiply(): pl.pallas_call(kernel, grid=(rows // step,), in_specs=[pl.BlockSpec((step...]
    unnamed x11 -> x30, local copies, waits for them, and re-layouts: 47.9 us -> 9.09 us
    pmax x1 -> x0, blocking collectives: 21.8 us -> none  [body(): block_scales = lax.pmax(local_max, 'dp') + 1e-06]
    convert_element_type x2 -> x0, other arithmetic: 19.8 us -> none  [the longest x1 12.6 us: body(): quantized = (partial_value / wide_scale).astype(jnp.bfloat16)]
  transfers between devices with their start and end apart: 3 -> 35, of which waited for: 3 -> 18; matrix products, arithmetic and copies ran while one was open for 4% -> 8% of each run, Pallas kernels for 0% -> 14%
where the time goes in v2:
time: 250 us; the launch traced here: 249 us
  waiting for transfers between devices  112 us (45%)
  starting transfers between devices  52.9 us (21%)
  Pallas kernels  52.7 us (21%)
  local copies, waits for them, and re-layouts  23.3 us (9%)
  other arithmetic  7.47 us (3%)
    ppermute x11, waiting for transfers between devices, x_perm(): return lax.ppermute(value, 'dp', pairs)  54.2 us
    ppermute x12, waiting for transfers between devices, z_perm(): lax.ppermute(value, 'dp', [(a * n_x + i, b * n_x + i) for a, b in pairs f...  40.1 us
    ppermute x12, starting transfers between devices, z_perm(): lax.ppermute(value, 'dp', [(a * n_x + i, b * n_x + i) for a, b in pairs f...  32.6 us
    pallas_call x4, Pallas kernels, multiply(): pl.pallas_call(kernel, grid=(rows // step,), in_specs=[pl.BlockSpec((step...  25 us
    ppermute x12, waiting for transfers between devices, seat_perm(): lax.ppermute(value, 'tensor', [(i, i ^ flip) for i in range(n_tensor)])  17.3 us
    pallas_call x5, Pallas kernels, add(): call(kernel, [jax.ShapeDtypeStruct((rows, columns), BF16)], terms, 'add')  15.4 us
    ppermute x11, starting transfers between devices, x_perm(): return lax.ppermute(value, 'dp', pairs)  14.3 us
    pallas_call x1, Pallas kernels, adamw(): call(kernel, shapes, list(terms) + list(states), 'adamw')(*terms, *states)  9.53 us
  transfers between devices with their start and end apart: 35, of which 18 were waited for; matrix products, arithmetic and copies ran while one was open for 8% of the time, Pallas kernels for 14%

profile of v2, /device:TPU:0, one launch (start us, length us, event | category | flops | bytes accessed | tf_op | source)
XLA Modules:
  0.0 248.9 jit_solution(2622934513956393442)
XLA Ops:
  0.6 2.8 %arrange.1 = (bf16[384,256]{1,0:T(8,128)(2,1)}, bf16[384,512]{1,0:T(8,128)(2,1)}, bf16[384,512]{1,0:T(8,128)(2,1)}, bf16[384,768]{1,0:T(8,128)(2,1)}) custom-call(bf16[384,2048]{1,0:T(8,128)(2,1)} %cot_ref.1), custom_call_target="tpu_custom_call" | custom-call | tf_op jit(solution)/shard_map/arrange/pallas_call | solution.py:55
  3.4 3.0 %collective-permute-start.1 = (bf16[384,256]{1,0:T(8,128)(2,1)}, bf16[384,256]{1,0:T(8,128)(2,1)S(1)}, u32[]{:S(2)}, u32[]{:S(2)}) collective-permute-start(bf16[384,256]{1,0:T(8,128)(2,1)} %get-tuple-element.66.refs_0_), channel_id=1, source_target_pairs={{0,2},{1,3},{2,0},{3,1},{4,6},{5,7},{6,4},{7,5},{8,10},{9,11},{10,... | collective-permute-start | bytes 589832 | tf_op jit(solution)/shard_map/ppermute | solution.py:181
  6.4 8.6 %copy.12 = bf16[1536,2048]{0,1:T(8,128)(2,1)} copy(bf16[1536,2048]{1,0:T(8,128)(2,1)} %param.5) | data formatting | bytes 12582912 | tf_op jit(solution)/shard_map/optimization_barrier | solution.py:159
  15.5 0.9 collective-permute-done.refs_1_
  16.7 4.8 %partials.4 = (bf16[2048,256]{1,0:T(8,128)(2,1)S(1)}, f32[4,4,256]{2,1,0:T(4,128)S(1)}) custom-call(bf16[2048,1536]{1,0:T(8,128)(2,1)} %bitcast.17, bf16[384,256]{1,0:T(8,128)(2,1)S(1)} %copy-done.7, bf16[384,256]{1,0:T(8,128)(2,1)S(1)} %collective-permute-done.refs_1_, bf16[384,256]{1,0:T(8,128)(2,1)S(1)} %collective-permute-done.1.refs_2_, ...), custom_call_target="tpu_custom_call" | custom-call | tf_op jit(solution)/shard_map/partials/pallas_call | solution.py:79
  21.5 1.5 collective-permute-start.6
  23.6 10.5 %collective-permute-done.4.refs_2_ = bf16[384,512]{1,0:T(8,128)(2,1)S(1)} collective-permute-done((bf16[384,512]{1,0:T(8,128)(2,1)S(1)}, bf16[384,512]{1,0:T(8,128)(2,1)S(1)}, u32[]{:S(2)}, u32[]{:S(2)}) %collective-permute-start.4) | collective-permute-done | bytes 393248 | tf_op jit(solution)/shard_map/ppermute | solution.py:181
  34.0 1.7 collective-permute-done.5.refs_3_
  35.8 6.8 %partials.5 = (bf16[2048,256]{1,0:T(8,128)(2,1)S(1)}, bf16[2048,256]{1,0:T(8,128)(2,1)}, f32[4,4,512]{2,1,0:T(4,128)S(1)}) custom-call(bf16[2048,1536]{1,0:T(8,128)(2,1)} %bitcast.18, bf16[384,512]{1,0:T(8,128)(2,1)S(1)} %copy-done.6, bf16[384,512]{1,0:T(8,128)(2,1)S(1)} %collective-permute-done.3.refs_1_, ...), custom_call_target="tpu_custom_call" | custom-call | tf_op jit(solution)/shard_map/partials/pallas_call | solution.py:79
  42.6 1.0 copy-done.1
  44.1 2.8 %collective-permute-done.6.refs_1_ = bf16[2048,256]{1,0:T(8,128)(2,1)S(1)} collective-permute-done((bf16[2048,256]{1,0:T(8,128)(2,1)S(1)}, bf16[2048,256]{1,0:T(8,128)(2,1)S(1)}, u32[]{:S(2)}, u32[]{:S(2)}) %collective-permute-start.6) | collective-permute-done | bytes 1048608 | tf_op jit(solution)/shard_map/ppermute | solution.py:178
  46.9 1.0 copy-done.10
  47.9 1.5 collective-permute-start.10
  49.3 2.8 %add.193 = bf16[2048,256]{1,0:T(8,128)(2,1)} custom-call(bf16[2048,256]{1,0:T(8,128)(2,1)} %copy-done.1, bf16[2048,256]{1,0:T(8,128)(2,1)} %copy-done.10), custom_call_target="tpu_custom_call" | custom-call | tf_op jit(solution)/shard_map/add/pallas_call | solution.py:111
  52.1 4.5 %collective-permute-start.11 = (bf16[2048,256]{1,0:T(8,128)(2,1)}, bf16[2048,256]{1,0:T(8,128)(2,1)}, u32[]{:S(2)}, u32[]{:S(2)}) collective-permute-start(bf16[2048,256]{1,0:T(8,128)(2,1)} %add.193), channel_id=1, source_target_pairs={{0,8},{4,12},{24,16},{28,20},{1,9},{5,13},{25,17},{29,21},{2,10},{... | collective-permute-start | bytes 3145736 | tf_op jit(solution)/shard_map/ppermute | solution.py:174
  57.2 1.2 collective-permute-done.7.refs_1_
  58.9 6.1 %partials.6 = (bf16[2048,256]{1,0:T(8,128)(2,1)S(1)}, bf16[2048,256]{1,0:T(8,128)(2,1)S(1)}, f32[4,4,512]{2,1,0:T(4,128)S(1)}) custom-call(bf16[2048,1536]{1,0:T(8,128)(2,1)} %bitcast.19, bf16[384,512]{1,0:T(8,128)(2,1)S(1)} %copy-done.5, bf16[384,512]{1,0:T(8,128)(2,1)S(1)} %collective-permute-done.7.refs_1_, ...), custom_call_target="tpu_custom_call" | custom-call | tf_op jit(solution)/shard_map/partials/pallas_call | solution.py:79
  65.0 1.0 copy-done
  66.5 6.0 %collective-permute-done.10.refs_1_ = bf16[2048,256]{1,0:T(8,128)(2,1)S(1)} collective-permute-done((bf16[2048,256]{1,0:T(8,128)(2,1)}, bf16[2048,256]{1,0:T(8,128)(2,1)S(1)}, u32[]{:S(2)}, u32[]{:S(2)}) %collective-permute-start.10) | collective-permute-done | bytes 1048608 | tf_op jit(solution)/shard_map/ppermute | solution.py:178
  72.5 1.0 copy-done.9
  73.5 2.8 %add.194 = bf16[2048,256]{1,0:T(8,128)(2,1)} custom-call(bf16[2048,256]{1,0:T(8,128)(2,1)} %copy-done, bf16[2048,256]{1,0:T(8,128)(2,1)} %copy-done.9), custom_call_target="tpu_custom_call" | custom-call | tf_op jit(solution)/shard_map/add/pallas_call | solution.py:111
  76.3 1.5 collective-permute-start.16
  77.8 3.3 %add.195 = bf16[2048,256]{1,0:T(8,128)(2,1)} custom-call(bf16[2048,256]{1,0:T(8,128)(2,1)} %copy-done.1, bf16[2048,256]{1,0:T(8,128)(2,1)} %copy-done.10, bf16[2048,256]{1,0:T(8,128)(2,1)} %collective-permute-done.11.refs_2_), custom_call_target="tpu_custom_call" | custom-call | tf_op jit(solution)/shard_map/add/pallas_call | solution.py:111
  81.1 1.6 collective-permute-start.17
  82.7 7.1 %collective-permute-start.18 = (bf16[2048,256]{1,0:T(8,128)(2,1)}, bf16[2048,256]{1,0:T(8,128)(2,1)}, u32[]{:S(2)}, u32[]{:S(2)}) collective-permute-start(bf16[2048,256]{1,0:T(8,128)(2,1)} %add.194), channel_id=1, source_target_pairs={{0,8},{4,12},{24,16},{28,20},{1,9},{5,13},{25,17},{29,21},{2,10},{... | collective-permute-start | bytes 3145736 | tf_op jit(solution)/shard_map/ppermute | solution.py:174
  90.5 1.3 collective-permute-done.12.refs_1_
  91.8 0.8 collective-permute-done.14.refs_3_
  92.7 7.3 %partials.7 = (bf16[2048,256]{1,0:T(8,128)(2,1)S(1)}, bf16[2048,256]{1,0:T(8,128)(2,1)S(1)}, bf16[2048,256]{1,0:T(8,128)(2,1)S(1)}, f32[4,4,768]{2,1,0:T(4,128)S(1)}) custom-call(bf16[2048,1536]{1,0:T(8,128)(2,1)} %bitcast.20, bf16[384,768]{1,0:T(8,128)(2,1)S(1)} %copy-done.4, bf16[384,768]{1,0:T(8,128)(2,1)S(1)} %collective-permute-done.12.refs_1_, ...), custom_call_target="tpu_custom_call" | custom-call | tf_op jit(solution)/shard_map/partials/pallas_call | solution.py:79
  99.9 1.0 copy-done.2
  100.9 1.0 copy-done.3
  101.9 1.0 copy-done.8
  104.2 3.1 %collective-permute-done.15 = f32[16,16]{1,0:T(8,128)S(1)} collective-permute-done((f32[16,16]{1,0:T(8,128)S(1)}, f32[16,16]{1,0:T(8,128)S(1)}, u32[]{:S(2)}, u32[]{:S(2)}) %collective-permute-start.15) | collective-permute-done | bytes 1056 | tf_op jit(solution)/shard_map/ppermute | solution.py:178
  107.3 3.3 %add.196 = bf16[2048,256]{1,0:T(8,128)(2,1)} custom-call(bf16[2048,256]{1,0:T(8,128)(2,1)} %copy-done.3, bf16[2048,256]{1,0:T(8,128)(2,1)} %collective-permute-done.16.refs_1_, bf16[2048,256]{1,0:T(8,128)(2,1)} %collective-permute-done.17.refs_2_), custom_call_target="tpu_custom_call" | custom-call | tf_op jit(solution)/shard_map/add/pallas_call | solution.py:111
  110.5 1.6 collective-permute-start.21
  112.7 3.2 %add.197 = bf16[2048,256]{1,0:T(8,128)(2,1)} custom-call(bf16[2048,256]{1,0:T(8,128)(2,1)} %copy-done, bf16[2048,256]{1,0:T(8,128)(2,1)} %copy-done.9, bf16[2048,256]{1,0:T(8,128)(2,1)} %collective-permute-done.18.refs_2_), custom_call_target="tpu_custom_call" | custom-call | tf_op jit(solution)/shard_map/add/pallas_call | solution.py:111
  116.7 2.8 %collective-permute-start.19 = (f32[16,16]{1,0:T(8,128)S(1)}, f32[16,16]{1,0:T(8,128)S(1)}, u32[]{:S(2)}, u32[]{:S(2)}) collective-permute-start(f32[16,16]{1,0:T(8,128)S(1)} %max.9), channel_id=1, source_target_pairs={{0,8},{4,12},{8,0},{12,4},{16,24},{20,28},{24,16},{28,20},{1,9},{5... | collective-permute-start | bytes 3080 | tf_op jit(solution)/shard_map/ppermute | solution.py:174
  119.5 15.5 %collective-permute-done.19 = f32[16,16]{1,0:T(8,128)S(1)} collective-permute-done((f32[16,16]{1,0:T(8,128)S(1)}, f32[16,16]{1,0:T(8,128)S(1)}, u32[]{:S(2)}, u32[]{:S(2)}) %collective-permute-start.19) | collective-permute-done | bytes 1056 | tf_op jit(solution)/shard_map/ppermute | solution.py:174
  135.0 0.9 copy-done.12
  136.3 1.0 copy-done.13
  137.3 9.5 %adamw.1 = (f32[2048,256]{1,0:T(8,128)}, f32[2048,256]{1,0:T(8,128)}, f32[2048,256]{1,0:T(8,128)}, bf16[2048,256]{1,0:T(8,128)(2,1)}) custom-call(bf16[2048,256]{1,0:T(8,128)(2,1)} %copy-done.2, bf16[2048,256]{1,0:T(8,128)(2,1)} %copy-done.12, bf16[2048,256]{1,0:T(8,128)(2,1)} %copy-done.11, bf16[2048,256]{1,0:T(8,128)(2,1)} %copy-done.13, ...), custom_call_target="tpu_custom_call" | custom-call | tf_op jit(solution)/shard_map/adamw/pallas_call | solution.py:145
  147.4 6.6 %collective-permute-start.24 = (bf16[2048,256]{1,0:T(8,128)(2,1)}, bf16[2048,256]{1,0:T(8,128)(2,1)S(1)}, u32[]{:S(2)}, u32[]{:S(2)}) collective-permute-start(bf16[2048,256]{1,0:T(8,128)(2,1)} %get-tuple-element.112), channel_id=1, source_target_pairs={{0,8},{4,12},{8,0},{12,4},{16,24},{20,28},{24,16},{28,20},{1,9},{5... | collective-permute-start | bytes 3145736 | tf_op jit(solution)/shard_map/ppermute | solution.py:174
  153.9 1.6 collective-permute-start.26
  155.6 1.8 collective-permute-start.27
  157.4 20.7 %collective-permute-done.27 = f32[16,16]{1,0:T(8,128)S(1)} collective-permute-done((f32[16,16]{1,0:T(8,128)S(1)}, f32[16,16]{1,0:T(8,128)S(1)}, u32[]{:S(2)}, u32[]{:S(2)}) %collective-permute-start.27) | collective-permute-done | bytes 1056 | tf_op jit(solution)/shard_map/ppermute | solution.py:174
  179.4 1.3 collective-permute-start.28
  180.7 1.7 collective-permute-start.31
  182.4 1.0 constant_dynamic-update-slice_fusion.3
  183.4 16.4 %collective-permute-done.25 = bf16[2048,256]{1,0:T(8,128)(2,1)} collective-permute-done((bf16[2048,256]{1,0:T(8,128)(2,1)S(1)}, bf16[2048,256]{1,0:T(8,128)(2,1)}, u32[]{:S(2)}, u32[]{:S(2)}) %collective-permute-start.25) | collective-permute-done | bytes 1048608 | tf_op jit(solution)/shard_map/ppermute | solution.py:178
  199.8 0.7 collective-permute-start.29
  200.5 1.9 collective-permute-done.28
  202.5 3.1 %collective-permute-start.30 = (bf16[2048,256]{1,0:T(8,128)(2,1)}, bf16[2048,256]{1,0:T(8,128)(2,1)S(1)}, u32[]{:S(2)}, u32[]{:S(2)}) collective-permute-start(bf16[2048,256]{1,0:T(8,128)(2,1)} %collective-permute-done.28), channel_id=1, source_target_pairs={{0,4},{4,0},{24,28},{28,24},{1,5},{5,1},{25,29},{29,25},{2,6},{6,2... | collective-permute-start | bytes 3145736 | tf_op jit(solution)/shard_map/ppermute | solution.py:178
  205.6 1.3 collective-permute-start.32
  206.9 1.0 constant_dynamic-update-slice_fusion.2
  207.9 1.0 constant_dynamic-update-slice_fusion.1
  209.0 2.3 constant_dynamic-update-slice_fusion
  211.2 2.4 select_dynamic-update-slice_fusion.3
  213.7 10.8 %collective-permute-done.30 = bf16[2048,256]{1,0:T(8,128)(2,1)S(1)} collective-permute-done((bf16[2048,256]{1,0:T(8,128)(2,1)}, bf16[2048,256]{1,0:T(8,128)(2,1)S(1)}, u32[]{:S(2)}, u32[]{:S(2)}) %collective-permute-start.30) | collective-permute-done | bytes 1048608 | tf_op jit(solution)/shard_map/ppermute | solution.py:178
  224.5 0.7 collective-permute-start.33
  225.2 2.0 collective-permute-done.32
  227.2 2.8 %collective-permute-start.34 = (bf16[2048,256]{1,0:T(8,128)(2,1)S(1)}, bf16[2048,256]{1,0:T(8,128)(2,1)S(1)}, u32[]{:S(2)}, u32[]{:S(2)}) collective-permute-start(bf16[2048,256]{1,0:T(8,128)(2,1)S(1)} %collective-permute-done.32), channel_id=1, source_target_pairs={{0,4},{4,0},{24,28},{28,24},{1,5},{5,1},{25,29},{29,25},{2,6},{6,2... | collective-permute-start | bytes 3145736 | tf_op jit(solution)/shard_map/ppermute | solution.py:178
  230.0 1.3 select_dynamic-update-slice_fusion.2
  231.3 1.3 select_dynamic-update-slice_fusion.1
  232.6 15.1 %collective-permute-done.34 = bf16[2048,256]{1,0:T(8,128)(2,1)S(1)} collective-permute-done((bf16[2048,256]{1,0:T(8,128)(2,1)S(1)}, bf16[2048,256]{1,0:T(8,128)(2,1)S(1)}, u32[]{:S(2)}, u32[]{:S(2)}) %collective-permute-start.34) | collective-permute-done | bytes 1048608 | tf_op jit(solution)/shard_map/ppermute | solution.py:178
  247.6 1.3 select_dynamic-update-slice_fusion
  (72 shorter events, 8.8 us)
Async XLA Ops:
  3.4 11.6 %copy-start.7 = (bf16[384,256]{1,0:T(8,128)(2,1)S(1)}, bf16[384,256]{1,0:T(8,128)(2,1)}, u32[]{:S(2)}) copy-start(bf16[384,256]{1,0:T(8,128)(2,1)} %get-tuple-element.66.refs_0_) | copy-start | bytes 589828
  3.4 19.7 %copy-start.6 = (bf16[384,512]{1,0:T(8,128)(2,1)S(1)}, bf16[384,512]{1,0:T(8,128)(2,1)}, u32[]{:S(2)}) copy-start(bf16[384,512]{1,0:T(8,128)(2,1)} %get-tuple-element.72.refs_0_) | copy-start | bytes 1179652
  3.4 11.6 %collective-permute-start.1 = (bf16[384,256]{1,0:T(8,128)(2,1)}, bf16[384,256]{1,0:T(8,128)(2,1)S(1)}, u32[]{:S(2)}, u32[]{:S(2)}) collective-permute-start(bf16[384,256]{1,0:T(8,128)(2,1)} %get-tuple-element.66.refs_0_), channel_id=1, source_target_pairs={{0,2},{1,3},{2,0},{3,1},{4,6},{5,7},{6,4},{7,5},{8,10},{9,11},{10,... | collective-permute-start | bytes 589832 | tf_op jit(solution)/shard_map/ppermute | solution.py:181
  15.0 28.6 %copy-start.5 = (bf16[384,512]{1,0:T(8,128)(2,1)S(1)}, bf16[384,512]{1,0:T(8,128)(2,1)}, u32[]{:S(2)}) copy-start(bf16[384,512]{1,0:T(8,128)(2,1)} %get-tuple-element.79.refs_0_) | copy-start | bytes 1179652
  15.0 1.4 collective-permute-start
  15.0 1.7 collective-permute-start.2
  21.5 25.4 %collective-permute-start.6 = (bf16[2048,256]{1,0:T(8,128)(2,1)S(1)}, bf16[2048,256]{1,0:T(8,128)(2,1)S(1)}, u32[]{:S(2)}, u32[]{:S(2)}) collective-permute-start(bf16[2048,256]{1,0:T(8,128)(2,1)S(1)} %get-tuple-element.68), channel_id=1, source_target_pairs={{0,4},{4,0},{8,12},{12,8},{16,20},{20,16},{24,28},{28,24},{1,5},{5... | collective-permute-start | bytes 3145736 | tf_op jit(solution)/shard_map/ppermute | solution.py:178
  23.1 42.9 %copy-start.4 = (bf16[384,768]{1,0:T(8,128)(2,1)S(1)}, bf16[384,768]{1,0:T(8,128)(2,1)}, u32[]{:S(2)}) copy-start(bf16[384,768]{1,0:T(8,128)(2,1)} %get-tuple-element.89.refs_0_) | copy-start | bytes 1769476
  23.1 11.0 %collective-permute-start.4 = (bf16[384,512]{1,0:T(8,128)(2,1)S(1)}, bf16[384,512]{1,0:T(8,128)(2,1)S(1)}, u32[]{:S(2)}, u32[]{:S(2)}) collective-permute-start(bf16[384,512]{1,0:T(8,128)(2,1)S(1)} %copy-done.6), channel_id=1, source_target_pairs={{0,2},{1,3},{2,0},{3,1},{4,6},{5,7},{6,4},{7,5},{8,10},{9,11},{10,... | collective-permute-start | bytes 1179656 | tf_op jit(solution)/shard_map/ppermute | solution.py:181
  23.6 10.5 %collective-permute-start.3 = (bf16[384,512]{1,0:T(8,128)(2,1)S(1)}, bf16[384,512]{1,0:T(8,128)(2,1)S(1)}, u32[]{:S(2)}, u32[]{:S(2)}) collective-permute-start(bf16[384,512]{1,0:T(8,128)(2,1)S(1)} %copy-done.6), channel_id=1, source_target_pairs={{0,1},{1,0},{2,3},{3,2},{4,5},{5,4},{6,7},{7,6},{8,9},{9,8},{10,11... | collective-permute-start | bytes 1179656 | tf_op jit(solution)/shard_map/ppermute | solution.py:181
  34.0 1.7 collective-permute-start.5
  42.6 1.0 copy-start.1
  43.6 13.1 %collective-permute-start.8 = (bf16[384,512]{1,0:T(8,128)(2,1)S(1)}, bf16[384,512]{1,0:T(8,128)(2,1)S(1)}, u32[]{:S(2)}, u32[]{:S(2)}) collective-permute-start(bf16[384,512]{1,0:T(8,128)(2,1)S(1)} %copy-done.5), channel_id=1, source_target_pairs={{0,2},{1,3},{2,0},{3,1},{4,6},{5,7},{6,4},{7,5},{8,10},{9,11},{10,... | collective-permute-start | bytes 1179656 | tf_op jit(solution)/shard_map/ppermute | solution.py:181
  46.9 1.0 copy-start.10
  47.9 24.7 %collective-permute-start.10 = (bf16[2048,256]{1,0:T(8,128)(2,1)}, bf16[2048,256]{1,0:T(8,128)(2,1)S(1)}, u32[]{:S(2)}, u32[]{:S(2)}) collective-permute-start(bf16[2048,256]{1,0:T(8,128)(2,1)} %get-tuple-element.84), channel_id=1, source_target_pairs={{0,4},{4,0},{8,12},{12,8},{16,20},{20,16},{24,28},{28,24},{1,5},{5... | collective-permute-start | bytes 3145736 | tf_op jit(solution)/shard_map/ppermute | solution.py:178
  52.1 25.6 %collective-permute-start.11 = (bf16[2048,256]{1,0:T(8,128)(2,1)}, bf16[2048,256]{1,0:T(8,128)(2,1)}, u32[]{:S(2)}, u32[]{:S(2)}) collective-permute-start(bf16[2048,256]{1,0:T(8,128)(2,1)} %add.193), channel_id=1, source_target_pairs={{0,8},{4,12},{24,16},{28,20},{1,9},{5,13},{25,17},{29,21},{2,10},{... | collective-permute-start | bytes 3145736 | tf_op jit(solution)/shard_map/ppermute | solution.py:174
  56.6 1.7 collective-permute-start.7
  56.6 2.3 collective-permute-start.9
  65.0 1.0 copy-start
  66.0 23.8 %collective-permute-start.13 = (bf16[384,768]{1,0:T(8,128)(2,1)S(1)}, bf16[384,768]{1,0:T(8,128)(2,1)S(1)}, u32[]{:S(2)}, u32[]{:S(2)}) collective-permute-start(bf16[384,768]{1,0:T(8,128)(2,1)S(1)} %copy-done.4), channel_id=1, source_target_pairs={{0,2},{1,3},{2,0},{3,1},{4,6},{5,7},{6,4},{7,5},{8,10},{9,11},{10,... | collective-permute-start | bytes 1769480 | tf_op jit(solution)/shard_map/ppermute | solution.py:181
  72.5 1.0 copy-start.9
  76.3 30.9 %collective-permute-start.16 = (bf16[2048,256]{1,0:T(8,128)(2,1)S(1)}, bf16[2048,256]{1,0:T(8,128)(2,1)}, u32[]{:S(2)}, u32[]{:S(2)}) collective-permute-start(bf16[2048,256]{1,0:T(8,128)(2,1)S(1)} %get-tuple-element.103), channel_id=1, source_target_pairs={{0,4},{4,0},{8,12},{12,8},{16,20},{20,16},{24,28},{28,24},{1,5},{5... | collective-permute-start | bytes 3145736 | tf_op jit(solution)/shard_map/ppermute | solution.py:178
  81.1 26.2 %collective-permute-start.17 = (bf16[2048,256]{1,0:T(8,128)(2,1)}, bf16[2048,256]{1,0:T(8,128)(2,1)}, u32[]{:S(2)}, u32[]{:S(2)}) collective-permute-start(bf16[2048,256]{1,0:T(8,128)(2,1)} %add.195), channel_id=1, source_target_pairs={{8,16},{12,20},{16,8},{20,12},{9,17},{13,21},{17,9},{21,13},{10,18... | collective-permute-start | bytes 3145736 | tf_op jit(solution)/shard_map/ppermute | solution.py:174
  82.7 30.0 %collective-permute-start.18 = (bf16[2048,256]{1,0:T(8,128)(2,1)}, bf16[2048,256]{1,0:T(8,128)(2,1)}, u32[]{:S(2)}, u32[]{:S(2)}) collective-permute-start(bf16[2048,256]{1,0:T(8,128)(2,1)} %add.194), channel_id=1, source_target_pairs={{0,8},{4,12},{24,16},{28,20},{1,9},{5,13},{25,17},{29,21},{2,10},{... | collective-permute-start | bytes 3145736 | tf_op jit(solution)/shard_map/ppermute | solution.py:174
  89.8 2.0 collective-permute-start.12
  89.8 2.8 %collective-permute-start.14 = (bf16[384,768]{1,0:T(8,128)(2,1)S(1)}, bf16[384,768]{1,0:T(8,128)(2,1)S(1)}, u32[]{:S(2)}, u32[]{:S(2)}) collective-permute-start(bf16[384,768]{1,0:T(8,128)(2,1)S(1)} %collective-permute-done.13.refs_2_), channel_id=1, source_target_pairs={{0,1},{1,0},{2,3},{3,2},{4,5},{5,4},{6,7},{7,6},{8,9},{9,8},{10,11... | collective-permute-start | bytes 1769480 | tf_op jit(solution)/shard_map/ppermute | solution.py:181
  99.9 1.0 copy-start.2
  100.9 1.0 copy-start.3
  101.9 1.0 copy-start.8
  103.5 3.7 %collective-permute-start.15 = (f32[16,16]{1,0:T(8,128)S(1)}, f32[16,16]{1,0:T(8,128)S(1)}, u32[]{:S(2)}, u32[]{:S(2)}) collective-permute-start(f32[16,16]{1,0:T(8,128)S(1)} %select_reduce_fusion), channel_id=1, source_target_pairs={{0,4},{4,0},{8,12},{12,8},{16,20},{20,16},{24,28},{28,24},{1,5},{5... | collective-permute-start | bytes 3080 | tf_op jit(solution)/shard_map/ppermute | solution.py:178
  110.5 24.5 %collective-permute-start.21 = (bf16[2048,256]{1,0:T(8,128)(2,1)}, bf16[2048,256]{1,0:T(8,128)(2,1)S(1)}, u32[]{:S(2)}, u32[]{:S(2)}) collective-permute-start(bf16[2048,256]{1,0:T(8,128)(2,1)} %add.196), channel_id=1, source_target_pairs={{0,8},{4,12},{8,0},{12,4},{16,24},{20,28},{24,16},{28,20},{1,9},{5... | collective-permute-start | bytes 3145736 | tf_op jit(solution)/shard_map/ppermute | solution.py:174
  112.1 22.8 %collective-permute-start.20 = (bf16[2048,256]{1,0:T(8,128)(2,1)}, bf16[2048,256]{1,0:T(8,128)(2,1)S(1)}, u32[]{:S(2)}, u32[]{:S(2)}) collective-permute-start(bf16[2048,256]{1,0:T(8,128)(2,1)} %copy-done.8), channel_id=1, source_target_pairs={{0,4},{4,0},{8,12},{12,8},{16,20},{20,16},{24,28},{28,24},{1,5},{5... | collective-permute-start | bytes 3145736 | tf_op jit(solution)/shard_map/ppermute | solution.py:178
  115.9 19.1 %collective-permute-start.22 = (bf16[2048,256]{1,0:T(8,128)(2,1)}, bf16[2048,256]{1,0:T(8,128)(2,1)S(1)}, u32[]{:S(2)}, u32[]{:S(2)}) collective-permute-start(bf16[2048,256]{1,0:T(8,128)(2,1)} %add.197), channel_id=1, source_target_pairs={{8,16},{12,20},{16,8},{20,12},{9,17},{13,21},{17,9},{21,13},{10,18... | collective-permute-start | bytes 3145736 | tf_op jit(solution)/shard_map/ppermute | solution.py:174
  116.7 18.3 %collective-permute-start.19 = (f32[16,16]{1,0:T(8,128)S(1)}, f32[16,16]{1,0:T(8,128)S(1)}, u32[]{:S(2)}, u32[]{:S(2)}) collective-permute-start(f32[16,16]{1,0:T(8,128)S(1)} %max.9), channel_id=1, source_target_pairs={{0,8},{4,12},{8,0},{12,4},{16,24},{20,28},{24,16},{28,20},{1,9},{5... | collective-permute-start | bytes 3080 | tf_op jit(solution)/shard_map/ppermute | solution.py:174
  135.0 1.0 copy-start.12
  135.0 1.3 copy-start.11
  136.3 1.0 copy-start.13
  146.8 35.6 %copy-start.14 = (bf16[2048,256]{1,0:T(8,128)(2,1)S(1)}, bf16[2048,256]{1,0:T(8,128)(2,1)}, u32[]{:S(2)}) copy-start(bf16[2048,256]{1,0:T(8,128)(2,1)} %get-tuple-element.112) | copy-start | bytes 3145732
  146.8 31.9 %collective-permute-start.23 = (bf16[2048,256]{1,0:T(8,128)(2,1)}, bf16[2048,256]{1,0:T(8,128)(2,1)S(1)}, u32[]{:S(2)}, u32[]{:S(2)}) collective-permute-start(bf16[2048,256]{1,0:T(8,128)(2,1)} %get-tuple-element.112), channel_id=1, source_target_pairs={{0,4},{4,0},{8,12},{12,8},{16,20},{20,16},{24,28},{28,24},{1,5},{5... | collective-permute-start | bytes 3145736 | tf_op jit(solution)/shard_map/ppermute | solution.py:178
  147.4 31.4 %collective-permute-start.24 = (bf16[2048,256]{1,0:T(8,128)(2,1)}, bf16[2048,256]{1,0:T(8,128)(2,1)S(1)}, u32[]{:S(2)}, u32[]{:S(2)}) collective-permute-start(bf16[2048,256]{1,0:T(8,128)(2,1)} %get-tuple-element.112), channel_id=1, source_target_pairs={{0,8},{4,12},{8,0},{12,4},{16,24},{20,28},{24,16},{28,20},{1,9},{5... | collective-permute-start | bytes 3145736 | tf_op jit(solution)/shard_map/ppermute | solution.py:174
  153.9 25.5 %collective-permute-start.26 = (bf16[2048,256]{1,0:T(8,128)(2,1)}, bf16[2048,256]{1,0:T(8,128)(2,1)}, u32[]{:S(2)}, u32[]{:S(2)}) collective-permute-start(bf16[2048,256]{1,0:T(8,128)(2,1)} %get-tuple-element.112), channel_id=1, source_target_pairs={{8,16},{12,20},{16,8},{20,12},{9,17},{13,21},{17,9},{21,13},{10,18... | collective-permute-start | bytes 3145736 | tf_op jit(solution)/shard_map/ppermute | solution.py:174
  155.6 22.5 %collective-permute-start.27 = (f32[16,16]{1,0:T(8,128)S(1)}, f32[16,16]{1,0:T(8,128)S(1)}, u32[]{:S(2)}, u32[]{:S(2)}) collective-permute-start(f32[16,16]{1,0:T(8,128)S(1)} %max.10), channel_id=1, source_target_pairs={{0,16},{4,20},{8,24},{12,28},{16,0},{20,4},{24,8},{28,12},{1,17},{... | collective-permute-start | bytes 3080 | tf_op jit(solution)/shard_map/ppermute | solution.py:174
  178.7 21.1 %collective-permute-start.25 = (bf16[2048,256]{1,0:T(8,128)(2,1)S(1)}, bf16[2048,256]{1,0:T(8,128)(2,1)}, u32[]{:S(2)}, u32[]{:S(2)}) collective-permute-start(bf16[2048,256]{1,0:T(8,128)(2,1)S(1)} %collective-permute-done.24), channel_id=1, source_target_pairs={{0,4},{4,0},{8,12},{12,8},{16,20},{20,16},{24,28},{28,24},{1,5},{5... | collective-permute-start | bytes 3145736 | tf_op jit(solution)/shard_map/ppermute | solution.py:178
  179.4 23.0 %collective-permute-start.28 = (bf16[2048,256]{1,0:T(8,128)(2,1)}, bf16[2048,256]{1,0:T(8,128)(2,1)}, u32[]{:S(2)}, u32[]{:S(2)}) collective-permute-start(bf16[2048,256]{1,0:T(8,128)(2,1)} %collective-permute-done.26), channel_id=1, source_target_pairs={{8,0},{12,4},{16,24},{20,28},{9,1},{13,5},{17,25},{21,29},{10,2},{... | collective-permute-start | bytes 3145736 | tf_op jit(solution)/shard_map/ppermute | solution.py:174
  180.7 24.9 %collective-permute-start.31 = (bf16[2048,256]{1,0:T(8,128)(2,1)S(1)}, bf16[2048,256]{1,0:T(8,128)(2,1)}, u32[]{:S(2)}, u32[]{:S(2)}) collective-permute-start(bf16[2048,256]{1,0:T(8,128)(2,1)S(1)} %collective-permute-done.24), channel_id=1, source_target_pairs={{8,16},{12,20},{16,8},{20,12},{9,17},{13,21},{17,9},{21,13},{10,18... | collective-permute-start | bytes 3145736 | tf_op jit(solution)/shard_map/ppermute | solution.py:174
  199.8 13.8 %collective-permute-start.29 = (bf16[2048,256]{1,0:T(8,128)(2,1)}, bf16[2048,256]{1,0:T(8,128)(2,1)S(1)}, u32[]{:S(2)}, u32[]{:S(2)}) collective-permute-start(bf16[2048,256]{1,0:T(8,128)(2,1)} %collective-permute-done.26), channel_id=1, source_target_pairs={{8,12},{12,8},{16,20},{20,16},{9,13},{13,9},{17,21},{21,17},{10,14... | collective-permute-start | bytes 3145736 | tf_op jit(solution)/shard_map/ppermute | solution.py:178
  202.5 22.0 %collective-permute-start.30 = (bf16[2048,256]{1,0:T(8,128)(2,1)}, bf16[2048,256]{1,0:T(8,128)(2,1)S(1)}, u32[]{:S(2)}, u32[]{:S(2)}) collective-permute-start(bf16[2048,256]{1,0:T(8,128)(2,1)} %collective-permute-done.28), channel_id=1, source_target_pairs={{0,4},{4,0},{24,28},{28,24},{1,5},{5,1},{25,29},{29,25},{2,6},{6,2... | collective-permute-start | bytes 3145736 | tf_op jit(solution)/shard_map/ppermute | solution.py:178
  205.6 21.6 %collective-permute-start.32 = (bf16[2048,256]{1,0:T(8,128)(2,1)}, bf16[2048,256]{1,0:T(8,128)(2,1)S(1)}, u32[]{:S(2)}, u32[]{:S(2)}) collective-permute-start(bf16[2048,256]{1,0:T(8,128)(2,1)} %collective-permute-done.31), channel_id=1, source_target_pairs={{8,0},{12,4},{16,24},{20,28},{9,1},{13,5},{17,25},{21,29},{10,2},{... | collective-permute-start | bytes 3145736 | tf_op jit(solution)/shard_map/ppermute | solution.py:174
  224.5 8.1 %collective-permute-start.33 = (bf16[2048,256]{1,0:T(8,128)(2,1)}, bf16[2048,256]{1,0:T(8,128)(2,1)S(1)}, u32[]{:S(2)}, u32[]{:S(2)}) collective-permute-start(bf16[2048,256]{1,0:T(8,128)(2,1)} %collective-permute-done.31), channel_id=1, source_target_pairs={{8,12},{12,8},{16,20},{20,16},{9,13},{13,9},{17,21},{21,17},{10,14... | collective-permute-start | bytes 3145736 | tf_op jit(solution)/shard_map/ppermute | solution.py:178
  227.2 20.5 %collective-permute-start.34 = (bf16[2048,256]{1,0:T(8,128)(2,1)S(1)}, bf16[2048,256]{1,0:T(8,128)(2,1)S(1)}, u32[]{:S(2)}, u32[]{:S(2)}) collective-permute-start(bf16[2048,256]{1,0:T(8,128)(2,1)S(1)} %collective-permute-done.32), channel_id=1, source_target_pairs={{0,4},{4,0},{24,28},{28,24},{1,5},{5,1},{25,29},{29,25},{2,6},{6,2... | collective-permute-start | bytes 3145736 | tf_op jit(solution)/shard_map/ppermute | solution.py:178

commit v3 on v2

--- a/solution.py
+++ b/solution.py
@@ -93,56 +93,26 @@
     return out[:chunks], out[chunks]
 
 
-def add(terms):
-    rows, columns = terms[0].shape
-    step = 64
-
-    def kernel(*refs):
-        def one(i, carry):
-            here = pl.ds(pl.multiple_of(i * step, step), step)
-            total = refs[0][here, :].astype(F32)
-            for ref in refs[1:-1]:
-                total = total + ref[here, :].astype(F32)
-            refs[-1][here, :] = total.astype(BF16)
-            return carry
-
-        lax.fori_loop(0, rows // step, one, 0, unroll=4)
-
-    return call(kernel, [jax.ShapeDtypeStruct((rows, columns), BF16)], terms, "add")(*terms)[0]
-
-
-def adamw(terms, states, factor):
-    rows, width = states[0].shape
-    rate = 0.01 / (1.0 - 0.9**10)
-    spread = 1.0 / (1.0 - 0.95**10)
-    step = 64
-
-    def kernel(*refs):
-        master_ref, first_ref, second_ref, new_master_ref, new_first_ref, new_second_ref, weights_ref = refs[len(terms) :]
-
-        def one(i, carry):
-            at = pl.ds(pl.multiple_of(i * step, step), step)
-            total = refs[0][at, :].astype(F32)
-            for ref in refs[1 : len(terms)]:
-                total = total + ref[at, :].astype(F32)
-            gradient = total * factor
-            new_first = 0.9 * first_ref[at, :] + 0.1 * gradient
-            new_second = 0.95 * second_ref[at, :] + (0.05 * gradient) * gradient
-            hat = new_second * spread
-            root = hat * lax.rsqrt(hat) + 1e-08
-            inverse = pl.reciprocal(root, approx=True)
-            inverse = inverse * (2.0 - root * inverse)
-            new_master = master_ref[at, :] * (1.0 - 0.01 * 0.1) - (rate * new_first) * inverse
-            new_master_ref[at, :] = new_master
-            new_first_ref[at, :] = new_first
-            new_second_ref[at, :] = new_second
-            weights_ref[at, :] = new_master.astype(BF16)
-            return carry
-
-        lax.fori_loop(0, rows // step, one, 0, unroll=2)
-
-    shapes = [jax.ShapeDtypeStruct((rows, width), F32)] * 3 + [jax.ShapeDtypeStruct((rows, width), BF16)]
-    return call(kernel, shapes, list(terms) + list(states), "adamw")(*terms, *states)
+def add(terms, *earlier):
+    held = lax.optimization_barrier((*terms, *earlier))[: len(terms)]
+    total = held[0].astype(F32)
+    for term in held[1:]:
+        total = total + term.astype(F32)
+    return lax.optimization_barrier(total.astype(BF16))
+
+
+def adamw(terms, states, factor, first, count):
+    total, *rest = [lax.slice_in_dim(term, first, first + count).astype(F32) for term in terms]
+    for term in rest:
+        total = total + term
+    master, first_moment, second_moment = [lax.slice_in_dim(state, first, first + count) for state in states]
+    gradient = total * factor
+    new_first = 0.9 * first_moment + 0.1 * gradient
+    new_second = 0.95 * second_moment + 0.05 * gradient * gradient
+    first_hat = new_first * (1.0 / (1.0 - 0.9**10))
+    second_hat = new_second * (1.0 / (1.0 - 0.95**10))
+    new_master = master * (1.0 - 0.01 * 0.1) - 0.01 * first_hat / (jnp.sqrt(second_hat) + 1e-08)
+    return new_master, new_first, new_second, new_master.astype(BF16)
 
 
 def blank(shape, dtype):
@@ -180,9 +150,12 @@
     def seat_perm(value, flip):
         return lax.ppermute(value, "tensor", [(i, i ^ flip) for i in range(n_tensor)])
 
-    pieces = [[(0, by) for by in others]]
-    pieces += [[(i, 0)] + [(i + 1, by) for by in others] for i in range(Z - 1)]
-    pieces[-1].append((Z - 1, 0))
+    pieces = [
+        [(0, by) for by in others],
+        [(0, 0)] + [(1, by) for by in others],
+        [(1, 0)] + [(i, by) for i in (2, 3) for by in others],
+        [(2, 0), (3, 0)],
+    ]
     own = arrange(cotangent, pieces, width, n_x)
     partial, tops, across = {}, [], []
 
@@ -206,20 +179,20 @@
     got0 = send_x(0)
     fetch(1, token)
     token = partials(1, token)
-    fetch(2, token)
-    got1 = send_x(1, *got0)
-    sum0 = add([after(partial[0, 0], token), *got0])
+    got1 = send_x(1)
+    fetch(2, across[1][-1])
+    sum0 = add([partial[0, 0], *got0], token)
     far = z_perm(sum0, INWARDS)
     token = partials(2, sum0)
-    fetch(3, token)
-    got2 = send_x(2, *got1, token)
-    sum1 = add([after(partial[1, 0], token), *got1])
+    got2, got3 = send_x(2), send_x(3)
+    fetch(3, across[2][-1], sum0)
+    token = partials(3, token)
+    sum1 = add([partial[1, 0], *got1], token)
     inwards = z_perm(sum1, INWARDS)
-    sum0 = add([after(partial[0, 0], sum1), *got0, far])
+    sum0 = add([partial[0, 0], *got0, far], sum1)
     middle = z_perm(sum0, MIDDLE)
-    token = partials(3, sum0)
-
-    top = jnp.concatenate([after(t, token).reshape(rows // BLOCK, -1, BLOCK).max(axis=2) for t in tops], axis=1)
+
+    top = jnp.concatenate([after(t, sum0).reshape(rows // BLOCK, -1, BLOCK).max(axis=2) for t in tops], axis=1)
     column = jnp.stack(
         [(owner_z(z, i) * n_x + (x + by) % n_x) * high + h for piece in pieces for i, by in piece for h in range(high)]
     )
@@ -227,46 +200,61 @@
     scales = jnp.max(jnp.where(here, top[:, :, None], 0.0), axis=1)
     scales_x = [x_perm(scales, by) for by in others]
 
-    got3 = send_x(3, *got2, scales)
+    sum1 = add([partial[1, 0], *got1, inwards], scales)
+    last = z_perm(sum1, MIDDLE)
+    sum2 = add([partial[2, 0], *got2, middle], sum1)
+    pairs = z_perm(sum2, PAIRS)
+    scales = after(scales, sum2)
     for got in scales_x:
         scales = jnp.maximum(scales, got)
-    sum2 = add([after(partial[2, 0], scales), *got2, middle])
-    pairs = z_perm(sum2, PAIRS)
-    sum1 = add([after(partial[1, 0], sum2), *got1, inwards])
-    last = z_perm(sum1, MIDDLE)
-    scales_z = z_perm(after(scales, sum1), PAIRS)
-
+    scales_z = z_perm(scales, PAIRS)
+
+    terms = [partial[3, 0], *got3, last, pairs]
+    states = [master, first_moment, second_moment]
+    factor = 1.0 / math.sqrt(acts.shape[0] * n_dp)
+    half = rows // 2
     scales = jnp.maximum(scales, scales_z)
-    new_master, new_first, new_second, owned = adamw(
-        [after(partial[3, 0], scales), *got3, pairs, last],
-        [master, first_moment, second_moment],
-        1.0 / math.sqrt(acts.shape[0] * n_dp),
-    )
+    owned, token = [], scales
+    for h in range(2):
+        held = lax.optimization_barrier((*terms, *states, token))
+        token = lax.optimization_barrier(adamw(held[: len(terms)], held[len(terms) : -1], factor, h * half, half)[3])
+        owned.append(token)
+    held = lax.optimization_barrier((*terms, *states, token))
+    new_master, new_first, new_second, _ = adamw(held[: len(terms)], held[len(terms) : -1], factor, 0, rows)
 
     weights = blank((rows, columns), BF16)
     low, between = z < 2, (z == 1) | (z == 2)
     sources = [z, z ^ 1, jnp.where(low, 2, 1), jnp.where(low, 3, 0)]
-    over0 = [[x_perm(owned, by)] for by in others]
-    pairs, mid = z_perm(owned, PAIRS), z_perm(owned, MIDDLE)
-    scales_z = z_perm(after(scales, owned), [(a, a ^ 2) for a in range(Z)])
+
+    def over_x(value, where=range(Z)):
+        return [x_perm(value, by, where) for by in others]
+
+    over0 = [over_x(value) for value in owned]
+    pairs = [z_perm(value, PAIRS) for value in owned]
+    mid = [z_perm(value, MIDDLE) for value in owned]
+    mid_far = [z_perm(value, MIDDLE) for value in pairs]
+    outwards = [z_perm(value, OUTWARDS) for value in mid]
+    over1 = [over_x(value) for value in pairs]
+    over_mid = [over_x(value, (1, 2)) for value in mid]
+    far = [z_perm(mid_far[0], OUTWARDS), z_perm(mid_far[1], OUTWARDS)]
+    over_outwards = [over_x(value, (0, 3)) for value in outwards]
+    over_mid_far = [over_x(value, (1, 2)) for value in mid_far]
+    over_far = [over_x(value, (0, 3)) for value in far]
+    scales_z = z_perm(after(scales, owned[0]), [(a, a ^ 2) for a in range(Z)])
     block_scales = jnp.maximum(scales, scales_z) + 1e-06
-    over1 = [[x_perm(after(pairs, *(v for vs in over0 for v in vs)), by)] for by in others]
-    outwards, mid_far = z_perm(after(mid, block_scales), OUTWARDS), z_perm(after(pairs, block_scales), MIDDLE)
-    before = [v for vs in over1 for v in vs]
-    over2 = [[x_perm(after(mid, *before), by, (1, 2)), x_perm(after(outwards, *before), by, (0, 3))] for by in others]
-    far = z_perm(mid_far, OUTWARDS)
-    before = [v for vs in over2 for v in vs]
-    over3 = [[x_perm(after(mid_far, *before), by, (1, 2)), x_perm(after(far, *before), by, (0, 3))] for by in others]
-
-    def put(weights, values, slot, by):
+
+    def put(weights, h, slot, by, *values):
         value = values[0] if len(values) == 1 else jnp.where(between, *values)
-        return lax.dynamic_update_slice(weights, value, (0, (sources[slot] * n_x + (x - by) % n_x) * width))
-
-    held = [owned], [pairs], [mid, outwards], [mid_far, far]
-    for slot, over in enumerate([over0, over1, over2, over3]):
-        weights = put(weights, held[slot], slot, 0)
-        for by in others:
-            weights = put(weights, over[by - 1], slot, by)
+        at = (sources[slot] * n_x + (x - by) % n_x) * width
+        return lax.dynamic_update_slice(weights, value, (h * half, at))
+
+    for slot, held in enumerate([(owned,), (pairs,), (mid, outwards), (mid_far, far)]):
+        over = [(over0,), (over1,), (over_mid, over_outwards), (over_mid_far, over_far)][slot]
+        for h in range(2):
+            weights = put(weights, h, slot, 0, *[value[h] for value in held])
+        for h in range(2):
+            for by in others:
+                weights = put(weights, h, slot, by, *[value[h][by - 1] for value in over])
     return (new_master, new_first, new_second, weights, block_scales)
 
 

time: 250 us -> 248 us (level)
  Pallas kernels: 52.7 us -> 27.7 us
  other arithmetic: 7.47 us -> 22.8 us
  waiting for transfers between devices: 112 us -> 124 us
  local copies, waits for them, and re-layouts: 23.3 us -> 12.8 us
  starting transfers between devices: 52.9 us -> 58 us
    pallas_call x6 -> x0, Pallas kernels: 24.9 us -> none  [the longest x5 15.4 us: add(): call(kernel, [jax.ShapeDtypeStruct((rows, columns), BF16)], terms, 'add')]
    ppermute x12 -> x17, waiting for transfers between devices: 40.1 us -> 57 us  [z_perm(): lax.ppermute(value, 'dp', [(a * n_x + i, b * n_x + i) for a, b in pairs f...]
    convert_element_type x0 -> x7, other arithmetic: none -> 14.5 us  [the longest x5 8.68 us: add(): return lax.optimization_barrier(total.astype(BF16))]
    ppermute x11 -> x17, starting transfers between devices: 14.3 us -> 24.4 us  [x_perm(): return lax.ppermute(value, 'dp', pairs)]
    sub x0 -> x1, other arithmetic: none -> 5.97 us  [adamw(): master * (1.0 - 0.01 * 0.1)]
    unnamed x30 -> x24, local copies, waits for them, and re-layouts: 9.09 us -> 3.45 us
    ppermute x12 -> x17, starting transfers between devices: 32.6 us -> 27.5 us  [z_perm(): lax.ppermute(value, 'dp', [(a * n_x + i, b * n_x + i) for a, b in pairs f...]
    dynamic_update_slice x4 -> x8, other arithmetic: 6.25 us -> 1.13 us  [put(): return lax.dynamic_update_slice(weights, value, (h * half, at))]
  transfers between devices with their start and end apart: 35 -> 46, of which waited for: 18 -> 21; matrix products, arithmetic and copies ran while one was open for 8% -> 12% of each run, Pallas kernels for 14% -> 8%
where the time goes in v3:
time: 248 us; the launch traced here: 247 us
  waiting for transfers between devices  124 us (50%)
  starting transfers between devices  58 us (23%)
  Pallas kernels  27.7 us (11%)
  other arithmetic  22.8 us (9%)
  local copies, waits for them, and re-layouts  12.8 us (5%)
    ppermute x17, waiting for transfers between devices, z_perm(): lax.ppermute(value, 'dp', [(a * n_x + i, b * n_x + i) for a, b in pairs f...  57 us
    ppermute x17, waiting for transfers between devices, x_perm(): return lax.ppermute(value, 'dp', pairs)  50.7 us
    ppermute x17, starting transfers between devices, z_perm(): lax.ppermute(value, 'dp', [(a * n_x + i, b * n_x + i) for a, b in pairs f...  27.5 us
    pallas_call x4, Pallas kernels, multiply(): pl.pallas_call(kernel, grid=(rows // step,), in_specs=[pl.BlockSpec((step...  24.9 us
    ppermute x17, starting transfers between devices, x_perm(): return lax.ppermute(value, 'dp', pairs)  24.4 us
    ppermute x12, waiting for transfers between devices, seat_perm(): lax.ppermute(value, 'tensor', [(i, i ^ flip) for i in range(n_tensor)])  16.6 us
    convert_element_type x5, other arithmetic, add(): return lax.optimization_barrier(total.astype(BF16))  8.68 us
    optimization_barrier x1, local copies, waits for them, and re-layouts, after(): return lax.optimization_barrier((value, *earlier))[0] if earlier else value  8.61 us
  transfers between devices with their start and end apart: 46, of which 21 were waited for; matrix products, arithmetic and copies ran while one was open for 12% of the time, Pallas kernels for 8%

profile of v3, /device:TPU:0, one launch (start us, length us, event | category | flops | bytes accessed | tf_op | source)
XLA Modules:
  0.0 246.8 jit_solution(13092660747829885013)
XLA Ops:
  0.6 2.8 %arrange.1 = (bf16[384,256]{1,0:T(8,128)(2,1)}, bf16[384,512]{1,0:T(8,128)(2,1)}, bf16[384,768]{1,0:T(8,128)(2,1)}, bf16[384,512]{1,0:T(8,128)(2,1)}) custom-call(bf16[384,2048]{1,0:T(8,128)(2,1)} %cot_ref.1), custom_call_target="tpu_custom_call" | custom-call | tf_op jit(solution)/shard_map/arrange/pallas_call | solution.py:55
  3.4 3.0 %collective-permute-start.1 = (bf16[384,256]{1,0:T(8,128)(2,1)}, bf16[384,256]{1,0:T(8,128)(2,1)S(1)}, u32[]{:S(2)}, u32[]{:S(2)}) collective-permute-start(bf16[384,256]{1,0:T(8,128)(2,1)} %get-tuple-element.80.refs_0_), channel_id=1, source_target_pairs={{0,2},{1,3},{2,0},{3,1},{4,6},{5,7},{6,4},{7,5},{8,10},{9,11},{10,... | collective-permute-start | bytes 589832 | tf_op jit(solution)/shard_map/ppermute | solution.py:151
  6.4 8.6 %copy.12 = bf16[1536,2048]{0,1:T(8,128)(2,1)} copy(bf16[1536,2048]{1,0:T(8,128)(2,1)} %param.5) | data formatting | bytes 12582912 | tf_op jit(solution)/shard_map/optimization_barrier | solution.py:129
  15.6 0.9 collective-permute-done.refs_1_
  16.8 4.8 %partials.4 = (bf16[2048,256]{1,0:T(8,128)(2,1)S(1)}, f32[4,4,256]{2,1,0:T(4,128)S(1)}) custom-call(bf16[2048,1536]{1,0:T(8,128)(2,1)} %bitcast.17, bf16[384,256]{1,0:T(8,128)(2,1)S(1)} %copy-done.3, bf16[384,256]{1,0:T(8,128)(2,1)S(1)} %collective-permute-done.refs_1_, bf16[384,256]{1,0:T(8,128)(2,1)S(1)} %collective-permute-done.1.refs_2_, ...), custom_call_target="tpu_custom_call" | custom-call | tf_op jit(solution)/shard_map/partials/pallas_call | solution.py:79
  21.6 1.5 collective-permute-start.6
  23.6 10.5 %collective-permute-done.4.refs_2_ = bf16[384,512]{1,0:T(8,128)(2,1)S(1)} collective-permute-done((bf16[384,512]{1,0:T(8,128)(2,1)S(1)}, bf16[384,512]{1,0:T(8,128)(2,1)S(1)}, u32[]{:S(2)}, u32[]{:S(2)}) %collective-permute-start.4) | collective-permute-done | bytes 393248 | tf_op jit(solution)/shard_map/ppermute | solution.py:151
  34.6 1.2 collective-permute-done.5.refs_3_
  35.8 6.1 %partials.5 = (bf16[2048,256]{1,0:T(8,128)(2,1)S(1)}, bf16[2048,256]{1,0:T(8,128)(2,1)S(1)}, f32[4,4,512]{2,1,0:T(4,128)S(1)}) custom-call(bf16[2048,1536]{1,0:T(8,128)(2,1)} %bitcast.18, bf16[384,512]{1,0:T(8,128)(2,1)S(1)} %copy-done.2, bf16[384,512]{1,0:T(8,128)(2,1)S(1)} %collective-permute-done.3.refs_1_, ...), custom_call_target="tpu_custom_call" | custom-call | tf_op jit(solution)/shard_map/partials/pallas_call | solution.py:79
  41.9 0.6 collective-permute-start.14
  42.5 5.1 %collective-permute-done.6 = bf16[2048,256]{1,0:T(8,128)(2,1)S(1)} collective-permute-done((bf16[2048,256]{1,0:T(8,128)(2,1)S(1)}, bf16[2048,256]{1,0:T(8,128)(2,1)S(1)}, u32[]{:S(2)}, u32[]{:S(2)}) %collective-permute-start.6) | collective-permute-done | bytes 1048608 | tf_op jit(solution)/shard_map/ppermute | solution.py:148
  47.9 1.9 collective-permute-done.8.refs_2_
  50.9 3.5 %collective-permute-start.16 = (bf16[2048,256]{1,0:T(8,128)(2,1)S(1)}, bf16[2048,256]{1,0:T(8,128)(2,1)S(1)}, u32[]{:S(2)}, u32[]{:S(2)}) collective-permute-start(bf16[2048,256]{1,0:T(8,128)(2,1)S(1)} %add_convert_fusion.4), channel_id=1, source_target_pairs={{0,8},{4,12},{24,16},{28,20},{1,9},{5,13},{25,17},{29,21},{2,10},{... | collective-permute-start | bytes 3145736 | tf_op jit(solution)/shard_map/ppermute | solution.py:144
  54.4 8.0 %partials.6 = (bf16[2048,256]{1,0:T(8,128)(2,1)S(1)}, bf16[2048,256]{1,0:T(8,128)(2,1)}, bf16[2048,256]{1,0:T(8,128)(2,1)S(1)}, f32[4,4,768]{2,1,0:T(4,128)S(1)}) custom-call(bf16[2048,1536]{1,0:T(8,128)(2,1)} %bitcast.19, bf16[384,768]{1,0:T(8,128)(2,1)S(1)} %copy-done, bf16[384,768]{1,0:T(8,128)(2,1)S(1)} %collective-permute-done.7.refs_1_, ...), custom_call_target="tpu_custom_call" | custom-call | tf_op jit(solution)/shard_map/partials/pallas_call | solution.py:79
  63.0 1.2 collective-permute-done.12.refs_3_
  64.8 6.1 %partials.7 = (bf16[2048,256]{1,0:T(8,128)(2,1)S(1)}, bf16[2048,256]{1,0:T(8,128)(2,1)S(1)}, f32[4,4,512]{2,1,0:T(4,128)S(1)}) custom-call(bf16[2048,1536]{1,0:T(8,128)(2,1)} %bitcast.20, bf16[384,512]{1,0:T(8,128)(2,1)S(1)} %copy-done.1, bf16[384,512]{1,0:T(8,128)(2,1)S(1)} %collective-permute-done.10.refs_1_, ...), custom_call_target="tpu_custom_call" | custom-call | tf_op jit(solution)/shard_map/partials/pallas_call | solution.py:79
  70.9 1.3 add_convert_fusion.3
  72.2 3.4 %collective-permute-start.15 = (bf16[2048,256]{1,0:T(8,128)(2,1)}, bf16[2048,256]{1,0:T(8,128)(2,1)}, u32[]{:S(2)}, u32[]{:S(2)}) collective-permute-start(bf16[2048,256]{1,0:T(8,128)(2,1)} %add_convert_fusion.3), channel_id=1, source_target_pairs={{0,8},{4,12},{24,16},{28,20},{1,9},{5,13},{25,17},{29,21},{2,10},{... | collective-permute-start | bytes 3145736 | tf_op jit(solution)/shard_map/ppermute | solution.py:144
  75.5 1.1 collective-permute-start.18
  76.7 1.2 collective-permute-done.16
  77.9 1.3 add_convert_fusion.2
  79.3 1.6 collective-permute-start.19
  82.3 16.9 %collective-permute-done.15 = bf16[2048,256]{1,0:T(8,128)(2,1)} collective-permute-done((bf16[2048,256]{1,0:T(8,128)(2,1)}, bf16[2048,256]{1,0:T(8,128)(2,1)}, u32[]{:S(2)}, u32[]{:S(2)}) %collective-permute-start.15) | collective-permute-done | bytes 1048608 | tf_op jit(solution)/shard_map/ppermute | solution.py:144
  99.2 2.9 %add_convert_fusion.1 = bf16[2048,256]{1,0:T(8,128)(2,1)} fusion(bf16[2048,256]{1,0:T(8,128)(2,1)} %collective-permute-done.15, bf16[2048,256]{1,0:T(8,128)(2,1)} %copy-done.9, bf16[2048,256]{1,0:T(8,128)(2,1)S(1)} %get-tuple-element.119), kind=kLoop, calls=%fused_computation.5 | loop fusion | flops 3145728 | bytes 4194304 | tf_op jit(solution)/shard_map/convert_element_type | solution.py:101
  102.1 1.6 collective-permute-start.17
  103.7 2.9 %add_convert_fusion = bf16[2048,256]{1,0:T(8,128)(2,1)} fusion(bf16[2048,256]{1,0:T(8,128)(2,1)} %collective-permute-done.19, bf16[2048,256]{1,0:T(8,128)(2,1)} %collective-permute-done.18, bf16[2048,256]{1,0:T(8,128)(2,1)S(1)} %get-tuple-element.123), kind=kLoop, calls=%fused_computation.4 | loop fusion | flops 3145728 | bytes 4194304 | tf_op jit(solution)/shard_map/convert_element_type | solution.py:101
  106.6 4.3 %collective-permute-start.20 = (bf16[2048,256]{1,0:T(8,128)(2,1)}, bf16[2048,256]{1,0:T(8,128)(2,1)}, u32[]{:S(2)}, u32[]{:S(2)}) collective-permute-start(bf16[2048,256]{1,0:T(8,128)(2,1)} %add_convert_fusion), channel_id=1, source_target_pairs={{0,8},{4,12},{8,0},{12,4},{16,24},{20,28},{24,16},{28,20},{1,9},{5... | collective-permute-start | bytes 3145736 | tf_op jit(solution)/shard_map/ppermute | solution.py:144
  111.5 11.8 %collective-permute-done.21 = f32[16,16]{1,0:T(8,128)S(1)} collective-permute-done((f32[16,16]{1,0:T(8,128)S(1)}, f32[16,16]{1,0:T(8,128)S(1)}, u32[]{:S(2)}, u32[]{:S(2)}) %collective-permute-start.21) | collective-permute-done | bytes 1056 | tf_op jit(solution)/shard_map/ppermute | solution.py:148
  123.3 9.9 %collective-permute-done.22 = f32[16,16]{1,0:T(8,128)S(1)} collective-permute-done((f32[16,16]{1,0:T(8,128)S(1)}, f32[16,16]{1,0:T(8,128)S(1)}, u32[]{:S(2)}, u32[]{:S(2)}) %collective-permute-start.22) | collective-permute-done | bytes 1056 | tf_op jit(solution)/shard_map/ppermute | solution.py:144
  133.3 3.2 %subtract_convert_fusion.1 = bf16[1024,256]{1,0:T(8,128)(2,1)S(1)} fusion(f32[2048,256]{1,0:T(8,128)} %param.9, f32[2048,256]{1,0:T(8,128)} %param.8, f32[2048,256]{1,0:T(8,128)S(1)} %copy-done.6, bf16[2048,256]{1,0:T(8,128)(2,1)} %collective-permute-done.20, bf16[2048,256]{1,0:T(8,128)(2,1)} %collective-permute-done.17, ...), kind=kLoop, calls=%fused_computation.10 | loop fusion | flops 5767168 | bytes 5767168 | tf_op jit(solution)/shard_map/convert_element_type | solution.py:115
  136.5 0.6 collective-permute-start.23
  137.1 1.7 collective-permute-start.25
  138.8 0.9 collective-permute-start.29
  139.8 2.6 %subtract_convert_fusion = bf16[1024,256]{1,0:T(8,128)(2,1)S(1)} fusion(f32[2048,256]{1,0:T(8,128)S(1)} %copy-done.8, f32[2048,256]{1,0:T(8,128)S(1)} %copy-done.7, f32[2048,256]{1,0:T(8,128)S(1)} %copy-done.6, bf16[2048,256]{1,0:T(8,128)(2,1)} %collective-permute-done.20, bf16[2048,256]{1,0:T(8,128)(2,1)} %collective-permute-done.17, ...), kind=kLoop, calls=%fused_computation.9 | loop fusion | flops 5767168 | bytes 5767168 | tf_op jit(solution)/shard_map/convert_element_type | solution.py:115
  142.4 2.0 collective-permute-start.26
  144.4 1.1 collective-permute-start.45
  145.5 6.0 %divide_subtract_fusion = (f32[2048,256]{1,0:T(8,128)}, f32[2048,256]{1,0:T(8,128)}, f32[2048,256]{1,0:T(8,128)}) fusion(f32[2048,256]{1,0:T(8,128)S(1)} %copy-done.6, bf16[2048,256]{1,0:T(8,128)(2,1)} %collective-permute-done.20, bf16[2048,256]{1,0:T(8,128)(2,1)} %collective-permute-done.17, bf16[2048,256]{1,0:T(8,128)(2,1)} %collective-permute-done.13, ...), kind=kLoop, calls=%fused_computation | loop fusion | flops 11010048 | bytes 16777216 | tf_op jit(solution)/shard_map/sub | solution.py:114
  151.4 7.6 %collective-permute-done.45 = f32[16,16]{1,0:T(8,128)S(1)} collective-permute-done((f32[16,16]{1,0:T(8,128)S(1)}, f32[16,16]{1,0:T(8,128)S(1)}, u32[]{:S(2)}, u32[]{:S(2)}) %collective-permute-start.45) | collective-permute-done | bytes 1056 | tf_op jit(solution)/shard_map/ppermute | solution.py:144
  159.0 1.5 collective-permute-start.24
  160.7 0.7 collective-permute-start.31
  162.0 1.5 collective-permute-start.28
  164.1 1.3 collective-permute-start.30
  165.5 8.4 %collective-permute-done.24 = bf16[1024,256]{1,0:T(8,128)(2,1)S(1)} collective-permute-done((bf16[1024,256]{1,0:T(8,128)(2,1)S(1)}, bf16[1024,256]{1,0:T(8,128)(2,1)S(1)}, u32[]{:S(2)}, u32[]{:S(2)}) %collective-permute-start.24) | collective-permute-done | bytes 524320 | tf_op jit(solution)/shard_map/ppermute | solution.py:148
  173.9 0.7 collective-permute-start.33
  174.8 0.7 collective-permute-start.37
  175.5 9.7 %collective-permute-done.27 = bf16[1024,256]{1,0:T(8,128)(2,1)S(1)} collective-permute-done((bf16[1024,256]{1,0:T(8,128)(2,1)S(1)}, bf16[1024,256]{1,0:T(8,128)(2,1)S(1)}, u32[]{:S(2)}, u32[]{:S(2)}) %collective-permute-start.27) | collective-permute-done | bytes 524320 | tf_op jit(solution)/shard_map/ppermute | solution.py:148
  185.1 0.7 collective-permute-start.39
  185.8 6.0 %collective-permute-done.28 = bf16[1024,256]{1,0:T(8,128)(2,1)S(1)} collective-permute-done((bf16[1024,256]{1,0:T(8,128)(2,1)S(1)}, bf16[1024,256]{1,0:T(8,128)(2,1)S(1)}, u32[]{:S(2)}, u32[]{:S(2)}) %collective-permute-start.28) | collective-permute-done | bytes 524320 | tf_op jit(solution)/shard_map/ppermute | solution.py:148
  191.9 1.3 collective-permute-start.32
  193.3 3.4 %collective-permute-start.34 = (bf16[1024,256]{1,0:T(8,128)(2,1)S(1)}, bf16[1024,256]{1,0:T(8,128)(2,1)S(1)}, u32[]{:S(2)}, u32[]{:S(2)}) collective-permute-start(bf16[1024,256]{1,0:T(8,128)(2,1)S(1)} %collective-permute-done.30), channel_id=1, source_target_pairs={{0,4},{4,0},{24,28},{28,24},{1,5},{5,1},{25,29},{29,25},{2,6},{6,2... | collective-permute-start | bytes 1572872 | tf_op jit(solution)/shard_map/ppermute | solution.py:148
  196.9 11.6 %collective-permute-done.32 = bf16[1024,256]{1,0:T(8,128)(2,1)S(1)} collective-permute-done((bf16[1024,256]{1,0:T(8,128)(2,1)S(1)}, bf16[1024,256]{1,0:T(8,128)(2,1)S(1)}, u32[]{:S(2)}, u32[]{:S(2)}) %collective-permute-start.32) | collective-permute-done | bytes 524320 | tf_op jit(solution)/shard_map/ppermute | solution.py:144
  208.6 0.7 collective-permute-start.35
  209.3 4.3 %collective-permute-start.36 = (bf16[1024,256]{1,0:T(8,128)(2,1)S(1)}, bf16[1024,256]{1,0:T(8,128)(2,1)S(1)}, u32[]{:S(2)}, u32[]{:S(2)}) collective-permute-start(bf16[1024,256]{1,0:T(8,128)(2,1)S(1)} %collective-permute-done.32), channel_id=1, source_target_pairs={{0,4},{4,0},{24,28},{28,24},{1,5},{5,1},{25,29},{29,25},{2,6},{6,2... | collective-permute-start | bytes 1572872 | tf_op jit(solution)/shard_map/ppermute | solution.py:148
  213.6 1.3 collective-permute-start.38
  214.9 1.3 collective-permute-start.40
  216.4 0.7 collective-permute-start.41
  217.3 0.7 collective-permute-start.43
  218.0 6.7 %collective-permute-done.38 = bf16[1024,256]{1,0:T(8,128)(2,1)S(1)} collective-permute-done((bf16[1024,256]{1,0:T(8,128)(2,1)S(1)}, bf16[1024,256]{1,0:T(8,128)(2,1)S(1)}, u32[]{:S(2)}, u32[]{:S(2)}) %collective-permute-start.38) | collective-permute-done | bytes 524320 | tf_op jit(solution)/shard_map/ppermute | solution.py:144
  224.7 2.7 %collective-permute-start.42 = (bf16[1024,256]{1,0:T(8,128)(2,1)S(1)}, bf16[1024,256]{1,0:T(8,128)(2,1)S(1)}, u32[]{:S(2)}, u32[]{:S(2)}) collective-permute-start(bf16[1024,256]{1,0:T(8,128)(2,1)S(1)} %collective-permute-done.38), channel_id=1, source_target_pairs={{0,4},{4,0},{24,28},{28,24},{1,5},{5,1},{25,29},{29,25},{2,6},{6,2... | collective-permute-start | bytes 1572872 | tf_op jit(solution)/shard_map/ppermute | solution.py:148
  227.4 2.9 %collective-permute-done.40 = bf16[1024,256]{1,0:T(8,128)(2,1)S(1)} collective-permute-done((bf16[1024,256]{1,0:T(8,128)(2,1)S(1)}, bf16[1024,256]{1,0:T(8,128)(2,1)S(1)}, u32[]{:S(2)}, u32[]{:S(2)}) %collective-permute-start.40) | collective-permute-done | bytes 524320 | tf_op jit(solution)/shard_map/ppermute | solution.py:144
  230.3 2.7 %collective-permute-start.44 = (bf16[1024,256]{1,0:T(8,128)(2,1)S(1)}, bf16[1024,256]{1,0:T(8,128)(2,1)S(1)}, u32[]{:S(2)}, u32[]{:S(2)}) collective-permute-start(bf16[1024,256]{1,0:T(8,128)(2,1)S(1)} %collective-permute-done.40), channel_id=1, source_target_pairs={{0,4},{4,0},{24,28},{28,24},{1,5},{5,1},{25,29},{29,25},{2,6},{6,2... | collective-permute-start | bytes 1572872 | tf_op jit(solution)/shard_map/ppermute | solution.py:148
  233.5 4.1 %collective-permute-done.42 = bf16[1024,256]{1,0:T(8,128)(2,1)S(1)} collective-permute-done((bf16[1024,256]{1,0:T(8,128)(2,1)S(1)}, bf16[1024,256]{1,0:T(8,128)(2,1)S(1)}, u32[]{:S(2)}, u32[]{:S(2)}) %collective-permute-start.42) | collective-permute-done | bytes 524320 | tf_op jit(solution)/shard_map/ppermute | solution.py:148
  237.8 5.5 %collective-permute-done.44 = bf16[1024,256]{1,0:T(8,128)(2,1)S(1)} collective-permute-done((bf16[1024,256]{1,0:T(8,128)(2,1)S(1)}, bf16[1024,256]{1,0:T(8,128)(2,1)S(1)}, u32[]{:S(2)}, u32[]{:S(2)}) %collective-permute-start.44) | collective-permute-done | bytes 524320 | tf_op jit(solution)/shard_map/ppermute | solution.py:148
  243.4 3.4 %copy-done.5 = bf16[2048,2048]{1,0:T(8,128)(2,1)} copy-done((bf16[2048,2048]{1,0:T(8,128)(2,1)}, bf16[2048,2048]{1,0:T(8,128)(2,1)S(1)}, u32[]{:S(2)}) %copy-start.5) | copy-done | bytes 8388632
  (99 shorter events, 9.1 us)
Async XLA Ops:
  3.4 11.6 %copy-start.3 = (bf16[384,256]{1,0:T(8,128)(2,1)S(1)}, bf16[384,256]{1,0:T(8,128)(2,1)}, u32[]{:S(2)}) copy-start(bf16[384,256]{1,0:T(8,128)(2,1)} %get-tuple-element.80.refs_0_) | copy-start | bytes 589828
  3.4 11.7 %collective-permute-start.1 = (bf16[384,256]{1,0:T(8,128)(2,1)}, bf16[384,256]{1,0:T(8,128)(2,1)S(1)}, u32[]{:S(2)}, u32[]{:S(2)}) collective-permute-start(bf16[384,256]{1,0:T(8,128)(2,1)} %get-tuple-element.80.refs_0_), channel_id=1, source_target_pairs={{0,2},{1,3},{2,0},{3,1},{4,6},{5,7},{6,4},{7,5},{8,10},{9,11},{10,... | collective-permute-start | bytes 589832 | tf_op jit(solution)/shard_map/ppermute | solution.py:151
  15.0 8.1 %copy-start.2 = (bf16[384,512]{1,0:T(8,128)(2,1)S(1)}, bf16[384,512]{1,0:T(8,128)(2,1)}, u32[]{:S(2)}) copy-start(bf16[384,512]{1,0:T(8,128)(2,1)} %get-tuple-element.86.refs_0_) | copy-start | bytes 1179652
  15.0 19.1 %copy-start = (bf16[384,768]{1,0:T(8,128)(2,1)S(1)}, bf16[384,768]{1,0:T(8,128)(2,1)}, u32[]{:S(2)}) copy-start(bf16[384,768]{1,0:T(8,128)(2,1)} %get-tuple-element.94.refs_0_) | copy-start | bytes 1769476
  15.0 1.5 collective-permute-start
  15.1 1.7 collective-permute-start.2
  21.6 26.1 %collective-permute-start.6 = (bf16[2048,256]{1,0:T(8,128)(2,1)S(1)}, bf16[2048,256]{1,0:T(8,128)(2,1)S(1)}, u32[]{:S(2)}, u32[]{:S(2)}) collective-permute-start(bf16[2048,256]{1,0:T(8,128)(2,1)S(1)} %get-tuple-element.82), channel_id=1, source_target_pairs={{0,4},{4,0},{8,12},{12,8},{16,20},{20,16},{24,28},{28,24},{1,5},{5... | collective-permute-start | bytes 3145736 | tf_op jit(solution)/shard_map/ppermute | solution.py:148
  23.1 11.0 %collective-permute-start.4 = (bf16[384,512]{1,0:T(8,128)(2,1)S(1)}, bf16[384,512]{1,0:T(8,128)(2,1)S(1)}, u32[]{:S(2)}, u32[]{:S(2)}) collective-permute-start(bf16[384,512]{1,0:T(8,128)(2,1)S(1)} %copy-done.2), channel_id=1, source_target_pairs={{0,2},{1,3},{2,0},{3,1},{4,6},{5,7},{6,4},{7,5},{8,10},{9,11},{10,... | collective-permute-start | bytes 1179656 | tf_op jit(solution)/shard_map/ppermute | solution.py:151
  23.6 11.0 %collective-permute-start.3 = (bf16[384,512]{1,0:T(8,128)(2,1)S(1)}, bf16[384,512]{1,0:T(8,128)(2,1)S(1)}, u32[]{:S(2)}, u32[]{:S(2)}) collective-permute-start(bf16[384,512]{1,0:T(8,128)(2,1)S(1)} %copy-done.2), channel_id=1, source_target_pairs={{0,1},{1,0},{2,3},{3,2},{4,5},{5,4},{6,7},{7,6},{8,9},{9,8},{10,11... | collective-permute-start | bytes 1179656 | tf_op jit(solution)/shard_map/ppermute | solution.py:151
  34.1 1.7 collective-permute-start.5
  34.1 15.7 %collective-permute-start.8 = (bf16[384,768]{1,0:T(8,128)(2,1)S(1)}, bf16[384,768]{1,0:T(8,128)(2,1)S(1)}, u32[]{:S(2)}, u32[]{:S(2)}) collective-permute-start(bf16[384,768]{1,0:T(8,128)(2,1)S(1)} %copy-done), channel_id=1, source_target_pairs={{0,2},{1,3},{2,0},{3,1},{4,6},{5,7},{6,4},{7,5},{8,10},{9,11},{10,... | collective-permute-start | bytes 1769480 | tf_op jit(solution)/shard_map/ppermute | solution.py:151
  41.9 8.5 %copy-start.1 = (bf16[384,512]{1,0:T(8,128)(2,1)S(1)}, bf16[384,512]{1,0:T(8,128)(2,1)}, u32[]{:S(2)}) copy-start(bf16[384,512]{1,0:T(8,128)(2,1)} %get-tuple-element.100.refs_0_) | copy-start | bytes 1179652
  41.9 28.9 %collective-permute-start.14 = (bf16[2048,256]{1,0:T(8,128)(2,1)S(1)}, bf16[2048,256]{1,0:T(8,128)(2,1)S(1)}, u32[]{:S(2)}, u32[]{:S(2)}) collective-permute-start(bf16[2048,256]{1,0:T(8,128)(2,1)S(1)} %get-tuple-element.104), channel_id=1, source_target_pairs={{0,4},{4,0},{8,12},{12,8},{16,20},{20,16},{24,28},{28,24},{1,5},{5... | collective-permute-start | bytes 3145736 | tf_op jit(solution)/shard_map/ppermute | solution.py:148
  49.8 4.6 %collective-permute-start.9 = (bf16[384,768]{1,0:T(8,128)(2,1)S(1)}, bf16[384,768]{1,0:T(8,128)(2,1)S(1)}, u32[]{:S(2)}, u32[]{:S(2)}) collective-permute-start(bf16[384,768]{1,0:T(8,128)(2,1)S(1)} %collective-permute-done.8.refs_2_), channel_id=1, source_target_pairs={{0,1},{1,0},{2,3},{3,2},{4,5},{5,4},{6,7},{7,6},{8,9},{9,8},{10,11... | collective-permute-start | bytes 1769480 | tf_op jit(solution)/shard_map/ppermute | solution.py:151
  49.8 4.6 %collective-permute-start.7 = (bf16[384,768]{1,0:T(8,128)(2,1)S(1)}, bf16[384,768]{1,0:T(8,128)(2,1)S(1)}, u32[]{:S(2)}, u32[]{:S(2)}) collective-permute-start(bf16[384,768]{1,0:T(8,128)(2,1)S(1)} %copy-done), channel_id=1, source_target_pairs={{0,1},{1,0},{2,3},{3,2},{4,5},{5,4},{6,7},{7,6},{8,9},{9,8},{10,11... | collective-permute-start | bytes 1769480 | tf_op jit(solution)/shard_map/ppermute | solution.py:151
  50.4 12.1 %collective-permute-start.11 = (bf16[384,512]{1,0:T(8,128)(2,1)S(1)}, bf16[384,512]{1,0:T(8,128)(2,1)S(1)}, u32[]{:S(2)}, u32[]{:S(2)}) collective-permute-start(bf16[384,512]{1,0:T(8,128)(2,1)S(1)} %copy-done.1), channel_id=1, source_target_pairs={{0,2},{1,3},{2,0},{3,1},{4,6},{5,7},{6,4},{7,5},{8,10},{9,11},{10,... | collective-permute-start | bytes 1179656 | tf_op jit(solution)/shard_map/ppermute | solution.py:151
  50.9 27.0 %collective-permute-start.16 = (bf16[2048,256]{1,0:T(8,128)(2,1)S(1)}, bf16[2048,256]{1,0:T(8,128)(2,1)S(1)}, u32[]{:S(2)}, u32[]{:S(2)}) collective-permute-start(bf16[2048,256]{1,0:T(8,128)(2,1)S(1)} %add_convert_fusion.4), channel_id=1, source_target_pairs={{0,8},{4,12},{24,16},{28,20},{1,9},{5,13},{25,17},{29,21},{2,10},{... | collective-permute-start | bytes 3145736 | tf_op jit(solution)/shard_map/ppermute | solution.py:144
  62.5 8.4 %copy-start.4 = (bf16[2048,256]{1,0:T(8,128)(2,1)}, bf16[2048,256]{1,0:T(8,128)(2,1)S(1)}, u32[]{:S(2)}) copy-start(bf16[2048,256]{1,0:T(8,128)(2,1)S(1)} %get-tuple-element.103) | copy-start | bytes 3145732
  62.5 1.7 collective-permute-start.12
  62.5 2.3 collective-permute-start.10
  70.8 8.4 %copy-start.9 = (bf16[2048,256]{1,0:T(8,128)(2,1)}, bf16[2048,256]{1,0:T(8,128)(2,1)S(1)}, u32[]{:S(2)}) copy-start(bf16[2048,256]{1,0:T(8,128)(2,1)S(1)} %collective-permute-done.14) | copy-start | bytes 3145732
  72.2 27.0 %collective-permute-start.15 = (bf16[2048,256]{1,0:T(8,128)(2,1)}, bf16[2048,256]{1,0:T(8,128)(2,1)}, u32[]{:S(2)}, u32[]{:S(2)}) collective-permute-start(bf16[2048,256]{1,0:T(8,128)(2,1)} %add_convert_fusion.3), channel_id=1, source_target_pairs={{0,8},{4,12},{24,16},{28,20},{1,9},{5,13},{25,17},{29,21},{2,10},{... | collective-permute-start | bytes 3145736 | tf_op jit(solution)/shard_map/ppermute | solution.py:144
  75.5 28.2 %collective-permute-start.18 = (bf16[2048,256]{1,0:T(8,128)(2,1)}, bf16[2048,256]{1,0:T(8,128)(2,1)}, u32[]{:S(2)}, u32[]{:S(2)}) collective-permute-start(bf16[2048,256]{1,0:T(8,128)(2,1)} %get-tuple-element.122), channel_id=1, source_target_pairs={{0,4},{4,0},{8,12},{12,8},{16,20},{20,16},{24,28},{28,24},{1,5},{5... | collective-permute-start | bytes 3145736 | tf_op jit(solution)/shard_map/ppermute | solution.py:148
  79.3 24.5 %collective-permute-start.19 = (bf16[2048,256]{1,0:T(8,128)(2,1)}, bf16[2048,256]{1,0:T(8,128)(2,1)}, u32[]{:S(2)}, u32[]{:S(2)}) collective-permute-start(bf16[2048,256]{1,0:T(8,128)(2,1)} %add_convert_fusion.2), channel_id=1, source_target_pairs={{8,16},{12,20},{16,8},{20,12},{9,17},{13,21},{17,9},{21,13},{10,18... | collective-permute-start | bytes 3145736 | tf_op jit(solution)/shard_map/ppermute | solution.py:144
  81.1 52.2 %collective-permute-start.13 = (bf16[2048,256]{1,0:T(8,128)(2,1)}, bf16[2048,256]{1,0:T(8,128)(2,1)}, u32[]{:S(2)}, u32[]{:S(2)}) collective-permute-start(bf16[2048,256]{1,0:T(8,128)(2,1)} %copy-done.4), channel_id=1, source_target_pairs={{0,4},{4,0},{8,12},{12,8},{16,20},{20,16},{24,28},{28,24},{1,5},{5... | collective-permute-start | bytes 3145736 | tf_op jit(solution)/shard_map/ppermute | solution.py:148
  102.1 31.2 %collective-permute-start.17 = (bf16[2048,256]{1,0:T(8,128)(2,1)}, bf16[2048,256]{1,0:T(8,128)(2,1)}, u32[]{:S(2)}, u32[]{:S(2)}) collective-permute-start(bf16[2048,256]{1,0:T(8,128)(2,1)} %add_convert_fusion.1), channel_id=1, source_target_pairs={{8,16},{12,20},{16,8},{20,12},{9,17},{13,21},{17,9},{21,13},{10,18... | collective-permute-start | bytes 3145736 | tf_op jit(solution)/shard_map/ppermute | solution.py:144
  106.6 26.6 %copy-start.6 = (f32[2048,256]{1,0:T(8,128)S(1)}, f32[2048,256]{1,0:T(8,128)}, u32[]{:S(2)}) copy-start(f32[2048,256]{1,0:T(8,128)} %param.7) | copy-start | bytes 6291460
  106.6 26.6 %collective-permute-start.20 = (bf16[2048,256]{1,0:T(8,128)(2,1)}, bf16[2048,256]{1,0:T(8,128)(2,1)}, u32[]{:S(2)}, u32[]{:S(2)}) collective-permute-start(bf16[2048,256]{1,0:T(8,128)(2,1)} %add_convert_fusion), channel_id=1, source_target_pairs={{0,8},{4,12},{8,0},{12,4},{16,24},{20,28},{24,16},{28,20},{1,9},{5... | collective-permute-start | bytes 3145736 | tf_op jit(solution)/shard_map/ppermute | solution.py:144
  111.0 12.4 %collective-permute-start.21 = (f32[16,16]{1,0:T(8,128)S(1)}, f32[16,16]{1,0:T(8,128)S(1)}, u32[]{:S(2)}, u32[]{:S(2)}) collective-permute-start(f32[16,16]{1,0:T(8,128)S(1)} %select_reduce_fusion), channel_id=1, source_target_pairs={{0,4},{4,0},{8,12},{12,8},{16,20},{20,16},{24,28},{28,24},{1,5},{5... | collective-permute-start | bytes 3080 | tf_op jit(solution)/shard_map/ppermute | solution.py:148
  123.3 9.9 %collective-permute-start.22 = (f32[16,16]{1,0:T(8,128)S(1)}, f32[16,16]{1,0:T(8,128)S(1)}, u32[]{:S(2)}, u32[]{:S(2)}) collective-permute-start(f32[16,16]{1,0:T(8,128)S(1)} %max.9), channel_id=1, source_target_pairs={{0,8},{4,12},{8,0},{12,4},{16,24},{20,28},{24,16},{28,20},{1,9},{5... | collective-permute-start | bytes 3080 | tf_op jit(solution)/shard_map/ppermute | solution.py:144
  133.3 6.5 %copy-start.7 = (f32[2048,256]{1,0:T(8,128)S(1)}, f32[2048,256]{1,0:T(8,128)}, u32[]{:S(2)}) copy-start(f32[2048,256]{1,0:T(8,128)} %param.8) | copy-start | bytes 6291460
  133.3 6.4 %copy-start.8 = (f32[2048,256]{1,0:T(8,128)S(1)}, f32[2048,256]{1,0:T(8,128)}, u32[]{:S(2)}) copy-start(f32[2048,256]{1,0:T(8,128)} %param.9) | copy-start | bytes 6291460
  136.5 24.2 %collective-permute-start.23 = (bf16[1024,256]{1,0:T(8,128)(2,1)S(1)}, bf16[1024,256]{1,0:T(8,128)(2,1)S(1)}, u32[]{:S(2)}, u32[]{:S(2)}) collective-permute-start(bf16[1024,256]{1,0:T(8,128)(2,1)S(1)} %subtract_convert_fusion.1), channel_id=1, source_target_pairs={{0,4},{4,0},{8,12},{12,8},{16,20},{20,16},{24,28},{28,24},{1,5},{5... | collective-permute-start | bytes 1572872 | tf_op jit(solution)/shard_map/ppermute | solution.py:148
  137.1 24.3 %collective-permute-start.25 = (bf16[1024,256]{1,0:T(8,128)(2,1)S(1)}, bf16[1024,256]{1,0:T(8,128)(2,1)S(1)}, u32[]{:S(2)}, u32[]{:S(2)}) collective-permute-start(bf16[1024,256]{1,0:T(8,128)(2,1)S(1)} %subtract_convert_fusion.1), channel_id=1, source_target_pairs={{0,8},{4,12},{8,0},{12,4},{16,24},{20,28},{24,16},{28,20},{1,9},{5... | collective-permute-start | bytes 1572872 | tf_op jit(solution)/shard_map/ppermute | solution.py:144
  138.8 25.3 %collective-permute-start.29 = (bf16[1024,256]{1,0:T(8,128)(2,1)S(1)}, bf16[1024,256]{1,0:T(8,128)(2,1)S(1)}, u32[]{:S(2)}, u32[]{:S(2)}) collective-permute-start(bf16[1024,256]{1,0:T(8,128)(2,1)S(1)} %subtract_convert_fusion.1), channel_id=1, source_target_pairs={{8,16},{12,20},{16,8},{20,12},{9,17},{13,21},{17,9},{21,13},{10,18... | collective-permute-start | bytes 1572872 | tf_op jit(solution)/shard_map/ppermute | solution.py:144
  139.7 20.8 %slice-start = ((s8[8388608]{0:T(1024)(128)(4,1)}), s8[4194304]{0:T(1024)(128)(4,1)S(1)}, s32[]{:S(2)}) async-start(s8[8388608]{0:T(1024)(128)(4,1)} %bitcast.21), calls=%async_computation | async-start | bytes 8388608
  142.3 18.2 %slice-start.1 = ((s8[8388608]{0:T(1024)(128)(4,1)}), s8[4194304]{0:T(1024)(128)(4,1)S(1)}, s32[]{:S(2)}) async-start(s8[8388608]{0:T(1024)(128)(4,1)} %bitcast.21), calls=%async_computation.1 | async-start | bytes 8388608
  142.4 19.7 %collective-permute-start.26 = (bf16[1024,256]{1,0:T(8,128)(2,1)S(1)}, bf16[1024,256]{1,0:T(8,128)(2,1)S(1)}, u32[]{:S(2)}, u32[]{:S(2)}) collective-permute-start(bf16[1024,256]{1,0:T(8,128)(2,1)S(1)} %subtract_convert_fusion), channel_id=1, source_target_pairs={{0,8},{4,12},{8,0},{12,4},{16,24},{20,28},{24,16},{28,20},{1,9},{5... | collective-permute-start | bytes 1572872 | tf_op jit(solution)/shard_map/ppermute | solution.py:144
  144.4 14.7 %collective-permute-start.45 = (f32[16,16]{1,0:T(8,128)S(1)}, f32[16,16]{1,0:T(8,128)S(1)}, u32[]{:S(2)}, u32[]{:S(2)}) collective-permute-start(f32[16,16]{1,0:T(8,128)S(1)} %max.10), channel_id=1, source_target_pairs={{0,16},{4,20},{8,24},{12,28},{16,0},{20,4},{24,8},{28,12},{1,17},{... | collective-permute-start | bytes 3080 | tf_op jit(solution)/shard_map/ppermute | solution.py:144
  159.0 14.9 %collective-permute-start.24 = (bf16[1024,256]{1,0:T(8,128)(2,1)S(1)}, bf16[1024,256]{1,0:T(8,128)(2,1)S(1)}, u32[]{:S(2)}, u32[]{:S(2)}) collective-permute-start(bf16[1024,256]{1,0:T(8,128)(2,1)S(1)} %subtract_convert_fusion), channel_id=1, source_target_pairs={{0,4},{4,0},{8,12},{12,8},{16,20},{20,16},{24,28},{28,24},{1,5},{5... | collective-permute-start | bytes 1572872 | tf_op jit(solution)/shard_map/ppermute | solution.py:148
  160.7 14.1 %collective-permute-start.31 = (bf16[1024,256]{1,0:T(8,128)(2,1)S(1)}, bf16[1024,256]{1,0:T(8,128)(2,1)S(1)}, u32[]{:S(2)}, u32[]{:S(2)}) collective-permute-start(bf16[1024,256]{1,0:T(8,128)(2,1)S(1)} %subtract_convert_fusion), channel_id=1, source_target_pairs={{8,16},{12,20},{16,8},{20,12},{9,17},{13,21},{17,9},{21,13},{10,18... | collective-permute-start | bytes 1572872 | tf_op jit(solution)/shard_map/ppermute | solution.py:144
  161.4 23.7 %collective-permute-start.27 = (bf16[1024,256]{1,0:T(8,128)(2,1)S(1)}, bf16[1024,256]{1,0:T(8,128)(2,1)S(1)}, u32[]{:S(2)}, u32[]{:S(2)}) collective-permute-start(bf16[1024,256]{1,0:T(8,128)(2,1)S(1)} %collective-permute-done.25), channel_id=1, source_target_pairs={{0,4},{4,0},{8,12},{12,8},{16,20},{20,16},{24,28},{28,24},{1,5},{5... | collective-permute-start | bytes 1572872 | tf_op jit(solution)/shard_map/ppermute | solution.py:148
  162.0 29.8 %collective-permute-start.28 = (bf16[1024,256]{1,0:T(8,128)(2,1)S(1)}, bf16[1024,256]{1,0:T(8,128)(2,1)S(1)}, u32[]{:S(2)}, u32[]{:S(2)}) collective-permute-start(bf16[1024,256]{1,0:T(8,128)(2,1)S(1)} %collective-permute-done.26), channel_id=1, source_target_pairs={{0,4},{4,0},{8,12},{12,8},{16,20},{20,16},{24,28},{28,24},{1,5},{5... | collective-permute-start | bytes 1572872 | tf_op jit(solution)/shard_map/ppermute | solution.py:148
  164.1 29.2 %collective-permute-start.30 = (bf16[1024,256]{1,0:T(8,128)(2,1)S(1)}, bf16[1024,256]{1,0:T(8,128)(2,1)S(1)}, u32[]{:S(2)}, u32[]{:S(2)}) collective-permute-start(bf16[1024,256]{1,0:T(8,128)(2,1)S(1)} %collective-permute-done.29), channel_id=1, source_target_pairs={{8,0},{12,4},{16,24},{20,28},{9,1},{13,5},{17,25},{21,29},{10,2},{... | collective-permute-start | bytes 1572872 | tf_op jit(solution)/shard_map/ppermute | solution.py:144
  173.9 35.4 %collective-permute-start.33 = (bf16[1024,256]{1,0:T(8,128)(2,1)S(1)}, bf16[1024,256]{1,0:T(8,128)(2,1)S(1)}, u32[]{:S(2)}, u32[]{:S(2)}) collective-permute-start(bf16[1024,256]{1,0:T(8,128)(2,1)S(1)} %collective-permute-done.29), channel_id=1, source_target_pairs={{8,12},{12,8},{16,20},{20,16},{9,13},{13,9},{17,21},{21,17},{10,14... | collective-permute-start | bytes 1572872 | tf_op jit(solution)/shard_map/ppermute | solution.py:148
  174.8 38.9 %collective-permute-start.37 = (bf16[1024,256]{1,0:T(8,128)(2,1)S(1)}, bf16[1024,256]{1,0:T(8,128)(2,1)S(1)}, u32[]{:S(2)}, u32[]{:S(2)}) collective-permute-start(bf16[1024,256]{1,0:T(8,128)(2,1)S(1)} %collective-permute-done.25), channel_id=1, source_target_pairs={{8,16},{12,20},{16,8},{20,12},{9,17},{13,21},{17,9},{21,13},{10,18... | collective-permute-start | bytes 1572872 | tf_op jit(solution)/shard_map/ppermute | solution.py:144
  185.1 29.8 %collective-permute-start.39 = (bf16[1024,256]{1,0:T(8,128)(2,1)S(1)}, bf16[1024,256]{1,0:T(8,128)(2,1)S(1)}, u32[]{:S(2)}, u32[]{:S(2)}) collective-permute-start(bf16[1024,256]{1,0:T(8,128)(2,1)S(1)} %collective-permute-done.26), channel_id=1, source_target_pairs={{8,16},{12,20},{16,8},{20,12},{9,17},{13,21},{17,9},{21,13},{10,18... | collective-permute-start | bytes 1572872 | tf_op jit(solution)/shard_map/ppermute | solution.py:144
  191.9 16.7 %collective-permute-start.32 = (bf16[1024,256]{1,0:T(8,128)(2,1)S(1)}, bf16[1024,256]{1,0:T(8,128)(2,1)S(1)}, u32[]{:S(2)}, u32[]{:S(2)}) collective-permute-start(bf16[1024,256]{1,0:T(8,128)(2,1)S(1)} %collective-permute-done.31), channel_id=1, source_target_pairs={{8,0},{12,4},{16,24},{20,28},{9,1},{13,5},{17,25},{21,29},{10,2},{... | collective-permute-start | bytes 1572872 | tf_op jit(solution)/shard_map/ppermute | solution.py:144
  193.3 23.1 %collective-permute-start.34 = (bf16[1024,256]{1,0:T(8,128)(2,1)S(1)}, bf16[1024,256]{1,0:T(8,128)(2,1)S(1)}, u32[]{:S(2)}, u32[]{:S(2)}) collective-permute-start(bf16[1024,256]{1,0:T(8,128)(2,1)S(1)} %collective-permute-done.30), channel_id=1, source_target_pairs={{0,4},{4,0},{24,28},{28,24},{1,5},{5,1},{25,29},{29,25},{2,6},{6,2... | collective-permute-start | bytes 1572872 | tf_op jit(solution)/shard_map/ppermute | solution.py:148
  208.6 8.7 %collective-permute-start.35 = (bf16[1024,256]{1,0:T(8,128)(2,1)S(1)}, bf16[1024,256]{1,0:T(8,128)(2,1)S(1)}, u32[]{:S(2)}, u32[]{:S(2)}) collective-permute-start(bf16[1024,256]{1,0:T(8,128)(2,1)S(1)} %collective-permute-done.31), channel_id=1, source_target_pairs={{8,12},{12,8},{16,20},{20,16},{9,13},{13,9},{17,21},{21,17},{10,14... | collective-permute-start | bytes 1572872 | tf_op jit(solution)/shard_map/ppermute | solution.py:148
  209.3 23.7 %collective-permute-start.36 = (bf16[1024,256]{1,0:T(8,128)(2,1)S(1)}, bf16[1024,256]{1,0:T(8,128)(2,1)S(1)}, u32[]{:S(2)}, u32[]{:S(2)}) collective-permute-start(bf16[1024,256]{1,0:T(8,128)(2,1)S(1)} %collective-permute-done.32), channel_id=1, source_target_pairs={{0,4},{4,0},{24,28},{28,24},{1,5},{5,1},{25,29},{29,25},{2,6},{6,2... | collective-permute-start | bytes 1572872 | tf_op jit(solution)/shard_map/ppermute | solution.py:148
  213.6 11.1 %collective-permute-start.38 = (bf16[1024,256]{1,0:T(8,128)(2,1)S(1)}, bf16[1024,256]{1,0:T(8,128)(2,1)S(1)}, u32[]{:S(2)}, u32[]{:S(2)}) collective-permute-start(bf16[1024,256]{1,0:T(8,128)(2,1)S(1)} %collective-permute-done.37), channel_id=1, source_target_pairs={{8,0},{12,4},{16,24},{20,28},{9,1},{13,5},{17,25},{21,29},{10,2},{... | collective-permute-start | bytes 1572872 | tf_op jit(solution)/shard_map/ppermute | solution.py:144
  214.9 15.4 %collective-permute-start.40 = (bf16[1024,256]{1,0:T(8,128)(2,1)S(1)}, bf16[1024,256]{1,0:T(8,128)(2,1)S(1)}, u32[]{:S(2)}, u32[]{:S(2)}) collective-permute-start(bf16[1024,256]{1,0:T(8,128)(2,1)S(1)} %collective-permute-done.39), channel_id=1, source_target_pairs={{8,0},{12,4},{16,24},{20,28},{9,1},{13,5},{17,25},{21,29},{10,2},{... | collective-permute-start | bytes 1572872 | tf_op jit(solution)/shard_map/ppermute | solution.py:144
  216.4 17.1 %collective-permute-start.41 = (bf16[1024,256]{1,0:T(8,128)(2,1)S(1)}, bf16[1024,256]{1,0:T(8,128)(2,1)S(1)}, u32[]{:S(2)}, u32[]{:S(2)}) collective-permute-start(bf16[1024,256]{1,0:T(8,128)(2,1)S(1)} %collective-permute-done.37), channel_id=1, source_target_pairs={{8,12},{12,8},{16,20},{20,16},{9,13},{13,9},{17,21},{21,17},{10,14... | collective-permute-start | bytes 1572872 | tf_op jit(solution)/shard_map/ppermute | solution.py:148
  217.3 20.5 %collective-permute-start.43 = (bf16[1024,256]{1,0:T(8,128)(2,1)S(1)}, bf16[1024,256]{1,0:T(8,128)(2,1)S(1)}, u32[]{:S(2)}, u32[]{:S(2)}) collective-permute-start(bf16[1024,256]{1,0:T(8,128)(2,1)S(1)} %collective-permute-done.39), channel_id=1, source_target_pairs={{8,12},{12,8},{16,20},{20,16},{9,13},{13,9},{17,21},{21,17},{10,14... | collective-permute-start | bytes 1572872 | tf_op jit(solution)/shard_map/ppermute | solution.py:148
  224.7 12.9 %collective-permute-start.42 = (bf16[1024,256]{1,0:T(8,128)(2,1)S(1)}, bf16[1024,256]{1,0:T(8,128)(2,1)S(1)}, u32[]{:S(2)}, u32[]{:S(2)}) collective-permute-start(bf16[1024,256]{1,0:T(8,128)(2,1)S(1)} %collective-permute-done.38), channel_id=1, source_target_pairs={{0,4},{4,0},{24,28},{28,24},{1,5},{5,1},{25,29},{29,25},{2,6},{6,2... | collective-permute-start | bytes 1572872 | tf_op jit(solution)/shard_map/ppermute | solution.py:148
  230.3 12.9 %collective-permute-start.44 = (bf16[1024,256]{1,0:T(8,128)(2,1)S(1)}, bf16[1024,256]{1,0:T(8,128)(2,1)S(1)}, u32[]{:S(2)}, u32[]{:S(2)}) collective-permute-start(bf16[1024,256]{1,0:T(8,128)(2,1)S(1)} %collective-permute-done.40), channel_id=1, source_target_pairs={{0,4},{4,0},{24,28},{28,24},{1,5},{5,1},{25,29},{29,25},{2,6},{6,2... | collective-permute-start | bytes 1572872 | tf_op jit(solution)/shard_map/ppermute | solution.py:148
  243.4 3.4 %copy-start.5 = (bf16[2048,2048]{1,0:T(8,128)(2,1)}, bf16[2048,2048]{1,0:T(8,128)(2,1)S(1)}, u32[]{:S(2)}) copy-start(bf16[2048,2048]{1,0:T(8,128)(2,1)S(1)} %select_dynamic-update-slice_fusion) | copy-start | bytes 25165828

commit v4 on v3

v4 whole, which is shorter than its diff:
```python
import math

import jax
import jax.numpy as jnp
from jax import lax
from jax.experimental import pallas as pl
from jax.experimental.pallas import tpu as pltpu
from jax.sharding import PartitionSpec as P

BLOCK = 128
Z = 4
F32 = jnp.float32
BF16 = jnp.bfloat16
VMEM = pl.BlockSpec(memory_space=pltpu.VMEM)
FREE = pl.CostEstimate(flops=0, bytes_accessed=0, transcendentals=0)

INWARDS = ((0, 1), (3, 2))
OUTWARDS = ((1, 0), (2, 3))
MIDDLE = ((1, 2), (2, 1))
PAIRS = ((0, 1), (1, 0), (2, 3), (3, 2))


def owner_z(z, slot):
    low = z < 2
    if slot == 3:
        return z
    if slot == 0:
        return jnp.where(low, 3, 0)
    end = (z == 0) | (z == Z - 1)
    two, one = jnp.where(low, 2, 1), jnp.where(end, jnp.where(low, 1, 2), jnp.where(low, 0, 3))
    return two if slot == 1 else one


def call(kernel, out_shape, operands, name):
    return pl.pallas_call(
        kernel,
        out_shape=list(out_shape),
        in_specs=[VMEM] * len(operands),
        out_specs=[VMEM] * len(out_shape),
        cost_estimate=FREE,
        name=name,
    )


def arrange(cot, pieces, width, n_x):
    def kernel(cot_ref, *outs):
        owner = lax.axis_index("dp")
        z, x = owner // n_x, owner % n_x
        for piece, out in zip(pieces, outs):
            for j, (slot, by) in enumerate(piece):
                at = pl.multiple_of((owner_z(z, slot) * n_x + (x + by) % n_x) * width, width)
                out[:, j * width : (j + 1) * width] = cot_ref[:, pl.ds(at, width)]

    shapes = [jax.ShapeDtypeStruct((cot.shape[0], len(piece) * width), BF16) for piece in pieces]
    return call(kernel, shapes, [cot], "arrange")(cot)


def multiply(acts_t, group, chunks, width, cost):
    rows, tokens = acts_t.shape
    depth, columns = group[0].shape
    step = min(rows, 512)
    blocks = step // BLOCK

    def kernel(acts_ref, *refs):
        parts, outs, top, cot = refs[: len(group)], refs[len(group) : -2], refs[-2], refs[-1]

        @pl.when(pl.program_id(0) == 0)
        def _():
            seat = lax.axis_index("tensor")
            for k, part in enumerate(parts):
                cot[pl.ds(pl.multiple_of((seat ^ k) * depth, depth), depth), :] = part[...]

        for j in range(chunks):
            here = slice(j * width, (j + 1) * width)
            acc = jnp.dot(acts_ref[...], cot[:, here], preferred_element_type=F32)
            top[0, :, here] = jnp.max(jnp.abs(acc).reshape(blocks, BLOCK, width), axis=1)
            outs[j][...] = acc.astype(BF16)

    out = pl.pallas_call(
        kernel,
        grid=(rows // step,),
        in_specs=[pl.BlockSpec((step, tokens), lambda i: (i, 0))]
        + [pl.BlockSpec((depth, columns), lambda i: (0, 0))] * len(group),
        out_specs=[pl.BlockSpec((step, width), lambda i: (i, 0))] * chunks
        + [pl.BlockSpec((1, blocks, columns), lambda i: (i, 0, 0))],
        out_shape=[jax.ShapeDtypeStruct((rows, width), BF16)] * chunks
        + [jax.ShapeDtypeStruct((rows // step, blocks, columns), F32)],
        scratch_shapes=[pltpu.VMEM((tokens, columns), BF16)],
        compiler_params=pltpu.CompilerParams(vmem_limit_bytes=48 * 1024 * 1024),
        cost_estimate=cost,
        name="partials",
    )(acts_t, *group)
    return out[:chunks], out[chunks]


def add(terms, *earlier, rows=None):
    held = lax.optimization_barrier((*terms, *earlier))[: len(terms)]
    if rows is not None:
        held = [term if term.shape[0] == rows[1] else lax.slice_in_dim(term, rows[0], sum(rows)) for term in held]
    total = held[0].astype(F32)
    for term in held[1:]:
        total = total + term.astype(F32)
    return lax.optimization_barrier(total.astype(BF16))


def adamw(terms, states, factor):
    total = terms[0].astype(F32)
    for term in terms[1:]:
        total = total + term.astype(F32)
    master, first_moment, second_moment = states
    gradient = total * factor
    new_first = 0.9 * first_moment + 0.1 * gradient
    new_second = 0.95 * second_moment + 0.05 * gradient * gradient
    first_hat = new_first * (1.0 / (1.0 - 0.9**10))
    second_hat = new_second * (1.0 / (1.0 - 0.95**10))
    new_master = master * (1.0 - 0.01 * 0.1) - 0.01 * first_hat / (jnp.sqrt(second_hat) + 1e-08)
    return new_master, new_first, new_second, new_master.astype(BF16)


def update(terms, states, factor, wanted, name):
    rows, width = states[0].shape
    step = min(rows // 2, 512)
    half = rows // 2 // step
    flat = [value for term in terms for value in (term if isinstance(term, tuple) else (term,))]
    dtypes = [(F32, F32, F32, BF16)[k] for k in wanted]

    def kernel(*refs):
        ins, outs = refs[: len(flat) + 3], refs[len(flat) + 3 :]
        values, at = [], 0
        for term in terms:
            if isinstance(term, tuple):
                values.append(jnp.where(pl.program_id(0) < half, ins[at][...], ins[at + 1][...]))
                at += 2
            else:
                values.append(ins[at][...])
                at += 1
        results = adamw(values, [ref[...] for ref in ins[at:]], factor)
        for out, k in zip(outs, wanted):
            out[...] = results[k]

    whole = pl.BlockSpec((step, width), lambda i: (i, 0))
    halves = [
        pl.BlockSpec((step, width), lambda i: (jnp.minimum(i, half - 1), 0)),
        pl.BlockSpec((step, width), lambda i: (jnp.maximum(i - half, 0), 0)),
    ]
    specs = [spec for term in terms for spec in (halves if isinstance(term, tuple) else [whole])]
    return pl.pallas_call(
        kernel,
        grid=(rows // step,),
        in_specs=specs + [whole] * 3,
        out_specs=[whole] * len(wanted),
        out_shape=[jax.ShapeDtypeStruct((rows, width), dtype) for dtype in dtypes],
        compiler_params=pltpu.CompilerParams(vmem_limit_bytes=48 * 1024 * 1024),
        cost_estimate=FREE,
        name=name,
    )(*flat, *states)


def blank(shape, dtype):
    return pl.pallas_call(
        lambda ref: None,
        out_specs=pl.BlockSpec(memory_space=pl.ANY),
        out_shape=jax.ShapeDtypeStruct(shape, dtype),
        cost_estimate=FREE,
        name="blank",
    )()


def after(value, *earlier):
    return lax.optimization_barrier((value, *earlier))[0] if earlier else value


def body(acts, cotangent, master, first_moment, second_moment):
    n_dp = lax.axis_size("dp")
    n_tensor = lax.axis_size("tensor")
    n_x = n_dp // Z
    owner = lax.axis_index("dp")
    z, x = owner // n_x, owner % n_x
    rows, columns = acts.shape[1], cotangent.shape[1]
    width = columns // n_dp
    high = width // BLOCK
    others = range(1, n_x)

    def z_perm(value, pairs):
        return lax.ppermute(value, "dp", [(a * n_x + i, b * n_x + i) for a, b in pairs for i in range(n_x)])

    def x_perm(value, by, where=range(Z)):
        pairs = [(a * n_x + i, a * n_x + (i + by) % n_x) for a in where for i in range(n_x)]
        return lax.ppermute(value, "dp", pairs)

    def seat_perm(value, flip):
        return lax.ppermute(value, "tensor", [(i, i ^ flip) for i in range(n_tensor)])

    pieces = [
        [(0, by) for by in others],
        [(0, 0)] + [(1, by) for by in others],
        [(i, by) for i in (2, 3) for by in others] + [(1, 0), (2, 0), (3, 0)],
    ]
    own = arrange(cotangent, pieces, width, n_x)
    partial, tops, across = {}, [], []

    def fetch(piece, *earlier):
        value = after(own[piece], *earlier)
        across.append([value] + [seat_perm(value, k) for k in range(2, n_tensor, 2)])

    def partials(piece, *earlier):
        group = [part for value in across[piece] for part in (value, seat_perm(after(value, *earlier), 1))]
        cost = FREE if piece else pl.CostEstimate(flops=10**10, bytes_accessed=acts.size, transcendentals=0)
        chunks, top = multiply(after(acts_t, *earlier), group, len(pieces[piece]), width, cost)
        partial.update(zip(pieces[piece], chunks))
        tops.append(top)
        return chunks[0]

    def send_x(slot):
        return [x_perm(partial[slot, by], by) for by in others]

    half = rows // 2
    halves = range(2)
    part = [(h * half, half) for h in halves]

    for piece in range(len(pieces)):
        fetch(piece)
    acts_t = after(acts, *own).T
    token = partials(0, acts_t)
    got0 = send_x(0)
    token = partials(1, token)
    got1 = send_x(1)
    far, middle = [None] * 2, [None] * 2
    for h in halves:
        token = add([partial[0, 0], *got0], token, rows=part[h])
        far[h] = z_perm(token, INWARDS)
    token = partials(2, token)
    got2, got3 = send_x(2), send_x(3)
    token = add([partial[1, 0], *got1], token)
    inwards = z_perm(token, INWARDS)
    for h in halves:
        token = add([partial[0, 0], *got0, far[h]], token, rows=part[h])
        middle[h] = z_perm(token, MIDDLE)

    top = jnp.concatenate([after(t, token).reshape(rows // BLOCK, -1, BLOCK).max(axis=2) for t in tops], axis=1)
    column = jnp.stack(
        [(owner_z(z, i) * n_x + (x + by) % n_x) * high + h for piece in pieces for i, by in piece for h in range(high)]
    )
    here = column[None, :, None] == jnp.arange(n_dp * high)[None, None, :]
    scales = jnp.max(jnp.where(here, top[:, :, None], 0.0), axis=1)
    scales_x = [x_perm(scales, by) for by in others]

    pairs = [None] * 2
    token = add([partial[2, 0], *got2, middle[0]], scales, rows=part[0])
    pairs[0] = z_perm(token, PAIRS)
    token = add([partial[1, 0], *got1, inwards], token)
    last = z_perm(token, MIDDLE)
    token = add([partial[2, 0], *got2, middle[1]], token, rows=part[1])
    pairs[1] = z_perm(token, PAIRS)

    terms = [after(partial[3, 0], *scales_x), *got3, last, tuple(pairs)]
    states = [master, first_moment, second_moment]
    factor = 1.0 / math.sqrt(acts.shape[0] * n_dp)
    (owned,) = update(terms, states, factor, [3], "weights")

    low, between = z < 2, (z == 1) | (z == 2)
    sources = [z, z ^ 1, jnp.where(low, 2, 1), jnp.where(low, 3, 0)]
    over0 = [x_perm(owned, by) for by in others]
    pairs, mid = z_perm(owned, PAIRS), z_perm(owned, MIDDLE)
    new_master, new_first, new_second = update(
        [after(terms[0], owned), *terms[1:]], states, factor, [0, 1, 2], "states"
    )
    scales = after(scales, owned)
    for got in scales_x:
        scales = jnp.maximum(scales, got)
    scales_z = z_perm(scales, PAIRS)

    come = [pairs, mid, new_master]
    mid_far, outwards = z_perm(after(pairs, *come), MIDDLE), z_perm(after(mid, *come), OUTWARDS)
    over1 = [x_perm(after(pairs, *come), by) for by in others]
    weights = blank((rows, columns), BF16)

    def put(weights, value, slot, by, h=0):
        at = (sources[slot] * n_x + (x - by) % n_x) * width
        return lax.dynamic_update_slice(weights, value, (h * half, at))

    weights = put(weights, owned, 0, 0)
    weights = put(weights, pairs, 1, 0)
    come = [mid_far, outwards, *over0]
    near = lax.optimization_barrier(jnp.where(between, after(mid, *come), outwards))
    far = [z_perm(after(lax.slice_in_dim(mid_far, h * half, (h + 1) * half), *come), OUTWARDS) for h in halves]
    over2 = [x_perm(near, by) for by in others]
    scales = after(scales, scales_z, near)
    scales = jnp.maximum(scales, scales_z)
    scales_z = z_perm(scales, [(a, a ^ 2) for a in range(Z)])
    for got, by in zip(over0, others):
        weights = put(weights, got, 0, by)
    weights = put(after(weights, near), near, 2, 0)
    for got, by in zip(over1, others):
        weights = put(weights, got, 1, by)
    distant, over3 = [None] * 2, [None] * 2
    for h in halves:
        come = [far[h], *over1] if h == 0 else [far[h], distant[0]]
        value = after(lax.slice_in_dim(mid_far, h * half, (h + 1) * half), *come)
        distant[h] = lax.optimization_barrier(jnp.where(between, value, far[h]))
        over3[h] = [x_perm(distant[h], by) for by in others]
    for h in halves:
        weights = put(weights, distant[h], 3, 0, h)
    for got, by in zip(over2, others):
        weights = put(weights, got, 2, by)
    for h in halves:
        for got, by in zip(over3[h], others):
            weights = put(weights, got, 3, by, h)
    block_scales = jnp.maximum(scales, after(scales_z, *distant)) + 1e-06
    return (new_master, new_first, new_second, weights, block_scales)


def solution(mesh):
    in_specs = (
        P("dp", "tensor"),
        P(("dp", "tensor"), None),
        P("tensor", "dp"),
        P("tensor", "dp"),
        P("tensor", "dp"),
    )
    out_specs = (
        P("tensor", "dp"),
        P("tensor", "dp"),
        P("tensor", "dp"),
        P("tensor", None),
        P("tensor", None),
    )
    return jax.shard_map(body, mesh=mesh, in_specs=in_specs, out_specs=out_specs, check_vma=False)
```

time: 248 us -> 242 us (0.976)
  starting transfers between devices: 58 us -> 47.6 us
  other arithmetic: 22.8 us -> 12.6 us
  Pallas kernels: 27.7 us -> 37.5 us
  local copies, waits for them, and re-layouts: 12.8 us -> 20.9 us
  waiting for transfers between devices: 124 us -> 121 us
    ppermute x17 -> x10, starting transfers between devices: 24.4 us -> 6.78 us  [x_perm(): return lax.ppermute(value, 'dp', pairs)]
    dynamic_update_slice x8 -> x10, local copies, waits for them, and re-layouts: 0.53 us -> 12 us  [put(): return lax.dynamic_update_slice(weights, value, (h * half, at))]
    pallas_call x0 -> x2, Pallas kernels: none -> 11 us  [update(): pl.pallas_call(kernel, grid=(rows // step,), in_specs=specs + [whole] * 3...]
    ppermute x17 -> x10, waiting for transfers between devices: 50.7 us -> 42 us  [x_perm(): return lax.ppermute(value, 'dp', pairs)]
    ppermute x17 -> x16, starting transfers between devices: 27.5 us -> 34.3 us  [z_perm(): lax.ppermute(value, 'dp', [(a * n_x + i, b * n_x + i) for a, b in pairs f...]
    sub x1 -> x0, other arithmetic: 5.97 us -> none  [adamw(): master * (1.0 - 0.01 * 0.1)]
    convert_element_type x2 -> x0, other arithmetic: 5.79 us -> none  [adamw(): return (new_master, new_first, new_second, new_master.astype(BF16))]
    unnamed x24 -> x14, local copies, waits for them, and re-layouts: 3.45 us -> 0.03 us
  transfers between devices with their start and end apart: 46 -> 35, of which waited for: 21 -> 20; matrix products, arithmetic and copies ran while one was open for 12% -> 14% of each run, Pallas kernels for 8% -> 11%
where the time goes in v4:
time: 242 us; the launch traced here: 241 us
  waiting for transfers between devices  121 us (50%)
  starting transfers between devices  47.6 us (20%)
  Pallas kernels  37.5 us (15%)
  local copies, waits for them, and re-layouts  20.9 us (9%)
  other arithmetic  12.6 us (5%)
    ppermute x16, waiting for transfers between devices, z_perm(): lax.ppermute(value, 'dp', [(a * n_x + i, b * n_x + i) for a, b in pairs f...  59.9 us
    ppermute x10, waiting for transfers between devices, x_perm(): return lax.ppermute(value, 'dp', pairs)  42 us
    ppermute x16, starting transfers between devices, z_perm(): lax.ppermute(value, 'dp', [(a * n_x + i, b * n_x + i) for a, b in pairs f...  34.3 us
    pallas_call x3, Pallas kernels, multiply(): pl.pallas_call(kernel, grid=(rows // step,), in_specs=[pl.BlockSpec((step...  23.7 us
    ppermute x9, waiting for transfers between devices, seat_perm(): lax.ppermute(value, 'tensor', [(i, i ^ flip) for i in range(n_tensor)])  19.2 us
    dynamic_update_slice x10, local copies, waits for them, and re-layouts, put(): return lax.dynamic_update_slice(weights, value, (h * half, at))  12 us
    convert_element_type x8, other arithmetic, add(): return lax.optimization_barrier(total.astype(BF16))  11.2 us
    pallas_call x2, Pallas kernels, update(): pl.pallas_call(kernel, grid=(rows // step,), in_specs=specs + [whole] * 3...  11 us
  transfers between devices with their start and end apart: 35, of which 20 were waited for; matrix products, arithmetic and copies ran while one was open for 14% of the time, Pallas kernels for 11%

profile of v4, /device:TPU:0, one launch (start us, length us, event | category | flops | bytes accessed | tf_op | source)
XLA Modules:
  0.0 240.7 jit_solution(17239067707784018870)
XLA Ops:
  0.6 2.8 %arrange.1 = (bf16[384,256]{1,0:T(8,128)(2,1)}, bf16[384,512]{1,0:T(8,128)(2,1)}, bf16[384,1280]{1,0:T(8,128)(2,1)}) custom-call(bf16[384,2048]{1,0:T(8,128)(2,1)} %cot_ref.1), custom_call_target="tpu_custom_call" | custom-call | tf_op jit(solution)/shard_map/arrange/pallas_call | solution.py:55
  3.4 3.0 %collective-permute-start.1 = (bf16[384,256]{1,0:T(8,128)(2,1)}, bf16[384,256]{1,0:T(8,128)(2,1)S(1)}, u32[]{:S(2)}, u32[]{:S(2)}) collective-permute-start(bf16[384,256]{1,0:T(8,128)(2,1)} %get-tuple-element.74.refs_0_), channel_id=1, source_target_pairs={{0,2},{1,3},{2,0},{3,1},{4,6},{5,7},{6,4},{7,5},{8,10},{9,11},{10,... | collective-permute-start | bytes 589832 | tf_op jit(solution)/shard_map/ppermute | solution.py:192
  6.4 8.6 %copy.12 = bf16[1536,2048]{0,1:T(8,128)(2,1)} copy(bf16[1536,2048]{1,0:T(8,128)(2,1)} %param.5) | data formatting | bytes 12582912 | tf_op jit(solution)/shard_map/optimization_barrier | solution.py:170
  15.6 0.9 collective-permute-done.refs_1_
  16.8 4.8 %partials.3 = (bf16[2048,256]{1,0:T(8,128)(2,1)S(1)}, f32[4,4,256]{2,1,0:T(4,128)S(1)}) custom-call(bf16[2048,1536]{1,0:T(8,128)(2,1)} %bitcast.17, bf16[384,256]{1,0:T(8,128)(2,1)S(1)} %copy-done.4, bf16[384,256]{1,0:T(8,128)(2,1)S(1)} %collective-permute-done.refs_1_, bf16[384,256]{1,0:T(8,128)(2,1)S(1)} %collective-permute-done.1.refs_2_, ...), custom_call_target="tpu_custom_call" | custom-call | flops 10000000000 | bytes 3145728 | tf_op jit(solution)/shard_map/partials/pallas_call | solution.py:79
  21.6 1.5 collective-permute-start.6
  23.6 1.5 collective-permute-start.8
  25.2 10.0 %collective-permute-done.4.refs_2_ = bf16[384,512]{1,0:T(8,128)(2,1)S(1)} collective-permute-done((bf16[384,512]{1,0:T(8,128)(2,1)S(1)}, bf16[384,512]{1,0:T(8,128)(2,1)S(1)}, u32[]{:S(2)}, u32[]{:S(2)}) %collective-permute-start.4) | collective-permute-done | bytes 393248 | tf_op jit(solution)/shard_map/ppermute | solution.py:192
  35.6 1.2 collective-permute-done.5.refs_3_
  37.4 6.8 %partials.4 = (bf16[2048,256]{1,0:T(8,128)(2,1)S(1)}, bf16[2048,256]{1,0:T(8,128)(2,1)}, f32[4,4,512]{2,1,0:T(4,128)S(1)}) custom-call(bf16[2048,1536]{1,0:T(8,128)(2,1)} %bitcast.18, bf16[384,512]{1,0:T(8,128)(2,1)S(1)} %copy-done.2, bf16[384,512]{1,0:T(8,128)(2,1)S(1)} %collective-permute-done.3.refs_1_, ...), custom_call_target="tpu_custom_call" | custom-call | tf_op jit(solution)/shard_map/partials/pallas_call | solution.py:79
  44.8 2.2 collective-permute-done.6
  46.9 1.0 add_convert_fusion.7
  48.0 0.9 add_convert_fusion.6
  48.9 6.2 %collective-permute-done.8.refs_2_ = bf16[384,1280]{1,0:T(8,128)(2,1)S(1)} collective-permute-done((bf16[384,1280]{1,0:T(8,128)(2,1)S(1)}, bf16[384,1280]{1,0:T(8,128)(2,1)S(1)}, u32[]{:S(2)}, u32[]{:S(2)}) %collective-permute-start.8) | collective-permute-done | bytes 983072 | tf_op jit(solution)/shard_map/ppermute | solution.py:192
  55.8 3.6 %collective-permute-start.11 = (bf16[1024,256]{1,0:T(8,128)(2,1)}, bf16[1024,256]{1,0:T(8,128)(2,1)S(1)}, u32[]{:S(2)}, u32[]{:S(2)}) collective-permute-start(bf16[1024,256]{1,0:T(8,128)(2,1)} %add_convert_fusion.7), channel_id=1, source_target_pairs={{0,8},{4,12},{24,16},{28,20},{1,9},{5,13},{25,17},{29,21},{2,10},{... | collective-permute-start | bytes 1572872 | tf_op jit(solution)/shard_map/ppermute | solution.py:185
  59.4 1.3 collective-permute-start.10
  60.8 12.1 %partials.5 = (bf16[2048,256]{1,0:T(8,128)(2,1)}, bf16[2048,256]{1,0:T(8,128)(2,1)S(1)}, bf16[2048,256]{1,0:T(8,128)(2,1)}, bf16[2048,256]{1,0:T(8,128)(2,1)}, b...) custom-call(bf16[2048,1536]{1,0:T(8,128)(2,1)} %bitcast.19, bf16[384,1280]{1,0:T(8,128)(2,1)S(1)} %copy-done.1, ...), custom_call_target="tpu_custom_call" | custom-call | tf_op jit(solution)/shard_map/partials/pallas_call | solution.py:79
  72.9 0.6 collective-permute-start.16
  73.5 2.9 %add_convert_fusion.1 = bf16[2048,256]{1,0:T(8,128)(2,1)} fusion(bf16[2048,256]{1,0:T(8,128)(2,1)} %collective-permute-done.12, bf16[2048,256]{1,0:T(8,128)(2,1)} %get-tuple-element.112), kind=kLoop, calls=%fused_computation.1 | loop fusion | flops 2097152 | bytes 3145728 | tf_op jit(solution)/shard_map/convert_element_type | solution.py:103
  76.4 2.9 %collective-permute-start.15 = (bf16[2048,256]{1,0:T(8,128)(2,1)}, bf16[2048,256]{1,0:T(8,128)(2,1)}, u32[]{:S(2)}, u32[]{:S(2)}) collective-permute-start(bf16[2048,256]{1,0:T(8,128)(2,1)} %add_convert_fusion.1), channel_id=1, source_target_pairs={{0,8},{4,12},{24,16},{28,20},{1,9},{5,13},{25,17},{29,21},{2,10},{... | collective-permute-start | bytes 3145736 | tf_op jit(solution)/shard_map/ppermute | solution.py:185
  79.3 1.0 add_convert_fusion.5
  80.3 1.4 collective-permute-start.17
  81.8 1.4 collective-permute-done.10
  83.4 0.7 collective-permute-start.20
  84.6 0.6 collective-permute-start.14
  85.4 14.0 %collective-permute-done.16 = bf16[2048,256]{1,0:T(8,128)(2,1)} collective-permute-done((bf16[2048,256]{1,0:T(8,128)(2,1)}, bf16[2048,256]{1,0:T(8,128)(2,1)}, u32[]{:S(2)}, u32[]{:S(2)}) %collective-permute-start.16) | collective-permute-done | bytes 1048608 | tf_op jit(solution)/shard_map/ppermute | solution.py:189
  99.3 1.5 add_convert_fusion.3
  100.9 3.9 %collective-permute-done.15 = bf16[2048,256]{1,0:T(8,128)(2,1)} collective-permute-done((bf16[2048,256]{1,0:T(8,128)(2,1)}, bf16[2048,256]{1,0:T(8,128)(2,1)}, u32[]{:S(2)}, u32[]{:S(2)}) %collective-permute-start.15) | collective-permute-done | bytes 1048608 | tf_op jit(solution)/shard_map/ppermute | solution.py:185
  104.8 2.2 add_convert_fusion
  107.0 0.7 collective-permute-start.18
  107.7 1.4 add_convert_fusion.2
  109.1 5.3 %collective-permute-start.21 = (bf16[1024,256]{1,0:T(8,128)(2,1)S(1)}, bf16[1024,256]{1,0:T(8,128)(2,1)S(1)}, u32[]{:S(2)}, u32[]{:S(2)}) collective-permute-start(bf16[1024,256]{1,0:T(8,128)(2,1)S(1)} %add_convert_fusion.2), channel_id=1, source_target_pairs={{0,8},{4,12},{8,0},{12,4},{16,24},{20,28},{24,16},{28,20},{1,9},{5... | collective-permute-start | bytes 1572872 | tf_op jit(solution)/shard_map/ppermute | solution.py:185
  115.1 5.5 %collective-permute-done.13 = f32[16,16]{1,0:T(8,128)S(1)} collective-permute-done((f32[16,16]{1,0:T(8,128)S(1)}, f32[16,16]{1,0:T(8,128)S(1)}, u32[]{:S(2)}, u32[]{:S(2)}) %collective-permute-start.13) | collective-permute-done | bytes 1056 | tf_op jit(solution)/shard_map/ppermute | solution.py:189
  120.6 6.7 %collective-permute-done.21.refs_4_ = bf16[1024,256]{1,0:T(8,128)(2,1)S(1)} collective-permute-done((bf16[1024,256]{1,0:T(8,128)(2,1)S(1)}, bf16[1024,256]{1,0:T(8,128)(2,1)S(1)}, u32[]{:S(2)}, u32[]{:S(2)}) %collective-permute-start.21) | collective-permute-done | bytes 524320 | tf_op jit(solution)/shard_map/ppermute | solution.py:185
  127.3 9.4 %collective-permute-done.19.refs_3_ = bf16[1024,256]{1,0:T(8,128)(2,1)S(1)} collective-permute-done((bf16[1024,256]{1,0:T(8,128)(2,1)S(1)}, bf16[1024,256]{1,0:T(8,128)(2,1)S(1)}, u32[]{:S(2)}, u32[]{:S(2)}) %collective-permute-start.19) | collective-permute-done | bytes 524320 | tf_op jit(solution)/shard_map/ppermute | solution.py:185
  136.6 4.6 %weights.1 = bf16[2048,256]{1,0:T(8,128)(2,1)S(1)} custom-call(bf16[2048,256]{1,0:T(8,128)(2,1)S(1)} %copy-done, bf16[2048,256]{1,0:T(8,128)(2,1)S(1)} %collective-permute-done.14.refs_1_, bf16[2048,256]{1,0:T(8,128)(2,1)S(1)} %collective-permute-done.18.refs_2_, bf16[1024,256]{1,0:T(8,128)(2,1)S(1)} %collective-permute-done.19.refs_3_, ...), custom_call_target="tpu_custom_call" | custom-call | tf_op jit(solution)/shard_map/weights/pallas_call | solution.py:147
  141.2 1.8 collective-permute-start.22
  143.0 1.6 collective-permute-start.24
  145.2 6.4 %states.1 = (f32[2048,256]{1,0:T(8,128)}, f32[2048,256]{1,0:T(8,128)}, f32[2048,256]{1,0:T(8,128)}) custom-call(bf16[2048,256]{1,0:T(8,128)(2,1)S(1)} %copy-done, bf16[2048,256]{1,0:T(8,128)(2,1)S(1)} %collective-permute-done.14.refs_1_, bf16[2048,256]{1,0:T(8,128)(2,1)S(1)} %collective-permute-done.18.refs_2_, ...), custom_call_target="tpu_custom_call" | custom-call | tf_op jit(solution)/shard_map/states/pallas_call | solution.py:147
  151.6 13.1 %collective-permute-done.22 = bf16[2048,256]{1,0:T(8,128)(2,1)} collective-permute-done((bf16[2048,256]{1,0:T(8,128)(2,1)S(1)}, bf16[2048,256]{1,0:T(8,128)(2,1)}, u32[]{:S(2)}, u32[]{:S(2)}) %collective-permute-start.22) | collective-permute-done | bytes 1048608 | tf_op jit(solution)/shard_map/ppermute | solution.py:185
  164.7 1.3 collective-permute-start.26
  166.0 0.7 collective-permute-start.25
  166.8 5.4 %collective-permute-start.33 = (f32[16,16]{1,0:T(8,128)S(1)}, f32[16,16]{1,0:T(8,128)S(1)}, u32[]{:S(2)}, u32[]{:S(2)}) collective-permute-start(f32[16,16]{1,0:T(8,128)S(1)} %max.9), channel_id=1, source_target_pairs={{0,8},{4,12},{8,0},{12,4},{16,24},{20,28},{24,16},{28,20},{1,9},{5... | collective-permute-start | bytes 3080 | tf_op jit(solution)/shard_map/ppermute | solution.py:185
  172.2 1.0 constant_dynamic-update-slice_fusion.7
  173.8 2.3 constant_dynamic-update-slice_fusion.6
  176.1 2.3 constant_dynamic-update-slice_fusion.5
  178.3 11.9 %collective-permute-done.26 = bf16[2048,256]{1,0:T(8,128)(2,1)S(1)} collective-permute-done((bf16[2048,256]{1,0:T(8,128)(2,1)}, bf16[2048,256]{1,0:T(8,128)(2,1)S(1)}, u32[]{:S(2)}, u32[]{:S(2)}) %collective-permute-start.26) | collective-permute-done | bytes 1048608 | tf_op jit(solution)/shard_map/ppermute | solution.py:185
  190.3 1.3 collective-permute-start.28
  191.7 0.6 collective-permute-start.30
  192.3 4.8 %collective-permute-start.34 = (f32[16,16]{1,0:T(8,128)S(1)}, f32[16,16]{1,0:T(8,128)S(1)}, u32[]{:S(2)}, u32[]{:S(2)}) collective-permute-start(f32[16,16]{1,0:T(8,128)S(1)} %max.10), channel_id=1, source_target_pairs={{0,16},{4,20},{8,24},{12,28},{16,0},{20,4},{24,8},{28,12},{1,17},{... | collective-permute-start | bytes 3080 | tf_op jit(solution)/shard_map/ppermute | solution.py:185
  197.1 1.3 collective-permute-start.29
  198.4 1.0 constant_dynamic-update-slice_fusion.4
  199.4 1.0 constant_dynamic-update-slice_fusion.3
  200.5 7.6 %collective-permute-done.28 = bf16[1024,256]{1,0:T(8,128)(2,1)S(1)} collective-permute-done((bf16[1024,256]{1,0:T(8,128)(2,1)S(1)}, bf16[1024,256]{1,0:T(8,128)(2,1)S(1)}, u32[]{:S(2)}, u32[]{:S(2)}) %collective-permute-start.28) | collective-permute-done | bytes 524320 | tf_op jit(solution)/shard_map/ppermute | solution.py:185
  208.2 0.6 collective-permute-start.31
  208.8 6.0 %collective-permute-done.29 = bf16[1024,256]{1,0:T(8,128)(2,1)S(1)} collective-permute-done((bf16[1024,256]{1,0:T(8,128)(2,1)S(1)}, bf16[1024,256]{1,0:T(8,128)(2,1)S(1)}, u32[]{:S(2)}, u32[]{:S(2)}) %collective-permute-start.29) | collective-permute-done | bytes 524320 | tf_op jit(solution)/shard_map/ppermute | solution.py:185
  216.1 0.8 constant_dynamic-update-slice_fusion.2
  216.9 0.8 constant_dynamic-update-slice_fusion.9
  217.7 3.9 %collective-permute-done.30 = bf16[2048,256]{1,0:T(8,128)(2,1)S(1)} collective-permute-done((bf16[2048,256]{1,0:T(8,128)(2,1)S(1)}, bf16[2048,256]{1,0:T(8,128)(2,1)S(1)}, u32[]{:S(2)}, u32[]{:S(2)}) %collective-permute-start.30) | collective-permute-done | bytes 1048608 | tf_op jit(solution)/shard_map/ppermute | solution.py:189
  221.7 1.0 constant_dynamic-update-slice_fusion.1
  222.7 10.2 %collective-permute-done.31 = bf16[1024,256]{1,0:T(8,128)(2,1)S(1)} collective-permute-done((bf16[1024,256]{1,0:T(8,128)(2,1)S(1)}, bf16[1024,256]{1,0:T(8,128)(2,1)S(1)}, u32[]{:S(2)}, u32[]{:S(2)}) %collective-permute-start.31) | collective-permute-done | bytes 524320 | tf_op jit(solution)/shard_map/ppermute | solution.py:189
  232.9 0.8 constant_dynamic-update-slice_fusion
  233.7 6.2 %collective-permute-done.32 = bf16[1024,256]{1,0:T(8,128)(2,1)S(1)} collective-permute-done((bf16[1024,256]{1,0:T(8,128)(2,1)S(1)}, bf16[1024,256]{1,0:T(8,128)(2,1)S(1)}, u32[]{:S(2)}, u32[]{:S(2)}) %collective-permute-start.32) | collective-permute-done | bytes 524320 | tf_op jit(solution)/shard_map/ppermute | solution.py:189
  239.9 0.8 constant_dynamic-update-slice_fusion.8
  (63 shorter events, 7.7 us)
Async XLA Ops:
  3.4 11.6 %copy-start.4 = (bf16[384,256]{1,0:T(8,128)(2,1)S(1)}, bf16[384,256]{1,0:T(8,128)(2,1)}, u32[]{:S(2)}) copy-start(bf16[384,256]{1,0:T(8,128)(2,1)} %get-tuple-element.74.refs_0_) | copy-start | bytes 589828
  3.4 11.7 %collective-permute-start.1 = (bf16[384,256]{1,0:T(8,128)(2,1)}, bf16[384,256]{1,0:T(8,128)(2,1)S(1)}, u32[]{:S(2)}, u32[]{:S(2)}) collective-permute-start(bf16[384,256]{1,0:T(8,128)(2,1)} %get-tuple-element.74.refs_0_), channel_id=1, source_target_pairs={{0,2},{1,3},{2,0},{3,1},{4,6},{5,7},{6,4},{7,5},{8,10},{9,11},{10,... | collective-permute-start | bytes 589832 | tf_op jit(solution)/shard_map/ppermute | solution.py:192
  15.0 8.1 %copy-start.2 = (bf16[384,512]{1,0:T(8,128)(2,1)S(1)}, bf16[384,512]{1,0:T(8,128)(2,1)}, u32[]{:S(2)}) copy-start(bf16[384,512]{1,0:T(8,128)(2,1)} %get-tuple-element.78.refs_0_) | copy-start | bytes 1179652
  15.0 8.7 %copy-start.1 = (bf16[384,1280]{1,0:T(8,128)(2,1)S(1)}, bf16[384,1280]{1,0:T(8,128)(2,1)}, u32[]{:S(2)}) copy-start(bf16[384,1280]{1,0:T(8,128)(2,1)} %get-tuple-element.86.refs_0_) | copy-start | bytes 2949124
  15.0 1.5 collective-permute-start
  15.1 1.7 collective-permute-start.2
  21.6 25.4 %collective-permute-start.6 = (bf16[2048,256]{1,0:T(8,128)(2,1)S(1)}, bf16[2048,256]{1,0:T(8,128)(2,1)S(1)}, u32[]{:S(2)}, u32[]{:S(2)}) collective-permute-start(bf16[2048,256]{1,0:T(8,128)(2,1)S(1)} %get-tuple-element.76), channel_id=1, source_target_pairs={{0,4},{4,0},{8,12},{12,8},{16,20},{20,16},{24,28},{28,24},{1,5},{5... | collective-permute-start | bytes 3145736 | tf_op jit(solution)/shard_map/ppermute | solution.py:189
  23.1 12.0 %collective-permute-start.4 = (bf16[384,512]{1,0:T(8,128)(2,1)S(1)}, bf16[384,512]{1,0:T(8,128)(2,1)S(1)}, u32[]{:S(2)}, u32[]{:S(2)}) collective-permute-start(bf16[384,512]{1,0:T(8,128)(2,1)S(1)} %copy-done.2), channel_id=1, source_target_pairs={{0,2},{1,3},{2,0},{3,1},{4,6},{5,7},{6,4},{7,5},{8,10},{9,11},{10,... | collective-permute-start | bytes 1179656 | tf_op jit(solution)/shard_map/ppermute | solution.py:192
  23.6 31.5 %collective-permute-start.8 = (bf16[384,1280]{1,0:T(8,128)(2,1)S(1)}, bf16[384,1280]{1,0:T(8,128)(2,1)S(1)}, u32[]{:S(2)}, u32[]{:S(2)}) collective-permute-start(bf16[384,1280]{1,0:T(8,128)(2,1)S(1)} %copy-done.1), channel_id=1, source_target_pairs={{0,2},{1,3},{2,0},{3,1},{4,6},{5,7},{6,4},{7,5},{8,10},{9,11},{10,... | collective-permute-start | bytes 2949128 | tf_op jit(solution)/shard_map/ppermute | solution.py:192
  35.1 1.7 collective-permute-start.5
  35.1 2.3 collective-permute-start.3
  44.2 29.3 %collective-permute-start.12 = (bf16[2048,256]{1,0:T(8,128)(2,1)}, bf16[2048,256]{1,0:T(8,128)(2,1)}, u32[]{:S(2)}, u32[]{:S(2)}) collective-permute-start(bf16[2048,256]{1,0:T(8,128)(2,1)} %get-tuple-element.91), channel_id=1, source_target_pairs={{0,4},{4,0},{8,12},{12,8},{16,20},{20,16},{24,28},{28,24},{1,5},{5... | collective-permute-start | bytes 3145736 | tf_op jit(solution)/shard_map/ppermute | solution.py:189
  46.9 8.2 %copy-start.5 = (bf16[2048,256]{1,0:T(8,128)(2,1)}, bf16[2048,256]{1,0:T(8,128)(2,1)S(1)}, u32[]{:S(2)}) copy-start(bf16[2048,256]{1,0:T(8,128)(2,1)S(1)} %collective-permute-done.6) | copy-start | bytes 3145732
  55.2 5.6 %collective-permute-start.9 = (bf16[384,1280]{1,0:T(8,128)(2,1)S(1)}, bf16[384,1280]{1,0:T(8,128)(2,1)}, u32[]{:S(2)}, u32[]{:S(2)}) collective-permute-start(bf16[384,1280]{1,0:T(8,128)(2,1)S(1)} %collective-permute-done.8.refs_2_), channel_id=1, source_target_pairs={{0,1},{1,0},{2,3},{3,2},{4,5},{5,4},{6,7},{7,6},{8,9},{9,8},{10,11... | collective-permute-start | bytes 2949128 | tf_op jit(solution)/shard_map/ppermute | solution.py:192
  55.2 5.6 %collective-permute-start.7 = (bf16[384,1280]{1,0:T(8,128)(2,1)S(1)}, bf16[384,1280]{1,0:T(8,128)(2,1)}, u32[]{:S(2)}, u32[]{:S(2)}) collective-permute-start(bf16[384,1280]{1,0:T(8,128)(2,1)S(1)} %copy-done.1), channel_id=1, source_target_pairs={{0,1},{1,0},{2,3},{3,2},{4,5},{5,4},{6,7},{7,6},{8,9},{9,8},{10,11... | collective-permute-start | bytes 2949128 | tf_op jit(solution)/shard_map/ppermute | solution.py:192
  55.8 23.5 %copy-start.6 = (bf16[2048,256]{1,0:T(8,128)(2,1)S(1)}, bf16[2048,256]{1,0:T(8,128)(2,1)}, u32[]{:S(2)}) copy-start(bf16[2048,256]{1,0:T(8,128)(2,1)} %copy-done.5) | copy-start | bytes 3145732
  55.8 23.5 %collective-permute-start.11 = (bf16[1024,256]{1,0:T(8,128)(2,1)}, bf16[1024,256]{1,0:T(8,128)(2,1)S(1)}, u32[]{:S(2)}, u32[]{:S(2)}) collective-permute-start(bf16[1024,256]{1,0:T(8,128)(2,1)} %add_convert_fusion.7), channel_id=1, source_target_pairs={{0,8},{4,12},{24,16},{28,20},{1,9},{5,13},{25,17},{29,21},{2,10},{... | collective-permute-start | bytes 1572872 | tf_op jit(solution)/shard_map/ppermute | solution.py:185
  59.4 23.8 %collective-permute-start.10 = (bf16[1024,256]{1,0:T(8,128)(2,1)}, bf16[1024,256]{1,0:T(8,128)(2,1)S(1)}, u32[]{:S(2)}, u32[]{:S(2)}) collective-permute-start(bf16[1024,256]{1,0:T(8,128)(2,1)} %add_convert_fusion.6), channel_id=1, source_target_pairs={{0,8},{4,12},{24,16},{28,20},{1,9},{5,13},{25,17},{29,21},{2,10},{... | collective-permute-start | bytes 1572872 | tf_op jit(solution)/shard_map/ppermute | solution.py:185
  72.9 10.6 %copy-start.3 = (bf16[2048,256]{1,0:T(8,128)(2,1)}, bf16[2048,256]{1,0:T(8,128)(2,1)S(1)}, u32[]{:S(2)}) copy-start(bf16[2048,256]{1,0:T(8,128)(2,1)S(1)} %get-tuple-element.107) | copy-start | bytes 3145732
  72.9 63.7 %copy-start = (bf16[2048,256]{1,0:T(8,128)(2,1)S(1)}, bf16[2048,256]{1,0:T(8,128)(2,1)}, u32[]{:S(2)}) copy-start(bf16[2048,256]{1,0:T(8,128)(2,1)} %get-tuple-element.118.refs_0_) | copy-start | bytes 3145732
  72.9 26.4 %collective-permute-start.16 = (bf16[2048,256]{1,0:T(8,128)(2,1)}, bf16[2048,256]{1,0:T(8,128)(2,1)}, u32[]{:S(2)}, u32[]{:S(2)}) collective-permute-start(bf16[2048,256]{1,0:T(8,128)(2,1)} %get-tuple-element.92), channel_id=1, source_target_pairs={{0,4},{4,0},{8,12},{12,8},{16,20},{20,16},{24,28},{28,24},{1,5},{5... | collective-permute-start | bytes 3145736 | tf_op jit(solution)/shard_map/ppermute | solution.py:189
  76.4 28.4 %collective-permute-start.15 = (bf16[2048,256]{1,0:T(8,128)(2,1)}, bf16[2048,256]{1,0:T(8,128)(2,1)}, u32[]{:S(2)}, u32[]{:S(2)}) collective-permute-start(bf16[2048,256]{1,0:T(8,128)(2,1)} %add_convert_fusion.1), channel_id=1, source_target_pairs={{0,8},{4,12},{24,16},{28,20},{1,9},{5,13},{25,17},{29,21},{2,10},{... | collective-permute-start | bytes 3145736 | tf_op jit(solution)/shard_map/ppermute | solution.py:185
  80.3 5.1 %collective-permute-start.17 = (bf16[1024,256]{1,0:T(8,128)(2,1)}, bf16[1024,256]{1,0:T(8,128)(2,1)}, u32[]{:S(2)}, u32[]{:S(2)}) collective-permute-start(bf16[1024,256]{1,0:T(8,128)(2,1)} %add_convert_fusion.5), channel_id=1, source_target_pairs={{8,16},{12,20},{16,8},{20,12},{9,17},{13,21},{17,9},{21,13},{10,18... | collective-permute-start | bytes 1572872 | tf_op jit(solution)/shard_map/ppermute | solution.py:185
  83.4 24.3 %collective-permute-start.20 = (bf16[1024,256]{1,0:T(8,128)(2,1)S(1)}, bf16[1024,256]{1,0:T(8,128)(2,1)S(1)}, u32[]{:S(2)}, u32[]{:S(2)}) collective-permute-start(bf16[1024,256]{1,0:T(8,128)(2,1)S(1)} %add_convert_fusion.4), channel_id=1, source_target_pairs={{8,16},{12,20},{16,8},{20,12},{9,17},{13,21},{17,9},{21,13},{10,18... | collective-permute-start | bytes 1572872 | tf_op jit(solution)/shard_map/ppermute | solution.py:185
  84.6 36.0 %collective-permute-start.14 = (bf16[2048,256]{1,0:T(8,128)(2,1)}, bf16[2048,256]{1,0:T(8,128)(2,1)S(1)}, u32[]{:S(2)}, u32[]{:S(2)}) collective-permute-start(bf16[2048,256]{1,0:T(8,128)(2,1)} %copy-done.3), channel_id=1, source_target_pairs={{0,4},{4,0},{8,12},{12,8},{16,20},{20,16},{24,28},{28,24},{1,5},{5... | collective-permute-start | bytes 3145736 | tf_op jit(solution)/shard_map/ppermute | solution.py:189
  107.0 29.6 %collective-permute-start.18 = (bf16[2048,256]{1,0:T(8,128)(2,1)S(1)}, bf16[2048,256]{1,0:T(8,128)(2,1)S(1)}, u32[]{:S(2)}, u32[]{:S(2)}) collective-permute-start(bf16[2048,256]{1,0:T(8,128)(2,1)S(1)} %add_convert_fusion), channel_id=1, source_target_pairs={{8,16},{12,20},{16,8},{20,12},{9,17},{13,21},{17,9},{21,13},{10,18... | collective-permute-start | bytes 3145736 | tf_op jit(solution)/shard_map/ppermute | solution.py:185
  109.1 18.1 %collective-permute-start.21 = (bf16[1024,256]{1,0:T(8,128)(2,1)S(1)}, bf16[1024,256]{1,0:T(8,128)(2,1)S(1)}, u32[]{:S(2)}, u32[]{:S(2)}) collective-permute-start(bf16[1024,256]{1,0:T(8,128)(2,1)S(1)} %add_convert_fusion.2), channel_id=1, source_target_pairs={{0,8},{4,12},{8,0},{12,4},{16,24},{20,28},{24,16},{28,20},{1,9},{5... | collective-permute-start | bytes 1572872 | tf_op jit(solution)/shard_map/ppermute | solution.py:185
  114.4 22.2 %collective-permute-start.19 = (bf16[1024,256]{1,0:T(8,128)(2,1)S(1)}, bf16[1024,256]{1,0:T(8,128)(2,1)S(1)}, u32[]{:S(2)}, u32[]{:S(2)}) collective-permute-start(bf16[1024,256]{1,0:T(8,128)(2,1)S(1)} %add_convert_fusion.3), channel_id=1, source_target_pairs={{0,8},{4,12},{8,0},{12,4},{16,24},{20,28},{24,16},{28,20},{1,9},{5... | collective-permute-start | bytes 1572872 | tf_op jit(solution)/shard_map/ppermute | solution.py:185
  114.5 6.1 %collective-permute-start.13 = (f32[16,16]{1,0:T(8,128)S(1)}, f32[16,16]{1,0:T(8,128)S(1)}, u32[]{:S(2)}, u32[]{:S(2)}) collective-permute-start(f32[16,16]{1,0:T(8,128)S(1)} %select_reduce_fusion), channel_id=1, source_target_pairs={{0,4},{4,0},{8,12},{12,8},{16,20},{20,16},{24,28},{28,24},{1,5},{5... | collective-permute-start | bytes 3080 | tf_op jit(solution)/shard_map/ppermute | solution.py:189
  141.2 23.5 %collective-permute-start.22 = (bf16[2048,256]{1,0:T(8,128)(2,1)S(1)}, bf16[2048,256]{1,0:T(8,128)(2,1)}, u32[]{:S(2)}, u32[]{:S(2)}) collective-permute-start(bf16[2048,256]{1,0:T(8,128)(2,1)S(1)} %weights.1), channel_id=1, source_target_pairs={{0,8},{4,12},{8,0},{12,4},{16,24},{20,28},{24,16},{28,20},{1,9},{5... | collective-permute-start | bytes 3145736 | tf_op jit(solution)/shard_map/ppermute | solution.py:185
  143.0 21.7 %collective-permute-start.24 = (bf16[2048,256]{1,0:T(8,128)(2,1)S(1)}, bf16[2048,256]{1,0:T(8,128)(2,1)}, u32[]{:S(2)}, u32[]{:S(2)}) collective-permute-start(bf16[2048,256]{1,0:T(8,128)(2,1)S(1)} %weights.1), channel_id=1, source_target_pairs={{8,16},{12,20},{16,8},{20,12},{9,17},{13,21},{17,9},{21,13},{10,18... | collective-permute-start | bytes 3145736 | tf_op jit(solution)/shard_map/ppermute | solution.py:185
  144.6 31.4 %collective-permute-start.23 = (bf16[2048,256]{1,0:T(8,128)(2,1)S(1)}, bf16[2048,256]{1,0:T(8,128)(2,1)}, u32[]{:S(2)}, u32[]{:S(2)}) collective-permute-start(bf16[2048,256]{1,0:T(8,128)(2,1)S(1)} %weights.1), channel_id=1, source_target_pairs={{0,4},{4,0},{8,12},{12,8},{16,20},{20,16},{24,28},{28,24},{1,5},{5... | collective-permute-start | bytes 3145736 | tf_op jit(solution)/shard_map/ppermute | solution.py:189
  164.7 25.5 %collective-permute-start.26 = (bf16[2048,256]{1,0:T(8,128)(2,1)}, bf16[2048,256]{1,0:T(8,128)(2,1)S(1)}, u32[]{:S(2)}, u32[]{:S(2)}) collective-permute-start(bf16[2048,256]{1,0:T(8,128)(2,1)} %collective-permute-done.24), channel_id=1, source_target_pairs={{8,0},{12,4},{16,24},{20,28},{9,1},{13,5},{17,25},{21,29},{10,2},{... | collective-permute-start | bytes 3145736 | tf_op jit(solution)/shard_map/ppermute | solution.py:185
  166.0 24.3 %collective-permute-start.25 = (bf16[2048,256]{1,0:T(8,128)(2,1)}, bf16[2048,256]{1,0:T(8,128)(2,1)S(1)}, u32[]{:S(2)}, u32[]{:S(2)}) collective-permute-start(bf16[2048,256]{1,0:T(8,128)(2,1)} %collective-permute-done.22), channel_id=1, source_target_pairs={{8,16},{12,20},{16,8},{20,12},{9,17},{13,21},{17,9},{21,13},{10,18... | collective-permute-start | bytes 3145736 | tf_op jit(solution)/shard_map/ppermute | solution.py:185
  166.8 25.5 %collective-permute-start.33 = (f32[16,16]{1,0:T(8,128)S(1)}, f32[16,16]{1,0:T(8,128)S(1)}, u32[]{:S(2)}, u32[]{:S(2)}) collective-permute-start(f32[16,16]{1,0:T(8,128)S(1)} %max.9), channel_id=1, source_target_pairs={{0,8},{4,12},{8,0},{12,4},{16,24},{20,28},{24,16},{28,20},{1,9},{5... | collective-permute-start | bytes 3080 | tf_op jit(solution)/shard_map/ppermute | solution.py:185
  173.2 26.2 %collective-permute-start.27 = (bf16[2048,256]{1,0:T(8,128)(2,1)}, bf16[2048,256]{1,0:T(8,128)(2,1)S(1)}, u32[]{:S(2)}, u32[]{:S(2)}) collective-permute-start(bf16[2048,256]{1,0:T(8,128)(2,1)} %collective-permute-done.22), channel_id=1, source_target_pairs={{0,4},{4,0},{8,12},{12,8},{16,20},{20,16},{24,28},{28,24},{1,5},{5... | collective-permute-start | bytes 3145736 | tf_op jit(solution)/shard_map/ppermute | solution.py:189
  190.3 17.8 %collective-permute-start.28 = (bf16[1024,256]{1,0:T(8,128)(2,1)S(1)}, bf16[1024,256]{1,0:T(8,128)(2,1)S(1)}, u32[]{:S(2)}, u32[]{:S(2)}) collective-permute-start(bf16[1024,256]{1,0:T(8,128)(2,1)S(1)} %get-tuple-element.127), channel_id=1, source_target_pairs={{8,0},{12,4},{16,24},{20,28},{9,1},{13,5},{17,25},{21,29},{10,2},{... | collective-permute-start | bytes 1572872 | tf_op jit(solution)/shard_map/ppermute | solution.py:185
  191.7 30.0 %collective-permute-start.30 = (bf16[2048,256]{1,0:T(8,128)(2,1)S(1)}, bf16[2048,256]{1,0:T(8,128)(2,1)S(1)}, u32[]{:S(2)}, u32[]{:S(2)}) collective-permute-start(bf16[2048,256]{1,0:T(8,128)(2,1)S(1)} %broadcast_select_fusion), channel_id=1, source_target_pairs={{0,4},{4,0},{8,12},{12,8},{16,20},{20,16},{24,28},{28,24},{1,5},{5... | collective-permute-start | bytes 3145736 | tf_op jit(solution)/shard_map/ppermute | solution.py:189
  192.3 23.2 %collective-permute-start.34 = (f32[16,16]{1,0:T(8,128)S(1)}, f32[16,16]{1,0:T(8,128)S(1)}, u32[]{:S(2)}, u32[]{:S(2)}) collective-permute-start(f32[16,16]{1,0:T(8,128)S(1)} %max.10), channel_id=1, source_target_pairs={{0,16},{4,20},{8,24},{12,28},{16,0},{20,4},{24,8},{28,12},{1,17},{... | collective-permute-start | bytes 3080 | tf_op jit(solution)/shard_map/ppermute | solution.py:185
  197.1 17.7 %collective-permute-start.29 = (bf16[1024,256]{1,0:T(8,128)(2,1)S(1)}, bf16[1024,256]{1,0:T(8,128)(2,1)S(1)}, u32[]{:S(2)}, u32[]{:S(2)}) collective-permute-start(bf16[1024,256]{1,0:T(8,128)(2,1)S(1)} %get-tuple-element.129), channel_id=1, source_target_pairs={{8,0},{12,4},{16,24},{20,28},{9,1},{13,5},{17,25},{21,29},{10,2},{... | collective-permute-start | bytes 1572872 | tf_op jit(solution)/shard_map/ppermute | solution.py:185
  208.2 24.7 %collective-permute-start.31 = (bf16[1024,256]{1,0:T(8,128)(2,1)S(1)}, bf16[1024,256]{1,0:T(8,128)(2,1)S(1)}, u32[]{:S(2)}, u32[]{:S(2)}) collective-permute-start(bf16[1024,256]{1,0:T(8,128)(2,1)S(1)} %broadcast_select_fusion.2), channel_id=1, source_target_pairs={{0,4},{4,0},{8,12},{12,8},{16,20},{20,16},{24,28},{28,24},{1,5},{5... | collective-permute-start | bytes 1572872 | tf_op jit(solution)/shard_map/ppermute | solution.py:189
  214.9 25.0 %collective-permute-start.32 = (bf16[1024,256]{1,0:T(8,128)(2,1)S(1)}, bf16[1024,256]{1,0:T(8,128)(2,1)S(1)}, u32[]{:S(2)}, u32[]{:S(2)}) collective-permute-start(bf16[1024,256]{1,0:T(8,128)(2,1)S(1)} %broadcast_select_fusion.1), channel_id=1, source_target_pairs={{0,4},{4,0},{8,12},{12,8},{16,20},{20,16},{24,28},{28,24},{1,5},{5... | collective-permute-start | bytes 1572872 | tf_op jit(solution)/shard_map/ppermute | solution.py:189

commit v5 on v4

--- a/solution.py
+++ b/solution.py
@@ -250,7 +250,7 @@
     pairs[0] = z_perm(token, PAIRS)
     token = add([partial[1, 0], *got1, inwards], token)
     last = z_perm(token, MIDDLE)
-    token = add([partial[2, 0], *got2, middle[1]], token, rows=part[1])
+    token = add([partial[2, 0], *got2, middle[1]], token, pairs[0], rows=part[1])
     pairs[1] = z_perm(token, PAIRS)
 
     terms = [after(partial[3, 0], *scales_x), *got3, last, tuple(pairs)]
@@ -265,38 +265,29 @@
     new_master, new_first, new_second = update(
         [after(terms[0], owned), *terms[1:]], states, factor, [0, 1, 2], "states"
     )
-    scales = after(scales, owned)
-    for got in scales_x:
-        scales = jnp.maximum(scales, got)
-    scales_z = z_perm(scales, PAIRS)
-
-    come = [pairs, mid, new_master]
+    come = [pairs, mid, new_master, *over0]
+    over1 = [x_perm(after(pairs, *come), by) for by in others]
     mid_far, outwards = z_perm(after(pairs, *come), MIDDLE), z_perm(after(mid, *come), OUTWARDS)
-    over1 = [x_perm(after(pairs, *come), by) for by in others]
-    weights = blank((rows, columns), BF16)
+    come = [mid_far, outwards]
+    near = lax.optimization_barrier(jnp.where(between, after(mid, *come, *over1), outwards))
+    over2 = [x_perm(near, by) for by in others]
+    cuts = [lax.slice_in_dim(mid_far, h * half, (h + 1) * half) for h in halves]
+    far = [z_perm(after(cuts[0], *come), OUTWARDS), z_perm(after(cuts[1], near), OUTWARDS)]
 
     def put(weights, value, slot, by, h=0):
         at = (sources[slot] * n_x + (x - by) % n_x) * width
         return lax.dynamic_update_slice(weights, value, (h * half, at))
 
+    weights = after(blank((rows, columns), BF16), near)
     weights = put(weights, owned, 0, 0)
     weights = put(weights, pairs, 1, 0)
-    come = [mid_far, outwards, *over0]
-    near = lax.optimization_barrier(jnp.where(between, after(mid, *come), outwards))
-    far = [z_perm(after(lax.slice_in_dim(mid_far, h * half, (h + 1) * half), *come), OUTWARDS) for h in halves]
-    over2 = [x_perm(near, by) for by in others]
-    scales = after(scales, scales_z, near)
-    scales = jnp.maximum(scales, scales_z)
-    scales_z = z_perm(scales, [(a, a ^ 2) for a in range(Z)])
-    for got, by in zip(over0, others):
-        weights = put(weights, got, 0, by)
-    weights = put(after(weights, near), near, 2, 0)
-    for got, by in zip(over1, others):
-        weights = put(weights, got, 1, by)
+    weights = put(weights, near, 2, 0)
+    for over, slot in ((over0, 0), (over1, 1)):
+        for got, by in zip(over, others):
+            weights = put(weights, got, slot, by)
     distant, over3 = [None] * 2, [None] * 2
     for h in halves:
-        come = [far[h], *over1] if h == 0 else [far[h], distant[0]]
-        value = after(lax.slice_in_dim(mid_far, h * half, (h + 1) * half), *come)
+        value = after(lax.slice_in_dim(mid_far, h * half, (h + 1) * half), far[h], *distant[:h])
         distant[h] = lax.optimization_barrier(jnp.where(between, value, far[h]))
         over3[h] = [x_perm(distant[h], by) for by in others]
     for h in halves:
@@ -306,7 +297,12 @@
     for h in halves:
         for got, by in zip(over3[h], others):
             weights = put(weights, got, 3, by, h)
-    block_scales = jnp.maximum(scales, after(scales_z, *distant)) + 1e-06
+    scales = after(scales, *distant, *over2)
+    for got in scales_x:
+        scales = jnp.maximum(scales, got)
+    scales = jnp.maximum(scales, z_perm(scales, PAIRS))
+    scales_z = z_perm(scales, [(a, a ^ 2) for a in range(Z)])
+    block_scales = jnp.maximum(scales, scales_z) + 1e-06
     return (new_master, new_first, new_second, weights, block_scales)
 
 

time: 242 us -> 239 us (0.988)
  waiting for transfers between devices: 121 us -> 115 us
    ppermute x10, waiting for transfers between devices: 42 us -> 27.9 us  [x_perm(): return lax.ppermute(value, 'dp', pairs)]
    ppermute x16, waiting for transfers between devices: 59.9 us -> 67.7 us  [z_perm(): lax.ppermute(value, 'dp', [(a * n_x + i, b * n_x + i) for a, b in pairs f...]
where the time goes in v5:
time: 239 us; the launch traced here: 238 us
  waiting for transfers between devices  115 us (48%)
  starting transfers between devices  48.3 us (20%)
  Pallas kernels  37.5 us (16%)
  local copies, waits for them, and re-layouts  21.8 us (9%)
  other arithmetic  14.6 us (6%)
    ppermute x16, waiting for transfers between devices, z_perm(): lax.ppermute(value, 'dp', [(a * n_x + i, b * n_x + i) for a, b in pairs f...  67.7 us
    ppermute x16, starting transfers between devices, z_perm(): lax.ppermute(value, 'dp', [(a * n_x + i, b * n_x + i) for a, b in pairs f...  34 us
    ppermute x10, waiting for transfers between devices, x_perm(): return lax.ppermute(value, 'dp', pairs)  27.9 us
    pallas_call x3, Pallas kernels, multiply(): pl.pallas_call(kernel, grid=(rows // step,), in_specs=[pl.BlockSpec((step...  23.7 us
    ppermute x9, waiting for transfers between devices, seat_perm(): lax.ppermute(value, 'tensor', [(i, i ^ flip) for i in range(n_tensor)])  19.2 us
    convert_element_type x8, other arithmetic, add(): return lax.optimization_barrier(total.astype(BF16))  12 us
    pallas_call x2, Pallas kernels, update(): pl.pallas_call(kernel, grid=(rows // step,), in_specs=specs + [whole] * 3...  11 us
    dynamic_update_slice x10, local copies, waits for them, and re-layouts, put(): return lax.dynamic_update_slice(weights, value, (h * half, at))  10.8 us
  transfers between devices with their start and end apart: 35, of which 20 were waited for; matrix products, arithmetic and copies ran while one was open for 14% of the time, Pallas kernels for 11%

profile of v5, /device:TPU:0, one launch (start us, length us, event | category | flops | bytes accessed | tf_op | source)
XLA Modules:
  0.0 237.8 jit_solution(5595717379035697864)
XLA Ops:
  0.6 2.8 %arrange.1 = (bf16[384,256]{1,0:T(8,128)(2,1)}, bf16[384,512]{1,0:T(8,128)(2,1)}, bf16[384,1280]{1,0:T(8,128)(2,1)}) custom-call(bf16[384,2048]{1,0:T(8,128)(2,1)} %cot_ref.1), custom_call_target="tpu_custom_call" | custom-call | tf_op jit(solution)/shard_map/arrange/pallas_call | solution.py:55
  3.4 3.0 %collective-permute-start.1 = (bf16[384,256]{1,0:T(8,128)(2,1)}, bf16[384,256]{1,0:T(8,128)(2,1)S(1)}, u32[]{:S(2)}, u32[]{:S(2)}) collective-permute-start(bf16[384,256]{1,0:T(8,128)(2,1)} %get-tuple-element.72.refs_0_), channel_id=1, source_target_pairs={{0,2},{1,3},{2,0},{3,1},{4,6},{5,7},{6,4},{7,5},{8,10},{9,11},{10,... | collective-permute-start | bytes 589832 | tf_op jit(solution)/shard_map/ppermute | solution.py:192
  6.4 8.6 %copy.12 = bf16[1536,2048]{0,1:T(8,128)(2,1)} copy(bf16[1536,2048]{1,0:T(8,128)(2,1)} %param.5) | data formatting | bytes 12582912 | tf_op jit(solution)/shard_map/optimization_barrier | solution.py:170
  15.6 0.9 collective-permute-done.refs_1_
  16.8 4.8 %partials.3 = (bf16[2048,256]{1,0:T(8,128)(2,1)S(1)}, f32[4,4,256]{2,1,0:T(4,128)S(1)}) custom-call(bf16[2048,1536]{1,0:T(8,128)(2,1)} %bitcast.17, bf16[384,256]{1,0:T(8,128)(2,1)S(1)} %copy-done.4, bf16[384,256]{1,0:T(8,128)(2,1)S(1)} %collective-permute-done.refs_1_, bf16[384,256]{1,0:T(8,128)(2,1)S(1)} %collective-permute-done.1.refs_2_, ...), custom_call_target="tpu_custom_call" | custom-call | flops 10000000000 | bytes 3145728 | tf_op jit(solution)/shard_map/partials/pallas_call | solution.py:79
  21.6 1.5 collective-permute-start.6
  23.6 1.5 collective-permute-start.8
  25.2 10.0 %collective-permute-done.4.refs_2_ = bf16[384,512]{1,0:T(8,128)(2,1)S(1)} collective-permute-done((bf16[384,512]{1,0:T(8,128)(2,1)S(1)}, bf16[384,512]{1,0:T(8,128)(2,1)S(1)}, u32[]{:S(2)}, u32[]{:S(2)}) %collective-permute-start.4) | collective-permute-done | bytes 393248 | tf_op jit(solution)/shard_map/ppermute | solution.py:192
  35.6 1.2 collective-permute-done.5.refs_3_
  37.4 6.8 %partials.4 = (bf16[2048,256]{1,0:T(8,128)(2,1)S(1)}, bf16[2048,256]{1,0:T(8,128)(2,1)}, f32[4,4,512]{2,1,0:T(4,128)S(1)}) custom-call(bf16[2048,1536]{1,0:T(8,128)(2,1)} %bitcast.18, bf16[384,512]{1,0:T(8,128)(2,1)S(1)} %copy-done.2, bf16[384,512]{1,0:T(8,128)(2,1)S(1)} %collective-permute-done.3.refs_1_, ...), custom_call_target="tpu_custom_call" | custom-call | tf_op jit(solution)/shard_map/partials/pallas_call | solution.py:79
  44.8 2.2 collective-permute-done.6
  46.9 1.0 add_convert_fusion.7
  48.0 0.9 add_convert_fusion.6
  48.9 6.2 %collective-permute-done.8.refs_2_ = bf16[384,1280]{1,0:T(8,128)(2,1)S(1)} collective-permute-done((bf16[384,1280]{1,0:T(8,128)(2,1)S(1)}, bf16[384,1280]{1,0:T(8,128)(2,1)S(1)}, u32[]{:S(2)}, u32[]{:S(2)}) %collective-permute-start.8) | collective-permute-done | bytes 983072 | tf_op jit(solution)/shard_map/ppermute | solution.py:192
  55.8 3.6 %collective-permute-start.11 = (bf16[1024,256]{1,0:T(8,128)(2,1)}, bf16[1024,256]{1,0:T(8,128)(2,1)S(1)}, u32[]{:S(2)}, u32[]{:S(2)}) collective-permute-start(bf16[1024,256]{1,0:T(8,128)(2,1)} %add_convert_fusion.7), channel_id=1, source_target_pairs={{0,8},{4,12},{24,16},{28,20},{1,9},{5,13},{25,17},{29,21},{2,10},{... | collective-permute-start | bytes 1572872 | tf_op jit(solution)/shard_map/ppermute | solution.py:185
  59.4 1.3 collective-permute-start.10
  60.8 12.1 %partials.5 = (bf16[2048,256]{1,0:T(8,128)(2,1)}, bf16[2048,256]{1,0:T(8,128)(2,1)S(1)}, bf16[2048,256]{1,0:T(8,128)(2,1)}, bf16[2048,256]{1,0:T(8,128)(2,1)}, b...) custom-call(bf16[2048,1536]{1,0:T(8,128)(2,1)} %bitcast.19, bf16[384,1280]{1,0:T(8,128)(2,1)S(1)} %copy-done.1, ...), custom_call_target="tpu_custom_call" | custom-call | tf_op jit(solution)/shard_map/partials/pallas_call | solution.py:79
  73.5 2.9 %add_convert_fusion.1 = bf16[2048,256]{1,0:T(8,128)(2,1)} fusion(bf16[2048,256]{1,0:T(8,128)(2,1)} %collective-permute-done.12, bf16[2048,256]{1,0:T(8,128)(2,1)} %get-tuple-element.110), kind=kLoop, calls=%fused_computation.1 | loop fusion | flops 2097152 | bytes 3145728 | tf_op jit(solution)/shard_map/convert_element_type | solution.py:103
  76.4 2.9 %collective-permute-start.15 = (bf16[2048,256]{1,0:T(8,128)(2,1)}, bf16[2048,256]{1,0:T(8,128)(2,1)}, u32[]{:S(2)}, u32[]{:S(2)}) collective-permute-start(bf16[2048,256]{1,0:T(8,128)(2,1)} %add_convert_fusion.1), channel_id=1, source_target_pairs={{0,8},{4,12},{24,16},{28,20},{1,9},{5,13},{25,17},{29,21},{2,10},{... | collective-permute-start | bytes 3145736 | tf_op jit(solution)/shard_map/ppermute | solution.py:185
  79.3 1.0 add_convert_fusion.5
  80.3 1.4 collective-permute-start.17
  81.8 1.4 collective-permute-done.10
  83.2 1.0 add_convert_fusion.4
  86.2 13.2 %collective-permute-done.16 = bf16[2048,256]{1,0:T(8,128)(2,1)} collective-permute-done((bf16[2048,256]{1,0:T(8,128)(2,1)}, bf16[2048,256]{1,0:T(8,128)(2,1)}, u32[]{:S(2)}, u32[]{:S(2)}) %collective-permute-start.16) | collective-permute-done | bytes 1048608 | tf_op jit(solution)/shard_map/ppermute | solution.py:189
  99.3 1.5 add_convert_fusion.3
  101.0 4.8 %collective-permute-done.15 = bf16[2048,256]{1,0:T(8,128)(2,1)} collective-permute-done((bf16[2048,256]{1,0:T(8,128)(2,1)}, bf16[2048,256]{1,0:T(8,128)(2,1)}, u32[]{:S(2)}, u32[]{:S(2)}) %collective-permute-start.15) | collective-permute-done | bytes 1048608 | tf_op jit(solution)/shard_map/ppermute | solution.py:185
  105.7 2.2 add_convert_fusion
  108.0 0.7 collective-permute-start.18
  108.7 7.2 %collective-permute-done.19.refs_3_ = bf16[1024,256]{1,0:T(8,128)(2,1)S(1)} collective-permute-done((bf16[1024,256]{1,0:T(8,128)(2,1)S(1)}, bf16[1024,256]{1,0:T(8,128)(2,1)S(1)}, u32[]{:S(2)}, u32[]{:S(2)}) %collective-permute-start.19) | collective-permute-done | bytes 524320 | tf_op jit(solution)/shard_map/ppermute | solution.py:185
  115.9 1.4 add_convert_fusion.2
  117.3 2.5 %collective-permute-start.21 = (bf16[1024,256]{1,0:T(8,128)(2,1)S(1)}, bf16[1024,256]{1,0:T(8,128)(2,1)S(1)}, u32[]{:S(2)}, u32[]{:S(2)}) collective-permute-start(bf16[1024,256]{1,0:T(8,128)(2,1)S(1)} %add_convert_fusion.2), channel_id=1, source_target_pairs={{0,8},{4,12},{8,0},{12,4},{16,24},{20,28},{24,16},{28,20},{1,9},{5... | collective-permute-start | bytes 1572872 | tf_op jit(solution)/shard_map/ppermute | solution.py:185
  120.4 3.1 %collective-permute-done.13 = f32[16,16]{1,0:T(8,128)S(1)} collective-permute-done((f32[16,16]{1,0:T(8,128)S(1)}, f32[16,16]{1,0:T(8,128)S(1)}, u32[]{:S(2)}, u32[]{:S(2)}) %collective-permute-start.13) | collective-permute-done | bytes 1056 | tf_op jit(solution)/shard_map/ppermute | solution.py:189
  123.5 7.6 %collective-permute-done.21.refs_4_ = bf16[1024,256]{1,0:T(8,128)(2,1)S(1)} collective-permute-done((bf16[1024,256]{1,0:T(8,128)(2,1)S(1)}, bf16[1024,256]{1,0:T(8,128)(2,1)S(1)}, u32[]{:S(2)}, u32[]{:S(2)}) %collective-permute-start.21) | collective-permute-done | bytes 524320 | tf_op jit(solution)/shard_map/ppermute | solution.py:185
  131.1 4.6 %weights.1 = bf16[2048,256]{1,0:T(8,128)(2,1)S(1)} custom-call(bf16[2048,256]{1,0:T(8,128)(2,1)S(1)} %copy-done, bf16[2048,256]{1,0:T(8,128)(2,1)S(1)} %collective-permute-done.14.refs_1_, bf16[2048,256]{1,0:T(8,128)(2,1)S(1)} %collective-permute-done.18.refs_2_, bf16[1024,256]{1,0:T(8,128)(2,1)S(1)} %collective-permute-done.19.refs_3_, ...), custom_call_target="tpu_custom_call" | custom-call | tf_op jit(solution)/shard_map/weights/pallas_call | solution.py:147
  135.6 1.7 collective-permute-start.22
  137.3 6.4 %collective-permute-start.23 = (bf16[2048,256]{1,0:T(8,128)(2,1)S(1)}, bf16[2048,256]{1,0:T(8,128)(2,1)}, u32[]{:S(2)}, u32[]{:S(2)}) collective-permute-start(bf16[2048,256]{1,0:T(8,128)(2,1)S(1)} %weights.1), channel_id=1, source_target_pairs={{0,8},{4,12},{8,0},{12,4},{16,24},{20,28},{24,16},{28,20},{1,9},{5... | collective-permute-start | bytes 3145736 | tf_op jit(solution)/shard_map/ppermute | solution.py:185
  144.2 6.4 %states.1 = (f32[2048,256]{1,0:T(8,128)}, f32[2048,256]{1,0:T(8,128)}, f32[2048,256]{1,0:T(8,128)}) custom-call(bf16[2048,256]{1,0:T(8,128)(2,1)S(1)} %copy-done, bf16[2048,256]{1,0:T(8,128)(2,1)S(1)} %collective-permute-done.14.refs_1_, bf16[2048,256]{1,0:T(8,128)(2,1)S(1)} %collective-permute-done.18.refs_2_, ...), custom_call_target="tpu_custom_call" | custom-call | tf_op jit(solution)/shard_map/states/pallas_call | solution.py:147
  150.7 13.4 %collective-permute-done.23 = bf16[2048,256]{1,0:T(8,128)(2,1)} collective-permute-done((bf16[2048,256]{1,0:T(8,128)(2,1)S(1)}, bf16[2048,256]{1,0:T(8,128)(2,1)}, u32[]{:S(2)}, u32[]{:S(2)}) %collective-permute-start.23) | collective-permute-done | bytes 1048608 | tf_op jit(solution)/shard_map/ppermute | solution.py:185
  164.1 1.4 collective-permute-done.24
  165.5 1.0 copy-done.7
  166.5 1.3 collective-permute-start.26
  167.7 1.7 collective-permute-start.25
  170.0 19.6 %collective-permute-done.26 = bf16[2048,256]{1,0:T(8,128)(2,1)} collective-permute-done((bf16[2048,256]{1,0:T(8,128)(2,1)}, bf16[2048,256]{1,0:T(8,128)(2,1)}, u32[]{:S(2)}, u32[]{:S(2)}) %collective-permute-start.26) | collective-permute-done | bytes 1048608 | tf_op jit(solution)/shard_map/ppermute | solution.py:185
  189.6 1.8 collective-permute-done.27
  191.5 1.3 broadcast_select_fusion
  193.4 1.3 fusion
  194.7 1.3 collective-permute-start.29
  196.0 1.3 collective-permute-start.28
  197.3 1.0 constant_dynamic-update-slice_fusion.7
  198.3 2.3 constant_dynamic-update-slice_fusion.6
  200.6 1.0 constant_dynamic-update-slice_fusion.5
  201.6 1.0 constant_dynamic-update-slice_fusion.4
  202.7 1.0 constant_dynamic-update-slice_fusion.3
  203.7 12.9 %collective-permute-done.28 = bf16[1024,256]{1,0:T(8,128)(2,1)S(1)} collective-permute-done((bf16[1024,256]{1,0:T(8,128)(2,1)S(1)}, bf16[1024,256]{1,0:T(8,128)(2,1)S(1)}, u32[]{:S(2)}, u32[]{:S(2)}) %collective-permute-start.28) | collective-permute-done | bytes 524320 | tf_op jit(solution)/shard_map/ppermute | solution.py:185
  216.6 1.5 collective-permute-start.31
  218.8 0.8 constant_dynamic-update-slice_fusion.2
  219.7 0.8 constant_dynamic-update-slice_fusion.9
  220.5 2.2 collective-permute-start.33
  222.7 1.0 constant_dynamic-update-slice_fusion.1
  223.7 6.2 %collective-permute-done.31 = bf16[1024,256]{1,0:T(8,128)(2,1)S(1)} collective-permute-done((bf16[1024,256]{1,0:T(8,128)(2,1)S(1)}, bf16[1024,256]{1,0:T(8,128)(2,1)S(1)}, u32[]{:S(2)}, u32[]{:S(2)}) %collective-permute-start.31) | collective-permute-done | bytes 524320 | tf_op jit(solution)/shard_map/ppermute | solution.py:189
  229.9 0.8 constant_dynamic-update-slice_fusion
  230.8 4.8 %collective-permute-start.34 = (f32[16,16]{1,0:T(8,128)S(1)}, f32[16,16]{1,0:T(8,128)S(1)}, u32[]{:S(2)}, u32[]{:S(2)}) collective-permute-start(f32[16,16]{1,0:T(8,128)S(1)} %max.10), channel_id=1, source_target_pairs={{0,16},{4,20},{8,24},{12,28},{16,0},{20,4},{24,8},{28,12},{1,17},{... | collective-permute-start | bytes 3080 | tf_op jit(solution)/shard_map/ppermute | solution.py:185
  235.6 0.8 constant_dynamic-update-slice_fusion.8
  236.4 0.8 collective-permute-done.34
  (67 shorter events, 9.8 us)
Async XLA Ops:
  3.4 11.6 %copy-start.4 = (bf16[384,256]{1,0:T(8,128)(2,1)S(1)}, bf16[384,256]{1,0:T(8,128)(2,1)}, u32[]{:S(2)}) copy-start(bf16[384,256]{1,0:T(8,128)(2,1)} %get-tuple-element.72.refs_0_) | copy-start | bytes 589828
  3.4 11.7 %collective-permute-start.1 = (bf16[384,256]{1,0:T(8,128)(2,1)}, bf16[384,256]{1,0:T(8,128)(2,1)S(1)}, u32[]{:S(2)}, u32[]{:S(2)}) collective-permute-start(bf16[384,256]{1,0:T(8,128)(2,1)} %get-tuple-element.72.refs_0_), channel_id=1, source_target_pairs={{0,2},{1,3},{2,0},{3,1},{4,6},{5,7},{6,4},{7,5},{8,10},{9,11},{10,... | collective-permute-start | bytes 589832 | tf_op jit(solution)/shard_map/ppermute | solution.py:192
  15.0 8.1 %copy-start.2 = (bf16[384,512]{1,0:T(8,128)(2,1)S(1)}, bf16[384,512]{1,0:T(8,128)(2,1)}, u32[]{:S(2)}) copy-start(bf16[384,512]{1,0:T(8,128)(2,1)} %get-tuple-element.76.refs_0_) | copy-start | bytes 1179652
  15.0 8.7 %copy-start.1 = (bf16[384,1280]{1,0:T(8,128)(2,1)S(1)}, bf16[384,1280]{1,0:T(8,128)(2,1)}, u32[]{:S(2)}) copy-start(bf16[384,1280]{1,0:T(8,128)(2,1)} %get-tuple-element.84.refs_0_) | copy-start | bytes 2949124
  15.0 1.5 collective-permute-start
  15.1 1.7 collective-permute-start.2
  21.6 25.4 %collective-permute-start.6 = (bf16[2048,256]{1,0:T(8,128)(2,1)S(1)}, bf16[2048,256]{1,0:T(8,128)(2,1)S(1)}, u32[]{:S(2)}, u32[]{:S(2)}) collective-permute-start(bf16[2048,256]{1,0:T(8,128)(2,1)S(1)} %get-tuple-element.74), channel_id=1, source_target_pairs={{0,4},{4,0},{8,12},{12,8},{16,20},{20,16},{24,28},{28,24},{1,5},{5... | collective-permute-start | bytes 3145736 | tf_op jit(solution)/shard_map/ppermute | solution.py:189
  23.1 12.0 %collective-permute-start.4 = (bf16[384,512]{1,0:T(8,128)(2,1)S(1)}, bf16[384,512]{1,0:T(8,128)(2,1)S(1)}, u32[]{:S(2)}, u32[]{:S(2)}) collective-permute-start(bf16[384,512]{1,0:T(8,128)(2,1)S(1)} %copy-done.2), channel_id=1, source_target_pairs={{0,2},{1,3},{2,0},{3,1},{4,6},{5,7},{6,4},{7,5},{8,10},{9,11},{10,... | collective-permute-start | bytes 1179656 | tf_op jit(solution)/shard_map/ppermute | solution.py:192
  23.6 31.5 %collective-permute-start.8 = (bf16[384,1280]{1,0:T(8,128)(2,1)S(1)}, bf16[384,1280]{1,0:T(8,128)(2,1)S(1)}, u32[]{:S(2)}, u32[]{:S(2)}) collective-permute-start(bf16[384,1280]{1,0:T(8,128)(2,1)S(1)} %copy-done.1), channel_id=1, source_target_pairs={{0,2},{1,3},{2,0},{3,1},{4,6},{5,7},{6,4},{7,5},{8,10},{9,11},{10,... | collective-permute-start | bytes 2949128 | tf_op jit(solution)/shard_map/ppermute | solution.py:192
  35.1 1.7 collective-permute-start.5
  35.1 2.3 collective-permute-start.3
  44.2 29.3 %collective-permute-start.12 = (bf16[2048,256]{1,0:T(8,128)(2,1)}, bf16[2048,256]{1,0:T(8,128)(2,1)}, u32[]{:S(2)}, u32[]{:S(2)}) collective-permute-start(bf16[2048,256]{1,0:T(8,128)(2,1)} %get-tuple-element.89), channel_id=1, source_target_pairs={{0,4},{4,0},{8,12},{12,8},{16,20},{20,16},{24,28},{28,24},{1,5},{5... | collective-permute-start | bytes 3145736 | tf_op jit(solution)/shard_map/ppermute | solution.py:189
  46.9 8.2 %copy-start.5 = (bf16[2048,256]{1,0:T(8,128)(2,1)}, bf16[2048,256]{1,0:T(8,128)(2,1)S(1)}, u32[]{:S(2)}) copy-start(bf16[2048,256]{1,0:T(8,128)(2,1)S(1)} %collective-permute-done.6) | copy-start | bytes 3145732
  55.2 5.6 %collective-permute-start.9 = (bf16[384,1280]{1,0:T(8,128)(2,1)S(1)}, bf16[384,1280]{1,0:T(8,128)(2,1)}, u32[]{:S(2)}, u32[]{:S(2)}) collective-permute-start(bf16[384,1280]{1,0:T(8,128)(2,1)S(1)} %collective-permute-done.8.refs_2_), channel_id=1, source_target_pairs={{0,1},{1,0},{2,3},{3,2},{4,5},{5,4},{6,7},{7,6},{8,9},{9,8},{10,11... | collective-permute-start | bytes 2949128 | tf_op jit(solution)/shard_map/ppermute | solution.py:192
  55.2 5.6 %collective-permute-start.7 = (bf16[384,1280]{1,0:T(8,128)(2,1)S(1)}, bf16[384,1280]{1,0:T(8,128)(2,1)}, u32[]{:S(2)}, u32[]{:S(2)}) collective-permute-start(bf16[384,1280]{1,0:T(8,128)(2,1)S(1)} %copy-done.1), channel_id=1, source_target_pairs={{0,1},{1,0},{2,3},{3,2},{4,5},{5,4},{6,7},{7,6},{8,9},{9,8},{10,11... | collective-permute-start | bytes 2949128 | tf_op jit(solution)/shard_map/ppermute | solution.py:192
  55.8 23.5 %copy-start.6 = (bf16[2048,256]{1,0:T(8,128)(2,1)S(1)}, bf16[2048,256]{1,0:T(8,128)(2,1)}, u32[]{:S(2)}) copy-start(bf16[2048,256]{1,0:T(8,128)(2,1)} %copy-done.5) | copy-start | bytes 3145732
  55.8 23.5 %collective-permute-start.11 = (bf16[1024,256]{1,0:T(8,128)(2,1)}, bf16[1024,256]{1,0:T(8,128)(2,1)S(1)}, u32[]{:S(2)}, u32[]{:S(2)}) collective-permute-start(bf16[1024,256]{1,0:T(8,128)(2,1)} %add_convert_fusion.7), channel_id=1, source_target_pairs={{0,8},{4,12},{24,16},{28,20},{1,9},{5,13},{25,17},{29,21},{2,10},{... | collective-permute-start | bytes 1572872 | tf_op jit(solution)/shard_map/ppermute | solution.py:185
  59.4 23.8 %collective-permute-start.10 = (bf16[1024,256]{1,0:T(8,128)(2,1)}, bf16[1024,256]{1,0:T(8,128)(2,1)S(1)}, u32[]{:S(2)}, u32[]{:S(2)}) collective-permute-start(bf16[1024,256]{1,0:T(8,128)(2,1)} %add_convert_fusion.6), channel_id=1, source_target_pairs={{0,8},{4,12},{24,16},{28,20},{1,9},{5,13},{25,17},{29,21},{2,10},{... | collective-permute-start | bytes 1572872 | tf_op jit(solution)/shard_map/ppermute | solution.py:185
  72.9 11.4 %copy-start.3 = (bf16[2048,256]{1,0:T(8,128)(2,1)}, bf16[2048,256]{1,0:T(8,128)(2,1)S(1)}, u32[]{:S(2)}) copy-start(bf16[2048,256]{1,0:T(8,128)(2,1)S(1)} %get-tuple-element.105) | copy-start | bytes 3145732
  72.9 58.2 %copy-start = (bf16[2048,256]{1,0:T(8,128)(2,1)S(1)}, bf16[2048,256]{1,0:T(8,128)(2,1)}, u32[]{:S(2)}) copy-start(bf16[2048,256]{1,0:T(8,128)(2,1)} %get-tuple-element.116.refs_0_) | copy-start | bytes 3145732
  72.9 26.4 %collective-permute-start.16 = (bf16[2048,256]{1,0:T(8,128)(2,1)}, bf16[2048,256]{1,0:T(8,128)(2,1)}, u32[]{:S(2)}, u32[]{:S(2)}) collective-permute-start(bf16[2048,256]{1,0:T(8,128)(2,1)} %get-tuple-element.90), channel_id=1, source_target_pairs={{0,4},{4,0},{8,12},{12,8},{16,20},{20,16},{24,28},{28,24},{1,5},{5... | collective-permute-start | bytes 3145736 | tf_op jit(solution)/shard_map/ppermute | solution.py:189
  76.4 29.3 %collective-permute-start.15 = (bf16[2048,256]{1,0:T(8,128)(2,1)}, bf16[2048,256]{1,0:T(8,128)(2,1)}, u32[]{:S(2)}, u32[]{:S(2)}) collective-permute-start(bf16[2048,256]{1,0:T(8,128)(2,1)} %add_convert_fusion.1), channel_id=1, source_target_pairs={{0,8},{4,12},{24,16},{28,20},{1,9},{5,13},{25,17},{29,21},{2,10},{... | collective-permute-start | bytes 3145736 | tf_op jit(solution)/shard_map/ppermute | solution.py:185
  80.3 5.9 %collective-permute-start.17 = (bf16[1024,256]{1,0:T(8,128)(2,1)}, bf16[1024,256]{1,0:T(8,128)(2,1)}, u32[]{:S(2)}, u32[]{:S(2)}) collective-permute-start(bf16[1024,256]{1,0:T(8,128)(2,1)} %add_convert_fusion.5), channel_id=1, source_target_pairs={{8,16},{12,20},{16,8},{20,12},{9,17},{13,21},{17,9},{21,13},{10,18... | collective-permute-start | bytes 1572872 | tf_op jit(solution)/shard_map/ppermute | solution.py:185
  84.2 24.4 %collective-permute-start.20 = (bf16[1024,256]{1,0:T(8,128)(2,1)}, bf16[1024,256]{1,0:T(8,128)(2,1)S(1)}, u32[]{:S(2)}, u32[]{:S(2)}) collective-permute-start(bf16[1024,256]{1,0:T(8,128)(2,1)} %add_convert_fusion.4), channel_id=1, source_target_pairs={{8,16},{12,20},{16,8},{20,12},{9,17},{13,21},{17,9},{21,13},{10,18... | collective-permute-start | bytes 1572872 | tf_op jit(solution)/shard_map/ppermute | solution.py:185
  85.3 38.1 %collective-permute-start.14 = (bf16[2048,256]{1,0:T(8,128)(2,1)}, bf16[2048,256]{1,0:T(8,128)(2,1)S(1)}, u32[]{:S(2)}, u32[]{:S(2)}) collective-permute-start(bf16[2048,256]{1,0:T(8,128)(2,1)} %copy-done.3), channel_id=1, source_target_pairs={{0,4},{4,0},{8,12},{12,8},{16,20},{20,16},{24,28},{28,24},{1,5},{5... | collective-permute-start | bytes 3145736 | tf_op jit(solution)/shard_map/ppermute | solution.py:189
  100.9 15.0 %collective-permute-start.19 = (bf16[1024,256]{1,0:T(8,128)(2,1)S(1)}, bf16[1024,256]{1,0:T(8,128)(2,1)S(1)}, u32[]{:S(2)}, u32[]{:S(2)}) collective-permute-start(bf16[1024,256]{1,0:T(8,128)(2,1)S(1)} %add_convert_fusion.3), channel_id=1, source_target_pairs={{0,8},{4,12},{8,0},{12,4},{16,24},{20,28},{24,16},{28,20},{1,9},{5... | collective-permute-start | bytes 1572872 | tf_op jit(solution)/shard_map/ppermute | solution.py:185
  108.0 23.1 %collective-permute-start.18 = (bf16[2048,256]{1,0:T(8,128)(2,1)S(1)}, bf16[2048,256]{1,0:T(8,128)(2,1)S(1)}, u32[]{:S(2)}, u32[]{:S(2)}) collective-permute-start(bf16[2048,256]{1,0:T(8,128)(2,1)S(1)} %add_convert_fusion), channel_id=1, source_target_pairs={{8,16},{12,20},{16,8},{20,12},{9,17},{13,21},{17,9},{21,13},{10,18... | collective-permute-start | bytes 3145736 | tf_op jit(solution)/shard_map/ppermute | solution.py:185
  117.3 13.8 %collective-permute-start.21 = (bf16[1024,256]{1,0:T(8,128)(2,1)S(1)}, bf16[1024,256]{1,0:T(8,128)(2,1)S(1)}, u32[]{:S(2)}, u32[]{:S(2)}) collective-permute-start(bf16[1024,256]{1,0:T(8,128)(2,1)S(1)} %add_convert_fusion.2), channel_id=1, source_target_pairs={{0,8},{4,12},{8,0},{12,4},{16,24},{20,28},{24,16},{28,20},{1,9},{5... | collective-permute-start | bytes 1572872 | tf_op jit(solution)/shard_map/ppermute | solution.py:185
  119.8 3.7 %collective-permute-start.13 = (f32[16,16]{1,0:T(8,128)S(1)}, f32[16,16]{1,0:T(8,128)S(1)}, u32[]{:S(2)}, u32[]{:S(2)}) collective-permute-start(f32[16,16]{1,0:T(8,128)S(1)} %select_reduce_fusion), channel_id=1, source_target_pairs={{0,4},{4,0},{8,12},{12,8},{16,20},{20,16},{24,28},{28,24},{1,5},{5... | collective-permute-start | bytes 3080 | tf_op jit(solution)/shard_map/ppermute | solution.py:189
  135.6 15.0 %collective-permute-start.22 = (bf16[2048,256]{1,0:T(8,128)(2,1)S(1)}, bf16[2048,256]{1,0:T(8,128)(2,1)}, u32[]{:S(2)}, u32[]{:S(2)}) collective-permute-start(bf16[2048,256]{1,0:T(8,128)(2,1)S(1)} %weights.1), channel_id=1, source_target_pairs={{8,16},{12,20},{16,8},{20,12},{9,17},{13,21},{17,9},{21,13},{10,18... | collective-permute-start | bytes 3145736 | tf_op jit(solution)/shard_map/ppermute | solution.py:185
  137.3 26.8 %collective-permute-start.23 = (bf16[2048,256]{1,0:T(8,128)(2,1)S(1)}, bf16[2048,256]{1,0:T(8,128)(2,1)}, u32[]{:S(2)}, u32[]{:S(2)}) collective-permute-start(bf16[2048,256]{1,0:T(8,128)(2,1)S(1)} %weights.1), channel_id=1, source_target_pairs={{0,8},{4,12},{8,0},{12,4},{16,24},{20,28},{24,16},{28,20},{1,9},{5... | collective-permute-start | bytes 3145736 | tf_op jit(solution)/shard_map/ppermute | solution.py:185
  143.7 21.8 %collective-permute-start.24 = (bf16[2048,256]{1,0:T(8,128)(2,1)S(1)}, bf16[2048,256]{1,0:T(8,128)(2,1)S(1)}, u32[]{:S(2)}, u32[]{:S(2)}) collective-permute-start(bf16[2048,256]{1,0:T(8,128)(2,1)S(1)} %weights.1), channel_id=1, source_target_pairs={{0,4},{4,0},{8,12},{12,8},{16,20},{20,16},{24,28},{28,24},{1,5},{5... | collective-permute-start | bytes 3145736 | tf_op jit(solution)/shard_map/ppermute | solution.py:189
  165.5 1.0 copy-start.7
  166.5 23.2 %collective-permute-start.26 = (bf16[2048,256]{1,0:T(8,128)(2,1)}, bf16[2048,256]{1,0:T(8,128)(2,1)}, u32[]{:S(2)}, u32[]{:S(2)}) collective-permute-start(bf16[2048,256]{1,0:T(8,128)(2,1)} %collective-permute-done.22), channel_id=1, source_target_pairs={{8,0},{12,4},{16,24},{20,28},{9,1},{13,5},{17,25},{21,29},{10,2},{... | collective-permute-start | bytes 3145736 | tf_op jit(solution)/shard_map/ppermute | solution.py:185
  167.7 21.9 %collective-permute-start.25 = (bf16[2048,256]{1,0:T(8,128)(2,1)}, bf16[2048,256]{1,0:T(8,128)(2,1)}, u32[]{:S(2)}, u32[]{:S(2)}) collective-permute-start(bf16[2048,256]{1,0:T(8,128)(2,1)} %collective-permute-done.23), channel_id=1, source_target_pairs={{8,16},{12,20},{16,8},{20,12},{9,17},{13,21},{17,9},{21,13},{10,18... | collective-permute-start | bytes 3145736 | tf_op jit(solution)/shard_map/ppermute | solution.py:185
  169.4 22.0 %collective-permute-start.27 = (bf16[2048,256]{1,0:T(8,128)(2,1)}, bf16[2048,256]{1,0:T(8,128)(2,1)S(1)}, u32[]{:S(2)}, u32[]{:S(2)}) collective-permute-start(bf16[2048,256]{1,0:T(8,128)(2,1)} %collective-permute-done.23), channel_id=1, source_target_pairs={{0,4},{4,0},{8,12},{12,8},{16,20},{20,16},{24,28},{28,24},{1,5},{5... | collective-permute-start | bytes 3145736 | tf_op jit(solution)/shard_map/ppermute | solution.py:189
  170.0 31.6 %copy-start.8 = (bf16[2048,256]{1,0:T(8,128)(2,1)S(1)}, bf16[2048,256]{1,0:T(8,128)(2,1)}, u32[]{:S(2)}) copy-start(bf16[2048,256]{1,0:T(8,128)(2,1)} %copy-done.7) | copy-start | bytes 3145732
  192.8 27.7 %collective-permute-start.30 = (bf16[2048,256]{1,0:T(8,128)(2,1)S(1)}, bf16[2048,256]{1,0:T(8,128)(2,1)S(1)}, u32[]{:S(2)}, u32[]{:S(2)}) collective-permute-start(bf16[2048,256]{1,0:T(8,128)(2,1)S(1)} %broadcast_select_fusion), channel_id=1, source_target_pairs={{0,4},{4,0},{8,12},{12,8},{16,20},{20,16},{24,28},{28,24},{1,5},{5... | collective-permute-start | bytes 3145736 | tf_op jit(solution)/shard_map/ppermute | solution.py:189
  194.7 23.5 %collective-permute-start.29 = (bf16[1024,256]{1,0:T(8,128)(2,1)S(1)}, bf16[1024,256]{1,0:T(8,128)(2,1)S(1)}, u32[]{:S(2)}, u32[]{:S(2)}) collective-permute-start(bf16[1024,256]{1,0:T(8,128)(2,1)S(1)} %get-tuple-element.127), channel_id=1, source_target_pairs={{8,0},{12,4},{16,24},{20,28},{9,1},{13,5},{17,25},{21,29},{10,2},{... | collective-permute-start | bytes 1572872 | tf_op jit(solution)/shard_map/ppermute | solution.py:185
  196.0 20.6 %collective-permute-start.28 = (bf16[1024,256]{1,0:T(8,128)(2,1)S(1)}, bf16[1024,256]{1,0:T(8,128)(2,1)S(1)}, u32[]{:S(2)}, u32[]{:S(2)}) collective-permute-start(bf16[1024,256]{1,0:T(8,128)(2,1)S(1)} %get-tuple-element.125), channel_id=1, source_target_pairs={{8,0},{12,4},{16,24},{20,28},{9,1},{13,5},{17,25},{21,29},{10,2},{... | collective-permute-start | bytes 1572872 | tf_op jit(solution)/shard_map/ppermute | solution.py:185
  216.6 13.3 %collective-permute-start.31 = (bf16[1024,256]{1,0:T(8,128)(2,1)S(1)}, bf16[1024,256]{1,0:T(8,128)(2,1)S(1)}, u32[]{:S(2)}, u32[]{:S(2)}) collective-permute-start(bf16[1024,256]{1,0:T(8,128)(2,1)S(1)} %broadcast_select_fusion.2), channel_id=1, source_target_pairs={{0,4},{4,0},{8,12},{12,8},{16,20},{20,16},{24,28},{28,24},{1,5},{5... | collective-permute-start | bytes 1572872 | tf_op jit(solution)/shard_map/ppermute | solution.py:189
  218.2 17.3 %collective-permute-start.32 = (bf16[1024,256]{1,0:T(8,128)(2,1)S(1)}, bf16[1024,256]{1,0:T(8,128)(2,1)S(1)}, u32[]{:S(2)}, u32[]{:S(2)}) collective-permute-start(bf16[1024,256]{1,0:T(8,128)(2,1)S(1)} %broadcast_select_fusion.1), channel_id=1, source_target_pairs={{0,4},{4,0},{8,12},{12,8},{16,20},{20,16},{24,28},{28,24},{1,5},{5... | collective-permute-start | bytes 1572872 | tf_op jit(solution)/shard_map/ppermute | solution.py:189
  220.5 10.3 %collective-permute-start.33 = (f32[16,16]{1,0:T(8,128)S(1)}, f32[16,16]{1,0:T(8,128)S(1)}, u32[]{:S(2)}, u32[]{:S(2)}) collective-permute-start(f32[16,16]{1,0:T(8,128)S(1)} %max.9), channel_id=1, source_target_pairs={{0,8},{4,12},{8,0},{12,4},{16,24},{20,28},{24,16},{28,20},{1,9},{5... | collective-permute-start | bytes 3080 | tf_op jit(solution)/shard_map/ppermute | solution.py:185
  230.8 6.4 %collective-permute-start.34 = (f32[16,16]{1,0:T(8,128)S(1)}, f32[16,16]{1,0:T(8,128)S(1)}, u32[]{:S(2)}, u32[]{:S(2)}) collective-permute-start(f32[16,16]{1,0:T(8,128)S(1)} %max.10), channel_id=1, source_target_pairs={{0,16},{4,20},{8,24},{12,28},{16,0},{20,4},{24,8},{28,12},{1,17},{... | collective-permute-start | bytes 3080 | tf_op jit(solution)/shard_map/ppermute | solution.py:185

commit v6 on v5

--- a/solution.py
+++ b/solution.py
@@ -55,9 +55,10 @@
     return call(kernel, shapes, [cot], "arrange")(cot)
 
 
-def multiply(acts_t, group, chunks, width, cost):
+def multiply(acts_t, group, first, chunks, width):
     rows, tokens = acts_t.shape
-    depth, columns = group[0].shape
+    depth = group[0].shape[0]
+    columns, left = chunks * width, first * width
     step = min(rows, 512)
     blocks = step // BLOCK
 
@@ -68,7 +69,8 @@
         def _():
             seat = lax.axis_index("tensor")
             for k, part in enumerate(parts):
-                cot[pl.ds(pl.multiple_of((seat ^ k) * depth, depth), depth), :] = part[...]
+                at = pl.multiple_of((seat ^ k) * depth, depth)
+                cot[pl.ds(at, depth), :] = part[:, left : left + columns]
 
         for j in range(chunks):
             here = slice(j * width, (j + 1) * width)
@@ -80,14 +82,14 @@
         kernel,
         grid=(rows // step,),
         in_specs=[pl.BlockSpec((step, tokens), lambda i: (i, 0))]
-        + [pl.BlockSpec((depth, columns), lambda i: (0, 0))] * len(group),
+        + [pl.BlockSpec(group[0].shape, lambda i: (0, 0))] * len(group),
         out_specs=[pl.BlockSpec((step, width), lambda i: (i, 0))] * chunks
         + [pl.BlockSpec((1, blocks, columns), lambda i: (i, 0, 0))],
         out_shape=[jax.ShapeDtypeStruct((rows, width), BF16)] * chunks
         + [jax.ShapeDtypeStruct((rows // step, blocks, columns), F32)],
         scratch_shapes=[pltpu.VMEM((tokens, columns), BF16)],
         compiler_params=pltpu.CompilerParams(vmem_limit_bytes=48 * 1024 * 1024),
-        cost_estimate=cost,
+        cost_estimate=FREE,
         name="partials",
     )(acts_t, *group)
     return out[:chunks], out[chunks]
@@ -170,6 +172,10 @@
     return lax.optimization_barrier((value, *earlier))[0] if earlier else value
 
 
+def tie(*values):
+    return lax.optimization_barrier(values)
+
+
 def body(acts, cotangent, master, first_moment, second_moment):
     n_dp = lax.axis_size("dp")
     n_tensor = lax.axis_size("tensor")
@@ -192,8 +198,7 @@
         return lax.ppermute(value, "tensor", [(i, i ^ flip) for i in range(n_tensor)])
 
     pieces = [
-        [(0, by) for by in others],
-        [(0, 0)] + [(1, by) for by in others],
+        [(0, by) for by in others] + [(0, 0)] + [(1, by) for by in others],
         [(i, by) for i in (2, 3) for by in others] + [(1, 0), (2, 0), (3, 0)],
     ]
     own = arrange(cotangent, pieces, width, n_x)
@@ -203,11 +208,12 @@
         value = after(own[piece], *earlier)
         across.append([value] + [seat_perm(value, k) for k in range(2, n_tensor, 2)])
 
-    def partials(piece, *earlier):
-        group = [part for value in across[piece] for part in (value, seat_perm(after(value, *earlier), 1))]
-        cost = FREE if piece else pl.CostEstimate(flops=10**10, bytes_accessed=acts.size, transcendentals=0)
-        chunks, top = multiply(after(acts_t, *earlier), group, len(pieces[piece]), width, cost)
-        partial.update(zip(pieces[piece], chunks))
+    def both_cores(piece, *earlier):
+        return [part for value in across[piece] for part in (value, seat_perm(after(value, *earlier), 1))]
+
+    def partials(group, which, first, *earlier):
+        chunks, top = multiply(after(acts_t, *earlier), group, first, len(which), width)
+        partial.update(zip(which, chunks))
         tops.append(top)
         return chunks[0]
 
@@ -221,15 +227,17 @@
     for piece in range(len(pieces)):
         fetch(piece)
     acts_t = after(acts, *own).T
-    token = partials(0, acts_t)
+    group = both_cores(0, acts_t)
+    sent = len(others)
+    token = partials(group, pieces[0][:sent], 0, acts_t)
     got0 = send_x(0)
-    token = partials(1, token)
+    token = partials(group, pieces[0][sent:], sent, token)
     got1 = send_x(1)
     far, middle = [None] * 2, [None] * 2
     for h in halves:
         token = add([partial[0, 0], *got0], token, rows=part[h])
         far[h] = z_perm(token, INWARDS)
-    token = partials(2, token)
+    token = partials(both_cores(1, token), pieces[1], 0, token)
     got2, got3 = send_x(2), send_x(3)
     token = add([partial[1, 0], *got1], token)
     inwards = z_perm(token, INWARDS)
@@ -260,36 +268,39 @@
 
     low, between = z < 2, (z == 1) | (z == 2)
     sources = [z, z ^ 1, jnp.where(low, 2, 1), jnp.where(low, 3, 0)]
+    terms[0], owned = tie(terms[0], owned)
+    new_master, new_first, new_second = update(terms, states, factor, [0, 1, 2], "states")
     over0 = [x_perm(owned, by) for by in others]
     pairs, mid = z_perm(owned, PAIRS), z_perm(owned, MIDDLE)
-    new_master, new_first, new_second = update(
-        [after(terms[0], owned), *terms[1:]], states, factor, [0, 1, 2], "states"
-    )
-    come = [pairs, mid, new_master, *over0]
-    over1 = [x_perm(after(pairs, *come), by) for by in others]
-    mid_far, outwards = z_perm(after(pairs, *come), MIDDLE), z_perm(after(mid, *come), OUTWARDS)
-    come = [mid_far, outwards]
-    near = lax.optimization_barrier(jnp.where(between, after(mid, *come, *over1), outwards))
-    over2 = [x_perm(near, by) for by in others]
-    cuts = [lax.slice_in_dim(mid_far, h * half, (h + 1) * half) for h in halves]
-    far = [z_perm(after(cuts[0], *come), OUTWARDS), z_perm(after(cuts[1], near), OUTWARDS)]
-
     def put(weights, value, slot, by, h=0):
         at = (sources[slot] * n_x + (x - by) % n_x) * width
         return lax.dynamic_update_slice(weights, value, (h * half, at))
 
-    weights = after(blank((rows, columns), BF16), near)
+    weights = blank((rows, columns), BF16)
+    for got, by in zip(over0, others):
+        weights = put(weights, got, 0, by)
+    weights = put(weights, pairs, 1, 0)
+    pairs, mid, weights = tie(pairs, mid, weights)
+    over1 = [x_perm(pairs, by) for by in others]
+    mid_far, outwards = z_perm(pairs, MIDDLE), z_perm(mid, OUTWARDS)
+    for got, by in zip(over1, others):
+        weights = put(weights, got, 1, by)
+    mid, mid_far, outwards, weights = tie(mid, mid_far, outwards, weights)
+    (near,) = tie(jnp.where(between, mid, outwards))
+    over2 = [x_perm(near, by) for by in others]
+    cuts = [lax.slice_in_dim(mid_far, h * half, (h + 1) * half) for h in halves]
+    far = [z_perm(cuts[0], OUTWARDS), None]
+    cuts[1], near = tie(cuts[1], near)
+    far[1] = z_perm(cuts[1], OUTWARDS)
+    weights, near = tie(weights, near)
     weights = put(weights, owned, 0, 0)
-    weights = put(weights, pairs, 1, 0)
     weights = put(weights, near, 2, 0)
-    for over, slot in ((over0, 0), (over1, 1)):
-        for got, by in zip(over, others):
-            weights = put(weights, got, slot, by)
     distant, over3 = [None] * 2, [None] * 2
     for h in halves:
-        value = after(lax.slice_in_dim(mid_far, h * half, (h + 1) * half), far[h], *distant[:h])
-        distant[h] = lax.optimization_barrier(jnp.where(between, value, far[h]))
+        (distant[h],) = tie(jnp.where(between, cuts[h], far[h]))
         over3[h] = [x_perm(distant[h], by) for by in others]
+        if h == 0:
+            far[1], distant[0] = tie(far[1], distant[0])
     for h in halves:
         weights = put(weights, distant[h], 3, 0, h)
     for got, by in zip(over2, others):

time: 239 us -> 244 us (1.021)
  waiting for transfers between devices: 115 us -> 107 us
  local copies, waits for them, and re-layouts: 21.8 us -> 28.9 us
  other arithmetic: 14.6 us -> 19 us
    ppermute x10, waiting for transfers between devices: 27.9 us -> 67.6 us  [x_perm(): return lax.ppermute(value, 'dp', pairs)]
    ppermute x16, waiting for transfers between devices: 67.7 us -> 32.9 us  [z_perm(): lax.ppermute(value, 'dp', [(a * n_x + i, b * n_x + i) for a, b in pairs f...]
    ppermute x9 -> x6, waiting for transfers between devices: 19.2 us -> 6.91 us  [seat_perm(): lax.ppermute(value, 'tensor', [(i, i ^ flip) for i in range(n_tensor)])]
    dynamic_update_slice x10, local copies, waits for them, and re-layouts: 10.8 us -> 16.9 us  [put(): return lax.dynamic_update_slice(weights, value, (h * half, at))]
    ppermute x10, starting transfers between devices: 7.71 us -> 12.4 us  [x_perm(): return lax.ppermute(value, 'dp', pairs)]
    select_n x3, other arithmetic: 1.45 us -> 5.78 us  [the longest x2 3.46 us: body(): distant[h], = tie(jnp.where(between, cuts[h], far[h]))]
    ppermute x16, starting transfers between devices: 34 us -> 30.6 us  [z_perm(): lax.ppermute(value, 'dp', [(a * n_x + i, b * n_x + i) for a, b in pairs f...]
    ppermute x9 -> x6, starting transfers between devices: 6.57 us -> 5 us  [seat_perm(): lax.ppermute(value, 'tensor', [(i, i ^ flip) for i in range(n_tensor)])]
  transfers between devices with their start and end apart: 35 -> 32, of which waited for: 20 -> 17; matrix products, arithmetic and copies ran while one was open for 14% -> 18% of each run, Pallas kernels for 11% -> 10%
where the time goes in v6:
time: 244 us; the launch traced here: 243 us
  waiting for transfers between devices  107 us (44%)
  starting transfers between devices  48 us (20%)
  Pallas kernels  38.4 us (16%)
  local copies, waits for them, and re-layouts  28.9 us (12%)
  other arithmetic  19 us (8%)
    ppermute x10, waiting for transfers between devices, x_perm(): return lax.ppermute(value, 'dp', pairs)  67.6 us
    ppermute x16, waiting for transfers between devices, z_perm(): lax.ppermute(value, 'dp', [(a * n_x + i, b * n_x + i) for a, b in pairs f...  32.9 us
    ppermute x16, starting transfers between devices, z_perm(): lax.ppermute(value, 'dp', [(a * n_x + i, b * n_x + i) for a, b in pairs f...  30.6 us
    pallas_call x3, Pallas kernels, multiply(): pl.pallas_call(kernel, grid=(rows // step,), in_specs=[pl.BlockSpec((step...  23.7 us
    dynamic_update_slice x10, local copies, waits for them, and re-layouts, put(): return lax.dynamic_update_slice(weights, value, (h * half, at))  16.9 us
    ppermute x10, starting transfers between devices, x_perm(): return lax.ppermute(value, 'dp', pairs)  12.4 us
    convert_element_type x8, other arithmetic, add(): return lax.optimization_barrier(total.astype(BF16))  12.1 us
    pallas_call x2, Pallas kernels, update(): pl.pallas_call(kernel, grid=(rows // step,), in_specs=specs + [whole] * 3...  11.9 us
  transfers between devices with their start and end apart: 32, of which 17 were waited for; matrix products, arithmetic and copies ran while one was open for 18% of the time, Pallas kernels for 10%

profile of v6, /device:TPU:0, one launch (start us, length us, event | category | flops | bytes accessed | tf_op | source)
XLA Modules:
  0.0 242.6 jit_solution(1562705521990526950)
XLA Ops:
  0.6 2.8 %arrange.1 = (bf16[384,768]{1,0:T(8,128)(2,1)}, bf16[384,1280]{1,0:T(8,128)(2,1)}) custom-call(bf16[384,2048]{1,0:T(8,128)(2,1)} %cot_ref.1), custom_call_target="tpu_custom_call" | custom-call | tf_op jit(solution)/shard_map/arrange/pallas_call | solution.py:55
  3.4 3.0 %collective-permute-start.1 = (bf16[384,768]{1,0:T(8,128)(2,1)}, bf16[384,768]{1,0:T(8,128)(2,1)S(1)}, u32[]{:S(2)}, u32[]{:S(2)}) collective-permute-start(bf16[384,768]{1,0:T(8,128)(2,1)} %get-tuple-element.74.refs_0_), channel_id=1, source_target_pairs={{0,2},{1,3},{2,0},{3,1},{4,6},{5,7},{6,4},{7,5},{8,10},{9,11},{10,... | collective-permute-start | bytes 1769480 | tf_op jit(solution)/shard_map/ppermute | solution.py:198
  6.4 8.7 %copy.12 = bf16[1536,2048]{0,1:T(8,128)(2,1)} copy(bf16[1536,2048]{1,0:T(8,128)(2,1)} %param.5) | data formatting | bytes 12582912 | tf_op jit(solution)/shard_map/optimization_barrier | solution.py:172
  15.1 4.9 %collective-permute-done.1.refs_2_ = bf16[384,768]{1,0:T(8,128)(2,1)S(1)} collective-permute-done((bf16[384,768]{1,0:T(8,128)(2,1)}, bf16[384,768]{1,0:T(8,128)(2,1)S(1)}, u32[]{:S(2)}, u32[]{:S(2)}) %collective-permute-start.1) | collective-permute-done | bytes 589856 | tf_op jit(solution)/shard_map/ppermute | solution.py:198
  20.0 2.0 collective-permute-done.2.refs_3_
  22.0 4.8 %partials.3 = (bf16[2048,256]{1,0:T(8,128)(2,1)S(1)}, f32[4,4,256]{2,1,0:T(4,128)S(1)}) custom-call(bf16[2048,1536]{1,0:T(8,128)(2,1)} %bitcast.17, bf16[384,768]{1,0:T(8,128)(2,1)S(1)} %copy-done.1, bf16[384,768]{1,0:T(8,128)(2,1)S(1)} %collective-permute-done.refs_1_, bf16[384,768]{1,0:T(8,128)(2,1)S(1)} %collective-permute-done.1.refs_2_, ...), custom_call_target="tpu_custom_call" | custom-call | tf_op jit(solution)/shard_map/partials/pallas_call | solution.py:81
  26.8 1.7 collective-permute-start.3
  28.5 1.5 collective-permute-start.5
  30.0 6.8 %partials.4 = (bf16[2048,256]{1,0:T(8,128)(2,1)S(1)}, bf16[2048,256]{1,0:T(8,128)(2,1)}, f32[4,4,512]{2,1,0:T(4,128)S(1)}) custom-call(bf16[2048,1536]{1,0:T(8,128)(2,1)} %bitcast.18, bf16[384,768]{1,0:T(8,128)(2,1)S(1)} %copy-done.1, bf16[384,768]{1,0:T(8,128)(2,1)S(1)} %collective-permute-done.refs_1_, ...), custom_call_target="tpu_custom_call" | custom-call | tf_op jit(solution)/shard_map/partials/pallas_call | solution.py:81
  37.4 15.5 %collective-permute-done.3 = bf16[2048,256]{1,0:T(8,128)(2,1)S(1)} collective-permute-done((bf16[2048,256]{1,0:T(8,128)(2,1)S(1)}, bf16[2048,256]{1,0:T(8,128)(2,1)S(1)}, u32[]{:S(2)}, u32[]{:S(2)}) %collective-permute-start.3) | collective-permute-done | bytes 1048608 | tf_op jit(solution)/shard_map/ppermute | solution.py:195
  52.8 1.1 add_convert_fusion.7
  53.9 0.9 add_convert_fusion.6
  55.5 3.8 %collective-permute-start.8 = (bf16[1024,256]{1,0:T(8,128)(2,1)}, bf16[1024,256]{1,0:T(8,128)(2,1)S(1)}, u32[]{:S(2)}, u32[]{:S(2)}) collective-permute-start(bf16[1024,256]{1,0:T(8,128)(2,1)} %add_convert_fusion.7), channel_id=1, source_target_pairs={{0,8},{4,12},{24,16},{28,20},{1,9},{5,13},{25,17},{29,21},{2,10},{... | collective-permute-start | bytes 1572872 | tf_op jit(solution)/shard_map/ppermute | solution.py:191
  59.3 1.3 collective-permute-start.7
  60.6 12.1 %partials.5 = (bf16[2048,256]{1,0:T(8,128)(2,1)}, bf16[2048,256]{1,0:T(8,128)(2,1)S(1)}, bf16[2048,256]{1,0:T(8,128)(2,1)}, bf16[2048,256]{1,0:T(8,128)(2,1)}, b...) custom-call(bf16[2048,1536]{1,0:T(8,128)(2,1)} %bitcast.19, bf16[384,1280]{1,0:T(8,128)(2,1)S(1)} %copy-done.6, ...), custom_call_target="tpu_custom_call" | custom-call | tf_op jit(solution)/shard_map/partials/pallas_call | solution.py:81
  72.7 1.6 collective-permute-start.13
  74.6 2.8 %add_convert_fusion.1 = bf16[2048,256]{1,0:T(8,128)(2,1)} fusion(bf16[2048,256]{1,0:T(8,128)(2,1)} %collective-permute-done.9, bf16[2048,256]{1,0:T(8,128)(2,1)} %get-tuple-element.110), kind=kLoop, calls=%fused_computation.1 | loop fusion | flops 2097152 | bytes 3145728 | tf_op jit(solution)/shard_map/convert_element_type | solution.py:105
  77.4 5.0 %collective-permute-start.12 = (bf16[2048,256]{1,0:T(8,128)(2,1)}, bf16[2048,256]{1,0:T(8,128)(2,1)}, u32[]{:S(2)}, u32[]{:S(2)}) collective-permute-start(bf16[2048,256]{1,0:T(8,128)(2,1)} %add_convert_fusion.1), channel_id=1, source_target_pairs={{0,8},{4,12},{24,16},{28,20},{1,9},{5,13},{25,17},{29,21},{2,10},{... | collective-permute-start | bytes 3145736 | tf_op jit(solution)/shard_map/ppermute | solution.py:191
  82.5 1.0 add_convert_fusion.5
  84.2 1.0 add_convert_fusion.4
  85.2 1.4 collective-permute-start.17
  87.0 1.6 collective-permute-start.11
  88.8 10.3 %collective-permute-done.13 = bf16[2048,256]{1,0:T(8,128)(2,1)} collective-permute-done((bf16[2048,256]{1,0:T(8,128)(2,1)}, bf16[2048,256]{1,0:T(8,128)(2,1)}, u32[]{:S(2)}, u32[]{:S(2)}) %collective-permute-start.13) | collective-permute-done | bytes 1048608 | tf_op jit(solution)/shard_map/ppermute | solution.py:195
  99.1 1.4 add_convert_fusion.3
  100.7 4.8 %collective-permute-done.12 = bf16[2048,256]{1,0:T(8,128)(2,1)} collective-permute-done((bf16[2048,256]{1,0:T(8,128)(2,1)}, bf16[2048,256]{1,0:T(8,128)(2,1)}, u32[]{:S(2)}, u32[]{:S(2)}) %collective-permute-start.12) | collective-permute-done | bytes 1048608 | tf_op jit(solution)/shard_map/ppermute | solution.py:191
  105.5 2.2 add_convert_fusion
  108.5 7.3 %collective-permute-done.16.refs_3_ = bf16[1024,256]{1,0:T(8,128)(2,1)S(1)} collective-permute-done((bf16[1024,256]{1,0:T(8,128)(2,1)S(1)}, bf16[1024,256]{1,0:T(8,128)(2,1)S(1)}, u32[]{:S(2)}, u32[]{:S(2)}) %collective-permute-start.16) | collective-permute-done | bytes 524320 | tf_op jit(solution)/shard_map/ppermute | solution.py:191
  115.8 1.7 add_convert_fusion.2
  117.5 2.5 %collective-permute-start.18 = (bf16[1024,256]{1,0:T(8,128)(2,1)S(1)}, bf16[1024,256]{1,0:T(8,128)(2,1)S(1)}, u32[]{:S(2)}, u32[]{:S(2)}) collective-permute-start(bf16[1024,256]{1,0:T(8,128)(2,1)S(1)} %add_convert_fusion.2), channel_id=1, source_target_pairs={{0,8},{4,12},{8,0},{12,4},{16,24},{20,28},{24,16},{28,20},{1,9},{5... | collective-permute-start | bytes 1572872 | tf_op jit(solution)/shard_map/ppermute | solution.py:191
  120.1 1.5 collective-permute-start.10
  121.6 2.2 collective-permute-done.10
  123.7 7.7 %collective-permute-done.18.refs_4_ = bf16[1024,256]{1,0:T(8,128)(2,1)S(1)} collective-permute-done((bf16[1024,256]{1,0:T(8,128)(2,1)S(1)}, bf16[1024,256]{1,0:T(8,128)(2,1)S(1)}, u32[]{:S(2)}, u32[]{:S(2)}) %collective-permute-start.18) | collective-permute-done | bytes 524320 | tf_op jit(solution)/shard_map/ppermute | solution.py:191
  131.4 5.5 %weights.1 = bf16[2048,256]{1,0:T(8,128)(2,1)} custom-call(bf16[2048,256]{1,0:T(8,128)(2,1)S(1)} %copy-done, bf16[2048,256]{1,0:T(8,128)(2,1)S(1)} %collective-permute-done.11.refs_1_, bf16[2048,256]{1,0:T(8,128)(2,1)S(1)} %collective-permute-done.15.refs_2_, bf16[1024,256]{1,0:T(8,128)(2,1)S(1)} %collective-permute-done.16.refs_3_, ...), custom_call_target="tpu_custom_call" | custom-call | tf_op jit(solution)/shard_map/weights/pallas_call | solution.py:149
  136.9 1.5 collective-permute-start.21
  138.4 4.0 %collective-permute-start.19 = (bf16[2048,256]{1,0:T(8,128)(2,1)}, bf16[2048,256]{1,0:T(8,128)(2,1)}, u32[]{:S(2)}, u32[]{:S(2)}) collective-permute-start(bf16[2048,256]{1,0:T(8,128)(2,1)} %weights.1), channel_id=1, source_target_pairs={{0,8},{4,12},{8,0},{12,4},{16,24},{20,28},{24,16},{28,20},{1,9},{5... | collective-permute-start | bytes 3145736 | tf_op jit(solution)/shard_map/ppermute | solution.py:191
  142.4 1.6 collective-permute-start.20
  144.0 16.8 %collective-permute-done.21 = bf16[2048,256]{1,0:T(8,128)(2,1)} collective-permute-done((bf16[2048,256]{1,0:T(8,128)(2,1)}, bf16[2048,256]{1,0:T(8,128)(2,1)}, u32[]{:S(2)}, u32[]{:S(2)}) %collective-permute-start.21) | collective-permute-done | bytes 1048608 | tf_op jit(solution)/shard_map/ppermute | solution.py:195
  160.9 2.3 constant_dynamic-update-slice_fusion.7
  163.2 2.3 constant_dynamic-update-slice_fusion.6
  165.5 1.4 collective-permute-start.24
  166.9 1.7 collective-permute-start.22
  168.5 1.3 collective-permute-start.23
  169.8 18.6 %collective-permute-done.24 = bf16[2048,256]{1,0:T(8,128)(2,1)} collective-permute-done((bf16[2048,256]{1,0:T(8,128)(2,1)}, bf16[2048,256]{1,0:T(8,128)(2,1)}, u32[]{:S(2)}, u32[]{:S(2)}) %collective-permute-start.24) | collective-permute-done | bytes 1048608 | tf_op jit(solution)/shard_map/ppermute | solution.py:195
  188.4 2.3 constant_dynamic-update-slice_fusion.5
  190.7 3.4 %collective-permute-done.23 = bf16[2048,256]{1,0:T(8,128)(2,1)} collective-permute-done((bf16[2048,256]{1,0:T(8,128)(2,1)}, bf16[2048,256]{1,0:T(8,128)(2,1)}, u32[]{:S(2)}, u32[]{:S(2)}) %collective-permute-start.23) | collective-permute-done | bytes 1048608 | tf_op jit(solution)/shard_map/ppermute | solution.py:191
  194.1 1.1 slice.55
  195.2 1.3 collective-permute-start.26
  196.5 2.3 broadcast_select_fusion
  199.3 6.9 %collective-permute-done.26 = bf16[1024,256]{1,0:T(8,128)(2,1)S(1)} collective-permute-done((bf16[1024,256]{1,0:T(8,128)(2,1)S(1)}, bf16[1024,256]{1,0:T(8,128)(2,1)S(1)}, u32[]{:S(2)}, u32[]{:S(2)}) %collective-permute-start.26) | collective-permute-done | bytes 524320 | tf_op jit(solution)/shard_map/ppermute | solution.py:191
  206.2 2.4 broadcast_select_fusion.2
  208.6 1.3 collective-permute-start.25
  209.9 1.0 copy-done.3
  211.0 1.0 copy-done.5
  212.0 6.4 %states.1 = (f32[2048,256]{1,0:T(8,128)}, f32[2048,256]{1,0:T(8,128)}, f32[2048,256]{1,0:T(8,128)}) custom-call(bf16[2048,256]{1,0:T(8,128)(2,1)S(1)} %copy-done, bf16[2048,256]{1,0:T(8,128)(2,1)S(1)} %collective-permute-done.11.refs_1_, bf16[2048,256]{1,0:T(8,128)(2,1)S(1)} %collective-permute-done.15.refs_2_, bf16[1024,256]{1,0:T(8,128)(2,1)S(1)} %copy-done.3, ...), custom_call_target="tpu_custom_call" | custom-call | tf_op jit(solution)/shard_map/states/pallas_call | solution.py:149
  219.0 2.3 constant_dynamic-update-slice_fusion.4
  221.3 2.3 constant_dynamic-update-slice_fusion.3
  223.6 1.1 broadcast_select_fusion.1
  224.7 1.6 collective-permute-start.29
  226.2 3.4 %collective-permute-start.30 = (f32[16,16]{1,0:T(8,128)S(1)}, f32[16,16]{1,0:T(8,128)S(1)}, u32[]{:S(2)}, u32[]{:S(2)}) collective-permute-start(f32[16,16]{1,0:T(8,128)S(1)} %max.9), channel_id=1, source_target_pairs={{0,8},{4,12},{8,0},{12,4},{16,24},{20,28},{24,16},{28,20},{1,9},{5... | collective-permute-start | bytes 3080 | tf_op jit(solution)/shard_map/ppermute | solution.py:191
  231.3 2.3 constant_dynamic-update-slice_fusion.1
  234.6 0.8 constant_dynamic-update-slice_fusion
  235.4 2.7 %collective-permute-done.31 = f32[16,16]{1,0:T(8,128)S(1)} collective-permute-done((f32[16,16]{1,0:T(8,128)S(1)}, f32[16,16]{1,0:T(8,128)S(1)}, u32[]{:S(2)}, u32[]{:S(2)}) %collective-permute-start.31) | collective-permute-done | bytes 1056 | tf_op jit(solution)/shard_map/ppermute | solution.py:191
  238.7 3.1 %collective-permute-done.29 = bf16[1024,256]{1,0:T(8,128)(2,1)S(1)} collective-permute-done((bf16[1024,256]{1,0:T(8,128)(2,1)S(1)}, bf16[1024,256]{1,0:T(8,128)(2,1)S(1)}, u32[]{:S(2)}, u32[]{:S(2)}) %collective-permute-start.29) | collective-permute-done | bytes 524320 | tf_op jit(solution)/shard_map/ppermute | solution.py:195
  241.8 0.8 constant_dynamic-update-slice_fusion.8
  (65 shorter events, 8.3 us)
Async XLA Ops:
  3.4 11.7 %copy-start.1 = (bf16[384,768]{1,0:T(8,128)(2,1)S(1)}, bf16[384,768]{1,0:T(8,128)(2,1)}, u32[]{:S(2)}) copy-start(bf16[384,768]{1,0:T(8,128)(2,1)} %get-tuple-element.74.refs_0_) | copy-start | bytes 1769476
  3.4 16.6 %collective-permute-start.1 = (bf16[384,768]{1,0:T(8,128)(2,1)}, bf16[384,768]{1,0:T(8,128)(2,1)S(1)}, u32[]{:S(2)}, u32[]{:S(2)}) collective-permute-start(bf16[384,768]{1,0:T(8,128)(2,1)} %get-tuple-element.74.refs_0_), channel_id=1, source_target_pairs={{0,2},{1,3},{2,0},{3,1},{4,6},{5,7},{6,4},{7,5},{8,10},{9,11},{10,... | collective-permute-start | bytes 1769480 | tf_op jit(solution)/shard_map/ppermute | solution.py:198
  6.4 22.1 %copy-start.6 = (bf16[384,1280]{1,0:T(8,128)(2,1)S(1)}, bf16[384,1280]{1,0:T(8,128)(2,1)}, u32[]{:S(2)}) copy-start(bf16[384,1280]{1,0:T(8,128)(2,1)} %get-tuple-element.84.refs_0_) | copy-start | bytes 2949124
  15.1 4.9 %collective-permute-start = (bf16[384,768]{1,0:T(8,128)(2,1)S(1)}, bf16[384,768]{1,0:T(8,128)(2,1)S(1)}, u32[]{:S(2)}, u32[]{:S(2)}) collective-permute-start(bf16[384,768]{1,0:T(8,128)(2,1)S(1)} %copy-done.1), channel_id=1, source_target_pairs={{0,1},{1,0},{2,3},{3,2},{4,5},{5,4},{6,7},{7,6},{8,9},{9,8},{10,11... | collective-permute-start | bytes 1769480 | tf_op jit(solution)/shard_map/ppermute | solution.py:198
  20.0 2.0 collective-permute-start.2
  26.8 26.1 %collective-permute-start.3 = (bf16[2048,256]{1,0:T(8,128)(2,1)S(1)}, bf16[2048,256]{1,0:T(8,128)(2,1)S(1)}, u32[]{:S(2)}, u32[]{:S(2)}) collective-permute-start(bf16[2048,256]{1,0:T(8,128)(2,1)S(1)} %get-tuple-element.76), channel_id=1, source_target_pairs={{0,4},{4,0},{8,12},{12,8},{16,20},{20,16},{24,28},{28,24},{1,5},{5... | collective-permute-start | bytes 3145736 | tf_op jit(solution)/shard_map/ppermute | solution.py:195
  28.5 26.3 %collective-permute-start.5 = (bf16[384,1280]{1,0:T(8,128)(2,1)S(1)}, bf16[384,1280]{1,0:T(8,128)(2,1)}, u32[]{:S(2)}, u32[]{:S(2)}) collective-permute-start(bf16[384,1280]{1,0:T(8,128)(2,1)S(1)} %copy-done.6), channel_id=1, source_target_pairs={{0,2},{1,3},{2,0},{3,1},{4,6},{5,7},{6,4},{7,5},{8,10},{9,11},{10,... | collective-permute-start | bytes 2949128 | tf_op jit(solution)/shard_map/ppermute | solution.py:198
  36.8 37.8 %collective-permute-start.9 = (bf16[2048,256]{1,0:T(8,128)(2,1)}, bf16[2048,256]{1,0:T(8,128)(2,1)}, u32[]{:S(2)}, u32[]{:S(2)}) collective-permute-start(bf16[2048,256]{1,0:T(8,128)(2,1)} %get-tuple-element.89), channel_id=1, source_target_pairs={{0,4},{4,0},{8,12},{12,8},{16,20},{20,16},{24,28},{28,24},{1,5},{5... | collective-permute-start | bytes 3145736 | tf_op jit(solution)/shard_map/ppermute | solution.py:195
  52.8 2.0 copy-start.8
  54.8 5.8 %collective-permute-start.6 = (bf16[384,1280]{1,0:T(8,128)(2,1)}, bf16[384,1280]{1,0:T(8,128)(2,1)S(1)}, u32[]{:S(2)}, u32[]{:S(2)}) collective-permute-start(bf16[384,1280]{1,0:T(8,128)(2,1)} %collective-permute-done.5.refs_2_), channel_id=1, source_target_pairs={{0,1},{1,0},{2,3},{3,2},{4,5},{5,4},{6,7},{7,6},{8,9},{9,8},{10,11... | collective-permute-start | bytes 2949128 | tf_op jit(solution)/shard_map/ppermute | solution.py:198
  54.8 5.8 %collective-permute-start.4 = (bf16[384,1280]{1,0:T(8,128)(2,1)S(1)}, bf16[384,1280]{1,0:T(8,128)(2,1)}, u32[]{:S(2)}, u32[]{:S(2)}) collective-permute-start(bf16[384,1280]{1,0:T(8,128)(2,1)S(1)} %copy-done.6), channel_id=1, source_target_pairs={{0,1},{1,0},{2,3},{3,2},{4,5},{5,4},{6,7},{7,6},{8,9},{9,8},{10,11... | collective-permute-start | bytes 2949128 | tf_op jit(solution)/shard_map/ppermute | solution.py:198
  55.4 27.0 %copy-start.9 = (bf16[2048,256]{1,0:T(8,128)(2,1)S(1)}, bf16[2048,256]{1,0:T(8,128)(2,1)}, u32[]{:S(2)}) copy-start(bf16[2048,256]{1,0:T(8,128)(2,1)} %copy-done.8) | copy-start | bytes 3145732
  55.5 27.0 %collective-permute-start.8 = (bf16[1024,256]{1,0:T(8,128)(2,1)}, bf16[1024,256]{1,0:T(8,128)(2,1)S(1)}, u32[]{:S(2)}, u32[]{:S(2)}) collective-permute-start(bf16[1024,256]{1,0:T(8,128)(2,1)} %add_convert_fusion.7), channel_id=1, source_target_pairs={{0,8},{4,12},{24,16},{28,20},{1,9},{5,13},{25,17},{29,21},{2,10},{... | collective-permute-start | bytes 1572872 | tf_op jit(solution)/shard_map/ppermute | solution.py:191
  59.3 24.9 %collective-permute-start.7 = (bf16[1024,256]{1,0:T(8,128)(2,1)}, bf16[1024,256]{1,0:T(8,128)(2,1)S(1)}, u32[]{:S(2)}, u32[]{:S(2)}) collective-permute-start(bf16[1024,256]{1,0:T(8,128)(2,1)} %add_convert_fusion.6), channel_id=1, source_target_pairs={{0,8},{4,12},{24,16},{28,20},{1,9},{5,13},{25,17},{29,21},{2,10},{... | collective-permute-start | bytes 1572872 | tf_op jit(solution)/shard_map/ppermute | solution.py:191
  72.7 12.5 %copy-start.7 = (bf16[2048,256]{1,0:T(8,128)(2,1)}, bf16[2048,256]{1,0:T(8,128)(2,1)S(1)}, u32[]{:S(2)}) copy-start(bf16[2048,256]{1,0:T(8,128)(2,1)S(1)} %get-tuple-element.105) | copy-start | bytes 3145732
  72.7 58.7 %copy-start = (bf16[2048,256]{1,0:T(8,128)(2,1)S(1)}, bf16[2048,256]{1,0:T(8,128)(2,1)}, u32[]{:S(2)}) copy-start(bf16[2048,256]{1,0:T(8,128)(2,1)} %get-tuple-element.116.refs_0_) | copy-start | bytes 3145732
  72.7 26.4 %collective-permute-start.13 = (bf16[2048,256]{1,0:T(8,128)(2,1)}, bf16[2048,256]{1,0:T(8,128)(2,1)}, u32[]{:S(2)}, u32[]{:S(2)}) collective-permute-start(bf16[2048,256]{1,0:T(8,128)(2,1)} %get-tuple-element.90), channel_id=1, source_target_pairs={{0,4},{4,0},{8,12},{12,8},{16,20},{20,16},{24,28},{28,24},{1,5},{5... | collective-permute-start | bytes 3145736 | tf_op jit(solution)/shard_map/ppermute | solution.py:195
  77.4 28.1 %collective-permute-start.12 = (bf16[2048,256]{1,0:T(8,128)(2,1)}, bf16[2048,256]{1,0:T(8,128)(2,1)}, u32[]{:S(2)}, u32[]{:S(2)}) collective-permute-start(bf16[2048,256]{1,0:T(8,128)(2,1)} %add_convert_fusion.1), channel_id=1, source_target_pairs={{0,8},{4,12},{24,16},{28,20},{1,9},{5,13},{25,17},{29,21},{2,10},{... | collective-permute-start | bytes 3145736 | tf_op jit(solution)/shard_map/ppermute | solution.py:191
  83.4 5.4 %collective-permute-start.14 = (bf16[1024,256]{1,0:T(8,128)(2,1)}, bf16[1024,256]{1,0:T(8,128)(2,1)S(1)}, u32[]{:S(2)}, u32[]{:S(2)}) collective-permute-start(bf16[1024,256]{1,0:T(8,128)(2,1)} %add_convert_fusion.5), channel_id=1, source_target_pairs={{8,16},{12,20},{16,8},{20,12},{9,17},{13,21},{17,9},{21,13},{10,18... | collective-permute-start | bytes 1572872 | tf_op jit(solution)/shard_map/ppermute | solution.py:191
  85.2 23.3 %collective-permute-start.17 = (bf16[1024,256]{1,0:T(8,128)(2,1)}, bf16[1024,256]{1,0:T(8,128)(2,1)}, u32[]{:S(2)}, u32[]{:S(2)}) collective-permute-start(bf16[1024,256]{1,0:T(8,128)(2,1)} %add_convert_fusion.4), channel_id=1, source_target_pairs={{8,16},{12,20},{16,8},{20,12},{9,17},{13,21},{17,9},{21,13},{10,18... | collective-permute-start | bytes 1572872 | tf_op jit(solution)/shard_map/ppermute | solution.py:191
  87.0 36.7 %collective-permute-start.11 = (bf16[2048,256]{1,0:T(8,128)(2,1)}, bf16[2048,256]{1,0:T(8,128)(2,1)S(1)}, u32[]{:S(2)}, u32[]{:S(2)}) collective-permute-start(bf16[2048,256]{1,0:T(8,128)(2,1)} %copy-done.7), channel_id=1, source_target_pairs={{0,4},{4,0},{8,12},{12,8},{16,20},{20,16},{24,28},{28,24},{1,5},{5... | collective-permute-start | bytes 3145736 | tf_op jit(solution)/shard_map/ppermute | solution.py:195
  100.5 15.2 %collective-permute-start.16 = (bf16[1024,256]{1,0:T(8,128)(2,1)S(1)}, bf16[1024,256]{1,0:T(8,128)(2,1)S(1)}, u32[]{:S(2)}, u32[]{:S(2)}) collective-permute-start(bf16[1024,256]{1,0:T(8,128)(2,1)S(1)} %add_convert_fusion.3), channel_id=1, source_target_pairs={{0,8},{4,12},{8,0},{12,4},{16,24},{20,28},{24,16},{28,20},{1,9},{5... | collective-permute-start | bytes 1572872 | tf_op jit(solution)/shard_map/ppermute | solution.py:191
  107.8 23.6 %collective-permute-start.15 = (bf16[2048,256]{1,0:T(8,128)(2,1)S(1)}, bf16[2048,256]{1,0:T(8,128)(2,1)S(1)}, u32[]{:S(2)}, u32[]{:S(2)}) collective-permute-start(bf16[2048,256]{1,0:T(8,128)(2,1)S(1)} %add_convert_fusion), channel_id=1, source_target_pairs={{8,16},{12,20},{16,8},{20,12},{9,17},{13,21},{17,9},{21,13},{10,18... | collective-permute-start | bytes 3145736 | tf_op jit(solution)/shard_map/ppermute | solution.py:191
  115.8 15.6 %copy-start.2 = (bf16[1024,256]{1,0:T(8,128)(2,1)}, bf16[1024,256]{1,0:T(8,128)(2,1)S(1)}, u32[]{:S(2)}) copy-start(bf16[1024,256]{1,0:T(8,128)(2,1)S(1)} %collective-permute-done.16.refs_3_) | copy-start | bytes 1572868
  117.5 13.9 %collective-permute-start.18 = (bf16[1024,256]{1,0:T(8,128)(2,1)S(1)}, bf16[1024,256]{1,0:T(8,128)(2,1)S(1)}, u32[]{:S(2)}, u32[]{:S(2)}) collective-permute-start(bf16[1024,256]{1,0:T(8,128)(2,1)S(1)} %add_convert_fusion.2), channel_id=1, source_target_pairs={{0,8},{4,12},{8,0},{12,4},{16,24},{20,28},{24,16},{28,20},{1,9},{5... | collective-permute-start | bytes 1572872 | tf_op jit(solution)/shard_map/ppermute | solution.py:191
  120.1 3.7 %collective-permute-start.10 = (f32[16,16]{1,0:T(8,128)S(1)}, f32[16,16]{1,0:T(8,128)S(1)}, u32[]{:S(2)}, u32[]{:S(2)}) collective-permute-start(f32[16,16]{1,0:T(8,128)S(1)} %select_reduce_fusion), channel_id=1, source_target_pairs={{0,4},{4,0},{8,12},{12,8},{16,20},{20,16},{24,28},{28,24},{1,5},{5... | collective-permute-start | bytes 3080 | tf_op jit(solution)/shard_map/ppermute | solution.py:195
  131.4 5.5 %copy-start.4 = (bf16[1024,256]{1,0:T(8,128)(2,1)}, bf16[1024,256]{1,0:T(8,128)(2,1)S(1)}, u32[]{:S(2)}) copy-start(bf16[1024,256]{1,0:T(8,128)(2,1)S(1)} %collective-permute-done.18.refs_4_) | copy-start | bytes 1572868
  136.9 24.0 %collective-permute-start.21 = (bf16[2048,256]{1,0:T(8,128)(2,1)}, bf16[2048,256]{1,0:T(8,128)(2,1)}, u32[]{:S(2)}, u32[]{:S(2)}) collective-permute-start(bf16[2048,256]{1,0:T(8,128)(2,1)} %weights.1), channel_id=1, source_target_pairs={{0,4},{4,0},{8,12},{12,8},{16,20},{20,16},{24,28},{28,24},{1,5},{5... | collective-permute-start | bytes 3145736 | tf_op jit(solution)/shard_map/ppermute | solution.py:195
  138.4 24.8 %collective-permute-start.19 = (bf16[2048,256]{1,0:T(8,128)(2,1)}, bf16[2048,256]{1,0:T(8,128)(2,1)}, u32[]{:S(2)}, u32[]{:S(2)}) collective-permute-start(bf16[2048,256]{1,0:T(8,128)(2,1)} %weights.1), channel_id=1, source_target_pairs={{0,8},{4,12},{8,0},{12,4},{16,24},{20,28},{24,16},{28,20},{1,9},{5... | collective-permute-start | bytes 3145736 | tf_op jit(solution)/shard_map/ppermute | solution.py:191
  142.4 23.1 %collective-permute-start.20 = (bf16[2048,256]{1,0:T(8,128)(2,1)}, bf16[2048,256]{1,0:T(8,128)(2,1)}, u32[]{:S(2)}, u32[]{:S(2)}) collective-permute-start(bf16[2048,256]{1,0:T(8,128)(2,1)} %weights.1), channel_id=1, source_target_pairs={{8,16},{12,20},{16,8},{20,12},{9,17},{13,21},{17,9},{21,13},{10,18... | collective-permute-start | bytes 3145736 | tf_op jit(solution)/shard_map/ppermute | solution.py:191
  165.5 23.0 %collective-permute-start.24 = (bf16[2048,256]{1,0:T(8,128)(2,1)}, bf16[2048,256]{1,0:T(8,128)(2,1)}, u32[]{:S(2)}, u32[]{:S(2)}) collective-permute-start(bf16[2048,256]{1,0:T(8,128)(2,1)} %collective-permute-done.19), channel_id=1, source_target_pairs={{0,4},{4,0},{8,12},{12,8},{16,20},{20,16},{24,28},{28,24},{1,5},{5... | collective-permute-start | bytes 3145736 | tf_op jit(solution)/shard_map/ppermute | solution.py:195
  166.9 23.8 %collective-permute-start.22 = (bf16[2048,256]{1,0:T(8,128)(2,1)}, bf16[2048,256]{1,0:T(8,128)(2,1)}, u32[]{:S(2)}, u32[]{:S(2)}) collective-permute-start(bf16[2048,256]{1,0:T(8,128)(2,1)} %collective-permute-done.19), channel_id=1, source_target_pairs={{8,16},{12,20},{16,8},{20,12},{9,17},{13,21},{17,9},{21,13},{10,18... | collective-permute-start | bytes 3145736 | tf_op jit(solution)/shard_map/ppermute | solution.py:191
  168.5 25.5 %collective-permute-start.23 = (bf16[2048,256]{1,0:T(8,128)(2,1)}, bf16[2048,256]{1,0:T(8,128)(2,1)}, u32[]{:S(2)}, u32[]{:S(2)}) collective-permute-start(bf16[2048,256]{1,0:T(8,128)(2,1)} %collective-permute-done.20), channel_id=1, source_target_pairs={{8,0},{12,4},{16,24},{20,28},{9,1},{13,5},{17,25},{21,29},{10,2},{... | collective-permute-start | bytes 3145736 | tf_op jit(solution)/shard_map/ppermute | solution.py:191
  195.2 11.1 %collective-permute-start.26 = (bf16[1024,256]{1,0:T(8,128)(2,1)S(1)}, bf16[1024,256]{1,0:T(8,128)(2,1)S(1)}, u32[]{:S(2)}, u32[]{:S(2)}) collective-permute-start(bf16[1024,256]{1,0:T(8,128)(2,1)S(1)} %slice.55), channel_id=1, source_target_pairs={{8,0},{12,4},{16,24},{20,28},{9,1},{13,5},{17,25},{21,29},{10,2},{... | collective-permute-start | bytes 1572872 | tf_op jit(solution)/shard_map/ppermute | solution.py:191
  198.8 27.5 %collective-permute-start.27 = (bf16[2048,256]{1,0:T(8,128)(2,1)}, bf16[2048,256]{1,0:T(8,128)(2,1)}, u32[]{:S(2)}, u32[]{:S(2)}) collective-permute-start(bf16[2048,256]{1,0:T(8,128)(2,1)} %broadcast_select_fusion), channel_id=1, source_target_pairs={{0,4},{4,0},{8,12},{12,8},{16,20},{20,16},{24,28},{28,24},{1,5},{5... | collective-permute-start | bytes 3145736 | tf_op jit(solution)/shard_map/ppermute | solution.py:195
  208.6 15.0 %collective-permute-start.25 = (bf16[1024,256]{1,0:T(8,128)(2,1)}, bf16[1024,256]{1,0:T(8,128)(2,1)}, u32[]{:S(2)}, u32[]{:S(2)}) collective-permute-start(bf16[1024,256]{1,0:T(8,128)(2,1)} %get-tuple-element.131), channel_id=1, source_target_pairs={{8,0},{12,4},{16,24},{20,28},{9,1},{13,5},{17,25},{21,29},{10,2},{... | collective-permute-start | bytes 1572872 | tf_op jit(solution)/shard_map/ppermute | solution.py:191
  209.9 1.0 copy-start.3
  211.0 1.0 copy-start.5
  212.0 6.4 %copy-start.10 = (bf16[1024,256]{1,0:T(8,128)(2,1)S(1)}, bf16[1024,256]{1,0:T(8,128)(2,1)}, u32[]{:S(2)}) copy-start(bf16[1024,256]{1,0:T(8,128)(2,1)} %get-tuple-element.132) | copy-start | bytes 1572868
  218.4 16.2 %collective-permute-start.28 = (bf16[1024,256]{1,0:T(8,128)(2,1)S(1)}, bf16[1024,256]{1,0:T(8,128)(2,1)S(1)}, u32[]{:S(2)}, u32[]{:S(2)}) collective-permute-start(bf16[1024,256]{1,0:T(8,128)(2,1)S(1)} %copy-done.10), channel_id=1, source_target_pairs={{0,4},{4,0},{8,12},{12,8},{16,20},{20,16},{24,28},{28,24},{1,5},{5... | collective-permute-start | bytes 1572872 | tf_op jit(solution)/shard_map/ppermute | solution.py:195
  224.7 17.1 %collective-permute-start.29 = (bf16[1024,256]{1,0:T(8,128)(2,1)S(1)}, bf16[1024,256]{1,0:T(8,128)(2,1)S(1)}, u32[]{:S(2)}, u32[]{:S(2)}) collective-permute-start(bf16[1024,256]{1,0:T(8,128)(2,1)S(1)} %broadcast_select_fusion.1), channel_id=1, source_target_pairs={{0,4},{4,0},{8,12},{12,8},{16,20},{20,16},{24,28},{28,24},{1,5},{5... | collective-permute-start | bytes 1572872 | tf_op jit(solution)/shard_map/ppermute | solution.py:195
  226.2 7.3 %collective-permute-start.30 = (f32[16,16]{1,0:T(8,128)S(1)}, f32[16,16]{1,0:T(8,128)S(1)}, u32[]{:S(2)}, u32[]{:S(2)}) collective-permute-start(f32[16,16]{1,0:T(8,128)S(1)} %max.9), channel_id=1, source_target_pairs={{0,8},{4,12},{8,0},{12,4},{16,24},{20,28},{24,16},{28,20},{1,9},{5... | collective-permute-start | bytes 3080 | tf_op jit(solution)/shard_map/ppermute | solution.py:191
  233.6 4.6 %collective-permute-start.31 = (f32[16,16]{1,0:T(8,128)S(1)}, f32[16,16]{1,0:T(8,128)S(1)}, u32[]{:S(2)}, u32[]{:S(2)}) collective-permute-start(f32[16,16]{1,0:T(8,128)S(1)} %max.10), channel_id=1, source_target_pairs={{0,16},{4,20},{8,24},{12,28},{16,0},{20,4},{24,8},{28,12},{1,17},{... | collective-permute-start | bytes 3080 | tf_op jit(solution)/shard_map/ppermute | solution.py:191

commit v7 on v5

--- a/solution.py
+++ b/solution.py
@@ -261,30 +261,32 @@
     low, between = z < 2, (z == 1) | (z == 2)
     sources = [z, z ^ 1, jnp.where(low, 2, 1), jnp.where(low, 3, 0)]
     over0 = [x_perm(owned, by) for by in others]
-    pairs, mid = z_perm(owned, PAIRS), z_perm(owned, MIDDLE)
+    pairs = z_perm(owned, PAIRS)
+    mid = z_perm(owned, MIDDLE)
     new_master, new_first, new_second = update(
         [after(terms[0], owned), *terms[1:]], states, factor, [0, 1, 2], "states"
     )
+    def put(weights, value, slot, by, h=0):
+        at = (sources[slot] * n_x + (x - by) % n_x) * width
+        return lax.dynamic_update_slice(weights, value, (h * half, at))
+
+    weights = put(after(blank((rows, columns), BF16), new_master), owned, 0, 0)
     come = [pairs, mid, new_master, *over0]
     over1 = [x_perm(after(pairs, *come), by) for by in others]
-    mid_far, outwards = z_perm(after(pairs, *come), MIDDLE), z_perm(after(mid, *come), OUTWARDS)
+    mid_far = z_perm(after(pairs, *come), MIDDLE)
+    outwards = z_perm(after(mid, *come), OUTWARDS)
+    weights = after(weights, mid_far)
+    for got, by in zip(over0, others):
+        weights = put(weights, got, 0, by)
+    weights = put(weights, pairs, 1, 0)
     come = [mid_far, outwards]
     near = lax.optimization_barrier(jnp.where(between, after(mid, *come, *over1), outwards))
     over2 = [x_perm(near, by) for by in others]
     cuts = [lax.slice_in_dim(mid_far, h * half, (h + 1) * half) for h in halves]
     far = [z_perm(after(cuts[0], *come), OUTWARDS), z_perm(after(cuts[1], near), OUTWARDS)]
-
-    def put(weights, value, slot, by, h=0):
-        at = (sources[slot] * n_x + (x - by) % n_x) * width
-        return lax.dynamic_update_slice(weights, value, (h * half, at))
-
-    weights = after(blank((rows, columns), BF16), near)
-    weights = put(weights, owned, 0, 0)
-    weights = put(weights, pairs, 1, 0)
-    weights = put(weights, near, 2, 0)
-    for over, slot in ((over0, 0), (over1, 1)):
-        for got, by in zip(over, others):
-            weights = put(weights, got, slot, by)
+    weights = put(after(weights, near), near, 2, 0)
+    for got, by in zip(over1, others):
+        weights = put(weights, got, 1, by)
     distant, over3 = [None] * 2, [None] * 2
     for h in halves:
         value = after(lax.slice_in_dim(mid_far, h * half, (h + 1) * half), far[h], *distant[:h])

time: 239 us -> 243 us (1.017)
  waiting for transfers between devices: 115 us -> 119 us
    ppermute x10, waiting for transfers between devices: 27.9 us -> 31 us  [x_perm(): return lax.ppermute(value, 'dp', pairs)]
  transfers between devices with their start and end apart: 35 -> 35, of which waited for: 20 -> 20; matrix products, arithmetic and copies ran while one was open for 14% -> 13% of each run, Pallas kernels for 11% -> 10%
where the time goes in v7:
time: 243 us; the launch traced here: 242 us
  waiting for transfers between devices  119 us (49%)
  starting transfers between devices  48.5 us (20%)
  Pallas kernels  37.5 us (15%)
  local copies, waits for them, and re-layouts  21.8 us (9%)
  other arithmetic  14.6 us (6%)
    ppermute x16, waiting for transfers between devices, z_perm(): lax.ppermute(value, 'dp', [(a * n_x + i, b * n_x + i) for a, b in pairs f...  69.3 us
    ppermute x16, starting transfers between devices, z_perm(): lax.ppermute(value, 'dp', [(a * n_x + i, b * n_x + i) for a, b in pairs f...  36.1 us
    ppermute x10, waiting for transfers between devices, x_perm(): return lax.ppermute(value, 'dp', pairs)  31 us
    pallas_call x3, Pallas kernels, multiply(): pl.pallas_call(kernel, grid=(rows // step,), in_specs=[pl.BlockSpec((step...  23.7 us
    ppermute x9, waiting for transfers between devices, seat_perm(): lax.ppermute(value, 'tensor', [(i, i ^ flip) for i in range(n_tensor)])  18.9 us
    convert_element_type x8, other arithmetic, add(): return lax.optimization_barrier(total.astype(BF16))  12 us
    pallas_call x2, Pallas kernels, update(): pl.pallas_call(kernel, grid=(rows // step,), in_specs=specs + [whole] * 3...  11 us
    dynamic_update_slice x10, local copies, waits for them, and re-layouts, put(): return lax.dynamic_update_slice(weights, value, (h * half, at))  10.8 us
  transfers between devices with their start and end apart: 35, of which 20 were waited for; matrix products, arithmetic and copies ran while one was open for 13% of the time, Pallas kernels for 10%

profile of v7, /device:TPU:0, one launch (start us, length us, event | category | flops | bytes accessed | tf_op | source)
XLA Modules:
  0.0 242.4 jit_solution(4467326479725921072)
XLA Ops:
  0.6 2.8 %arrange.1 = (bf16[384,256]{1,0:T(8,128)(2,1)}, bf16[384,512]{1,0:T(8,128)(2,1)}, bf16[384,1280]{1,0:T(8,128)(2,1)}) custom-call(bf16[384,2048]{1,0:T(8,128)(2,1)} %cot_ref.1), custom_call_target="tpu_custom_call" | custom-call | tf_op jit(solution)/shard_map/arrange/pallas_call | solution.py:55
  3.4 3.0 %collective-permute-start.1 = (bf16[384,256]{1,0:T(8,128)(2,1)}, bf16[384,256]{1,0:T(8,128)(2,1)S(1)}, u32[]{:S(2)}, u32[]{:S(2)}) collective-permute-start(bf16[384,256]{1,0:T(8,128)(2,1)} %get-tuple-element.74.refs_0_), channel_id=1, source_target_pairs={{0,2},{1,3},{2,0},{3,1},{4,6},{5,7},{6,4},{7,5},{8,10},{9,11},{10,... | collective-permute-start | bytes 589832 | tf_op jit(solution)/shard_map/ppermute | solution.py:192
  6.4 8.6 %copy.12 = bf16[1536,2048]{0,1:T(8,128)(2,1)} copy(bf16[1536,2048]{1,0:T(8,128)(2,1)} %param.5) | data formatting | bytes 12582912 | tf_op jit(solution)/shard_map/optimization_barrier | solution.py:170
  15.6 0.9 collective-permute-done.refs_1_
  16.8 4.8 %partials.3 = (bf16[2048,256]{1,0:T(8,128)(2,1)S(1)}, f32[4,4,256]{2,1,0:T(4,128)S(1)}) custom-call(bf16[2048,1536]{1,0:T(8,128)(2,1)} %bitcast.17, bf16[384,256]{1,0:T(8,128)(2,1)S(1)} %copy-done.4, bf16[384,256]{1,0:T(8,128)(2,1)S(1)} %collective-permute-done.refs_1_, bf16[384,256]{1,0:T(8,128)(2,1)S(1)} %collective-permute-done.1.refs_2_, ...), custom_call_target="tpu_custom_call" | custom-call | flops 10000000000 | bytes 3145728 | tf_op jit(solution)/shard_map/partials/pallas_call | solution.py:79
  21.6 1.5 collective-permute-start.6
  23.6 1.5 collective-permute-start.8
  25.2 10.0 %collective-permute-done.4.refs_2_ = bf16[384,512]{1,0:T(8,128)(2,1)S(1)} collective-permute-done((bf16[384,512]{1,0:T(8,128)(2,1)S(1)}, bf16[384,512]{1,0:T(8,128)(2,1)S(1)}, u32[]{:S(2)}, u32[]{:S(2)}) %collective-permute-start.4) | collective-permute-done | bytes 393248 | tf_op jit(solution)/shard_map/ppermute | solution.py:192
  35.1 1.7 collective-permute-done.5.refs_3_
  36.8 6.8 %partials.4 = (bf16[2048,256]{1,0:T(8,128)(2,1)S(1)}, bf16[2048,256]{1,0:T(8,128)(2,1)}, f32[4,4,512]{2,1,0:T(4,128)S(1)}) custom-call(bf16[2048,1536]{1,0:T(8,128)(2,1)} %bitcast.18, bf16[384,512]{1,0:T(8,128)(2,1)S(1)} %copy-done.2, bf16[384,512]{1,0:T(8,128)(2,1)S(1)} %collective-permute-done.3.refs_1_, ...), custom_call_target="tpu_custom_call" | custom-call | tf_op jit(solution)/shard_map/partials/pallas_call | solution.py:79
  44.2 3.0 %collective-permute-done.6 = bf16[2048,256]{1,0:T(8,128)(2,1)S(1)} collective-permute-done((bf16[2048,256]{1,0:T(8,128)(2,1)S(1)}, bf16[2048,256]{1,0:T(8,128)(2,1)S(1)}, u32[]{:S(2)}, u32[]{:S(2)}) %collective-permute-start.6) | collective-permute-done | bytes 1048608 | tf_op jit(solution)/shard_map/ppermute | solution.py:189
  47.2 1.0 add_convert_fusion.7
  48.3 0.9 add_convert_fusion.6
  49.2 6.0 %collective-permute-done.8.refs_2_ = bf16[384,1280]{1,0:T(8,128)(2,1)S(1)} collective-permute-done((bf16[384,1280]{1,0:T(8,128)(2,1)S(1)}, bf16[384,1280]{1,0:T(8,128)(2,1)S(1)}, u32[]{:S(2)}, u32[]{:S(2)}) %collective-permute-start.8) | collective-permute-done | bytes 983072 | tf_op jit(solution)/shard_map/ppermute | solution.py:192
  55.3 3.6 %collective-permute-start.10 = (bf16[1024,256]{1,0:T(8,128)(2,1)}, bf16[1024,256]{1,0:T(8,128)(2,1)S(1)}, u32[]{:S(2)}, u32[]{:S(2)}) collective-permute-start(bf16[1024,256]{1,0:T(8,128)(2,1)} %add_convert_fusion.6), channel_id=1, source_target_pairs={{0,8},{4,12},{24,16},{28,20},{1,9},{5,13},{25,17},{29,21},{2,10},{... | collective-permute-start | bytes 1572872 | tf_op jit(solution)/shard_map/ppermute | solution.py:185
  58.9 1.3 collective-permute-start.11
  60.3 12.1 %partials.5 = (bf16[2048,256]{1,0:T(8,128)(2,1)}, bf16[2048,256]{1,0:T(8,128)(2,1)S(1)}, bf16[2048,256]{1,0:T(8,128)(2,1)}, bf16[2048,256]{1,0:T(8,128)(2,1)}, b...) custom-call(bf16[2048,1536]{1,0:T(8,128)(2,1)} %bitcast.19, bf16[384,1280]{1,0:T(8,128)(2,1)S(1)} %copy-done.1, ...), custom_call_target="tpu_custom_call" | custom-call | tf_op jit(solution)/shard_map/partials/pallas_call | solution.py:79
  73.0 2.9 %add_convert_fusion.1 = bf16[2048,256]{1,0:T(8,128)(2,1)} fusion(bf16[2048,256]{1,0:T(8,128)(2,1)} %collective-permute-done.12, bf16[2048,256]{1,0:T(8,128)(2,1)} %get-tuple-element.112), kind=kLoop, calls=%fused_computation.1 | loop fusion | flops 2097152 | bytes 3145728 | tf_op jit(solution)/shard_map/convert_element_type | solution.py:103
  75.9 2.3 collective-permute-start.15
  78.1 4.5 %collective-permute-done.11 = bf16[1024,256]{1,0:T(8,128)(2,1)S(1)} collective-permute-done((bf16[1024,256]{1,0:T(8,128)(2,1)}, bf16[1024,256]{1,0:T(8,128)(2,1)S(1)}, u32[]{:S(2)}, u32[]{:S(2)}) %collective-permute-start.11) | collective-permute-done | bytes 524320 | tf_op jit(solution)/shard_map/ppermute | solution.py:185
  82.7 1.0 add_convert_fusion.5
  83.7 1.4 collective-permute-start.17
  85.2 1.0 add_convert_fusion.4
  88.1 10.7 %collective-permute-done.16 = bf16[2048,256]{1,0:T(8,128)(2,1)} collective-permute-done((bf16[2048,256]{1,0:T(8,128)(2,1)}, bf16[2048,256]{1,0:T(8,128)(2,1)}, u32[]{:S(2)}, u32[]{:S(2)}) %collective-permute-start.16) | collective-permute-done | bytes 1048608 | tf_op jit(solution)/shard_map/ppermute | solution.py:189
  98.8 1.5 add_convert_fusion.3
  100.3 4.4 %collective-permute-start.19 = (bf16[1024,256]{1,0:T(8,128)(2,1)S(1)}, bf16[1024,256]{1,0:T(8,128)(2,1)S(1)}, u32[]{:S(2)}, u32[]{:S(2)}) collective-permute-start(bf16[1024,256]{1,0:T(8,128)(2,1)S(1)} %add_convert_fusion.3), channel_id=1, source_target_pairs={{0,8},{4,12},{8,0},{12,4},{16,24},{20,28},{24,16},{28,20},{1,9},{5... | collective-permute-start | bytes 1572872 | tf_op jit(solution)/shard_map/ppermute | solution.py:185
  105.1 2.2 add_convert_fusion
  107.4 0.7 collective-permute-start.18
  108.1 7.8 %collective-permute-done.19.refs_3_ = bf16[1024,256]{1,0:T(8,128)(2,1)S(1)} collective-permute-done((bf16[1024,256]{1,0:T(8,128)(2,1)S(1)}, bf16[1024,256]{1,0:T(8,128)(2,1)S(1)}, u32[]{:S(2)}, u32[]{:S(2)}) %collective-permute-start.19) | collective-permute-done | bytes 524320 | tf_op jit(solution)/shard_map/ppermute | solution.py:185
  115.9 1.4 add_convert_fusion.2
  117.3 2.5 %collective-permute-start.21 = (bf16[1024,256]{1,0:T(8,128)(2,1)S(1)}, bf16[1024,256]{1,0:T(8,128)(2,1)S(1)}, u32[]{:S(2)}, u32[]{:S(2)}) collective-permute-start(bf16[1024,256]{1,0:T(8,128)(2,1)S(1)} %add_convert_fusion.2), channel_id=1, source_target_pairs={{0,8},{4,12},{8,0},{12,4},{16,24},{20,28},{24,16},{28,20},{1,9},{5... | collective-permute-start | bytes 1572872 | tf_op jit(solution)/shard_map/ppermute | solution.py:185
  120.4 3.1 %collective-permute-done.13 = f32[16,16]{1,0:T(8,128)S(1)} collective-permute-done((f32[16,16]{1,0:T(8,128)S(1)}, f32[16,16]{1,0:T(8,128)S(1)}, u32[]{:S(2)}, u32[]{:S(2)}) %collective-permute-start.13) | collective-permute-done | bytes 1056 | tf_op jit(solution)/shard_map/ppermute | solution.py:189
  123.5 7.3 %collective-permute-done.21.refs_4_ = bf16[1024,256]{1,0:T(8,128)(2,1)S(1)} collective-permute-done((bf16[1024,256]{1,0:T(8,128)(2,1)S(1)}, bf16[1024,256]{1,0:T(8,128)(2,1)S(1)}, u32[]{:S(2)}, u32[]{:S(2)}) %collective-permute-start.21) | collective-permute-done | bytes 524320 | tf_op jit(solution)/shard_map/ppermute | solution.py:185
  130.8 4.6 %weights.1 = bf16[2048,256]{1,0:T(8,128)(2,1)S(1)} custom-call(bf16[2048,256]{1,0:T(8,128)(2,1)S(1)} %copy-done, bf16[2048,256]{1,0:T(8,128)(2,1)S(1)} %collective-permute-done.14.refs_1_, bf16[2048,256]{1,0:T(8,128)(2,1)S(1)} %collective-permute-done.18.refs_2_, bf16[1024,256]{1,0:T(8,128)(2,1)S(1)} %collective-permute-done.19.refs_3_, ...), custom_call_target="tpu_custom_call" | custom-call | tf_op jit(solution)/shard_map/weights/pallas_call | solution.py:147
  135.4 5.4 %collective-permute-start.22 = (bf16[2048,256]{1,0:T(8,128)(2,1)S(1)}, bf16[2048,256]{1,0:T(8,128)(2,1)}, u32[]{:S(2)}, u32[]{:S(2)}) collective-permute-start(bf16[2048,256]{1,0:T(8,128)(2,1)S(1)} %weights.1), channel_id=1, source_target_pairs={{0,8},{4,12},{8,0},{12,4},{16,24},{20,28},{24,16},{28,20},{1,9},{5... | collective-permute-start | bytes 3145736 | tf_op jit(solution)/shard_map/ppermute | solution.py:185
  140.8 1.6 collective-permute-start.23
  143.0 6.4 %states.1 = (f32[2048,256]{1,0:T(8,128)}, f32[2048,256]{1,0:T(8,128)}, f32[2048,256]{1,0:T(8,128)}) custom-call(bf16[2048,256]{1,0:T(8,128)(2,1)S(1)} %copy-done, bf16[2048,256]{1,0:T(8,128)(2,1)S(1)} %collective-permute-done.14.refs_1_, bf16[2048,256]{1,0:T(8,128)(2,1)S(1)} %collective-permute-done.18.refs_2_, ...), custom_call_target="tpu_custom_call" | custom-call | tf_op jit(solution)/shard_map/states/pallas_call | solution.py:147
  149.4 13.2 %collective-permute-done.22 = bf16[2048,256]{1,0:T(8,128)(2,1)} collective-permute-done((bf16[2048,256]{1,0:T(8,128)(2,1)S(1)}, bf16[2048,256]{1,0:T(8,128)(2,1)}, u32[]{:S(2)}, u32[]{:S(2)}) %collective-permute-start.22) | collective-permute-done | bytes 1048608 | tf_op jit(solution)/shard_map/ppermute | solution.py:185
  162.6 3.0 %collective-permute-done.24 = bf16[2048,256]{1,0:T(8,128)(2,1)S(1)} collective-permute-done((bf16[2048,256]{1,0:T(8,128)(2,1)S(1)}, bf16[2048,256]{1,0:T(8,128)(2,1)S(1)}, u32[]{:S(2)}, u32[]{:S(2)}) %collective-permute-start.24) | collective-permute-done | bytes 1048608 | tf_op jit(solution)/shard_map/ppermute | solution.py:189
  165.6 1.0 copy-done.7
  166.6 1.8 collective-permute-start.25
  168.4 1.3 collective-permute-start.26
  170.3 1.0 constant_dynamic-update-slice_fusion.7
  171.3 21.7 %collective-permute-done.26 = bf16[2048,256]{1,0:T(8,128)(2,1)} collective-permute-done((bf16[2048,256]{1,0:T(8,128)(2,1)}, bf16[2048,256]{1,0:T(8,128)(2,1)}, u32[]{:S(2)}, u32[]{:S(2)}) %collective-permute-start.26) | collective-permute-done | bytes 1048608 | tf_op jit(solution)/shard_map/ppermute | solution.py:185
  193.0 1.3 broadcast_select_fusion
  194.4 1.3 fusion
  195.6 1.3 collective-permute-start.28
  197.5 1.0 constant_dynamic-update-slice_fusion.6
  198.6 2.3 constant_dynamic-update-slice_fusion.5
  200.8 1.3 collective-permute-start.29
  202.1 1.0 constant_dynamic-update-slice_fusion.4
  203.2 1.0 constant_dynamic-update-slice_fusion.3
  204.2 8.2 %collective-permute-done.28 = bf16[1024,256]{1,0:T(8,128)(2,1)S(1)} collective-permute-done((bf16[1024,256]{1,0:T(8,128)(2,1)S(1)}, bf16[1024,256]{1,0:T(8,128)(2,1)S(1)}, u32[]{:S(2)}, u32[]{:S(2)}) %collective-permute-start.28) | collective-permute-done | bytes 524320 | tf_op jit(solution)/shard_map/ppermute | solution.py:185
  213.1 6.1 %collective-permute-done.29 = bf16[1024,256]{1,0:T(8,128)(2,1)S(1)} collective-permute-done((bf16[1024,256]{1,0:T(8,128)(2,1)S(1)}, bf16[1024,256]{1,0:T(8,128)(2,1)S(1)}, u32[]{:S(2)}, u32[]{:S(2)}) %collective-permute-start.29) | collective-permute-done | bytes 524320 | tf_op jit(solution)/shard_map/ppermute | solution.py:185
  219.8 0.8 constant_dynamic-update-slice_fusion.2
  220.7 0.8 constant_dynamic-update-slice_fusion.9
  221.5 1.6 collective-permute-done.30
  223.1 2.7 %collective-permute-start.33 = (f32[16,16]{1,0:T(8,128)S(1)}, f32[16,16]{1,0:T(8,128)S(1)}, u32[]{:S(2)}, u32[]{:S(2)}) collective-permute-start(f32[16,16]{1,0:T(8,128)S(1)} %max.9), channel_id=1, source_target_pairs={{0,8},{4,12},{8,0},{12,4},{16,24},{20,28},{24,16},{28,20},{1,9},{5... | collective-permute-start | bytes 3080 | tf_op jit(solution)/shard_map/ppermute | solution.py:185
  225.8 1.0 constant_dynamic-update-slice_fusion.1
  226.8 7.5 %collective-permute-done.31 = bf16[1024,256]{1,0:T(8,128)(2,1)S(1)} collective-permute-done((bf16[1024,256]{1,0:T(8,128)(2,1)S(1)}, bf16[1024,256]{1,0:T(8,128)(2,1)S(1)}, u32[]{:S(2)}, u32[]{:S(2)}) %collective-permute-start.31) | collective-permute-done | bytes 524320 | tf_op jit(solution)/shard_map/ppermute | solution.py:189
  234.3 0.8 constant_dynamic-update-slice_fusion
  235.2 3.7 %collective-permute-start.34 = (f32[16,16]{1,0:T(8,128)S(1)}, f32[16,16]{1,0:T(8,128)S(1)}, u32[]{:S(2)}, u32[]{:S(2)}) collective-permute-start(f32[16,16]{1,0:T(8,128)S(1)} %max.10), channel_id=1, source_target_pairs={{0,16},{4,20},{8,24},{12,28},{16,0},{20,4},{24,8},{28,12},{1,17},{... | collective-permute-start | bytes 3080 | tf_op jit(solution)/shard_map/ppermute | solution.py:185
  238.9 2.1 collective-permute-done.32
  241.0 0.8 constant_dynamic-update-slice_fusion.8
  (67 shorter events, 9.3 us)
Async XLA Ops:
  3.4 11.6 %copy-start.4 = (bf16[384,256]{1,0:T(8,128)(2,1)S(1)}, bf16[384,256]{1,0:T(8,128)(2,1)}, u32[]{:S(2)}) copy-start(bf16[384,256]{1,0:T(8,128)(2,1)} %get-tuple-element.74.refs_0_) | copy-start | bytes 589828
  3.4 11.7 %collective-permute-start.1 = (bf16[384,256]{1,0:T(8,128)(2,1)}, bf16[384,256]{1,0:T(8,128)(2,1)S(1)}, u32[]{:S(2)}, u32[]{:S(2)}) collective-permute-start(bf16[384,256]{1,0:T(8,128)(2,1)} %get-tuple-element.74.refs_0_), channel_id=1, source_target_pairs={{0,2},{1,3},{2,0},{3,1},{4,6},{5,7},{6,4},{7,5},{8,10},{9,11},{10,... | collective-permute-start | bytes 589832 | tf_op jit(solution)/shard_map/ppermute | solution.py:192
  15.0 8.1 %copy-start.2 = (bf16[384,512]{1,0:T(8,128)(2,1)S(1)}, bf16[384,512]{1,0:T(8,128)(2,1)}, u32[]{:S(2)}) copy-start(bf16[384,512]{1,0:T(8,128)(2,1)} %get-tuple-element.78.refs_0_) | copy-start | bytes 1179652
  15.0 8.7 %copy-start.1 = (bf16[384,1280]{1,0:T(8,128)(2,1)S(1)}, bf16[384,1280]{1,0:T(8,128)(2,1)}, u32[]{:S(2)}) copy-start(bf16[384,1280]{1,0:T(8,128)(2,1)} %get-tuple-element.86.refs_0_) | copy-start | bytes 2949124
  15.0 1.5 collective-permute-start
  15.1 1.7 collective-permute-start.2
  21.6 25.6 %collective-permute-start.6 = (bf16[2048,256]{1,0:T(8,128)(2,1)S(1)}, bf16[2048,256]{1,0:T(8,128)(2,1)S(1)}, u32[]{:S(2)}, u32[]{:S(2)}) collective-permute-start(bf16[2048,256]{1,0:T(8,128)(2,1)S(1)} %get-tuple-element.76), channel_id=1, source_target_pairs={{0,4},{4,0},{8,12},{12,8},{16,20},{20,16},{24,28},{28,24},{1,5},{5... | collective-permute-start | bytes 3145736 | tf_op jit(solution)/shard_map/ppermute | solution.py:189
  23.1 12.0 %collective-permute-start.4 = (bf16[384,512]{1,0:T(8,128)(2,1)S(1)}, bf16[384,512]{1,0:T(8,128)(2,1)S(1)}, u32[]{:S(2)}, u32[]{:S(2)}) collective-permute-start(bf16[384,512]{1,0:T(8,128)(2,1)S(1)} %copy-done.2), channel_id=1, source_target_pairs={{0,2},{1,3},{2,0},{3,1},{4,6},{5,7},{6,4},{7,5},{8,10},{9,11},{10,... | collective-permute-start | bytes 1179656 | tf_op jit(solution)/shard_map/ppermute | solution.py:192
  23.6 31.5 %collective-permute-start.8 = (bf16[384,1280]{1,0:T(8,128)(2,1)S(1)}, bf16[384,1280]{1,0:T(8,128)(2,1)S(1)}, u32[]{:S(2)}, u32[]{:S(2)}) collective-permute-start(bf16[384,1280]{1,0:T(8,128)(2,1)S(1)} %copy-done.1), channel_id=1, source_target_pairs={{0,2},{1,3},{2,0},{3,1},{4,6},{5,7},{6,4},{7,5},{8,10},{9,11},{10,... | collective-permute-start | bytes 2949128 | tf_op jit(solution)/shard_map/ppermute | solution.py:192
  25.2 10.0 %collective-permute-start.3 = (bf16[384,512]{1,0:T(8,128)(2,1)S(1)}, bf16[384,512]{1,0:T(8,128)(2,1)S(1)}, u32[]{:S(2)}, u32[]{:S(2)}) collective-permute-start(bf16[384,512]{1,0:T(8,128)(2,1)S(1)} %copy-done.2), channel_id=1, source_target_pairs={{0,1},{1,0},{2,3},{3,2},{4,5},{5,4},{6,7},{7,6},{8,9},{9,8},{10,11... | collective-permute-start | bytes 1179656 | tf_op jit(solution)/shard_map/ppermute | solution.py:192
  35.1 1.7 collective-permute-start.5
  43.7 29.3 %collective-permute-start.12 = (bf16[2048,256]{1,0:T(8,128)(2,1)}, bf16[2048,256]{1,0:T(8,128)(2,1)}, u32[]{:S(2)}, u32[]{:S(2)}) collective-permute-start(bf16[2048,256]{1,0:T(8,128)(2,1)} %get-tuple-element.91), channel_id=1, source_target_pairs={{0,4},{4,0},{8,12},{12,8},{16,20},{20,16},{24,28},{28,24},{1,5},{5... | collective-permute-start | bytes 3145736 | tf_op jit(solution)/shard_map/ppermute | solution.py:189
  47.2 8.0 %copy-start.5 = (bf16[2048,256]{1,0:T(8,128)(2,1)}, bf16[2048,256]{1,0:T(8,128)(2,1)S(1)}, u32[]{:S(2)}) copy-start(bf16[2048,256]{1,0:T(8,128)(2,1)S(1)} %collective-permute-done.6) | copy-start | bytes 3145732
  49.2 11.1 %collective-permute-start.7 = (bf16[384,1280]{1,0:T(8,128)(2,1)S(1)}, bf16[384,1280]{1,0:T(8,128)(2,1)}, u32[]{:S(2)}, u32[]{:S(2)}) collective-permute-start(bf16[384,1280]{1,0:T(8,128)(2,1)S(1)} %copy-done.1), channel_id=1, source_target_pairs={{0,1},{1,0},{2,3},{3,2},{4,5},{5,4},{6,7},{7,6},{8,9},{9,8},{10,11... | collective-permute-start | bytes 2949128 | tf_op jit(solution)/shard_map/ppermute | solution.py:192
  55.2 5.1 %collective-permute-start.9 = (bf16[384,1280]{1,0:T(8,128)(2,1)S(1)}, bf16[384,1280]{1,0:T(8,128)(2,1)}, u32[]{:S(2)}, u32[]{:S(2)}) collective-permute-start(bf16[384,1280]{1,0:T(8,128)(2,1)S(1)} %collective-permute-done.8.refs_2_), channel_id=1, source_target_pairs={{0,1},{1,0},{2,3},{3,2},{4,5},{5,4},{6,7},{7,6},{8,9},{9,8},{10,11... | collective-permute-start | bytes 2949128 | tf_op jit(solution)/shard_map/ppermute | solution.py:192
  55.3 27.4 %copy-start.6 = (bf16[2048,256]{1,0:T(8,128)(2,1)S(1)}, bf16[2048,256]{1,0:T(8,128)(2,1)}, u32[]{:S(2)}) copy-start(bf16[2048,256]{1,0:T(8,128)(2,1)} %copy-done.5) | copy-start | bytes 3145732
  55.3 29.9 %collective-permute-start.10 = (bf16[1024,256]{1,0:T(8,128)(2,1)}, bf16[1024,256]{1,0:T(8,128)(2,1)S(1)}, u32[]{:S(2)}, u32[]{:S(2)}) collective-permute-start(bf16[1024,256]{1,0:T(8,128)(2,1)} %add_convert_fusion.6), channel_id=1, source_target_pairs={{0,8},{4,12},{24,16},{28,20},{1,9},{5,13},{25,17},{29,21},{2,10},{... | collective-permute-start | bytes 1572872 | tf_op jit(solution)/shard_map/ppermute | solution.py:185
  58.9 23.7 %collective-permute-start.11 = (bf16[1024,256]{1,0:T(8,128)(2,1)}, bf16[1024,256]{1,0:T(8,128)(2,1)S(1)}, u32[]{:S(2)}, u32[]{:S(2)}) collective-permute-start(bf16[1024,256]{1,0:T(8,128)(2,1)} %add_convert_fusion.7), channel_id=1, source_target_pairs={{0,8},{4,12},{24,16},{28,20},{1,9},{5,13},{25,17},{29,21},{2,10},{... | collective-permute-start | bytes 1572872 | tf_op jit(solution)/shard_map/ppermute | solution.py:185
  72.4 13.8 %copy-start.3 = (bf16[2048,256]{1,0:T(8,128)(2,1)}, bf16[2048,256]{1,0:T(8,128)(2,1)S(1)}, u32[]{:S(2)}) copy-start(bf16[2048,256]{1,0:T(8,128)(2,1)S(1)} %get-tuple-element.107) | copy-start | bytes 3145732
  72.4 58.4 %copy-start = (bf16[2048,256]{1,0:T(8,128)(2,1)S(1)}, bf16[2048,256]{1,0:T(8,128)(2,1)}, u32[]{:S(2)}) copy-start(bf16[2048,256]{1,0:T(8,128)(2,1)} %get-tuple-element.118.refs_0_) | copy-start | bytes 3145732
  72.4 26.4 %collective-permute-start.16 = (bf16[2048,256]{1,0:T(8,128)(2,1)}, bf16[2048,256]{1,0:T(8,128)(2,1)}, u32[]{:S(2)}, u32[]{:S(2)}) collective-permute-start(bf16[2048,256]{1,0:T(8,128)(2,1)} %get-tuple-element.92), channel_id=1, source_target_pairs={{0,4},{4,0},{8,12},{12,8},{16,20},{20,16},{24,28},{28,24},{1,5},{5... | collective-permute-start | bytes 3145736 | tf_op jit(solution)/shard_map/ppermute | solution.py:189
  75.9 29.3 %collective-permute-start.15 = (bf16[2048,256]{1,0:T(8,128)(2,1)}, bf16[2048,256]{1,0:T(8,128)(2,1)}, u32[]{:S(2)}, u32[]{:S(2)}) collective-permute-start(bf16[2048,256]{1,0:T(8,128)(2,1)} %add_convert_fusion.1), channel_id=1, source_target_pairs={{0,8},{4,12},{24,16},{28,20},{1,9},{5,13},{25,17},{29,21},{2,10},{... | collective-permute-start | bytes 3145736 | tf_op jit(solution)/shard_map/ppermute | solution.py:185
  83.7 4.4 %collective-permute-start.17 = (bf16[1024,256]{1,0:T(8,128)(2,1)}, bf16[1024,256]{1,0:T(8,128)(2,1)}, u32[]{:S(2)}, u32[]{:S(2)}) collective-permute-start(bf16[1024,256]{1,0:T(8,128)(2,1)} %add_convert_fusion.5), channel_id=1, source_target_pairs={{8,16},{12,20},{16,8},{20,12},{9,17},{13,21},{17,9},{21,13},{10,18... | collective-permute-start | bytes 1572872 | tf_op jit(solution)/shard_map/ppermute | solution.py:185
  86.2 21.9 %collective-permute-start.20 = (bf16[1024,256]{1,0:T(8,128)(2,1)}, bf16[1024,256]{1,0:T(8,128)(2,1)S(1)}, u32[]{:S(2)}, u32[]{:S(2)}) collective-permute-start(bf16[1024,256]{1,0:T(8,128)(2,1)} %add_convert_fusion.4), channel_id=1, source_target_pairs={{8,16},{12,20},{16,8},{20,12},{9,17},{13,21},{17,9},{21,13},{10,18... | collective-permute-start | bytes 1572872 | tf_op jit(solution)/shard_map/ppermute | solution.py:185
  87.3 36.2 %collective-permute-start.14 = (bf16[2048,256]{1,0:T(8,128)(2,1)}, bf16[2048,256]{1,0:T(8,128)(2,1)S(1)}, u32[]{:S(2)}, u32[]{:S(2)}) collective-permute-start(bf16[2048,256]{1,0:T(8,128)(2,1)} %copy-done.3), channel_id=1, source_target_pairs={{0,4},{4,0},{8,12},{12,8},{16,20},{20,16},{24,28},{28,24},{1,5},{5... | collective-permute-start | bytes 3145736 | tf_op jit(solution)/shard_map/ppermute | solution.py:189
  100.3 15.6 %collective-permute-start.19 = (bf16[1024,256]{1,0:T(8,128)(2,1)S(1)}, bf16[1024,256]{1,0:T(8,128)(2,1)S(1)}, u32[]{:S(2)}, u32[]{:S(2)}) collective-permute-start(bf16[1024,256]{1,0:T(8,128)(2,1)S(1)} %add_convert_fusion.3), channel_id=1, source_target_pairs={{0,8},{4,12},{8,0},{12,4},{16,24},{20,28},{24,16},{28,20},{1,9},{5... | collective-permute-start | bytes 1572872 | tf_op jit(solution)/shard_map/ppermute | solution.py:185
  107.4 23.4 %collective-permute-start.18 = (bf16[2048,256]{1,0:T(8,128)(2,1)S(1)}, bf16[2048,256]{1,0:T(8,128)(2,1)S(1)}, u32[]{:S(2)}, u32[]{:S(2)}) collective-permute-start(bf16[2048,256]{1,0:T(8,128)(2,1)S(1)} %add_convert_fusion), channel_id=1, source_target_pairs={{8,16},{12,20},{16,8},{20,12},{9,17},{13,21},{17,9},{21,13},{10,18... | collective-permute-start | bytes 3145736 | tf_op jit(solution)/shard_map/ppermute | solution.py:185
  117.3 13.5 %collective-permute-start.21 = (bf16[1024,256]{1,0:T(8,128)(2,1)S(1)}, bf16[1024,256]{1,0:T(8,128)(2,1)S(1)}, u32[]{:S(2)}, u32[]{:S(2)}) collective-permute-start(bf16[1024,256]{1,0:T(8,128)(2,1)S(1)} %add_convert_fusion.2), channel_id=1, source_target_pairs={{0,8},{4,12},{8,0},{12,4},{16,24},{20,28},{24,16},{28,20},{1,9},{5... | collective-permute-start | bytes 1572872 | tf_op jit(solution)/shard_map/ppermute | solution.py:185
  119.8 3.7 %collective-permute-start.13 = (f32[16,16]{1,0:T(8,128)S(1)}, f32[16,16]{1,0:T(8,128)S(1)}, u32[]{:S(2)}, u32[]{:S(2)}) collective-permute-start(f32[16,16]{1,0:T(8,128)S(1)} %select_reduce_fusion), channel_id=1, source_target_pairs={{0,4},{4,0},{8,12},{12,8},{16,20},{20,16},{24,28},{28,24},{1,5},{5... | collective-permute-start | bytes 3080 | tf_op jit(solution)/shard_map/ppermute | solution.py:189
  135.4 27.3 %collective-permute-start.22 = (bf16[2048,256]{1,0:T(8,128)(2,1)S(1)}, bf16[2048,256]{1,0:T(8,128)(2,1)}, u32[]{:S(2)}, u32[]{:S(2)}) collective-permute-start(bf16[2048,256]{1,0:T(8,128)(2,1)S(1)} %weights.1), channel_id=1, source_target_pairs={{0,8},{4,12},{8,0},{12,4},{16,24},{20,28},{24,16},{28,20},{1,9},{5... | collective-permute-start | bytes 3145736 | tf_op jit(solution)/shard_map/ppermute | solution.py:185
  140.8 21.9 %collective-permute-start.23 = (bf16[2048,256]{1,0:T(8,128)(2,1)S(1)}, bf16[2048,256]{1,0:T(8,128)(2,1)}, u32[]{:S(2)}, u32[]{:S(2)}) collective-permute-start(bf16[2048,256]{1,0:T(8,128)(2,1)S(1)} %weights.1), channel_id=1, source_target_pairs={{8,16},{12,20},{16,8},{20,12},{9,17},{13,21},{17,9},{21,13},{10,18... | collective-permute-start | bytes 3145736 | tf_op jit(solution)/shard_map/ppermute | solution.py:185
  142.4 23.2 %collective-permute-start.24 = (bf16[2048,256]{1,0:T(8,128)(2,1)S(1)}, bf16[2048,256]{1,0:T(8,128)(2,1)S(1)}, u32[]{:S(2)}, u32[]{:S(2)}) collective-permute-start(bf16[2048,256]{1,0:T(8,128)(2,1)S(1)} %weights.1), channel_id=1, source_target_pairs={{0,4},{4,0},{8,12},{12,8},{16,20},{20,16},{24,28},{28,24},{1,5},{5... | collective-permute-start | bytes 3145736 | tf_op jit(solution)/shard_map/ppermute | solution.py:189
  165.6 1.0 copy-start.7
  166.6 30.9 %copy-start.8 = (bf16[2048,256]{1,0:T(8,128)(2,1)S(1)}, bf16[2048,256]{1,0:T(8,128)(2,1)}, u32[]{:S(2)}) copy-start(bf16[2048,256]{1,0:T(8,128)(2,1)} %copy-done.7) | copy-start | bytes 3145732
  166.6 4.7 %collective-permute-start.25 = (bf16[2048,256]{1,0:T(8,128)(2,1)}, bf16[2048,256]{1,0:T(8,128)(2,1)}, u32[]{:S(2)}, u32[]{:S(2)}) collective-permute-start(bf16[2048,256]{1,0:T(8,128)(2,1)} %collective-permute-done.22), channel_id=1, source_target_pairs={{8,16},{12,20},{16,8},{20,12},{9,17},{13,21},{17,9},{21,13},{10,18... | collective-permute-start | bytes 3145736 | tf_op jit(solution)/shard_map/ppermute | solution.py:185
  168.4 24.6 %collective-permute-start.26 = (bf16[2048,256]{1,0:T(8,128)(2,1)}, bf16[2048,256]{1,0:T(8,128)(2,1)}, u32[]{:S(2)}, u32[]{:S(2)}) collective-permute-start(bf16[2048,256]{1,0:T(8,128)(2,1)} %collective-permute-done.23), channel_id=1, source_target_pairs={{8,0},{12,4},{16,24},{20,28},{9,1},{13,5},{17,25},{21,29},{10,2},{... | collective-permute-start | bytes 3145736 | tf_op jit(solution)/shard_map/ppermute | solution.py:185
  169.7 23.3 %collective-permute-start.27 = (bf16[2048,256]{1,0:T(8,128)(2,1)}, bf16[2048,256]{1,0:T(8,128)(2,1)S(1)}, u32[]{:S(2)}, u32[]{:S(2)}) collective-permute-start(bf16[2048,256]{1,0:T(8,128)(2,1)} %collective-permute-done.22), channel_id=1, source_target_pairs={{0,4},{4,0},{8,12},{12,8},{16,20},{20,16},{24,28},{28,24},{1,5},{5... | collective-permute-start | bytes 3145736 | tf_op jit(solution)/shard_map/ppermute | solution.py:189
  195.6 16.8 %collective-permute-start.28 = (bf16[1024,256]{1,0:T(8,128)(2,1)S(1)}, bf16[1024,256]{1,0:T(8,128)(2,1)S(1)}, u32[]{:S(2)}, u32[]{:S(2)}) collective-permute-start(bf16[1024,256]{1,0:T(8,128)(2,1)S(1)} %get-tuple-element.129), channel_id=1, source_target_pairs={{8,0},{12,4},{16,24},{20,28},{9,1},{13,5},{17,25},{21,29},{10,2},{... | collective-permute-start | bytes 1572872 | tf_op jit(solution)/shard_map/ppermute | solution.py:185
  196.9 26.2 %collective-permute-start.30 = (bf16[2048,256]{1,0:T(8,128)(2,1)S(1)}, bf16[2048,256]{1,0:T(8,128)(2,1)S(1)}, u32[]{:S(2)}, u32[]{:S(2)}) collective-permute-start(bf16[2048,256]{1,0:T(8,128)(2,1)S(1)} %broadcast_select_fusion), channel_id=1, source_target_pairs={{0,4},{4,0},{8,12},{12,8},{16,20},{20,16},{24,28},{28,24},{1,5},{5... | collective-permute-start | bytes 3145736 | tf_op jit(solution)/shard_map/ppermute | solution.py:189
  200.8 18.3 %collective-permute-start.29 = (bf16[1024,256]{1,0:T(8,128)(2,1)S(1)}, bf16[1024,256]{1,0:T(8,128)(2,1)S(1)}, u32[]{:S(2)}, u32[]{:S(2)}) collective-permute-start(bf16[1024,256]{1,0:T(8,128)(2,1)S(1)} %get-tuple-element.131), channel_id=1, source_target_pairs={{8,0},{12,4},{16,24},{20,28},{9,1},{13,5},{17,25},{21,29},{10,2},{... | collective-permute-start | bytes 1572872 | tf_op jit(solution)/shard_map/ppermute | solution.py:185
  212.5 21.8 %collective-permute-start.31 = (bf16[1024,256]{1,0:T(8,128)(2,1)S(1)}, bf16[1024,256]{1,0:T(8,128)(2,1)S(1)}, u32[]{:S(2)}, u32[]{:S(2)}) collective-permute-start(bf16[1024,256]{1,0:T(8,128)(2,1)S(1)} %broadcast_select_fusion.2), channel_id=1, source_target_pairs={{0,4},{4,0},{8,12},{12,8},{16,20},{20,16},{24,28},{28,24},{1,5},{5... | collective-permute-start | bytes 1572872 | tf_op jit(solution)/shard_map/ppermute | solution.py:189
  219.2 21.7 %collective-permute-start.32 = (bf16[1024,256]{1,0:T(8,128)(2,1)S(1)}, bf16[1024,256]{1,0:T(8,128)(2,1)S(1)}, u32[]{:S(2)}, u32[]{:S(2)}) collective-permute-start(bf16[1024,256]{1,0:T(8,128)(2,1)S(1)} %broadcast_select_fusion.1), channel_id=1, source_target_pairs={{0,4},{4,0},{8,12},{12,8},{16,20},{20,16},{24,28},{28,24},{1,5},{5... | collective-permute-start | bytes 1572872 | tf_op jit(solution)/shard_map/ppermute | solution.py:189
  223.1 12.1 %collective-permute-start.33 = (f32[16,16]{1,0:T(8,128)S(1)}, f32[16,16]{1,0:T(8,128)S(1)}, u32[]{:S(2)}, u32[]{:S(2)}) collective-permute-start(f32[16,16]{1,0:T(8,128)S(1)} %max.9), channel_id=1, source_target_pairs={{0,8},{4,12},{8,0},{12,4},{16,24},{20,28},{24,16},{28,20},{1,9},{5... | collective-permute-start | bytes 3080 | tf_op jit(solution)/shard_map/ppermute | solution.py:185
  235.2 6.6 %collective-permute-start.34 = (f32[16,16]{1,0:T(8,128)S(1)}, f32[16,16]{1,0:T(8,128)S(1)}, u32[]{:S(2)}, u32[]{:S(2)}) collective-permute-start(f32[16,16]{1,0:T(8,128)S(1)} %max.10), channel_id=1, source_target_pairs={{0,16},{4,20},{8,24},{12,28},{16,0},{20,4},{24,8},{28,12},{1,17},{... | collective-permute-start | bytes 3080 | tf_op jit(solution)/shard_map/ppermute | solution.py:185

commit v8 on v5

--- a/solution.py
+++ b/solution.py
@@ -170,6 +170,10 @@
     return lax.optimization_barrier((value, *earlier))[0] if earlier else value
 
 
+def tie(*values):
+    return lax.optimization_barrier(values)
+
+
 def body(acts, cotangent, master, first_moment, second_moment):
     n_dp = lax.axis_size("dp")
     n_tensor = lax.axis_size("tensor")
@@ -256,48 +260,62 @@
     terms = [after(partial[3, 0], *scales_x), *got3, last, tuple(pairs)]
     states = [master, first_moment, second_moment]
     factor = 1.0 / math.sqrt(acts.shape[0] * n_dp)
-    (owned,) = update(terms, states, factor, [3], "weights")
+    owned = []
+    for h in halves:
+        held = lax.optimization_barrier((*terms[:-1], *states, pairs[h]))
+        cut = [lax.slice_in_dim(value, h * half, (h + 1) * half) for value in held[:-1]]
+        value = adamw(cut[: len(terms) - 1] + [held[-1]], cut[len(terms) - 1 :], factor)[3]
+        owned.append(lax.optimization_barrier(value))
+        if h == 0:
+            terms[0], owned[0] = tie(terms[0], owned[0])
+    terms[0], owned[1] = tie(terms[0], owned[1])
+    new_master, new_first, new_second = update(terms, states, factor, [0, 1, 2], "states")
 
     low, between = z < 2, (z == 1) | (z == 2)
     sources = [z, z ^ 1, jnp.where(low, 2, 1), jnp.where(low, 3, 0)]
-    over0 = [x_perm(owned, by) for by in others]
-    pairs, mid = z_perm(owned, PAIRS), z_perm(owned, MIDDLE)
-    new_master, new_first, new_second = update(
-        [after(terms[0], owned), *terms[1:]], states, factor, [0, 1, 2], "states"
-    )
-    come = [pairs, mid, new_master, *over0]
-    over1 = [x_perm(after(pairs, *come), by) for by in others]
-    mid_far, outwards = z_perm(after(pairs, *come), MIDDLE), z_perm(after(mid, *come), OUTWARDS)
-    come = [mid_far, outwards]
-    near = lax.optimization_barrier(jnp.where(between, after(mid, *come, *over1), outwards))
-    over2 = [x_perm(near, by) for by in others]
-    cuts = [lax.slice_in_dim(mid_far, h * half, (h + 1) * half) for h in halves]
-    far = [z_perm(after(cuts[0], *come), OUTWARDS), z_perm(after(cuts[1], near), OUTWARDS)]
-
-    def put(weights, value, slot, by, h=0):
+    over = [[None] * 2 for _ in range(Z)]
+    pairs, mid, mid_far, outwards, near, far, distant = [[None] * 2 for _ in range(7)]
+
+    def over_x(value):
+        return [x_perm(value, by) for by in others]
+
+    for h in halves:
+        over[0][h] = over_x(owned[h])
+        pairs[h], mid[h] = z_perm(owned[h], PAIRS), z_perm(owned[h], MIDDLE)
+    for h in halves:
+        pairs[h], mid[h], *over[0][h] = tie(pairs[h], mid[h], *over[0][h])
+        over[1][h] = over_x(pairs[h])
+        mid_far[h], outwards[h] = z_perm(pairs[h], MIDDLE), z_perm(mid[h], OUTWARDS)
+    for h in halves:
+        mid_far[h], outwards[h], mid[h], *over[1][h] = tie(mid_far[h], outwards[h], mid[h], *over[1][h])
+        far[h] = z_perm(mid_far[h], OUTWARDS)
+        (near[h],) = tie(jnp.where(between, mid[h], outwards[h]))
+        over[2][h] = over_x(near[h])
+    for h in halves:
+        if h:
+            far[h], distant[0] = tie(far[h], distant[0])
+        (distant[h],) = tie(jnp.where(between, mid_far[h], far[h]))
+        over[3][h] = over_x(distant[h])
+
+    def put(weights, h, slot, by):
+        value = [owned, pairs, near, distant][slot][h] if by == 0 else over[slot][h][by - 1]
         at = (sources[slot] * n_x + (x - by) % n_x) * width
         return lax.dynamic_update_slice(weights, value, (h * half, at))
 
-    weights = after(blank((rows, columns), BF16), near)
-    weights = put(weights, owned, 0, 0)
-    weights = put(weights, pairs, 1, 0)
-    weights = put(weights, near, 2, 0)
-    for over, slot in ((over0, 0), (over1, 1)):
-        for got, by in zip(over, others):
-            weights = put(weights, got, slot, by)
-    distant, over3 = [None] * 2, [None] * 2
-    for h in halves:
-        value = after(lax.slice_in_dim(mid_far, h * half, (h + 1) * half), far[h], *distant[:h])
-        distant[h] = lax.optimization_barrier(jnp.where(between, value, far[h]))
-        over3[h] = [x_perm(distant[h], by) for by in others]
-    for h in halves:
-        weights = put(weights, distant[h], 3, 0, h)
-    for got, by in zip(over2, others):
-        weights = put(weights, got, 2, by)
-    for h in halves:
-        for got, by in zip(over3[h], others):
-            weights = put(weights, got, 3, by, h)
-    scales = after(scales, *distant, *over2)
+    weights, near[1] = tie(blank((rows, columns), BF16), near[1])
+    for slot in range(2):
+        for h in halves:
+            for by in range(n_x):
+                weights = put(weights, h, slot, by)
+    weights, distant[1] = tie(weights, distant[1])
+    for slot in range(2, Z):
+        for h in halves:
+            weights = put(weights, h, slot, 0)
+    for slot in range(2, Z):
+        for h in halves:
+            for by in others:
+                weights = put(weights, h, slot, by)
+    scales, distant[1] = tie(scales, distant[1])
     for got in scales_x:
         scales = jnp.maximum(scales, got)
     scales = jnp.maximum(scales, z_perm(scales, PAIRS))

time: 239 us -> 262 us (1.096)
  starting transfers between devices: 48.3 us -> 70 us
  other arithmetic: 14.6 us -> 21.2 us
  Pallas kernels: 37.5 us -> 33.9 us
  waiting for transfers between devices: 115 us -> 112 us
    ppermute x16 -> x20, starting transfers between devices: 34 us -> 53.7 us  [z_perm(): lax.ppermute(value, 'dp', [(a * n_x + i, b * n_x + i) for a, b in pairs f...]
    convert_element_type x0 -> x2, other arithmetic: none -> 6.67 us  [adamw(): return (new_master, new_first, new_second, new_master.astype(BF16))]
    ppermute x16 -> x20, waiting for transfers between devices: 67.7 us -> 61.4 us  [z_perm(): lax.ppermute(value, 'dp', [(a * n_x + i, b * n_x + i) for a, b in pairs f...]
    unnamed x18 -> x34, local copies, waits for them, and re-layouts: 1.01 us -> 7.1 us
    dynamic_update_slice x10 -> x16, local copies, waits for them, and re-layouts: 10.8 us -> 6.25 us  [put(): return lax.dynamic_update_slice(weights, value, (h * half, at))]
    ppermute x10 -> x13, waiting for transfers between devices: 27.9 us -> 32 us  [x_perm(): return lax.ppermute(value, 'dp', pairs)]
    pallas_call x2 -> x1, Pallas kernels: 11 us -> 7.37 us  [update(): pl.pallas_call(kernel, grid=(rows // step,), in_specs=specs + [whole] * 3...]
    ppermute x10 -> x13, starting transfers between devices: 7.71 us -> 10.8 us  [x_perm(): return lax.ppermute(value, 'dp', pairs)]
  transfers between devices with their start and end apart: 35 -> 42, of which waited for: 20 -> 23; matrix products, arithmetic and copies ran while one was open for 14% -> 13% of each run, Pallas kernels for 11% -> 10%
where the time goes in v8:
time: 262 us; the launch traced here: 261 us
  waiting for transfers between devices  112 us (43%)
  starting transfers between devices  70 us (27%)
  Pallas kernels  33.9 us (13%)
  local copies, waits for them, and re-layouts  22.1 us (8%)
  other arithmetic  21.2 us (8%)
    ppermute x20, waiting for transfers between devices, z_perm(): lax.ppermute(value, 'dp', [(a * n_x + i, b * n_x + i) for a, b in pairs f...  61.4 us
    ppermute x20, starting transfers between devices, z_perm(): lax.ppermute(value, 'dp', [(a * n_x + i, b * n_x + i) for a, b in pairs f...  53.7 us
    ppermute x13, waiting for transfers between devices, x_perm(): return lax.ppermute(value, 'dp', pairs)  32 us
    pallas_call x3, Pallas kernels, multiply(): pl.pallas_call(kernel, grid=(rows // step,), in_specs=[pl.BlockSpec((step...  23.7 us
    ppermute x9, waiting for transfers between devices, seat_perm(): lax.ppermute(value, 'tensor', [(i, i ^ flip) for i in range(n_tensor)])  18.9 us
    convert_element_type x8, other arithmetic, add(): return lax.optimization_barrier(total.astype(BF16))  12.1 us
    ppermute x13, starting transfers between devices, x_perm(): return lax.ppermute(value, 'dp', pairs)  10.8 us
    optimization_barrier x1, local copies, waits for them, and re-layouts, after(): return lax.optimization_barrier((value, *earlier))[0] if earlier else value  8.61 us
  transfers between devices with their start and end apart: 42, of which 23 were waited for; matrix products, arithmetic and copies ran while one was open for 13% of the time, Pallas kernels for 10%

profile of v8, /device:TPU:0, one launch (start us, length us, event | category | flops | bytes accessed | tf_op | source)
XLA Modules:
  0.0 260.5 jit_solution(7447937955499755869)
XLA Ops:
  0.6 2.8 %arrange.1 = (bf16[384,256]{1,0:T(8,128)(2,1)}, bf16[384,512]{1,0:T(8,128)(2,1)}, bf16[384,1280]{1,0:T(8,128)(2,1)}) custom-call(bf16[384,2048]{1,0:T(8,128)(2,1)} %cot_ref.1), custom_call_target="tpu_custom_call" | custom-call | tf_op jit(solution)/shard_map/arrange/pallas_call | solution.py:55
  3.4 3.0 %collective-permute-start.1 = (bf16[384,256]{1,0:T(8,128)(2,1)}, bf16[384,256]{1,0:T(8,128)(2,1)S(1)}, u32[]{:S(2)}, u32[]{:S(2)}) collective-permute-start(bf16[384,256]{1,0:T(8,128)(2,1)} %get-tuple-element.101.refs_0_), channel_id=1, source_target_pairs={{0,2},{1,3},{2,0},{3,1},{4,6},{5,7},{6,4},{7,5},{8,10},{9,11},{10,... | collective-permute-start | bytes 589832 | tf_op jit(solution)/shard_map/ppermute | solution.py:196
  6.4 8.6 %copy.12 = bf16[1536,2048]{0,1:T(8,128)(2,1)} copy(bf16[1536,2048]{1,0:T(8,128)(2,1)} %param.5) | data formatting | bytes 12582912 | tf_op jit(solution)/shard_map/optimization_barrier | solution.py:170
  16.8 4.8 %partials.3 = (bf16[2048,256]{1,0:T(8,128)(2,1)S(1)}, f32[4,4,256]{2,1,0:T(4,128)S(1)}) custom-call(bf16[2048,1536]{1,0:T(8,128)(2,1)} %bitcast.17, bf16[384,256]{1,0:T(8,128)(2,1)S(1)} %copy-done.8, bf16[384,256]{1,0:T(8,128)(2,1)S(1)} %collective-permute-done.refs_1_, bf16[384,256]{1,0:T(8,128)(2,1)S(1)} %collective-permute-done.1.refs_2_, ...), custom_call_target="tpu_custom_call" | custom-call | flops 10000000000 | bytes 3145728 | tf_op jit(solution)/shard_map/partials/pallas_call | solution.py:79
  21.6 1.5 collective-permute-start.6
  23.6 1.5 collective-permute-start.8
  25.2 10.0 %collective-permute-done.4.refs_2_ = bf16[384,512]{1,0:T(8,128)(2,1)S(1)} collective-permute-done((bf16[384,512]{1,0:T(8,128)(2,1)S(1)}, bf16[384,512]{1,0:T(8,128)(2,1)S(1)}, u32[]{:S(2)}, u32[]{:S(2)}) %collective-permute-start.4) | collective-permute-done | bytes 393248 | tf_op jit(solution)/shard_map/ppermute | solution.py:196
  35.1 1.7 collective-permute-done.5.refs_3_
  36.8 6.8 %partials.4 = (bf16[2048,256]{1,0:T(8,128)(2,1)S(1)}, bf16[2048,256]{1,0:T(8,128)(2,1)}, f32[4,4,512]{2,1,0:T(4,128)S(1)}) custom-call(bf16[2048,1536]{1,0:T(8,128)(2,1)} %bitcast.18, bf16[384,512]{1,0:T(8,128)(2,1)S(1)} %copy-done.6, bf16[384,512]{1,0:T(8,128)(2,1)S(1)} %collective-permute-done.3.refs_1_, ...), custom_call_target="tpu_custom_call" | custom-call | tf_op jit(solution)/shard_map/partials/pallas_call | solution.py:79
  44.2 3.0 %collective-permute-done.6 = bf16[2048,256]{1,0:T(8,128)(2,1)S(1)} collective-permute-done((bf16[2048,256]{1,0:T(8,128)(2,1)S(1)}, bf16[2048,256]{1,0:T(8,128)(2,1)S(1)}, u32[]{:S(2)}, u32[]{:S(2)}) %collective-permute-start.6) | collective-permute-done | bytes 1048608 | tf_op jit(solution)/shard_map/ppermute | solution.py:193
  47.2 1.1 add_convert_fusion.7
  49.2 6.0 %collective-permute-done.8.refs_2_ = bf16[384,1280]{1,0:T(8,128)(2,1)S(1)} collective-permute-done((bf16[384,1280]{1,0:T(8,128)(2,1)S(1)}, bf16[384,1280]{1,0:T(8,128)(2,1)S(1)}, u32[]{:S(2)}, u32[]{:S(2)}) %collective-permute-start.8) | collective-permute-done | bytes 983072 | tf_op jit(solution)/shard_map/ppermute | solution.py:196
  55.3 3.6 %collective-permute-start.10 = (bf16[1024,256]{1,0:T(8,128)(2,1)}, bf16[1024,256]{1,0:T(8,128)(2,1)S(1)}, u32[]{:S(2)}, u32[]{:S(2)}) collective-permute-start(bf16[1024,256]{1,0:T(8,128)(2,1)} %add_convert_fusion.6), channel_id=1, source_target_pairs={{0,8},{4,12},{24,16},{28,20},{1,9},{5,13},{25,17},{29,21},{2,10},{... | collective-permute-start | bytes 1572872 | tf_op jit(solution)/shard_map/ppermute | solution.py:189
  58.9 1.3 collective-permute-start.11
  60.3 12.1 %partials.5 = (bf16[2048,256]{1,0:T(8,128)(2,1)}, bf16[2048,256]{1,0:T(8,128)(2,1)S(1)}, bf16[2048,256]{1,0:T(8,128)(2,1)}, bf16[2048,256]{1,0:T(8,128)(2,1)}, b...) custom-call(bf16[2048,1536]{1,0:T(8,128)(2,1)} %bitcast.19, bf16[384,1280]{1,0:T(8,128)(2,1)S(1)} %copy-done.5, ...), custom_call_target="tpu_custom_call" | custom-call | tf_op jit(solution)/shard_map/partials/pallas_call | solution.py:79
  73.0 2.9 %add_convert_fusion.1 = bf16[2048,256]{1,0:T(8,128)(2,1)} fusion(bf16[2048,256]{1,0:T(8,128)(2,1)} %collective-permute-done.12, bf16[2048,256]{1,0:T(8,128)(2,1)} %get-tuple-element.139), kind=kLoop, calls=%fused_computation.1 | loop fusion | flops 2097152 | bytes 3145728 | tf_op jit(solution)/shard_map/convert_element_type | solution.py:103
  75.9 2.3 collective-permute-start.15
  78.1 4.6 %collective-permute-done.11 = bf16[1024,256]{1,0:T(8,128)(2,1)S(1)} collective-permute-done((bf16[1024,256]{1,0:T(8,128)(2,1)}, bf16[1024,256]{1,0:T(8,128)(2,1)S(1)}, u32[]{:S(2)}, u32[]{:S(2)}) %collective-permute-start.11) | collective-permute-done | bytes 524320 | tf_op jit(solution)/shard_map/ppermute | solution.py:189
  84.4 1.0 add_convert_fusion.4
  86.7 12.1 %collective-permute-done.16 = bf16[2048,256]{1,0:T(8,128)(2,1)} collective-permute-done((bf16[2048,256]{1,0:T(8,128)(2,1)}, bf16[2048,256]{1,0:T(8,128)(2,1)}, u32[]{:S(2)}, u32[]{:S(2)}) %collective-permute-start.16) | collective-permute-done | bytes 1048608 | tf_op jit(solution)/shard_map/ppermute | solution.py:193
  98.8 1.4 add_convert_fusion.3
  100.1 4.6 %collective-permute-done.15 = bf16[2048,256]{1,0:T(8,128)(2,1)} collective-permute-done((bf16[2048,256]{1,0:T(8,128)(2,1)}, bf16[2048,256]{1,0:T(8,128)(2,1)}, u32[]{:S(2)}, u32[]{:S(2)}) %collective-permute-start.15) | collective-permute-done | bytes 1048608 | tf_op jit(solution)/shard_map/ppermute | solution.py:189
  104.8 2.2 add_convert_fusion
  108.4 7.0 %collective-permute-start.19 = (bf16[1024,256]{1,0:T(8,128)(2,1)S(1)}, bf16[1024,256]{1,0:T(8,128)(2,1)S(1)}, u32[]{:S(2)}, u32[]{:S(2)}) collective-permute-start(bf16[1024,256]{1,0:T(8,128)(2,1)S(1)} %add_convert_fusion.3), channel_id=1, source_target_pairs={{0,8},{4,12},{8,0},{12,4},{16,24},{20,28},{24,16},{28,20},{1,9},{5... | collective-permute-start | bytes 1572872 | tf_op jit(solution)/shard_map/ppermute | solution.py:189
  115.4 11.3 %collective-permute-done.19.refs_3_ = bf16[1024,256]{1,0:T(8,128)(2,1)S(1)} collective-permute-done((bf16[1024,256]{1,0:T(8,128)(2,1)S(1)}, bf16[1024,256]{1,0:T(8,128)(2,1)S(1)}, u32[]{:S(2)}, u32[]{:S(2)}) %collective-permute-start.19) | collective-permute-done | bytes 524320 | tf_op jit(solution)/shard_map/ppermute | solution.py:189
  126.6 1.6 add_convert_fusion.2
  128.3 20.8 %collective-permute-start.21 = (bf16[1024,256]{1,0:T(8,128)(2,1)S(1)}, bf16[1024,256]{1,0:T(8,128)(2,1)S(1)}, u32[]{:S(2)}, u32[]{:S(2)}) collective-permute-start(bf16[1024,256]{1,0:T(8,128)(2,1)S(1)} %add_convert_fusion.2), channel_id=1, source_target_pairs={{0,8},{4,12},{8,0},{12,4},{16,24},{20,28},{24,16},{28,20},{1,9},{5... | collective-permute-start | bytes 1572872 | tf_op jit(solution)/shard_map/ppermute | solution.py:189
  149.6 3.1 %collective-permute-done.13 = f32[16,16]{1,0:T(8,128)S(1)} collective-permute-done((f32[16,16]{1,0:T(8,128)S(1)}, f32[16,16]{1,0:T(8,128)S(1)}, u32[]{:S(2)}, u32[]{:S(2)}) %collective-permute-start.13) | collective-permute-done | bytes 1056 | tf_op jit(solution)/shard_map/ppermute | solution.py:193
  152.8 3.7 %subtract_convert_fusion.1 = bf16[1024,256]{1,0:T(8,128)(2,1)} fusion(f32[2048,256]{1,0:T(8,128)} %refs_7_.1, bf16[1024,256]{1,0:T(8,128)(2,1)S(1)} %collective-permute-done.19.refs_3_, f32[2048,256]{1,0:T(8,128)} %refs_6_.1, f32[2048,256]{1,0:T(8,128)} %refs_5_.1, bf16[2048,256]{1,0:T(8,128)(2,1)S(1)} %collective-permute-done.18.refs_2_, ...), kind=kLoop, calls=%fused_computation.4 | loop fusion | flops 5767168 | bytes 5767168 | tf_op jit(solution)/shard_map/convert_element_type | solution.py:117
  156.5 3.5 %collective-permute-done.21.refs_4_ = bf16[1024,256]{1,0:T(8,128)(2,1)S(1)} collective-permute-done((bf16[1024,256]{1,0:T(8,128)(2,1)S(1)}, bf16[1024,256]{1,0:T(8,128)(2,1)S(1)}, u32[]{:S(2)}, u32[]{:S(2)}) %collective-permute-start.21) | collective-permute-done | bytes 524320 | tf_op jit(solution)/shard_map/ppermute | solution.py:189
  160.0 2.9 %subtract_convert_fusion = bf16[1024,256]{1,0:T(8,128)(2,1)S(1)} fusion(f32[2048,256]{1,0:T(8,128)} %refs_7_.1, bf16[1024,256]{1,0:T(8,128)(2,1)S(1)} %collective-permute-done.21.refs_4_, f32[2048,256]{1,0:T(8,128)} %refs_6_.1, f32[2048,256]{1,0:T(8,128)} %refs_5_.1, bf16[2048,256]{1,0:T(8,128)(2,1)S(1)} %collective-permute-done.18.refs_2_, ...), kind=kLoop, calls=%fused_computation.2 | loop fusion | flops 5767168 | bytes 5767168 | tf_op jit(solution)/shard_map/convert_element_type | solution.py:117
  163.7 1.7 collective-permute-start.22
  165.5 1.5 collective-permute-start.23
  167.5 2.4 collective-permute-start.28
  169.9 1.4 collective-permute-start.29
  171.3 7.4 %collective-permute-done.22 = bf16[1024,256]{1,0:T(8,128)(2,1)} collective-permute-done((bf16[1024,256]{1,0:T(8,128)(2,1)S(1)}, bf16[1024,256]{1,0:T(8,128)(2,1)}, u32[]{:S(2)}, u32[]{:S(2)}) %collective-permute-start.22) | collective-permute-done | bytes 524320 | tf_op jit(solution)/shard_map/ppermute | solution.py:189
  179.3 1.6 collective-permute-done.24
  181.6 1.5 collective-permute-start.25
  183.1 1.3 collective-permute-start.26
  184.4 5.6 %collective-permute-done.28 = bf16[1024,256]{1,0:T(8,128)(2,1)} collective-permute-done((bf16[1024,256]{1,0:T(8,128)(2,1)}, bf16[1024,256]{1,0:T(8,128)(2,1)}, u32[]{:S(2)}, u32[]{:S(2)}) %collective-permute-start.28) | collective-permute-done | bytes 524320 | tf_op jit(solution)/shard_map/ppermute | solution.py:189
  190.5 1.0 copy-done.2
  191.5 1.0 copy-done.4
  192.6 7.4 %states.1 = (f32[2048,256]{1,0:T(8,128)}, f32[2048,256]{1,0:T(8,128)}, f32[2048,256]{1,0:T(8,128)}) custom-call(bf16[2048,256]{1,0:T(8,128)(2,1)S(1)} %copy-done, bf16[2048,256]{1,0:T(8,128)(2,1)S(1)} %collective-permute-done.14.refs_1_, bf16[2048,256]{1,0:T(8,128)(2,1)S(1)} %collective-permute-done.18.refs_2_, bf16[1024,256]{1,0:T(8,128)(2,1)S(1)} %copy-done.2, ...), custom_call_target="tpu_custom_call" | custom-call | tf_op jit(solution)/shard_map/states/pallas_call | solution.py:147
  200.7 1.5 collective-permute-start.33
  202.2 1.3 collective-permute-start.32
  204.1 1.1 broadcast_select_fusion.3
  205.3 1.1 constant_dynamic-update-slice_fusion.15
  206.4 1.1 constant_dynamic-update-slice_fusion.14
  207.6 6.0 %collective-permute-done.32 = bf16[1024,256]{1,0:T(8,128)(2,1)S(1)} collective-permute-done((bf16[1024,256]{1,0:T(8,128)(2,1)}, bf16[1024,256]{1,0:T(8,128)(2,1)S(1)}, u32[]{:S(2)}, u32[]{:S(2)}) %collective-permute-start.32) | collective-permute-done | bytes 524320 | tf_op jit(solution)/shard_map/ppermute | solution.py:189
  213.6 2.2 collective-permute-done.33
  215.8 1.3 collective-permute-start.34
  217.1 1.3 collective-permute-start.35
  218.5 1.5 collective-permute-start.36
  220.1 1.1 constant_dynamic-update-slice_fusion.13
  221.3 1.1 constant_dynamic-update-slice_fusion.5
  222.4 1.1 constant_dynamic-update-slice_fusion.4
  223.5 12.5 %collective-permute-done.35 = bf16[1024,256]{1,0:T(8,128)(2,1)S(1)} collective-permute-done((bf16[1024,256]{1,0:T(8,128)(2,1)S(1)}, bf16[1024,256]{1,0:T(8,128)(2,1)S(1)}, u32[]{:S(2)}, u32[]{:S(2)}) %collective-permute-start.35) | collective-permute-done | bytes 524320 | tf_op jit(solution)/shard_map/ppermute | solution.py:189
  236.8 1.5 collective-permute-start.39
  239.4 3.0 %collective-permute-done.40 = f32[16,16]{1,0:T(8,128)S(1)} collective-permute-done((f32[16,16]{1,0:T(8,128)S(1)}, f32[16,16]{1,0:T(8,128)S(1)}, u32[]{:S(2)}, u32[]{:S(2)}) %collective-permute-start.40) | collective-permute-done | bytes 1056 | tf_op jit(solution)/shard_map/ppermute | solution.py:189
  242.4 1.6 collective-permute-start.41
  244.0 2.9 %collective-permute-done.41 = f32[16,16]{1,0:T(8,128)S(1)} collective-permute-done((f32[16,16]{1,0:T(8,128)S(1)}, f32[16,16]{1,0:T(8,128)S(1)}, u32[]{:S(2)}, u32[]{:S(2)}) %collective-permute-start.41) | collective-permute-done | bytes 1056 | tf_op jit(solution)/shard_map/ppermute | solution.py:189
  247.5 3.5 %collective-permute-done.38 = bf16[1024,256]{1,0:T(8,128)(2,1)S(1)} collective-permute-done((bf16[1024,256]{1,0:T(8,128)(2,1)S(1)}, bf16[1024,256]{1,0:T(8,128)(2,1)S(1)}, u32[]{:S(2)}, u32[]{:S(2)}) %collective-permute-start.38) | collective-permute-done | bytes 524320 | tf_op jit(solution)/shard_map/ppermute | solution.py:193
  251.1 6.0 %collective-permute-done.39 = bf16[1024,256]{1,0:T(8,128)(2,1)S(1)} collective-permute-done((bf16[1024,256]{1,0:T(8,128)(2,1)S(1)}, bf16[1024,256]{1,0:T(8,128)(2,1)S(1)}, u32[]{:S(2)}, u32[]{:S(2)}) %collective-permute-start.39) | collective-permute-done | bytes 524320 | tf_op jit(solution)/shard_map/ppermute | solution.py:193
  257.1 3.4 %copy-done.10 = bf16[2048,2048]{1,0:T(8,128)(2,1)} copy-done((bf16[2048,2048]{1,0:T(8,128)(2,1)}, bf16[2048,2048]{1,0:T(8,128)(2,1)S(1)}, u32[]{:S(2)}) %copy-start.10) | copy-done | bytes 8388632
  (104 shorter events, 16.8 us)
Async XLA Ops:
  3.4 11.6 %copy-start.8 = (bf16[384,256]{1,0:T(8,128)(2,1)S(1)}, bf16[384,256]{1,0:T(8,128)(2,1)}, u32[]{:S(2)}) copy-start(bf16[384,256]{1,0:T(8,128)(2,1)} %get-tuple-element.101.refs_0_) | copy-start | bytes 589828
  3.4 11.7 %collective-permute-start.1 = (bf16[384,256]{1,0:T(8,128)(2,1)}, bf16[384,256]{1,0:T(8,128)(2,1)S(1)}, u32[]{:S(2)}, u32[]{:S(2)}) collective-permute-start(bf16[384,256]{1,0:T(8,128)(2,1)} %get-tuple-element.101.refs_0_), channel_id=1, source_target_pairs={{0,2},{1,3},{2,0},{3,1},{4,6},{5,7},{6,4},{7,5},{8,10},{9,11},{10,... | collective-permute-start | bytes 589832 | tf_op jit(solution)/shard_map/ppermute | solution.py:196
  15.0 8.1 %copy-start.6 = (bf16[384,512]{1,0:T(8,128)(2,1)S(1)}, bf16[384,512]{1,0:T(8,128)(2,1)}, u32[]{:S(2)}) copy-start(bf16[384,512]{1,0:T(8,128)(2,1)} %get-tuple-element.105.refs_0_) | copy-start | bytes 1179652
  15.0 8.7 %copy-start.5 = (bf16[384,1280]{1,0:T(8,128)(2,1)S(1)}, bf16[384,1280]{1,0:T(8,128)(2,1)}, u32[]{:S(2)}) copy-start(bf16[384,1280]{1,0:T(8,128)(2,1)} %get-tuple-element.113.refs_0_) | copy-start | bytes 2949124
  15.0 1.5 collective-permute-start
  15.1 1.7 collective-permute-start.2
  21.6 25.6 %collective-permute-start.6 = (bf16[2048,256]{1,0:T(8,128)(2,1)S(1)}, bf16[2048,256]{1,0:T(8,128)(2,1)S(1)}, u32[]{:S(2)}, u32[]{:S(2)}) collective-permute-start(bf16[2048,256]{1,0:T(8,128)(2,1)S(1)} %get-tuple-element.103), channel_id=1, source_target_pairs={{0,4},{4,0},{8,12},{12,8},{16,20},{20,16},{24,28},{28,24},{1,5},{5... | collective-permute-start | bytes 3145736 | tf_op jit(solution)/shard_map/ppermute | solution.py:193
  23.1 12.0 %collective-permute-start.4 = (bf16[384,512]{1,0:T(8,128)(2,1)S(1)}, bf16[384,512]{1,0:T(8,128)(2,1)S(1)}, u32[]{:S(2)}, u32[]{:S(2)}) collective-permute-start(bf16[384,512]{1,0:T(8,128)(2,1)S(1)} %copy-done.6), channel_id=1, source_target_pairs={{0,2},{1,3},{2,0},{3,1},{4,6},{5,7},{6,4},{7,5},{8,10},{9,11},{10,... | collective-permute-start | bytes 1179656 | tf_op jit(solution)/shard_map/ppermute | solution.py:196
  23.6 31.5 %collective-permute-start.8 = (bf16[384,1280]{1,0:T(8,128)(2,1)S(1)}, bf16[384,1280]{1,0:T(8,128)(2,1)S(1)}, u32[]{:S(2)}, u32[]{:S(2)}) collective-permute-start(bf16[384,1280]{1,0:T(8,128)(2,1)S(1)} %copy-done.5), channel_id=1, source_target_pairs={{0,2},{1,3},{2,0},{3,1},{4,6},{5,7},{6,4},{7,5},{8,10},{9,11},{10,... | collective-permute-start | bytes 2949128 | tf_op jit(solution)/shard_map/ppermute | solution.py:196
  25.2 10.0 %collective-permute-start.3 = (bf16[384,512]{1,0:T(8,128)(2,1)S(1)}, bf16[384,512]{1,0:T(8,128)(2,1)S(1)}, u32[]{:S(2)}, u32[]{:S(2)}) collective-permute-start(bf16[384,512]{1,0:T(8,128)(2,1)S(1)} %copy-done.6), channel_id=1, source_target_pairs={{0,1},{1,0},{2,3},{3,2},{4,5},{5,4},{6,7},{7,6},{8,9},{9,8},{10,11... | collective-permute-start | bytes 1179656 | tf_op jit(solution)/shard_map/ppermute | solution.py:196
  35.1 1.7 collective-permute-start.5
  43.7 29.3 %collective-permute-start.12 = (bf16[2048,256]{1,0:T(8,128)(2,1)}, bf16[2048,256]{1,0:T(8,128)(2,1)}, u32[]{:S(2)}, u32[]{:S(2)}) collective-permute-start(bf16[2048,256]{1,0:T(8,128)(2,1)} %get-tuple-element.118), channel_id=1, source_target_pairs={{0,4},{4,0},{8,12},{12,8},{16,20},{20,16},{24,28},{28,24},{1,5},{5... | collective-permute-start | bytes 3145736 | tf_op jit(solution)/shard_map/ppermute | solution.py:193
  47.2 8.0 %copy-start.11 = (bf16[2048,256]{1,0:T(8,128)(2,1)}, bf16[2048,256]{1,0:T(8,128)(2,1)S(1)}, u32[]{:S(2)}) copy-start(bf16[2048,256]{1,0:T(8,128)(2,1)S(1)} %collective-permute-done.6) | copy-start | bytes 3145732
  49.2 11.1 %collective-permute-start.7 = (bf16[384,1280]{1,0:T(8,128)(2,1)S(1)}, bf16[384,1280]{1,0:T(8,128)(2,1)}, u32[]{:S(2)}, u32[]{:S(2)}) collective-permute-start(bf16[384,1280]{1,0:T(8,128)(2,1)S(1)} %copy-done.5), channel_id=1, source_target_pairs={{0,1},{1,0},{2,3},{3,2},{4,5},{5,4},{6,7},{7,6},{8,9},{9,8},{10,11... | collective-permute-start | bytes 2949128 | tf_op jit(solution)/shard_map/ppermute | solution.py:196
  55.2 5.1 %collective-permute-start.9 = (bf16[384,1280]{1,0:T(8,128)(2,1)S(1)}, bf16[384,1280]{1,0:T(8,128)(2,1)}, u32[]{:S(2)}, u32[]{:S(2)}) collective-permute-start(bf16[384,1280]{1,0:T(8,128)(2,1)S(1)} %collective-permute-done.8.refs_2_), channel_id=1, source_target_pairs={{0,1},{1,0},{2,3},{3,2},{4,5},{5,4},{6,7},{7,6},{8,9},{9,8},{10,11... | collective-permute-start | bytes 2949128 | tf_op jit(solution)/shard_map/ppermute | solution.py:196
  55.3 27.4 %copy-start.12 = (bf16[2048,256]{1,0:T(8,128)(2,1)S(1)}, bf16[2048,256]{1,0:T(8,128)(2,1)}, u32[]{:S(2)}) copy-start(bf16[2048,256]{1,0:T(8,128)(2,1)} %copy-done.11) | copy-start | bytes 3145732
  55.3 29.1 %collective-permute-start.10 = (bf16[1024,256]{1,0:T(8,128)(2,1)}, bf16[1024,256]{1,0:T(8,128)(2,1)S(1)}, u32[]{:S(2)}, u32[]{:S(2)}) collective-permute-start(bf16[1024,256]{1,0:T(8,128)(2,1)} %add_convert_fusion.6), channel_id=1, source_target_pairs={{0,8},{4,12},{24,16},{28,20},{1,9},{5,13},{25,17},{29,21},{2,10},{... | collective-permute-start | bytes 1572872 | tf_op jit(solution)/shard_map/ppermute | solution.py:189
  58.9 23.7 %collective-permute-start.11 = (bf16[1024,256]{1,0:T(8,128)(2,1)}, bf16[1024,256]{1,0:T(8,128)(2,1)S(1)}, u32[]{:S(2)}, u32[]{:S(2)}) collective-permute-start(bf16[1024,256]{1,0:T(8,128)(2,1)} %add_convert_fusion.7), channel_id=1, source_target_pairs={{0,8},{4,12},{24,16},{28,20},{1,9},{5,13},{25,17},{29,21},{2,10},{... | collective-permute-start | bytes 1572872 | tf_op jit(solution)/shard_map/ppermute | solution.py:189
  72.4 13.1 %copy-start.7 = (bf16[2048,256]{1,0:T(8,128)(2,1)}, bf16[2048,256]{1,0:T(8,128)(2,1)S(1)}, u32[]{:S(2)}) copy-start(bf16[2048,256]{1,0:T(8,128)(2,1)S(1)} %get-tuple-element.134) | copy-start | bytes 3145732
  72.4 80.4 %copy-start = (bf16[2048,256]{1,0:T(8,128)(2,1)S(1)}, bf16[2048,256]{1,0:T(8,128)(2,1)}, u32[]{:S(2)}) copy-start(bf16[2048,256]{1,0:T(8,128)(2,1)} %get-tuple-element.160.refs_0_) | copy-start | bytes 3145732
  72.4 26.4 %collective-permute-start.16 = (bf16[2048,256]{1,0:T(8,128)(2,1)}, bf16[2048,256]{1,0:T(8,128)(2,1)}, u32[]{:S(2)}, u32[]{:S(2)}) collective-permute-start(bf16[2048,256]{1,0:T(8,128)(2,1)} %get-tuple-element.119), channel_id=1, source_target_pairs={{0,4},{4,0},{8,12},{12,8},{16,20},{20,16},{24,28},{28,24},{1,5},{5... | collective-permute-start | bytes 3145736 | tf_op jit(solution)/shard_map/ppermute | solution.py:193
  75.9 28.9 %collective-permute-start.15 = (bf16[2048,256]{1,0:T(8,128)(2,1)}, bf16[2048,256]{1,0:T(8,128)(2,1)}, u32[]{:S(2)}, u32[]{:S(2)}) collective-permute-start(bf16[2048,256]{1,0:T(8,128)(2,1)} %add_convert_fusion.1), channel_id=1, source_target_pairs={{0,8},{4,12},{24,16},{28,20},{1,9},{5,13},{25,17},{29,21},{2,10},{... | collective-permute-start | bytes 3145736 | tf_op jit(solution)/shard_map/ppermute | solution.py:189
  83.7 3.0 %collective-permute-start.17 = (bf16[1024,256]{1,0:T(8,128)(2,1)}, bf16[1024,256]{1,0:T(8,128)(2,1)S(1)}, u32[]{:S(2)}, u32[]{:S(2)}) collective-permute-start(bf16[1024,256]{1,0:T(8,128)(2,1)} %add_convert_fusion.5), channel_id=1, source_target_pairs={{8,16},{12,20},{16,8},{20,12},{9,17},{13,21},{17,9},{21,13},{10,18... | collective-permute-start | bytes 1572872 | tf_op jit(solution)/shard_map/ppermute | solution.py:189
  85.8 66.9 %collective-permute-start.14 = (bf16[2048,256]{1,0:T(8,128)(2,1)}, bf16[2048,256]{1,0:T(8,128)(2,1)S(1)}, u32[]{:S(2)}, u32[]{:S(2)}) collective-permute-start(bf16[2048,256]{1,0:T(8,128)(2,1)} %copy-done.7), channel_id=1, source_target_pairs={{0,4},{4,0},{8,12},{12,8},{16,20},{20,16},{24,28},{28,24},{1,5},{5... | collective-permute-start | bytes 3145736 | tf_op jit(solution)/shard_map/ppermute | solution.py:193
  107.0 45.8 %collective-permute-start.18 = (bf16[2048,256]{1,0:T(8,128)(2,1)S(1)}, bf16[2048,256]{1,0:T(8,128)(2,1)S(1)}, u32[]{:S(2)}, u32[]{:S(2)}) collective-permute-start(bf16[2048,256]{1,0:T(8,128)(2,1)S(1)} %add_convert_fusion), channel_id=1, source_target_pairs={{8,16},{12,20},{16,8},{20,12},{9,17},{13,21},{17,9},{21,13},{10,18... | collective-permute-start | bytes 3145736 | tf_op jit(solution)/shard_map/ppermute | solution.py:189
  107.7 7.7 %collective-permute-start.20 = (bf16[1024,256]{1,0:T(8,128)(2,1)}, bf16[1024,256]{1,0:T(8,128)(2,1)S(1)}, u32[]{:S(2)}, u32[]{:S(2)}) collective-permute-start(bf16[1024,256]{1,0:T(8,128)(2,1)} %add_convert_fusion.4), channel_id=1, source_target_pairs={{8,16},{12,20},{16,8},{20,12},{9,17},{13,21},{17,9},{21,13},{10,18... | collective-permute-start | bytes 1572872 | tf_op jit(solution)/shard_map/ppermute | solution.py:189
  108.4 18.2 %collective-permute-start.19 = (bf16[1024,256]{1,0:T(8,128)(2,1)S(1)}, bf16[1024,256]{1,0:T(8,128)(2,1)S(1)}, u32[]{:S(2)}, u32[]{:S(2)}) collective-permute-start(bf16[1024,256]{1,0:T(8,128)(2,1)S(1)} %add_convert_fusion.3), channel_id=1, source_target_pairs={{0,8},{4,12},{8,0},{12,4},{16,24},{20,28},{24,16},{28,20},{1,9},{5... | collective-permute-start | bytes 1572872 | tf_op jit(solution)/shard_map/ppermute | solution.py:189
  126.6 26.1 %copy-start.1 = (bf16[1024,256]{1,0:T(8,128)(2,1)}, bf16[1024,256]{1,0:T(8,128)(2,1)S(1)}, u32[]{:S(2)}) copy-start(bf16[1024,256]{1,0:T(8,128)(2,1)S(1)} %collective-permute-done.19.refs_3_) | copy-start | bytes 1572868
  128.3 31.7 %collective-permute-start.21 = (bf16[1024,256]{1,0:T(8,128)(2,1)S(1)}, bf16[1024,256]{1,0:T(8,128)(2,1)S(1)}, u32[]{:S(2)}, u32[]{:S(2)}) collective-permute-start(bf16[1024,256]{1,0:T(8,128)(2,1)S(1)} %add_convert_fusion.2), channel_id=1, source_target_pairs={{0,8},{4,12},{8,0},{12,4},{16,24},{20,28},{24,16},{28,20},{1,9},{5... | collective-permute-start | bytes 1572872 | tf_op jit(solution)/shard_map/ppermute | solution.py:189
  149.1 3.7 %collective-permute-start.13 = (f32[16,16]{1,0:T(8,128)S(1)}, f32[16,16]{1,0:T(8,128)S(1)}, u32[]{:S(2)}, u32[]{:S(2)}) collective-permute-start(f32[16,16]{1,0:T(8,128)S(1)} %select_reduce_fusion), channel_id=1, source_target_pairs={{0,4},{4,0},{8,12},{12,8},{16,20},{20,16},{24,28},{28,24},{1,5},{5... | collective-permute-start | bytes 3080 | tf_op jit(solution)/shard_map/ppermute | solution.py:193
  162.9 0.8 copy-start.3
  163.7 3.2 %copy-start.13 = (bf16[1024,256]{1,0:T(8,128)(2,1)}, bf16[1024,256]{1,0:T(8,128)(2,1)S(1)}, u32[]{:S(2)}) copy-start(bf16[1024,256]{1,0:T(8,128)(2,1)S(1)} %subtract_convert_fusion) | copy-start | bytes 1572868
  163.7 15.0 %collective-permute-start.22 = (bf16[1024,256]{1,0:T(8,128)(2,1)S(1)}, bf16[1024,256]{1,0:T(8,128)(2,1)}, u32[]{:S(2)}, u32[]{:S(2)}) collective-permute-start(bf16[1024,256]{1,0:T(8,128)(2,1)S(1)} %subtract_convert_fusion), channel_id=1, source_target_pairs={{0,8},{4,12},{8,0},{12,4},{16,24},{20,28},{24,16},{28,20},{1,9},{5... | collective-permute-start | bytes 1572872 | tf_op jit(solution)/shard_map/ppermute | solution.py:189
  165.5 13.8 %collective-permute-start.23 = (bf16[1024,256]{1,0:T(8,128)(2,1)S(1)}, bf16[1024,256]{1,0:T(8,128)(2,1)}, u32[]{:S(2)}, u32[]{:S(2)}) collective-permute-start(bf16[1024,256]{1,0:T(8,128)(2,1)S(1)} %subtract_convert_fusion), channel_id=1, source_target_pairs={{8,16},{12,20},{16,8},{20,12},{9,17},{13,21},{17,9},{21,13},{10,18... | collective-permute-start | bytes 1572872 | tf_op jit(solution)/shard_map/ppermute | solution.py:189
  167.0 13.9 %collective-permute-start.24 = (bf16[1024,256]{1,0:T(8,128)(2,1)S(1)}, bf16[1024,256]{1,0:T(8,128)(2,1)S(1)}, u32[]{:S(2)}, u32[]{:S(2)}) collective-permute-start(bf16[1024,256]{1,0:T(8,128)(2,1)S(1)} %subtract_convert_fusion), channel_id=1, source_target_pairs={{0,4},{4,0},{8,12},{12,8},{16,20},{20,16},{24,28},{28,24},{1,5},{5... | collective-permute-start | bytes 1572872 | tf_op jit(solution)/shard_map/ppermute | solution.py:193
  167.5 22.4 %collective-permute-start.28 = (bf16[1024,256]{1,0:T(8,128)(2,1)}, bf16[1024,256]{1,0:T(8,128)(2,1)}, u32[]{:S(2)}, u32[]{:S(2)}) collective-permute-start(bf16[1024,256]{1,0:T(8,128)(2,1)} %subtract_convert_fusion.1), channel_id=1, source_target_pairs={{0,8},{4,12},{8,0},{12,4},{16,24},{20,28},{24,16},{28,20},{1,9},{5... | collective-permute-start | bytes 1572872 | tf_op jit(solution)/shard_map/ppermute | solution.py:189
  169.9 30.1 %collective-permute-start.29 = (bf16[1024,256]{1,0:T(8,128)(2,1)}, bf16[1024,256]{1,0:T(8,128)(2,1)}, u32[]{:S(2)}, u32[]{:S(2)}) collective-permute-start(bf16[1024,256]{1,0:T(8,128)(2,1)} %subtract_convert_fusion.1), channel_id=1, source_target_pairs={{8,16},{12,20},{16,8},{20,12},{9,17},{13,21},{17,9},{21,13},{10,18... | collective-permute-start | bytes 1572872 | tf_op jit(solution)/shard_map/ppermute | solution.py:189
  178.7 21.3 %collective-permute-start.30 = (bf16[1024,256]{1,0:T(8,128)(2,1)}, bf16[1024,256]{1,0:T(8,128)(2,1)}, u32[]{:S(2)}, u32[]{:S(2)}) collective-permute-start(bf16[1024,256]{1,0:T(8,128)(2,1)} %subtract_convert_fusion.1), channel_id=1, source_target_pairs={{0,4},{4,0},{8,12},{12,8},{16,20},{20,16},{24,28},{28,24},{1,5},{5... | collective-permute-start | bytes 1572872 | tf_op jit(solution)/shard_map/ppermute | solution.py:193
  180.8 0.8 copy-start.15
  181.6 20.6 %collective-permute-start.25 = (bf16[1024,256]{1,0:T(8,128)(2,1)}, bf16[1024,256]{1,0:T(8,128)(2,1)}, u32[]{:S(2)}, u32[]{:S(2)}) collective-permute-start(bf16[1024,256]{1,0:T(8,128)(2,1)} %collective-permute-done.22), channel_id=1, source_target_pairs={{8,16},{12,20},{16,8},{20,12},{9,17},{13,21},{17,9},{21,13},{10,18... | collective-permute-start | bytes 1572872 | tf_op jit(solution)/shard_map/ppermute | solution.py:189
  183.1 20.4 %collective-permute-start.26 = (bf16[1024,256]{1,0:T(8,128)(2,1)}, bf16[1024,256]{1,0:T(8,128)(2,1)}, u32[]{:S(2)}, u32[]{:S(2)}) collective-permute-start(bf16[1024,256]{1,0:T(8,128)(2,1)} %collective-permute-done.23), channel_id=1, source_target_pairs={{8,0},{12,4},{16,24},{20,28},{9,1},{13,5},{17,25},{21,29},{10,2},{... | collective-permute-start | bytes 1572872 | tf_op jit(solution)/shard_map/ppermute | solution.py:189
  189.9 14.2 %collective-permute-start.27 = (bf16[1024,256]{1,0:T(8,128)(2,1)}, bf16[1024,256]{1,0:T(8,128)(2,1)}, u32[]{:S(2)}, u32[]{:S(2)}) collective-permute-start(bf16[1024,256]{1,0:T(8,128)(2,1)} %collective-permute-done.22), channel_id=1, source_target_pairs={{0,4},{4,0},{8,12},{12,8},{16,20},{20,16},{24,28},{28,24},{1,5},{5... | collective-permute-start | bytes 1572872 | tf_op jit(solution)/shard_map/ppermute | solution.py:193
  190.5 1.0 copy-start.2
  191.5 1.0 copy-start.4
  192.6 12.7 %copy-start.9 = (bf16[2048,2048]{1,0:T(8,128)(2,1)S(1)}, bf16[2048,2048]{1,0:T(8,128)(2,1)}, u32[]{:S(2)}) copy-start(bf16[2048,2048]{1,0:T(8,128)(2,1)} %blank.1) | copy-start | bytes 25165828
  192.6 15.0 %copy-start.14 = (bf16[1024,256]{1,0:T(8,128)(2,1)S(1)}, bf16[1024,256]{1,0:T(8,128)(2,1)}, u32[]{:S(2)}) copy-start(bf16[1024,256]{1,0:T(8,128)(2,1)} %copy-done.13) | copy-start | bytes 1572868
  192.6 27.4 %copy-start.16 = (bf16[1024,256]{1,0:T(8,128)(2,1)S(1)}, bf16[1024,256]{1,0:T(8,128)(2,1)}, u32[]{:S(2)}) copy-start(bf16[1024,256]{1,0:T(8,128)(2,1)} %copy-done.15) | copy-start | bytes 1572868
  200.0 7.7 %collective-permute-start.31 = (bf16[1024,256]{1,0:T(8,128)(2,1)}, bf16[1024,256]{1,0:T(8,128)(2,1)S(1)}, u32[]{:S(2)}, u32[]{:S(2)}) collective-permute-start(bf16[1024,256]{1,0:T(8,128)(2,1)} %collective-permute-done.28), channel_id=1, source_target_pairs={{8,16},{12,20},{16,8},{20,12},{9,17},{13,21},{17,9},{21,13},{10,18... | collective-permute-start | bytes 1572872 | tf_op jit(solution)/shard_map/ppermute | solution.py:189
  200.7 15.1 %collective-permute-start.33 = (bf16[1024,256]{1,0:T(8,128)(2,1)}, bf16[1024,256]{1,0:T(8,128)(2,1)S(1)}, u32[]{:S(2)}, u32[]{:S(2)}) collective-permute-start(bf16[1024,256]{1,0:T(8,128)(2,1)} %collective-permute-done.28), channel_id=1, source_target_pairs={{0,4},{4,0},{8,12},{12,8},{16,20},{20,16},{24,28},{28,24},{1,5},{5... | collective-permute-start | bytes 1572872 | tf_op jit(solution)/shard_map/ppermute | solution.py:193
  202.2 11.4 %collective-permute-start.32 = (bf16[1024,256]{1,0:T(8,128)(2,1)}, bf16[1024,256]{1,0:T(8,128)(2,1)S(1)}, u32[]{:S(2)}, u32[]{:S(2)}) collective-permute-start(bf16[1024,256]{1,0:T(8,128)(2,1)} %collective-permute-done.29), channel_id=1, source_target_pairs={{8,0},{12,4},{16,24},{20,28},{9,1},{13,5},{17,25},{21,29},{10,2},{... | collective-permute-start | bytes 1572872 | tf_op jit(solution)/shard_map/ppermute | solution.py:189
  205.2 38.7 %collective-permute-start.37 = (bf16[1024,256]{1,0:T(8,128)(2,1)S(1)}, bf16[1024,256]{1,0:T(8,128)(2,1)S(1)}, u32[]{:S(2)}, u32[]{:S(2)}) collective-permute-start(bf16[1024,256]{1,0:T(8,128)(2,1)S(1)} %broadcast_select_fusion.3), channel_id=1, source_target_pairs={{0,4},{4,0},{8,12},{12,8},{16,20},{20,16},{24,28},{28,24},{1,5},{5... | collective-permute-start | bytes 1572872 | tf_op jit(solution)/shard_map/ppermute | solution.py:193
  215.8 20.9 %collective-permute-start.34 = (bf16[1024,256]{1,0:T(8,128)(2,1)}, bf16[1024,256]{1,0:T(8,128)(2,1)S(1)}, u32[]{:S(2)}, u32[]{:S(2)}) collective-permute-start(bf16[1024,256]{1,0:T(8,128)(2,1)} %collective-permute-done.25), channel_id=1, source_target_pairs={{8,0},{12,4},{16,24},{20,28},{9,1},{13,5},{17,25},{21,29},{10,2},{... | collective-permute-start | bytes 1572872 | tf_op jit(solution)/shard_map/ppermute | solution.py:189
  217.1 19.0 %collective-permute-start.35 = (bf16[1024,256]{1,0:T(8,128)(2,1)S(1)}, bf16[1024,256]{1,0:T(8,128)(2,1)S(1)}, u32[]{:S(2)}, u32[]{:S(2)}) collective-permute-start(bf16[1024,256]{1,0:T(8,128)(2,1)S(1)} %collective-permute-done.31), channel_id=1, source_target_pairs={{8,0},{12,4},{16,24},{20,28},{9,1},{13,5},{17,25},{21,29},{10,2},{... | collective-permute-start | bytes 1572872 | tf_op jit(solution)/shard_map/ppermute | solution.py:189
  218.5 20.8 %collective-permute-start.36 = (bf16[1024,256]{1,0:T(8,128)(2,1)S(1)}, bf16[1024,256]{1,0:T(8,128)(2,1)S(1)}, u32[]{:S(2)}, u32[]{:S(2)}) collective-permute-start(bf16[1024,256]{1,0:T(8,128)(2,1)S(1)} %broadcast_select_fusion), channel_id=1, source_target_pairs={{0,4},{4,0},{8,12},{12,8},{16,20},{20,16},{24,28},{28,24},{1,5},{5... | collective-permute-start | bytes 1572872 | tf_op jit(solution)/shard_map/ppermute | solution.py:193
  236.1 14.9 %collective-permute-start.38 = (bf16[1024,256]{1,0:T(8,128)(2,1)S(1)}, bf16[1024,256]{1,0:T(8,128)(2,1)S(1)}, u32[]{:S(2)}, u32[]{:S(2)}) collective-permute-start(bf16[1024,256]{1,0:T(8,128)(2,1)S(1)} %broadcast_select_fusion.2), channel_id=1, source_target_pairs={{0,4},{4,0},{8,12},{12,8},{16,20},{20,16},{24,28},{28,24},{1,5},{5... | collective-permute-start | bytes 1572872 | tf_op jit(solution)/shard_map/ppermute | solution.py:193
  236.8 20.3 %collective-permute-start.39 = (bf16[1024,256]{1,0:T(8,128)(2,1)S(1)}, bf16[1024,256]{1,0:T(8,128)(2,1)S(1)}, u32[]{:S(2)}, u32[]{:S(2)}) collective-permute-start(bf16[1024,256]{1,0:T(8,128)(2,1)S(1)} %broadcast_select_fusion.1), channel_id=1, source_target_pairs={{0,4},{4,0},{8,12},{12,8},{16,20},{20,16},{24,28},{28,24},{1,5},{5... | collective-permute-start | bytes 1572872 | tf_op jit(solution)/shard_map/ppermute | solution.py:193
  238.6 3.7 %collective-permute-start.40 = (f32[16,16]{1,0:T(8,128)S(1)}, f32[16,16]{1,0:T(8,128)S(1)}, u32[]{:S(2)}, u32[]{:S(2)}) collective-permute-start(f32[16,16]{1,0:T(8,128)S(1)} %max.9), channel_id=1, source_target_pairs={{0,8},{4,12},{8,0},{12,4},{16,24},{20,28},{24,16},{28,20},{1,9},{5... | collective-permute-start | bytes 3080 | tf_op jit(solution)/shard_map/ppermute | solution.py:189
  242.4 4.6 %collective-permute-start.41 = (f32[16,16]{1,0:T(8,128)S(1)}, f32[16,16]{1,0:T(8,128)S(1)}, u32[]{:S(2)}, u32[]{:S(2)}) collective-permute-start(f32[16,16]{1,0:T(8,128)S(1)} %max.10), channel_id=1, source_target_pairs={{0,16},{4,20},{8,24},{12,28},{16,0},{20,4},{24,8},{28,12},{1,17},{... | collective-permute-start | bytes 3080 | tf_op jit(solution)/shard_map/ppermute | solution.py:189
  257.1 3.4 %copy-start.10 = (bf16[2048,2048]{1,0:T(8,128)(2,1)}, bf16[2048,2048]{1,0:T(8,128)(2,1)S(1)}, u32[]{:S(2)}) copy-start(bf16[2048,2048]{1,0:T(8,128)(2,1)S(1)} %constant_dynamic-update-slice_fusion) | copy-start | bytes 25165828

commit v9 on v8

--- a/solution.py
+++ b/solution.py
@@ -117,7 +117,7 @@
     return new_master, new_first, new_second, new_master.astype(BF16)
 
 
-def update(terms, states, factor, wanted, name):
+def update(terms, states, factor, wanted, name, split=False):
     rows, width = states[0].shape
     step = min(rows // 2, 512)
     half = rows // 2 // step
@@ -135,8 +135,16 @@
                 values.append(ins[at][...])
                 at += 1
         results = adamw(values, [ref[...] for ref in ins[at:]], factor)
-        for out, k in zip(outs, wanted):
-            out[...] = results[k]
+        if split:
+            for k, out in enumerate(outs):
+
+                @pl.when(pl.program_id(0) // half == k)
+                def _(out=out):
+                    out[...] = results[wanted[0]]
+
+        else:
+            for out, k in zip(outs, wanted):
+                out[...] = results[k]
 
     whole = pl.BlockSpec((step, width), lambda i: (i, 0))
     halves = [
@@ -148,8 +156,10 @@
         kernel,
         grid=(rows // step,),
         in_specs=specs + [whole] * 3,
-        out_specs=[whole] * len(wanted),
-        out_shape=[jax.ShapeDtypeStruct((rows, width), dtype) for dtype in dtypes],
+        out_specs=halves if split else [whole] * len(wanted),
+        out_shape=[jax.ShapeDtypeStruct((rows // 2, width), dtypes[0])] * 2
+        if split
+        else [jax.ShapeDtypeStruct((rows, width), dtype) for dtype in dtypes],
         compiler_params=pltpu.CompilerParams(vmem_limit_bytes=48 * 1024 * 1024),
         cost_estimate=FREE,
         name=name,
@@ -260,15 +270,8 @@
     terms = [after(partial[3, 0], *scales_x), *got3, last, tuple(pairs)]
     states = [master, first_moment, second_moment]
     factor = 1.0 / math.sqrt(acts.shape[0] * n_dp)
-    owned = []
-    for h in halves:
-        held = lax.optimization_barrier((*terms[:-1], *states, pairs[h]))
-        cut = [lax.slice_in_dim(value, h * half, (h + 1) * half) for value in held[:-1]]
-        value = adamw(cut[: len(terms) - 1] + [held[-1]], cut[len(terms) - 1 :], factor)[3]
-        owned.append(lax.optimization_barrier(value))
-        if h == 0:
-            terms[0], owned[0] = tie(terms[0], owned[0])
-    terms[0], owned[1] = tie(terms[0], owned[1])
+    owned = update(terms, states, factor, [3], "weights", split=True)
+    terms[0], *owned = tie(terms[0], *owned)
     new_master, new_first, new_second = update(terms, states, factor, [0, 1, 2], "states")
 
     low, between = z < 2, (z == 1) | (z == 2)
@@ -282,18 +285,19 @@
     for h in halves:
         over[0][h] = over_x(owned[h])
         pairs[h], mid[h] = z_perm(owned[h], PAIRS), z_perm(owned[h], MIDDLE)
-    for h in halves:
-        pairs[h], mid[h], *over[0][h] = tie(pairs[h], mid[h], *over[0][h])
+    for h in (1, 0):
+        if h == 1:
+            pairs[h], mid[h], new_master, *over[0][h] = tie(pairs[h], mid[h], new_master, *over[0][h])
+        else:
+            pairs[h], mid[h], *over[0][h] = tie(pairs[h], mid[h], *over[0][h])
         over[1][h] = over_x(pairs[h])
         mid_far[h], outwards[h] = z_perm(pairs[h], MIDDLE), z_perm(mid[h], OUTWARDS)
-    for h in halves:
+    for h in (0, 1):
         mid_far[h], outwards[h], mid[h], *over[1][h] = tie(mid_far[h], outwards[h], mid[h], *over[1][h])
         far[h] = z_perm(mid_far[h], OUTWARDS)
         (near[h],) = tie(jnp.where(between, mid[h], outwards[h]))
         over[2][h] = over_x(near[h])
-    for h in halves:
-        if h:
-            far[h], distant[0] = tie(far[h], distant[0])
+    for h in (0, 1):
         (distant[h],) = tie(jnp.where(between, mid_far[h], far[h]))
         over[3][h] = over_x(distant[h])
 

time: 262 us -> 237 us (0.905)
  starting transfers between devices: 70 us -> 49.1 us
  other arithmetic: 21.2 us -> 13.4 us
  Pallas kernels: 33.9 us -> 39 us
  waiting for transfers between devices: 112 us -> 107 us
  local copies, waits for them, and re-layouts: 22.1 us -> 26.3 us
    ppermute x20, starting transfers between devices: 53.7 us -> 34 us  [z_perm(): lax.ppermute(value, 'dp', [(a * n_x + i, b * n_x + i) for a, b in pairs f...]
    dynamic_update_slice x16, local copies, waits for them, and re-layouts: 6.25 us -> 16.4 us  [put(): return lax.dynamic_update_slice(weights, value, (h * half, at))]
    ppermute x20, waiting for transfers between devices: 61.4 us -> 52.4 us  [z_perm(): lax.ppermute(value, 'dp', [(a * n_x + i, b * n_x + i) for a, b in pairs f...]
    convert_element_type x2 -> x0, other arithmetic: 6.67 us -> none  [adamw(): return (new_master, new_first, new_second, new_master.astype(BF16))]
    unnamed x34 -> x22, local copies, waits for them, and re-layouts: 7.1 us -> 1.13 us
    pallas_call x1 -> x2, Pallas kernels: 7.37 us -> 12.5 us  [update(): pl.pallas_call(kernel, grid=(rows // step,), in_specs=specs + [whole] * 3...]
    ppermute x13, waiting for transfers between devices: 32 us -> 36.1 us  [x_perm(): return lax.ppermute(value, 'dp', pairs)]
  transfers between devices with their start and end apart: 42 -> 42, of which waited for: 23 -> 25; matrix products, arithmetic and copies ran while one was open for 13% -> 16% of each run, Pallas kernels for 10% -> 11%
where the time goes in v9:
time: 237 us; the launch traced here: 236 us
  waiting for transfers between devices  107 us (45%)
  starting transfers between devices  49.1 us (21%)
  Pallas kernels  39 us (16%)
  local copies, waits for them, and re-layouts  26.3 us (11%)
  other arithmetic  13.4 us (6%)
    ppermute x20, waiting for transfers between devices, z_perm(): lax.ppermute(value, 'dp', [(a * n_x + i, b * n_x + i) for a, b in pairs f...  52.4 us
    ppermute x13, waiting for transfers between devices, x_perm(): return lax.ppermute(value, 'dp', pairs)  36.1 us
    ppermute x20, starting transfers between devices, z_perm(): lax.ppermute(value, 'dp', [(a * n_x + i, b * n_x + i) for a, b in pairs f...  34 us
    pallas_call x3, Pallas kernels, multiply(): pl.pallas_call(kernel, grid=(rows // step,), in_specs=[pl.BlockSpec((step...  23.7 us
    ppermute x9, waiting for transfers between devices, seat_perm(): lax.ppermute(value, 'tensor', [(i, i ^ flip) for i in range(n_tensor)])  18.9 us
    dynamic_update_slice x16, local copies, waits for them, and re-layouts, put(): return lax.dynamic_update_slice(weights, value, (h * half, at))  16.4 us
    pallas_call x2, Pallas kernels, update(): pl.pallas_call(kernel, grid=(rows // step,), in_specs=specs + [whole] * 3...  12.5 us
    convert_element_type x8, other arithmetic, add(): return lax.optimization_barrier(total.astype(BF16))  12 us
  transfers between devices with their start and end apart: 42, of which 25 were waited for; matrix products, arithmetic and copies ran while one was open for 16% of the time, Pallas kernels for 11%

profile of v9, /device:TPU:0, one launch (start us, length us, event | category | flops | bytes accessed | tf_op | source)
XLA Modules:
  0.0 236.0 jit_solution(4182287729522888353)
XLA Ops:
  0.6 2.8 %arrange.1 = (bf16[384,256]{1,0:T(8,128)(2,1)}, bf16[384,512]{1,0:T(8,128)(2,1)}, bf16[384,1280]{1,0:T(8,128)(2,1)}) custom-call(bf16[384,2048]{1,0:T(8,128)(2,1)} %cot_ref.1), custom_call_target="tpu_custom_call" | custom-call | tf_op jit(solution)/shard_map/arrange/pallas_call | solution.py:55
  3.4 3.0 %collective-permute-start.1 = (bf16[384,256]{1,0:T(8,128)(2,1)}, bf16[384,256]{1,0:T(8,128)(2,1)S(1)}, u32[]{:S(2)}, u32[]{:S(2)}) collective-permute-start(bf16[384,256]{1,0:T(8,128)(2,1)} %get-tuple-element.87.refs_0_), channel_id=1, source_target_pairs={{0,2},{1,3},{2,0},{3,1},{4,6},{5,7},{6,4},{7,5},{8,10},{9,11},{10,... | collective-permute-start | bytes 589832 | tf_op jit(solution)/shard_map/ppermute | solution.py:206
  6.4 8.6 %copy.12 = bf16[1536,2048]{0,1:T(8,128)(2,1)} copy(bf16[1536,2048]{1,0:T(8,128)(2,1)} %param.5) | data formatting | bytes 12582912 | tf_op jit(solution)/shard_map/optimization_barrier | solution.py:180
  15.6 0.9 collective-permute-done.refs_1_
  16.8 4.8 %partials.3 = (bf16[2048,256]{1,0:T(8,128)(2,1)S(1)}, f32[4,4,256]{2,1,0:T(4,128)S(1)}) custom-call(bf16[2048,1536]{1,0:T(8,128)(2,1)} %bitcast.17, bf16[384,256]{1,0:T(8,128)(2,1)S(1)} %copy-done.4, bf16[384,256]{1,0:T(8,128)(2,1)S(1)} %collective-permute-done.refs_1_, bf16[384,256]{1,0:T(8,128)(2,1)S(1)} %collective-permute-done.1.refs_2_, ...), custom_call_target="tpu_custom_call" | custom-call | flops 10000000000 | bytes 3145728 | tf_op jit(solution)/shard_map/partials/pallas_call | solution.py:79
  21.6 1.5 collective-permute-start.6
  23.6 1.5 collective-permute-start.8
  25.2 10.0 %collective-permute-done.4.refs_2_ = bf16[384,512]{1,0:T(8,128)(2,1)S(1)} collective-permute-done((bf16[384,512]{1,0:T(8,128)(2,1)S(1)}, bf16[384,512]{1,0:T(8,128)(2,1)S(1)}, u32[]{:S(2)}, u32[]{:S(2)}) %collective-permute-start.4) | collective-permute-done | bytes 393248 | tf_op jit(solution)/shard_map/ppermute | solution.py:206
  35.1 1.7 collective-permute-done.5.refs_3_
  36.8 6.8 %partials.4 = (bf16[2048,256]{1,0:T(8,128)(2,1)S(1)}, bf16[2048,256]{1,0:T(8,128)(2,1)}, f32[4,4,512]{2,1,0:T(4,128)S(1)}) custom-call(bf16[2048,1536]{1,0:T(8,128)(2,1)} %bitcast.18, bf16[384,512]{1,0:T(8,128)(2,1)S(1)} %copy-done.2, bf16[384,512]{1,0:T(8,128)(2,1)S(1)} %collective-permute-done.3.refs_1_, ...), custom_call_target="tpu_custom_call" | custom-call | tf_op jit(solution)/shard_map/partials/pallas_call | solution.py:79
  44.2 3.0 %collective-permute-done.6 = bf16[2048,256]{1,0:T(8,128)(2,1)S(1)} collective-permute-done((bf16[2048,256]{1,0:T(8,128)(2,1)S(1)}, bf16[2048,256]{1,0:T(8,128)(2,1)S(1)}, u32[]{:S(2)}, u32[]{:S(2)}) %collective-permute-start.6) | collective-permute-done | bytes 1048608 | tf_op jit(solution)/shard_map/ppermute | solution.py:203
  47.2 1.0 add_convert_fusion.7
  48.2 0.9 add_convert_fusion.6
  49.2 6.0 %collective-permute-done.8.refs_2_ = bf16[384,1280]{1,0:T(8,128)(2,1)S(1)} collective-permute-done((bf16[384,1280]{1,0:T(8,128)(2,1)S(1)}, bf16[384,1280]{1,0:T(8,128)(2,1)S(1)}, u32[]{:S(2)}, u32[]{:S(2)}) %collective-permute-start.8) | collective-permute-done | bytes 983072 | tf_op jit(solution)/shard_map/ppermute | solution.py:206
  55.3 3.6 %collective-permute-start.10 = (bf16[1024,256]{1,0:T(8,128)(2,1)}, bf16[1024,256]{1,0:T(8,128)(2,1)S(1)}, u32[]{:S(2)}, u32[]{:S(2)}) collective-permute-start(bf16[1024,256]{1,0:T(8,128)(2,1)} %add_convert_fusion.6), channel_id=1, source_target_pairs={{0,8},{4,12},{24,16},{28,20},{1,9},{5,13},{25,17},{29,21},{2,10},{... | collective-permute-start | bytes 1572872 | tf_op jit(solution)/shard_map/ppermute | solution.py:199
  58.9 1.3 collective-permute-start.11
  60.3 12.1 %partials.5 = (bf16[2048,256]{1,0:T(8,128)(2,1)}, bf16[2048,256]{1,0:T(8,128)(2,1)S(1)}, bf16[2048,256]{1,0:T(8,128)(2,1)}, bf16[2048,256]{1,0:T(8,128)(2,1)}, b...) custom-call(bf16[2048,1536]{1,0:T(8,128)(2,1)} %bitcast.19, bf16[384,1280]{1,0:T(8,128)(2,1)S(1)} %copy-done.1, ...), custom_call_target="tpu_custom_call" | custom-call | tf_op jit(solution)/shard_map/partials/pallas_call | solution.py:79
  73.0 2.9 %add_convert_fusion.1 = bf16[2048,256]{1,0:T(8,128)(2,1)} fusion(bf16[2048,256]{1,0:T(8,128)(2,1)} %collective-permute-done.12, bf16[2048,256]{1,0:T(8,128)(2,1)} %get-tuple-element.125), kind=kLoop, calls=%fused_computation.1 | loop fusion | flops 2097152 | bytes 3145728 | tf_op jit(solution)/shard_map/convert_element_type | solution.py:103
  75.8 2.3 collective-permute-start.15
  78.1 4.6 %collective-permute-done.11 = bf16[1024,256]{1,0:T(8,128)(2,1)S(1)} collective-permute-done((bf16[1024,256]{1,0:T(8,128)(2,1)}, bf16[1024,256]{1,0:T(8,128)(2,1)S(1)}, u32[]{:S(2)}, u32[]{:S(2)}) %collective-permute-start.11) | collective-permute-done | bytes 524320 | tf_op jit(solution)/shard_map/ppermute | solution.py:199
  82.7 1.0 add_convert_fusion.5
  83.7 1.5 collective-permute-start.17
  85.2 1.0 add_convert_fusion.4
  88.1 10.6 %collective-permute-done.16 = bf16[2048,256]{1,0:T(8,128)(2,1)} collective-permute-done((bf16[2048,256]{1,0:T(8,128)(2,1)}, bf16[2048,256]{1,0:T(8,128)(2,1)}, u32[]{:S(2)}, u32[]{:S(2)}) %collective-permute-start.16) | collective-permute-done | bytes 1048608 | tf_op jit(solution)/shard_map/ppermute | solution.py:203
  98.7 1.5 add_convert_fusion.3
  100.3 4.4 %collective-permute-start.19 = (bf16[1024,256]{1,0:T(8,128)(2,1)S(1)}, bf16[1024,256]{1,0:T(8,128)(2,1)S(1)}, u32[]{:S(2)}, u32[]{:S(2)}) collective-permute-start(bf16[1024,256]{1,0:T(8,128)(2,1)S(1)} %add_convert_fusion.3), channel_id=1, source_target_pairs={{0,8},{4,12},{8,0},{12,4},{16,24},{20,28},{24,16},{28,20},{1,9},{5... | collective-permute-start | bytes 1572872 | tf_op jit(solution)/shard_map/ppermute | solution.py:199
  105.1 2.2 add_convert_fusion
  108.1 7.8 %collective-permute-done.19.refs_3_ = bf16[1024,256]{1,0:T(8,128)(2,1)S(1)} collective-permute-done((bf16[1024,256]{1,0:T(8,128)(2,1)S(1)}, bf16[1024,256]{1,0:T(8,128)(2,1)S(1)}, u32[]{:S(2)}, u32[]{:S(2)}) %collective-permute-start.19) | collective-permute-done | bytes 524320 | tf_op jit(solution)/shard_map/ppermute | solution.py:199
  115.9 1.4 add_convert_fusion.2
  117.3 2.5 %collective-permute-start.21 = (bf16[1024,256]{1,0:T(8,128)(2,1)S(1)}, bf16[1024,256]{1,0:T(8,128)(2,1)S(1)}, u32[]{:S(2)}, u32[]{:S(2)}) collective-permute-start(bf16[1024,256]{1,0:T(8,128)(2,1)S(1)} %add_convert_fusion.2), channel_id=1, source_target_pairs={{0,8},{4,12},{8,0},{12,4},{16,24},{20,28},{24,16},{28,20},{1,9},{5... | collective-permute-start | bytes 1572872 | tf_op jit(solution)/shard_map/ppermute | solution.py:199
  120.4 3.1 %collective-permute-done.13 = f32[16,16]{1,0:T(8,128)S(1)} collective-permute-done((f32[16,16]{1,0:T(8,128)S(1)}, f32[16,16]{1,0:T(8,128)S(1)}, u32[]{:S(2)}, u32[]{:S(2)}) %collective-permute-start.13) | collective-permute-done | bytes 1056 | tf_op jit(solution)/shard_map/ppermute | solution.py:203
  123.5 7.3 %collective-permute-done.21.refs_4_ = bf16[1024,256]{1,0:T(8,128)(2,1)S(1)} collective-permute-done((bf16[1024,256]{1,0:T(8,128)(2,1)S(1)}, bf16[1024,256]{1,0:T(8,128)(2,1)S(1)}, u32[]{:S(2)}, u32[]{:S(2)}) %collective-permute-start.21) | collective-permute-done | bytes 524320 | tf_op jit(solution)/shard_map/ppermute | solution.py:199
  130.8 6.1 %weights.1 = (bf16[1024,256]{1,0:T(8,128)(2,1)S(1)}, bf16[1024,256]{1,0:T(8,128)(2,1)S(1)}) custom-call(bf16[2048,256]{1,0:T(8,128)(2,1)S(1)} %copy-done, bf16[2048,256]{1,0:T(8,128)(2,1)S(1)} %collective-permute-done.14.refs_1_, bf16[2048,256]{1,0:T(8,128)(2,1)S(1)} %collective-permute-done.18.refs_2_, ...), custom_call_target="tpu_custom_call" | custom-call | tf_op jit(solution)/shard_map/weights/pallas_call | solution.py:155
  136.9 5.4 %collective-permute-start.22 = (bf16[1024,256]{1,0:T(8,128)(2,1)S(1)}, bf16[1024,256]{1,0:T(8,128)(2,1)}, u32[]{:S(2)}, u32[]{:S(2)}) collective-permute-start(bf16[1024,256]{1,0:T(8,128)(2,1)S(1)} %get-tuple-element.133), channel_id=1, source_target_pairs={{0,8},{4,12},{8,0},{12,4},{16,24},{20,28},{24,16},{28,20},{1,9},{5... | collective-permute-start | bytes 1572872 | tf_op jit(solution)/shard_map/ppermute | solution.py:199
  142.3 1.5 collective-permute-start.23
  144.3 2.1 collective-permute-start.28
  146.4 1.5 collective-permute-start.29
  147.9 6.4 %states.1 = (f32[2048,256]{1,0:T(8,128)}, f32[2048,256]{1,0:T(8,128)}, f32[2048,256]{1,0:T(8,128)}) custom-call(bf16[2048,256]{1,0:T(8,128)(2,1)S(1)} %copy-done, bf16[2048,256]{1,0:T(8,128)(2,1)S(1)} %collective-permute-done.14.refs_1_, bf16[2048,256]{1,0:T(8,128)(2,1)S(1)} %collective-permute-done.18.refs_2_, ...), custom_call_target="tpu_custom_call" | custom-call | tf_op jit(solution)/shard_map/states/pallas_call | solution.py:155
  154.3 0.9 collective-permute-done.22
  155.9 0.9 collective-permute-done.24
  157.5 1.3 collective-permute-start.26
  158.8 7.6 %collective-permute-done.28 = bf16[1024,256]{1,0:T(8,128)(2,1)S(1)} collective-permute-done((bf16[1024,256]{1,0:T(8,128)(2,1)S(1)}, bf16[1024,256]{1,0:T(8,128)(2,1)S(1)}, u32[]{:S(2)}, u32[]{:S(2)}) %collective-permute-start.28) | collective-permute-done | bytes 524320 | tf_op jit(solution)/shard_map/ppermute | solution.py:199
  169.4 1.5 collective-permute-start.33
  171.0 1.3 collective-permute-start.32
  172.3 3.0 %collective-permute-done.26 = bf16[1024,256]{1,0:T(8,128)(2,1)S(1)} collective-permute-done((bf16[1024,256]{1,0:T(8,128)(2,1)}, bf16[1024,256]{1,0:T(8,128)(2,1)S(1)}, u32[]{:S(2)}, u32[]{:S(2)}) %collective-permute-start.26) | collective-permute-done | bytes 524320 | tf_op jit(solution)/shard_map/ppermute | solution.py:199
  175.3 7.1 %collective-permute-done.27 = bf16[1024,256]{1,0:T(8,128)(2,1)} collective-permute-done((bf16[1024,256]{1,0:T(8,128)(2,1)}, bf16[1024,256]{1,0:T(8,128)(2,1)}, u32[]{:S(2)}, u32[]{:S(2)}) %collective-permute-start.27) | collective-permute-done | bytes 524320 | tf_op jit(solution)/shard_map/ppermute | solution.py:203
  183.0 0.8 constant_dynamic-update-slice_fusion.15
  183.8 1.9 constant_dynamic-update-slice_fusion.14
  186.5 3.6 %collective-permute-done.32 = bf16[1024,256]{1,0:T(8,128)(2,1)S(1)} collective-permute-done((bf16[1024,256]{1,0:T(8,128)(2,1)}, bf16[1024,256]{1,0:T(8,128)(2,1)S(1)}, u32[]{:S(2)}, u32[]{:S(2)}) %collective-permute-start.32) | collective-permute-done | bytes 524320 | tf_op jit(solution)/shard_map/ppermute | solution.py:199
  190.2 3.3 %collective-permute-done.33 = bf16[1024,256]{1,0:T(8,128)(2,1)S(1)} collective-permute-done((bf16[1024,256]{1,0:T(8,128)(2,1)S(1)}, bf16[1024,256]{1,0:T(8,128)(2,1)S(1)}, u32[]{:S(2)}, u32[]{:S(2)}) %collective-permute-start.33) | collective-permute-done | bytes 524320 | tf_op jit(solution)/shard_map/ppermute | solution.py:203
  193.5 1.3 collective-permute-start.34
  194.8 1.3 collective-permute-start.35
  196.8 0.8 constant_dynamic-update-slice_fusion.6
  199.2 1.9 constant_dynamic-update-slice_fusion.5
  201.1 1.9 constant_dynamic-update-slice_fusion.4
  203.0 5.6 %collective-permute-done.34 = bf16[1024,256]{1,0:T(8,128)(2,1)S(1)} collective-permute-done((bf16[1024,256]{1,0:T(8,128)(2,1)S(1)}, bf16[1024,256]{1,0:T(8,128)(2,1)S(1)}, u32[]{:S(2)}, u32[]{:S(2)}) %collective-permute-start.34) | collective-permute-done | bytes 524320 | tf_op jit(solution)/shard_map/ppermute | solution.py:199
  209.3 5.0 %collective-permute-done.35 = bf16[1024,256]{1,0:T(8,128)(2,1)S(1)} collective-permute-done((bf16[1024,256]{1,0:T(8,128)(2,1)S(1)}, bf16[1024,256]{1,0:T(8,128)(2,1)S(1)}, u32[]{:S(2)}, u32[]{:S(2)}) %collective-permute-start.35) | collective-permute-done | bytes 524320 | tf_op jit(solution)/shard_map/ppermute | solution.py:199
  218.2 0.8 constant_dynamic-update-slice_fusion.9
  219.0 2.8 %collective-permute-done.40 = f32[16,16]{1,0:T(8,128)S(1)} collective-permute-done((f32[16,16]{1,0:T(8,128)S(1)}, f32[16,16]{1,0:T(8,128)S(1)}, u32[]{:S(2)}, u32[]{:S(2)}) %collective-permute-start.40) | collective-permute-done | bytes 1056 | tf_op jit(solution)/shard_map/ppermute | solution.py:199
  221.9 0.8 constant_dynamic-update-slice_fusion.1
  222.7 3.7 %collective-permute-done.41 = f32[16,16]{1,0:T(8,128)S(1)} collective-permute-done((f32[16,16]{1,0:T(8,128)S(1)}, f32[16,16]{1,0:T(8,128)S(1)}, u32[]{:S(2)}, u32[]{:S(2)}) %collective-permute-start.41) | collective-permute-done | bytes 1056 | tf_op jit(solution)/shard_map/ppermute | solution.py:199
  227.0 7.4 %collective-permute-done.38 = bf16[1024,256]{1,0:T(8,128)(2,1)S(1)} collective-permute-done((bf16[1024,256]{1,0:T(8,128)(2,1)S(1)}, bf16[1024,256]{1,0:T(8,128)(2,1)S(1)}, u32[]{:S(2)}, u32[]{:S(2)}) %collective-permute-start.38) | collective-permute-done | bytes 524320 | tf_op jit(solution)/shard_map/ppermute | solution.py:203
  234.4 0.8 constant_dynamic-update-slice_fusion.8
  235.2 0.8 constant_dynamic-update-slice_fusion
  (91 shorter events, 20.2 us)
Async XLA Ops:
  3.4 11.6 %copy-start.4 = (bf16[384,256]{1,0:T(8,128)(2,1)S(1)}, bf16[384,256]{1,0:T(8,128)(2,1)}, u32[]{:S(2)}) copy-start(bf16[384,256]{1,0:T(8,128)(2,1)} %get-tuple-element.87.refs_0_) | copy-start | bytes 589828
  3.4 11.7 %collective-permute-start.1 = (bf16[384,256]{1,0:T(8,128)(2,1)}, bf16[384,256]{1,0:T(8,128)(2,1)S(1)}, u32[]{:S(2)}, u32[]{:S(2)}) collective-permute-start(bf16[384,256]{1,0:T(8,128)(2,1)} %get-tuple-element.87.refs_0_), channel_id=1, source_target_pairs={{0,2},{1,3},{2,0},{3,1},{4,6},{5,7},{6,4},{7,5},{8,10},{9,11},{10,... | collective-permute-start | bytes 589832 | tf_op jit(solution)/shard_map/ppermute | solution.py:206
  15.0 8.1 %copy-start.2 = (bf16[384,512]{1,0:T(8,128)(2,1)S(1)}, bf16[384,512]{1,0:T(8,128)(2,1)}, u32[]{:S(2)}) copy-start(bf16[384,512]{1,0:T(8,128)(2,1)} %get-tuple-element.91.refs_0_) | copy-start | bytes 1179652
  15.0 8.7 %copy-start.1 = (bf16[384,1280]{1,0:T(8,128)(2,1)S(1)}, bf16[384,1280]{1,0:T(8,128)(2,1)}, u32[]{:S(2)}) copy-start(bf16[384,1280]{1,0:T(8,128)(2,1)} %get-tuple-element.99.refs_0_) | copy-start | bytes 2949124
  15.0 1.5 collective-permute-start
  15.1 1.7 collective-permute-start.2
  21.6 25.6 %collective-permute-start.6 = (bf16[2048,256]{1,0:T(8,128)(2,1)S(1)}, bf16[2048,256]{1,0:T(8,128)(2,1)S(1)}, u32[]{:S(2)}, u32[]{:S(2)}) collective-permute-start(bf16[2048,256]{1,0:T(8,128)(2,1)S(1)} %get-tuple-element.89), channel_id=1, source_target_pairs={{0,4},{4,0},{8,12},{12,8},{16,20},{20,16},{24,28},{28,24},{1,5},{5... | collective-permute-start | bytes 3145736 | tf_op jit(solution)/shard_map/ppermute | solution.py:203
  23.1 12.0 %collective-permute-start.4 = (bf16[384,512]{1,0:T(8,128)(2,1)S(1)}, bf16[384,512]{1,0:T(8,128)(2,1)S(1)}, u32[]{:S(2)}, u32[]{:S(2)}) collective-permute-start(bf16[384,512]{1,0:T(8,128)(2,1)S(1)} %copy-done.2), channel_id=1, source_target_pairs={{0,2},{1,3},{2,0},{3,1},{4,6},{5,7},{6,4},{7,5},{8,10},{9,11},{10,... | collective-permute-start | bytes 1179656 | tf_op jit(solution)/shard_map/ppermute | solution.py:206
  23.6 31.5 %collective-permute-start.8 = (bf16[384,1280]{1,0:T(8,128)(2,1)S(1)}, bf16[384,1280]{1,0:T(8,128)(2,1)S(1)}, u32[]{:S(2)}, u32[]{:S(2)}) collective-permute-start(bf16[384,1280]{1,0:T(8,128)(2,1)S(1)} %copy-done.1), channel_id=1, source_target_pairs={{0,2},{1,3},{2,0},{3,1},{4,6},{5,7},{6,4},{7,5},{8,10},{9,11},{10,... | collective-permute-start | bytes 2949128 | tf_op jit(solution)/shard_map/ppermute | solution.py:206
  25.2 10.0 %collective-permute-start.3 = (bf16[384,512]{1,0:T(8,128)(2,1)S(1)}, bf16[384,512]{1,0:T(8,128)(2,1)S(1)}, u32[]{:S(2)}, u32[]{:S(2)}) collective-permute-start(bf16[384,512]{1,0:T(8,128)(2,1)S(1)} %copy-done.2), channel_id=1, source_target_pairs={{0,1},{1,0},{2,3},{3,2},{4,5},{5,4},{6,7},{7,6},{8,9},{9,8},{10,11... | collective-permute-start | bytes 1179656 | tf_op jit(solution)/shard_map/ppermute | solution.py:206
  35.1 1.7 collective-permute-start.5
  43.7 29.3 %collective-permute-start.12 = (bf16[2048,256]{1,0:T(8,128)(2,1)}, bf16[2048,256]{1,0:T(8,128)(2,1)}, u32[]{:S(2)}, u32[]{:S(2)}) collective-permute-start(bf16[2048,256]{1,0:T(8,128)(2,1)} %get-tuple-element.104), channel_id=1, source_target_pairs={{0,4},{4,0},{8,12},{12,8},{16,20},{20,16},{24,28},{28,24},{1,5},{5... | collective-permute-start | bytes 3145736 | tf_op jit(solution)/shard_map/ppermute | solution.py:203
  47.2 8.0 %copy-start.5 = (bf16[2048,256]{1,0:T(8,128)(2,1)}, bf16[2048,256]{1,0:T(8,128)(2,1)S(1)}, u32[]{:S(2)}) copy-start(bf16[2048,256]{1,0:T(8,128)(2,1)S(1)} %collective-permute-done.6) | copy-start | bytes 3145732
  49.2 11.1 %collective-permute-start.7 = (bf16[384,1280]{1,0:T(8,128)(2,1)S(1)}, bf16[384,1280]{1,0:T(8,128)(2,1)}, u32[]{:S(2)}, u32[]{:S(2)}) collective-permute-start(bf16[384,1280]{1,0:T(8,128)(2,1)S(1)} %copy-done.1), channel_id=1, source_target_pairs={{0,1},{1,0},{2,3},{3,2},{4,5},{5,4},{6,7},{7,6},{8,9},{9,8},{10,11... | collective-permute-start | bytes 2949128 | tf_op jit(solution)/shard_map/ppermute | solution.py:206
  55.2 5.1 %collective-permute-start.9 = (bf16[384,1280]{1,0:T(8,128)(2,1)S(1)}, bf16[384,1280]{1,0:T(8,128)(2,1)}, u32[]{:S(2)}, u32[]{:S(2)}) collective-permute-start(bf16[384,1280]{1,0:T(8,128)(2,1)S(1)} %collective-permute-done.8.refs_2_), channel_id=1, source_target_pairs={{0,1},{1,0},{2,3},{3,2},{4,5},{5,4},{6,7},{7,6},{8,9},{9,8},{10,11... | collective-permute-start | bytes 2949128 | tf_op jit(solution)/shard_map/ppermute | solution.py:206
  55.3 27.4 %copy-start.6 = (bf16[2048,256]{1,0:T(8,128)(2,1)S(1)}, bf16[2048,256]{1,0:T(8,128)(2,1)}, u32[]{:S(2)}) copy-start(bf16[2048,256]{1,0:T(8,128)(2,1)} %copy-done.5) | copy-start | bytes 3145732
  55.3 29.9 %collective-permute-start.10 = (bf16[1024,256]{1,0:T(8,128)(2,1)}, bf16[1024,256]{1,0:T(8,128)(2,1)S(1)}, u32[]{:S(2)}, u32[]{:S(2)}) collective-permute-start(bf16[1024,256]{1,0:T(8,128)(2,1)} %add_convert_fusion.6), channel_id=1, source_target_pairs={{0,8},{4,12},{24,16},{28,20},{1,9},{5,13},{25,17},{29,21},{2,10},{... | collective-permute-start | bytes 1572872 | tf_op jit(solution)/shard_map/ppermute | solution.py:199
  58.9 23.7 %collective-permute-start.11 = (bf16[1024,256]{1,0:T(8,128)(2,1)}, bf16[1024,256]{1,0:T(8,128)(2,1)S(1)}, u32[]{:S(2)}, u32[]{:S(2)}) collective-permute-start(bf16[1024,256]{1,0:T(8,128)(2,1)} %add_convert_fusion.7), channel_id=1, source_target_pairs={{0,8},{4,12},{24,16},{28,20},{1,9},{5,13},{25,17},{29,21},{2,10},{... | collective-permute-start | bytes 1572872 | tf_op jit(solution)/shard_map/ppermute | solution.py:199
  72.4 13.8 %copy-start.3 = (bf16[2048,256]{1,0:T(8,128)(2,1)}, bf16[2048,256]{1,0:T(8,128)(2,1)S(1)}, u32[]{:S(2)}) copy-start(bf16[2048,256]{1,0:T(8,128)(2,1)S(1)} %get-tuple-element.120) | copy-start | bytes 3145732
  72.4 58.4 %copy-start = (bf16[2048,256]{1,0:T(8,128)(2,1)S(1)}, bf16[2048,256]{1,0:T(8,128)(2,1)}, u32[]{:S(2)}) copy-start(bf16[2048,256]{1,0:T(8,128)(2,1)} %get-tuple-element.134.refs_0_) | copy-start | bytes 3145732
  72.4 26.4 %collective-permute-start.16 = (bf16[2048,256]{1,0:T(8,128)(2,1)}, bf16[2048,256]{1,0:T(8,128)(2,1)}, u32[]{:S(2)}, u32[]{:S(2)}) collective-permute-start(bf16[2048,256]{1,0:T(8,128)(2,1)} %get-tuple-element.105), channel_id=1, source_target_pairs={{0,4},{4,0},{8,12},{12,8},{16,20},{20,16},{24,28},{28,24},{1,5},{5... | collective-permute-start | bytes 3145736 | tf_op jit(solution)/shard_map/ppermute | solution.py:203
  75.8 29.3 %collective-permute-start.15 = (bf16[2048,256]{1,0:T(8,128)(2,1)}, bf16[2048,256]{1,0:T(8,128)(2,1)}, u32[]{:S(2)}, u32[]{:S(2)}) collective-permute-start(bf16[2048,256]{1,0:T(8,128)(2,1)} %add_convert_fusion.1), channel_id=1, source_target_pairs={{0,8},{4,12},{24,16},{28,20},{1,9},{5,13},{25,17},{29,21},{2,10},{... | collective-permute-start | bytes 3145736 | tf_op jit(solution)/shard_map/ppermute | solution.py:199
  83.7 4.4 %collective-permute-start.17 = (bf16[1024,256]{1,0:T(8,128)(2,1)}, bf16[1024,256]{1,0:T(8,128)(2,1)}, u32[]{:S(2)}, u32[]{:S(2)}) collective-permute-start(bf16[1024,256]{1,0:T(8,128)(2,1)} %add_convert_fusion.5), channel_id=1, source_target_pairs={{8,16},{12,20},{16,8},{20,12},{9,17},{13,21},{17,9},{21,13},{10,18... | collective-permute-start | bytes 1572872 | tf_op jit(solution)/shard_map/ppermute | solution.py:199
  86.2 21.9 %collective-permute-start.20 = (bf16[1024,256]{1,0:T(8,128)(2,1)}, bf16[1024,256]{1,0:T(8,128)(2,1)S(1)}, u32[]{:S(2)}, u32[]{:S(2)}) collective-permute-start(bf16[1024,256]{1,0:T(8,128)(2,1)} %add_convert_fusion.4), channel_id=1, source_target_pairs={{8,16},{12,20},{16,8},{20,12},{9,17},{13,21},{17,9},{21,13},{10,18... | collective-permute-start | bytes 1572872 | tf_op jit(solution)/shard_map/ppermute | solution.py:199
  87.3 36.2 %collective-permute-start.14 = (bf16[2048,256]{1,0:T(8,128)(2,1)}, bf16[2048,256]{1,0:T(8,128)(2,1)S(1)}, u32[]{:S(2)}, u32[]{:S(2)}) collective-permute-start(bf16[2048,256]{1,0:T(8,128)(2,1)} %copy-done.3), channel_id=1, source_target_pairs={{0,4},{4,0},{8,12},{12,8},{16,20},{20,16},{24,28},{28,24},{1,5},{5... | collective-permute-start | bytes 3145736 | tf_op jit(solution)/shard_map/ppermute | solution.py:203
  100.3 15.6 %collective-permute-start.19 = (bf16[1024,256]{1,0:T(8,128)(2,1)S(1)}, bf16[1024,256]{1,0:T(8,128)(2,1)S(1)}, u32[]{:S(2)}, u32[]{:S(2)}) collective-permute-start(bf16[1024,256]{1,0:T(8,128)(2,1)S(1)} %add_convert_fusion.3), channel_id=1, source_target_pairs={{0,8},{4,12},{8,0},{12,4},{16,24},{20,28},{24,16},{28,20},{1,9},{5... | collective-permute-start | bytes 1572872 | tf_op jit(solution)/shard_map/ppermute | solution.py:199
  107.4 23.4 %collective-permute-start.18 = (bf16[2048,256]{1,0:T(8,128)(2,1)S(1)}, bf16[2048,256]{1,0:T(8,128)(2,1)S(1)}, u32[]{:S(2)}, u32[]{:S(2)}) collective-permute-start(bf16[2048,256]{1,0:T(8,128)(2,1)S(1)} %add_convert_fusion), channel_id=1, source_target_pairs={{8,16},{12,20},{16,8},{20,12},{9,17},{13,21},{17,9},{21,13},{10,18... | collective-permute-start | bytes 3145736 | tf_op jit(solution)/shard_map/ppermute | solution.py:199
  117.3 13.5 %collective-permute-start.21 = (bf16[1024,256]{1,0:T(8,128)(2,1)S(1)}, bf16[1024,256]{1,0:T(8,128)(2,1)S(1)}, u32[]{:S(2)}, u32[]{:S(2)}) collective-permute-start(bf16[1024,256]{1,0:T(8,128)(2,1)S(1)} %add_convert_fusion.2), channel_id=1, source_target_pairs={{0,8},{4,12},{8,0},{12,4},{16,24},{20,28},{24,16},{28,20},{1,9},{5... | collective-permute-start | bytes 1572872 | tf_op jit(solution)/shard_map/ppermute | solution.py:199
  119.8 3.7 %collective-permute-start.13 = (f32[16,16]{1,0:T(8,128)S(1)}, f32[16,16]{1,0:T(8,128)S(1)}, u32[]{:S(2)}, u32[]{:S(2)}) collective-permute-start(f32[16,16]{1,0:T(8,128)S(1)} %select_reduce_fusion), channel_id=1, source_target_pairs={{0,4},{4,0},{8,12},{12,8},{16,20},{20,16},{24,28},{28,24},{1,5},{5... | collective-permute-start | bytes 3080 | tf_op jit(solution)/shard_map/ppermute | solution.py:203
  136.9 18.4 %collective-permute-start.22 = (bf16[1024,256]{1,0:T(8,128)(2,1)S(1)}, bf16[1024,256]{1,0:T(8,128)(2,1)}, u32[]{:S(2)}, u32[]{:S(2)}) collective-permute-start(bf16[1024,256]{1,0:T(8,128)(2,1)S(1)} %get-tuple-element.133), channel_id=1, source_target_pairs={{0,8},{4,12},{8,0},{12,4},{16,24},{20,28},{24,16},{28,20},{1,9},{5... | collective-permute-start | bytes 1572872 | tf_op jit(solution)/shard_map/ppermute | solution.py:199
  142.3 13.6 %collective-permute-start.23 = (bf16[1024,256]{1,0:T(8,128)(2,1)S(1)}, bf16[1024,256]{1,0:T(8,128)(2,1)}, u32[]{:S(2)}, u32[]{:S(2)}) collective-permute-start(bf16[1024,256]{1,0:T(8,128)(2,1)S(1)} %get-tuple-element.133), channel_id=1, source_target_pairs={{8,16},{12,20},{16,8},{20,12},{9,17},{13,21},{17,9},{21,13},{10,18... | collective-permute-start | bytes 1572872 | tf_op jit(solution)/shard_map/ppermute | solution.py:199
  143.8 13.1 %collective-permute-start.24 = (bf16[1024,256]{1,0:T(8,128)(2,1)S(1)}, bf16[1024,256]{1,0:T(8,128)(2,1)S(1)}, u32[]{:S(2)}, u32[]{:S(2)}) collective-permute-start(bf16[1024,256]{1,0:T(8,128)(2,1)S(1)} %get-tuple-element.133), channel_id=1, source_target_pairs={{0,4},{4,0},{8,12},{12,8},{16,20},{20,16},{24,28},{28,24},{1,5},{5... | collective-permute-start | bytes 1572872 | tf_op jit(solution)/shard_map/ppermute | solution.py:203
  144.3 22.1 %collective-permute-start.28 = (bf16[1024,256]{1,0:T(8,128)(2,1)S(1)}, bf16[1024,256]{1,0:T(8,128)(2,1)S(1)}, u32[]{:S(2)}, u32[]{:S(2)}) collective-permute-start(bf16[1024,256]{1,0:T(8,128)(2,1)S(1)} %get-tuple-element.144), channel_id=1, source_target_pairs={{0,8},{4,12},{8,0},{12,4},{16,24},{20,28},{24,16},{28,20},{1,9},{5... | collective-permute-start | bytes 1572872 | tf_op jit(solution)/shard_map/ppermute | solution.py:199
  146.4 21.3 %collective-permute-start.29 = (bf16[1024,256]{1,0:T(8,128)(2,1)S(1)}, bf16[1024,256]{1,0:T(8,128)(2,1)}, u32[]{:S(2)}, u32[]{:S(2)}) collective-permute-start(bf16[1024,256]{1,0:T(8,128)(2,1)S(1)} %get-tuple-element.144), channel_id=1, source_target_pairs={{8,16},{12,20},{16,8},{20,12},{9,17},{13,21},{17,9},{21,13},{10,18... | collective-permute-start | bytes 1572872 | tf_op jit(solution)/shard_map/ppermute | solution.py:199
  155.2 13.2 %collective-permute-start.30 = (bf16[1024,256]{1,0:T(8,128)(2,1)S(1)}, bf16[1024,256]{1,0:T(8,128)(2,1)}, u32[]{:S(2)}, u32[]{:S(2)}) collective-permute-start(bf16[1024,256]{1,0:T(8,128)(2,1)S(1)} %get-tuple-element.144), channel_id=1, source_target_pairs={{0,4},{4,0},{8,12},{12,8},{16,20},{20,16},{24,28},{28,24},{1,5},{5... | collective-permute-start | bytes 1572872 | tf_op jit(solution)/shard_map/ppermute | solution.py:203
  156.8 9.5 %copy-start.7 = (bf16[1024,256]{1,0:T(8,128)(2,1)}, bf16[1024,256]{1,0:T(8,128)(2,1)S(1)}, u32[]{:S(2)}) copy-start(bf16[1024,256]{1,0:T(8,128)(2,1)S(1)} %collective-permute-done.24) | copy-start | bytes 1572868
  156.8 14.2 %collective-permute-start.25 = (bf16[1024,256]{1,0:T(8,128)(2,1)}, bf16[1024,256]{1,0:T(8,128)(2,1)S(1)}, u32[]{:S(2)}, u32[]{:S(2)}) collective-permute-start(bf16[1024,256]{1,0:T(8,128)(2,1)} %collective-permute-done.22), channel_id=1, source_target_pairs={{8,16},{12,20},{16,8},{20,12},{9,17},{13,21},{17,9},{21,13},{10,18... | collective-permute-start | bytes 1572872 | tf_op jit(solution)/shard_map/ppermute | solution.py:199
  157.5 17.8 %collective-permute-start.26 = (bf16[1024,256]{1,0:T(8,128)(2,1)}, bf16[1024,256]{1,0:T(8,128)(2,1)S(1)}, u32[]{:S(2)}, u32[]{:S(2)}) collective-permute-start(bf16[1024,256]{1,0:T(8,128)(2,1)} %collective-permute-done.23), channel_id=1, source_target_pairs={{8,0},{12,4},{16,24},{20,28},{9,1},{13,5},{17,25},{21,29},{10,2},{... | collective-permute-start | bytes 1572872 | tf_op jit(solution)/shard_map/ppermute | solution.py:199
  166.4 0.8 copy-start.9
  167.2 15.2 %collective-permute-start.27 = (bf16[1024,256]{1,0:T(8,128)(2,1)}, bf16[1024,256]{1,0:T(8,128)(2,1)}, u32[]{:S(2)}, u32[]{:S(2)}) collective-permute-start(bf16[1024,256]{1,0:T(8,128)(2,1)} %collective-permute-done.22), channel_id=1, source_target_pairs={{0,4},{4,0},{8,12},{12,8},{16,20},{20,16},{24,28},{28,24},{1,5},{5... | collective-permute-start | bytes 1572872 | tf_op jit(solution)/shard_map/ppermute | solution.py:203
  167.7 1.0 copy-start.10
  167.7 29.0 %copy-start.8 = (bf16[1024,256]{1,0:T(8,128)(2,1)S(1)}, bf16[1024,256]{1,0:T(8,128)(2,1)}, u32[]{:S(2)}) copy-start(bf16[1024,256]{1,0:T(8,128)(2,1)} %copy-done.7) | copy-start | bytes 1572868
  168.8 17.8 %collective-permute-start.31 = (bf16[1024,256]{1,0:T(8,128)(2,1)S(1)}, bf16[1024,256]{1,0:T(8,128)(2,1)S(1)}, u32[]{:S(2)}, u32[]{:S(2)}) collective-permute-start(bf16[1024,256]{1,0:T(8,128)(2,1)S(1)} %copy-done.10), channel_id=1, source_target_pairs={{8,16},{12,20},{16,8},{20,12},{9,17},{13,21},{17,9},{21,13},{10,18... | collective-permute-start | bytes 1572872 | tf_op jit(solution)/shard_map/ppermute | solution.py:199
  169.4 24.0 %collective-permute-start.33 = (bf16[1024,256]{1,0:T(8,128)(2,1)S(1)}, bf16[1024,256]{1,0:T(8,128)(2,1)S(1)}, u32[]{:S(2)}, u32[]{:S(2)}) collective-permute-start(bf16[1024,256]{1,0:T(8,128)(2,1)S(1)} %copy-done.10), channel_id=1, source_target_pairs={{0,4},{4,0},{8,12},{12,8},{16,20},{20,16},{24,28},{28,24},{1,5},{5... | collective-permute-start | bytes 1572872 | tf_op jit(solution)/shard_map/ppermute | solution.py:203
  171.0 19.2 %collective-permute-start.32 = (bf16[1024,256]{1,0:T(8,128)(2,1)}, bf16[1024,256]{1,0:T(8,128)(2,1)S(1)}, u32[]{:S(2)}, u32[]{:S(2)}) collective-permute-start(bf16[1024,256]{1,0:T(8,128)(2,1)} %collective-permute-done.29), channel_id=1, source_target_pairs={{8,0},{12,4},{16,24},{20,28},{9,1},{13,5},{17,25},{21,29},{10,2},{... | collective-permute-start | bytes 1572872 | tf_op jit(solution)/shard_map/ppermute | solution.py:199
  182.4 39.5 %collective-permute-start.37 = (bf16[1024,256]{1,0:T(8,128)(2,1)S(1)}, bf16[1024,256]{1,0:T(8,128)(2,1)S(1)}, u32[]{:S(2)}, u32[]{:S(2)}) collective-permute-start(bf16[1024,256]{1,0:T(8,128)(2,1)S(1)} %broadcast_select_fusion.3), channel_id=1, source_target_pairs={{0,4},{4,0},{8,12},{12,8},{16,20},{20,16},{24,28},{28,24},{1,5},{5... | collective-permute-start | bytes 1572872 | tf_op jit(solution)/shard_map/ppermute | solution.py:203
  193.5 15.1 %collective-permute-start.34 = (bf16[1024,256]{1,0:T(8,128)(2,1)S(1)}, bf16[1024,256]{1,0:T(8,128)(2,1)S(1)}, u32[]{:S(2)}, u32[]{:S(2)}) collective-permute-start(bf16[1024,256]{1,0:T(8,128)(2,1)S(1)} %collective-permute-done.25), channel_id=1, source_target_pairs={{8,0},{12,4},{16,24},{20,28},{9,1},{13,5},{17,25},{21,29},{10,2},{... | collective-permute-start | bytes 1572872 | tf_op jit(solution)/shard_map/ppermute | solution.py:199
  194.8 19.5 %collective-permute-start.35 = (bf16[1024,256]{1,0:T(8,128)(2,1)S(1)}, bf16[1024,256]{1,0:T(8,128)(2,1)S(1)}, u32[]{:S(2)}, u32[]{:S(2)}) collective-permute-start(bf16[1024,256]{1,0:T(8,128)(2,1)S(1)} %collective-permute-done.31), channel_id=1, source_target_pairs={{8,0},{12,4},{16,24},{20,28},{9,1},{13,5},{17,25},{21,29},{10,2},{... | collective-permute-start | bytes 1572872 | tf_op jit(solution)/shard_map/ppermute | solution.py:199
  196.1 22.1 %collective-permute-start.36 = (bf16[1024,256]{1,0:T(8,128)(2,1)S(1)}, bf16[1024,256]{1,0:T(8,128)(2,1)S(1)}, u32[]{:S(2)}, u32[]{:S(2)}) collective-permute-start(bf16[1024,256]{1,0:T(8,128)(2,1)S(1)} %broadcast_select_fusion.1), channel_id=1, source_target_pairs={{0,4},{4,0},{8,12},{12,8},{16,20},{20,16},{24,28},{28,24},{1,5},{5... | collective-permute-start | bytes 1572872 | tf_op jit(solution)/shard_map/ppermute | solution.py:203
  208.7 26.6 %collective-permute-start.39 = (bf16[1024,256]{1,0:T(8,128)(2,1)S(1)}, bf16[1024,256]{1,0:T(8,128)(2,1)S(1)}, u32[]{:S(2)}, u32[]{:S(2)}) collective-permute-start(bf16[1024,256]{1,0:T(8,128)(2,1)S(1)} %broadcast_select_fusion.2), channel_id=1, source_target_pairs={{0,4},{4,0},{8,12},{12,8},{16,20},{20,16},{24,28},{28,24},{1,5},{5... | collective-permute-start | bytes 1572872 | tf_op jit(solution)/shard_map/ppermute | solution.py:203
  214.4 20.0 %collective-permute-start.38 = (bf16[1024,256]{1,0:T(8,128)(2,1)S(1)}, bf16[1024,256]{1,0:T(8,128)(2,1)S(1)}, u32[]{:S(2)}, u32[]{:S(2)}) collective-permute-start(bf16[1024,256]{1,0:T(8,128)(2,1)S(1)} %broadcast_select_fusion), channel_id=1, source_target_pairs={{0,4},{4,0},{8,12},{12,8},{16,20},{20,16},{24,28},{28,24},{1,5},{5... | collective-permute-start | bytes 1572872 | tf_op jit(solution)/shard_map/ppermute | solution.py:203
  218.2 3.7 %collective-permute-start.40 = (f32[16,16]{1,0:T(8,128)S(1)}, f32[16,16]{1,0:T(8,128)S(1)}, u32[]{:S(2)}, u32[]{:S(2)}) collective-permute-start(f32[16,16]{1,0:T(8,128)S(1)} %max.9), channel_id=1, source_target_pairs={{0,8},{4,12},{8,0},{12,4},{16,24},{20,28},{24,16},{28,20},{1,9},{5... | collective-permute-start | bytes 3080 | tf_op jit(solution)/shard_map/ppermute | solution.py:199
  221.9 4.5 %collective-permute-start.41 = (f32[16,16]{1,0:T(8,128)S(1)}, f32[16,16]{1,0:T(8,128)S(1)}, u32[]{:S(2)}, u32[]{:S(2)}) collective-permute-start(f32[16,16]{1,0:T(8,128)S(1)} %max.10), channel_id=1, source_target_pairs={{0,16},{4,20},{8,24},{12,28},{16,0},{20,4},{24,8},{28,12},{1,17},{... | collective-permute-start | bytes 3080 | tf_op jit(solution)/shard_map/ppermute | solution.py:199

commit v10 on v9

--- a/solution.py
+++ b/solution.py
@@ -285,11 +285,19 @@
     for h in halves:
         over[0][h] = over_x(owned[h])
         pairs[h], mid[h] = z_perm(owned[h], PAIRS), z_perm(owned[h], MIDDLE)
+    def put(weights, h, slot, by, count=half):
+        value = [owned, pairs, near, distant][slot][h] if by == 0 else over[slot][h][by - 1]
+        at = (sources[slot] * n_x + (x - by) % n_x) * width
+        return lax.dynamic_update_slice(weights, value[:count], (h * half, at))
+
+    weights = blank((rows, columns), BF16)
+    for h in (1,):
+        weights = put(weights, h, 0, 1, 16)
     for h in (1, 0):
         if h == 1:
+            pairs[h], mid[h], weights = tie(pairs[h], mid[h], weights)
+        else:
             pairs[h], mid[h], new_master, *over[0][h] = tie(pairs[h], mid[h], new_master, *over[0][h])
-        else:
-            pairs[h], mid[h], *over[0][h] = tie(pairs[h], mid[h], *over[0][h])
         over[1][h] = over_x(pairs[h])
         mid_far[h], outwards[h] = z_perm(pairs[h], MIDDLE), z_perm(mid[h], OUTWARDS)
     for h in (0, 1):
@@ -301,12 +309,7 @@
         (distant[h],) = tie(jnp.where(between, mid_far[h], far[h]))
         over[3][h] = over_x(distant[h])
 
-    def put(weights, h, slot, by):
-        value = [owned, pairs, near, distant][slot][h] if by == 0 else over[slot][h][by - 1]
-        at = (sources[slot] * n_x + (x - by) % n_x) * width
-        return lax.dynamic_update_slice(weights, value, (h * half, at))
-
-    weights, near[1] = tie(blank((rows, columns), BF16), near[1])
+    weights, near[1] = tie(weights, near[1])
     for slot in range(2):
         for h in halves:
             for by in range(n_x):

time: 237 us -> 237 us (level)
  waiting for transfers between devices: 107 us -> 93.5 us
  local copies, waits for them, and re-layouts: 26.3 us -> 32.7 us
  starting transfers between devices: 49.1 us -> 53.6 us
    ppermute x13, waiting for transfers between devices: 36.1 us -> 27.4 us  [x_perm(): return lax.ppermute(value, 'dp', pairs)]
    dynamic_update_slice x16 -> x17, local copies, waits for them, and re-layouts: 16.4 us -> 21.8 us  [put(): return lax.dynamic_update_slice(weights, value[:count], (h * half, at))]
    ppermute x20, waiting for transfers between devices: 52.4 us -> 47.2 us  [z_perm(): lax.ppermute(value, 'dp', [(a * n_x + i, b * n_x + i) for a, b in pairs f...]
    ppermute x13, starting transfers between devices: 9.49 us -> 13.2 us  [x_perm(): return lax.ppermute(value, 'dp', pairs)]
  transfers between devices with their start and end apart: 42 -> 42, of which waited for: 25 -> 22; matrix products, arithmetic and copies ran while one was open for 16% -> 19% of each run, Pallas kernels for 11% -> 11%
where the time goes in v10:
time: 237 us; the launch traced here: 235 us
  waiting for transfers between devices  93.5 us (39%)
  starting transfers between devices  53.6 us (23%)
  Pallas kernels  39.9 us (17%)
  local copies, waits for them, and re-layouts  32.7 us (14%)
  other arithmetic  14.6 us (6%)
    ppermute x20, waiting for transfers between devices, z_perm(): lax.ppermute(value, 'dp', [(a * n_x + i, b * n_x + i) for a, b in pairs f...  47.2 us
    ppermute x20, starting transfers between devices, z_perm(): lax.ppermute(value, 'dp', [(a * n_x + i, b * n_x + i) for a, b in pairs f...  34.9 us
    ppermute x13, waiting for transfers between devices, x_perm(): return lax.ppermute(value, 'dp', pairs)  27.4 us
    pallas_call x3, Pallas kernels, multiply(): pl.pallas_call(kernel, grid=(rows // step,), in_specs=[pl.BlockSpec((step...  23.7 us
    dynamic_update_slice x17, local copies, waits for them, and re-layouts, put(): return lax.dynamic_update_slice(weights, value[:count], (h * half, at))  21.8 us
    ppermute x9, waiting for transfers between devices, seat_perm(): lax.ppermute(value, 'tensor', [(i, i ^ flip) for i in range(n_tensor)])  18.9 us
    pallas_call x2, Pallas kernels, update(): pl.pallas_call(kernel, grid=(rows // step,), in_specs=specs + [whole] * 3...  13.5 us
    ppermute x13, starting transfers between devices, x_perm(): return lax.ppermute(value, 'dp', pairs)  13.2 us
  transfers between devices with their start and end apart: 42, of which 22 were waited for; matrix products, arithmetic and copies ran while one was open for 19% of the time, Pallas kernels for 11%

profile of v10, /device:TPU:0, one launch (start us, length us, event | category | flops | bytes accessed | tf_op | source)
XLA Modules:
  0.0 235.3 jit_solution(8137360496828436407)
XLA Ops:
  0.6 2.8 %arrange.1 = (bf16[384,256]{1,0:T(8,128)(2,1)}, bf16[384,512]{1,0:T(8,128)(2,1)}, bf16[384,1280]{1,0:T(8,128)(2,1)}) custom-call(bf16[384,2048]{1,0:T(8,128)(2,1)} %cot_ref.1), custom_call_target="tpu_custom_call" | custom-call | tf_op jit(solution)/shard_map/arrange/pallas_call | solution.py:55
  3.4 3.0 %collective-permute-start.1 = (bf16[384,256]{1,0:T(8,128)(2,1)}, bf16[384,256]{1,0:T(8,128)(2,1)S(1)}, u32[]{:S(2)}, u32[]{:S(2)}) collective-permute-start(bf16[384,256]{1,0:T(8,128)(2,1)} %get-tuple-element.87.refs_0_), channel_id=1, source_target_pairs={{0,2},{1,3},{2,0},{3,1},{4,6},{5,7},{6,4},{7,5},{8,10},{9,11},{10,... | collective-permute-start | bytes 589832 | tf_op jit(solution)/shard_map/ppermute | solution.py:206
  6.4 8.6 %copy.12 = bf16[1536,2048]{0,1:T(8,128)(2,1)} copy(bf16[1536,2048]{1,0:T(8,128)(2,1)} %param.5) | data formatting | bytes 12582912 | tf_op jit(solution)/shard_map/optimization_barrier | solution.py:180
  16.8 4.8 %partials.3 = (bf16[2048,256]{1,0:T(8,128)(2,1)S(1)}, f32[4,4,256]{2,1,0:T(4,128)S(1)}) custom-call(bf16[2048,1536]{1,0:T(8,128)(2,1)} %bitcast.17, bf16[384,256]{1,0:T(8,128)(2,1)S(1)} %copy-done.8, bf16[384,256]{1,0:T(8,128)(2,1)S(1)} %collective-permute-done.refs_1_, bf16[384,256]{1,0:T(8,128)(2,1)S(1)} %collective-permute-done.1.refs_2_, ...), custom_call_target="tpu_custom_call" | custom-call | flops 10000000000 | bytes 3145728 | tf_op jit(solution)/shard_map/partials/pallas_call | solution.py:79
  21.6 1.5 collective-permute-start.6
  23.6 1.5 collective-permute-start.8
  25.2 10.0 %collective-permute-done.4.refs_2_ = bf16[384,512]{1,0:T(8,128)(2,1)S(1)} collective-permute-done((bf16[384,512]{1,0:T(8,128)(2,1)S(1)}, bf16[384,512]{1,0:T(8,128)(2,1)S(1)}, u32[]{:S(2)}, u32[]{:S(2)}) %collective-permute-start.4) | collective-permute-done | bytes 393248 | tf_op jit(solution)/shard_map/ppermute | solution.py:206
  35.1 1.7 collective-permute-done.5.refs_3_
  36.8 6.8 %partials.4 = (bf16[2048,256]{1,0:T(8,128)(2,1)S(1)}, bf16[2048,256]{1,0:T(8,128)(2,1)}, f32[4,4,512]{2,1,0:T(4,128)S(1)}) custom-call(bf16[2048,1536]{1,0:T(8,128)(2,1)} %bitcast.18, bf16[384,512]{1,0:T(8,128)(2,1)S(1)} %copy-done.6, bf16[384,512]{1,0:T(8,128)(2,1)S(1)} %collective-permute-done.3.refs_1_, ...), custom_call_target="tpu_custom_call" | custom-call | tf_op jit(solution)/shard_map/partials/pallas_call | solution.py:79
  44.2 3.0 %collective-permute-done.6 = bf16[2048,256]{1,0:T(8,128)(2,1)S(1)} collective-permute-done((bf16[2048,256]{1,0:T(8,128)(2,1)S(1)}, bf16[2048,256]{1,0:T(8,128)(2,1)S(1)}, u32[]{:S(2)}, u32[]{:S(2)}) %collective-permute-start.6) | collective-permute-done | bytes 1048608 | tf_op jit(solution)/shard_map/ppermute | solution.py:203
  47.2 1.0 add_convert_fusion.7
  49.2 6.0 %collective-permute-done.8.refs_2_ = bf16[384,1280]{1,0:T(8,128)(2,1)S(1)} collective-permute-done((bf16[384,1280]{1,0:T(8,128)(2,1)S(1)}, bf16[384,1280]{1,0:T(8,128)(2,1)S(1)}, u32[]{:S(2)}, u32[]{:S(2)}) %collective-permute-start.8) | collective-permute-done | bytes 983072 | tf_op jit(solution)/shard_map/ppermute | solution.py:206
  55.3 3.6 %collective-permute-start.10 = (bf16[1024,256]{1,0:T(8,128)(2,1)}, bf16[1024,256]{1,0:T(8,128)(2,1)S(1)}, u32[]{:S(2)}, u32[]{:S(2)}) collective-permute-start(bf16[1024,256]{1,0:T(8,128)(2,1)} %add_convert_fusion.6), channel_id=1, source_target_pairs={{0,8},{4,12},{24,16},{28,20},{1,9},{5,13},{25,17},{29,21},{2,10},{... | collective-permute-start | bytes 1572872 | tf_op jit(solution)/shard_map/ppermute | solution.py:199
  58.9 1.3 collective-permute-start.11
  60.3 12.1 %partials.5 = (bf16[2048,256]{1,0:T(8,128)(2,1)}, bf16[2048,256]{1,0:T(8,128)(2,1)S(1)}, bf16[2048,256]{1,0:T(8,128)(2,1)}, bf16[2048,256]{1,0:T(8,128)(2,1)}, b...) custom-call(bf16[2048,1536]{1,0:T(8,128)(2,1)} %bitcast.19, bf16[384,1280]{1,0:T(8,128)(2,1)S(1)} %copy-done.5, ...), custom_call_target="tpu_custom_call" | custom-call | tf_op jit(solution)/shard_map/partials/pallas_call | solution.py:79
  73.0 2.9 %add_convert_fusion.1 = bf16[2048,256]{1,0:T(8,128)(2,1)} fusion(bf16[2048,256]{1,0:T(8,128)(2,1)} %collective-permute-done.12, bf16[2048,256]{1,0:T(8,128)(2,1)} %get-tuple-element.125), kind=kLoop, calls=%fused_computation.1 | loop fusion | flops 2097152 | bytes 3145728 | tf_op jit(solution)/shard_map/convert_element_type | solution.py:103
  75.8 2.3 collective-permute-start.15
  78.1 4.6 %collective-permute-done.11 = bf16[1024,256]{1,0:T(8,128)(2,1)S(1)} collective-permute-done((bf16[1024,256]{1,0:T(8,128)(2,1)}, bf16[1024,256]{1,0:T(8,128)(2,1)S(1)}, u32[]{:S(2)}, u32[]{:S(2)}) %collective-permute-start.11) | collective-permute-done | bytes 524320 | tf_op jit(solution)/shard_map/ppermute | solution.py:199
  85.4 1.5 collective-permute-start.20
  88.1 10.6 %collective-permute-done.16 = bf16[2048,256]{1,0:T(8,128)(2,1)} collective-permute-done((bf16[2048,256]{1,0:T(8,128)(2,1)}, bf16[2048,256]{1,0:T(8,128)(2,1)}, u32[]{:S(2)}, u32[]{:S(2)}) %collective-permute-start.16) | collective-permute-done | bytes 1048608 | tf_op jit(solution)/shard_map/ppermute | solution.py:203
  98.7 1.4 add_convert_fusion.3
  100.1 4.3 %collective-permute-start.19 = (bf16[1024,256]{1,0:T(8,128)(2,1)S(1)}, bf16[1024,256]{1,0:T(8,128)(2,1)S(1)}, u32[]{:S(2)}, u32[]{:S(2)}) collective-permute-start(bf16[1024,256]{1,0:T(8,128)(2,1)S(1)} %add_convert_fusion.3), channel_id=1, source_target_pairs={{0,8},{4,12},{8,0},{12,4},{16,24},{20,28},{24,16},{28,20},{1,9},{5... | collective-permute-start | bytes 1572872 | tf_op jit(solution)/shard_map/ppermute | solution.py:199
  105.1 2.2 add_convert_fusion
  108.1 7.8 %collective-permute-done.19.refs_3_ = bf16[1024,256]{1,0:T(8,128)(2,1)S(1)} collective-permute-done((bf16[1024,256]{1,0:T(8,128)(2,1)S(1)}, bf16[1024,256]{1,0:T(8,128)(2,1)S(1)}, u32[]{:S(2)}, u32[]{:S(2)}) %collective-permute-start.19) | collective-permute-done | bytes 524320 | tf_op jit(solution)/shard_map/ppermute | solution.py:199
  115.9 1.7 add_convert_fusion.2
  117.6 2.5 %collective-permute-start.21 = (bf16[1024,256]{1,0:T(8,128)(2,1)S(1)}, bf16[1024,256]{1,0:T(8,128)(2,1)S(1)}, u32[]{:S(2)}, u32[]{:S(2)}) collective-permute-start(bf16[1024,256]{1,0:T(8,128)(2,1)S(1)} %add_convert_fusion.2), channel_id=1, source_target_pairs={{0,8},{4,12},{8,0},{12,4},{16,24},{20,28},{24,16},{28,20},{1,9},{5... | collective-permute-start | bytes 1572872 | tf_op jit(solution)/shard_map/ppermute | solution.py:199
  120.7 3.1 %collective-permute-done.13 = f32[16,16]{1,0:T(8,128)S(1)} collective-permute-done((f32[16,16]{1,0:T(8,128)S(1)}, f32[16,16]{1,0:T(8,128)S(1)}, u32[]{:S(2)}, u32[]{:S(2)}) %collective-permute-start.13) | collective-permute-done | bytes 1056 | tf_op jit(solution)/shard_map/ppermute | solution.py:203
  123.8 7.6 %collective-permute-done.21.refs_4_ = bf16[1024,256]{1,0:T(8,128)(2,1)S(1)} collective-permute-done((bf16[1024,256]{1,0:T(8,128)(2,1)S(1)}, bf16[1024,256]{1,0:T(8,128)(2,1)S(1)}, u32[]{:S(2)}, u32[]{:S(2)}) %collective-permute-start.21) | collective-permute-done | bytes 524320 | tf_op jit(solution)/shard_map/ppermute | solution.py:199
  131.4 7.0 %weights.1 = (bf16[1024,256]{1,0:T(8,128)(2,1)}, bf16[1024,256]{1,0:T(8,128)(2,1)}) custom-call(bf16[2048,256]{1,0:T(8,128)(2,1)S(1)} %copy-done, bf16[2048,256]{1,0:T(8,128)(2,1)S(1)} %collective-permute-done.14.refs_1_, bf16[2048,256]{1,0:T(8,128)(2,1)S(1)} %collective-permute-done.18.refs_2_, bf16[1024,256]{1,0:T(8,128)(2,1)S(1)} %collective-permute-done.19.refs_3_, ...), custom_call_target="tpu_custom_call" | custom-call | tf_op jit(solution)/shard_map/weights/pallas_call | solution.py:155
  139.0 4.6 %collective-permute-start.25 = (bf16[1024,256]{1,0:T(8,128)(2,1)}, bf16[1024,256]{1,0:T(8,128)(2,1)}, u32[]{:S(2)}, u32[]{:S(2)}) collective-permute-start(bf16[1024,256]{1,0:T(8,128)(2,1)} %get-tuple-element.139), channel_id=1, source_target_pairs={{0,8},{4,12},{8,0},{12,4},{16,24},{20,28},{24,16},{28,20},{1,9},{5... | collective-permute-start | bytes 1572872 | tf_op jit(solution)/shard_map/ppermute | solution.py:199
  143.6 1.5 collective-permute-start.26
  145.1 2.1 collective-permute-start.22
  147.2 1.5 collective-permute-start.23
  148.6 2.5 %collective-permute-done.27 = bf16[1024,256]{1,0:T(8,128)(2,1)} collective-permute-done((bf16[1024,256]{1,0:T(8,128)(2,1)}, bf16[1024,256]{1,0:T(8,128)(2,1)}, u32[]{:S(2)}, u32[]{:S(2)}) %collective-permute-start.27) | collective-permute-done | bytes 524320 | tf_op jit(solution)/shard_map/ppermute | solution.py:203
  151.7 1.3 slice_dynamic-update-slice_fusion
  153.0 3.8 %collective-permute-done.25 = bf16[1024,256]{1,0:T(8,128)(2,1)} collective-permute-done((bf16[1024,256]{1,0:T(8,128)(2,1)}, bf16[1024,256]{1,0:T(8,128)(2,1)}, u32[]{:S(2)}, u32[]{:S(2)}) %collective-permute-start.25) | collective-permute-done | bytes 524320 | tf_op jit(solution)/shard_map/ppermute | solution.py:199
  156.8 1.5 collective-permute-start.28
  158.3 1.3 collective-permute-start.29
  159.6 8.5 %collective-permute-done.22 = bf16[1024,256]{1,0:T(8,128)(2,1)} collective-permute-done((bf16[1024,256]{1,0:T(8,128)(2,1)}, bf16[1024,256]{1,0:T(8,128)(2,1)}, u32[]{:S(2)}, u32[]{:S(2)}) %collective-permute-start.22) | collective-permute-done | bytes 524320 | tf_op jit(solution)/shard_map/ppermute | solution.py:199
  168.1 1.5 collective-permute-start.30
  169.5 1.0 copy-done.2
  170.6 1.0 copy-done.4
  171.6 6.4 %states.1 = (f32[2048,256]{1,0:T(8,128)}, f32[2048,256]{1,0:T(8,128)}, f32[2048,256]{1,0:T(8,128)}) custom-call(bf16[2048,256]{1,0:T(8,128)(2,1)S(1)} %copy-done, bf16[2048,256]{1,0:T(8,128)(2,1)S(1)} %collective-permute-done.14.refs_1_, bf16[2048,256]{1,0:T(8,128)(2,1)S(1)} %collective-permute-done.18.refs_2_, bf16[1024,256]{1,0:T(8,128)(2,1)S(1)} %copy-done.2, ...), custom_call_target="tpu_custom_call" | custom-call | tf_op jit(solution)/shard_map/states/pallas_call | solution.py:155
  179.4 1.3 collective-permute-start.32
  180.7 1.1 broadcast_select_fusion.3
  181.8 1.5 collective-permute-start.37
  183.4 1.9 constant_dynamic-update-slice_fusion.15
  185.2 1.9 constant_dynamic-update-slice_fusion.14
  187.1 1.9 constant_dynamic-update-slice_fusion.7
  189.0 2.5 %collective-permute-done.32 = bf16[1024,256]{1,0:T(8,128)(2,1)S(1)} collective-permute-done((bf16[1024,256]{1,0:T(8,128)(2,1)}, bf16[1024,256]{1,0:T(8,128)(2,1)S(1)}, u32[]{:S(2)}, u32[]{:S(2)}) %collective-permute-start.32) | collective-permute-done | bytes 524320 | tf_op jit(solution)/shard_map/ppermute | solution.py:199
  191.5 2.4 %collective-permute-done.33 = bf16[1024,256]{1,0:T(8,128)(2,1)S(1)} collective-permute-done((bf16[1024,256]{1,0:T(8,128)(2,1)}, bf16[1024,256]{1,0:T(8,128)(2,1)S(1)}, u32[]{:S(2)}, u32[]{:S(2)}) %collective-permute-start.33) | collective-permute-done | bytes 524320 | tf_op jit(solution)/shard_map/ppermute | solution.py:203
  193.9 1.3 collective-permute-start.34
  195.3 1.3 collective-permute-start.35
  197.2 1.9 constant_dynamic-update-slice_fusion.6
  199.0 1.9 constant_dynamic-update-slice_fusion.13
  201.7 1.9 constant_dynamic-update-slice_fusion.5
  203.6 1.9 constant_dynamic-update-slice_fusion.4
  205.5 2.6 %collective-permute-done.34 = bf16[1024,256]{1,0:T(8,128)(2,1)S(1)} collective-permute-done((bf16[1024,256]{1,0:T(8,128)(2,1)}, bf16[1024,256]{1,0:T(8,128)(2,1)S(1)}, u32[]{:S(2)}, u32[]{:S(2)}) %collective-permute-start.34) | collective-permute-done | bytes 524320 | tf_op jit(solution)/shard_map/ppermute | solution.py:199
  208.1 1.9 collective-permute-start.39
  210.1 3.6 %collective-permute-done.35 = bf16[1024,256]{1,0:T(8,128)(2,1)S(1)} collective-permute-done((bf16[1024,256]{1,0:T(8,128)(2,1)S(1)}, bf16[1024,256]{1,0:T(8,128)(2,1)S(1)}, u32[]{:S(2)}, u32[]{:S(2)}) %collective-permute-start.35) | collective-permute-done | bytes 524320 | tf_op jit(solution)/shard_map/ppermute | solution.py:199
  213.7 2.0 collective-permute-start.38
  219.9 2.8 %collective-permute-done.40 = f32[16,16]{1,0:T(8,128)S(1)} collective-permute-done((f32[16,16]{1,0:T(8,128)S(1)}, f32[16,16]{1,0:T(8,128)S(1)}, u32[]{:S(2)}, u32[]{:S(2)}) %collective-permute-start.40) | collective-permute-done | bytes 1056 | tf_op jit(solution)/shard_map/ppermute | solution.py:199
  224.6 2.7 %collective-permute-done.41 = f32[16,16]{1,0:T(8,128)S(1)} collective-permute-done((f32[16,16]{1,0:T(8,128)S(1)}, f32[16,16]{1,0:T(8,128)S(1)}, u32[]{:S(2)}, u32[]{:S(2)}) %collective-permute-start.41) | collective-permute-done | bytes 1056 | tf_op jit(solution)/shard_map/ppermute | solution.py:199
  227.9 5.7 %collective-permute-done.38 = bf16[1024,256]{1,0:T(8,128)(2,1)S(1)} collective-permute-done((bf16[1024,256]{1,0:T(8,128)(2,1)S(1)}, bf16[1024,256]{1,0:T(8,128)(2,1)S(1)}, u32[]{:S(2)}, u32[]{:S(2)}) %collective-permute-start.38) | collective-permute-done | bytes 524320 | tf_op jit(solution)/shard_map/ppermute | solution.py:203
  (92 shorter events, 22.7 us)
Async XLA Ops:
  3.4 11.6 %copy-start.8 = (bf16[384,256]{1,0:T(8,128)(2,1)S(1)}, bf16[384,256]{1,0:T(8,128)(2,1)}, u32[]{:S(2)}) copy-start(bf16[384,256]{1,0:T(8,128)(2,1)} %get-tuple-element.87.refs_0_) | copy-start | bytes 589828
  3.4 11.7 %collective-permute-start.1 = (bf16[384,256]{1,0:T(8,128)(2,1)}, bf16[384,256]{1,0:T(8,128)(2,1)S(1)}, u32[]{:S(2)}, u32[]{:S(2)}) collective-permute-start(bf16[384,256]{1,0:T(8,128)(2,1)} %get-tuple-element.87.refs_0_), channel_id=1, source_target_pairs={{0,2},{1,3},{2,0},{3,1},{4,6},{5,7},{6,4},{7,5},{8,10},{9,11},{10,... | collective-permute-start | bytes 589832 | tf_op jit(solution)/shard_map/ppermute | solution.py:206
  15.0 8.1 %copy-start.6 = (bf16[384,512]{1,0:T(8,128)(2,1)S(1)}, bf16[384,512]{1,0:T(8,128)(2,1)}, u32[]{:S(2)}) copy-start(bf16[384,512]{1,0:T(8,128)(2,1)} %get-tuple-element.91.refs_0_) | copy-start | bytes 1179652
  15.0 8.7 %copy-start.5 = (bf16[384,1280]{1,0:T(8,128)(2,1)S(1)}, bf16[384,1280]{1,0:T(8,128)(2,1)}, u32[]{:S(2)}) copy-start(bf16[384,1280]{1,0:T(8,128)(2,1)} %get-tuple-element.99.refs_0_) | copy-start | bytes 2949124
  15.0 1.5 collective-permute-start
  15.1 1.7 collective-permute-start.2
  21.6 25.6 %collective-permute-start.6 = (bf16[2048,256]{1,0:T(8,128)(2,1)S(1)}, bf16[2048,256]{1,0:T(8,128)(2,1)S(1)}, u32[]{:S(2)}, u32[]{:S(2)}) collective-permute-start(bf16[2048,256]{1,0:T(8,128)(2,1)S(1)} %get-tuple-element.89), channel_id=1, source_target_pairs={{0,4},{4,0},{8,12},{12,8},{16,20},{20,16},{24,28},{28,24},{1,5},{5... | collective-permute-start | bytes 3145736 | tf_op jit(solution)/shard_map/ppermute | solution.py:203
  23.1 12.0 %collective-permute-start.4 = (bf16[384,512]{1,0:T(8,128)(2,1)S(1)}, bf16[384,512]{1,0:T(8,128)(2,1)S(1)}, u32[]{:S(2)}, u32[]{:S(2)}) collective-permute-start(bf16[384,512]{1,0:T(8,128)(2,1)S(1)} %copy-done.6), channel_id=1, source_target_pairs={{0,2},{1,3},{2,0},{3,1},{4,6},{5,7},{6,4},{7,5},{8,10},{9,11},{10,... | collective-permute-start | bytes 1179656 | tf_op jit(solution)/shard_map/ppermute | solution.py:206
  23.6 31.5 %collective-permute-start.8 = (bf16[384,1280]{1,0:T(8,128)(2,1)S(1)}, bf16[384,1280]{1,0:T(8,128)(2,1)S(1)}, u32[]{:S(2)}, u32[]{:S(2)}) collective-permute-start(bf16[384,1280]{1,0:T(8,128)(2,1)S(1)} %copy-done.5), channel_id=1, source_target_pairs={{0,2},{1,3},{2,0},{3,1},{4,6},{5,7},{6,4},{7,5},{8,10},{9,11},{10,... | collective-permute-start | bytes 2949128 | tf_op jit(solution)/shard_map/ppermute | solution.py:206
  25.2 10.0 %collective-permute-start.3 = (bf16[384,512]{1,0:T(8,128)(2,1)S(1)}, bf16[384,512]{1,0:T(8,128)(2,1)S(1)}, u32[]{:S(2)}, u32[]{:S(2)}) collective-permute-start(bf16[384,512]{1,0:T(8,128)(2,1)S(1)} %copy-done.6), channel_id=1, source_target_pairs={{0,1},{1,0},{2,3},{3,2},{4,5},{5,4},{6,7},{7,6},{8,9},{9,8},{10,11... | collective-permute-start | bytes 1179656 | tf_op jit(solution)/shard_map/ppermute | solution.py:206
  35.1 1.7 collective-permute-start.5
  43.7 29.3 %collective-permute-start.12 = (bf16[2048,256]{1,0:T(8,128)(2,1)}, bf16[2048,256]{1,0:T(8,128)(2,1)}, u32[]{:S(2)}, u32[]{:S(2)}) collective-permute-start(bf16[2048,256]{1,0:T(8,128)(2,1)} %get-tuple-element.104), channel_id=1, source_target_pairs={{0,4},{4,0},{8,12},{12,8},{16,20},{20,16},{24,28},{28,24},{1,5},{5... | collective-permute-start | bytes 3145736 | tf_op jit(solution)/shard_map/ppermute | solution.py:203
  47.2 8.0 %copy-start.9 = (bf16[2048,256]{1,0:T(8,128)(2,1)}, bf16[2048,256]{1,0:T(8,128)(2,1)S(1)}, u32[]{:S(2)}) copy-start(bf16[2048,256]{1,0:T(8,128)(2,1)S(1)} %collective-permute-done.6) | copy-start | bytes 3145732
  49.2 11.1 %collective-permute-start.7 = (bf16[384,1280]{1,0:T(8,128)(2,1)S(1)}, bf16[384,1280]{1,0:T(8,128)(2,1)}, u32[]{:S(2)}, u32[]{:S(2)}) collective-permute-start(bf16[384,1280]{1,0:T(8,128)(2,1)S(1)} %copy-done.5), channel_id=1, source_target_pairs={{0,1},{1,0},{2,3},{3,2},{4,5},{5,4},{6,7},{7,6},{8,9},{9,8},{10,11... | collective-permute-start | bytes 2949128 | tf_op jit(solution)/shard_map/ppermute | solution.py:206
  55.2 5.1 %collective-permute-start.9 = (bf16[384,1280]{1,0:T(8,128)(2,1)S(1)}, bf16[384,1280]{1,0:T(8,128)(2,1)}, u32[]{:S(2)}, u32[]{:S(2)}) collective-permute-start(bf16[384,1280]{1,0:T(8,128)(2,1)S(1)} %collective-permute-done.8.refs_2_), channel_id=1, source_target_pairs={{0,1},{1,0},{2,3},{3,2},{4,5},{5,4},{6,7},{7,6},{8,9},{9,8},{10,11... | collective-permute-start | bytes 2949128 | tf_op jit(solution)/shard_map/ppermute | solution.py:206
  55.3 27.4 %copy-start.10 = (bf16[2048,256]{1,0:T(8,128)(2,1)S(1)}, bf16[2048,256]{1,0:T(8,128)(2,1)}, u32[]{:S(2)}) copy-start(bf16[2048,256]{1,0:T(8,128)(2,1)} %copy-done.9) | copy-start | bytes 3145732
  55.3 29.1 %collective-permute-start.10 = (bf16[1024,256]{1,0:T(8,128)(2,1)}, bf16[1024,256]{1,0:T(8,128)(2,1)S(1)}, u32[]{:S(2)}, u32[]{:S(2)}) collective-permute-start(bf16[1024,256]{1,0:T(8,128)(2,1)} %add_convert_fusion.6), channel_id=1, source_target_pairs={{0,8},{4,12},{24,16},{28,20},{1,9},{5,13},{25,17},{29,21},{2,10},{... | collective-permute-start | bytes 1572872 | tf_op jit(solution)/shard_map/ppermute | solution.py:199
  58.9 23.7 %collective-permute-start.11 = (bf16[1024,256]{1,0:T(8,128)(2,1)}, bf16[1024,256]{1,0:T(8,128)(2,1)S(1)}, u32[]{:S(2)}, u32[]{:S(2)}) collective-permute-start(bf16[1024,256]{1,0:T(8,128)(2,1)} %add_convert_fusion.7), channel_id=1, source_target_pairs={{0,8},{4,12},{24,16},{28,20},{1,9},{5,13},{25,17},{29,21},{2,10},{... | collective-permute-start | bytes 1572872 | tf_op jit(solution)/shard_map/ppermute | solution.py:199
  72.4 13.1 %copy-start.7 = (bf16[2048,256]{1,0:T(8,128)(2,1)}, bf16[2048,256]{1,0:T(8,128)(2,1)S(1)}, u32[]{:S(2)}) copy-start(bf16[2048,256]{1,0:T(8,128)(2,1)S(1)} %get-tuple-element.120) | copy-start | bytes 3145732
  72.4 59.1 %copy-start = (bf16[2048,256]{1,0:T(8,128)(2,1)S(1)}, bf16[2048,256]{1,0:T(8,128)(2,1)}, u32[]{:S(2)}) copy-start(bf16[2048,256]{1,0:T(8,128)(2,1)} %get-tuple-element.134.refs_0_) | copy-start | bytes 3145732
  72.4 26.4 %collective-permute-start.16 = (bf16[2048,256]{1,0:T(8,128)(2,1)}, bf16[2048,256]{1,0:T(8,128)(2,1)}, u32[]{:S(2)}, u32[]{:S(2)}) collective-permute-start(bf16[2048,256]{1,0:T(8,128)(2,1)} %get-tuple-element.105), channel_id=1, source_target_pairs={{0,4},{4,0},{8,12},{12,8},{16,20},{20,16},{24,28},{28,24},{1,5},{5... | collective-permute-start | bytes 3145736 | tf_op jit(solution)/shard_map/ppermute | solution.py:203
  75.8 29.3 %collective-permute-start.15 = (bf16[2048,256]{1,0:T(8,128)(2,1)}, bf16[2048,256]{1,0:T(8,128)(2,1)}, u32[]{:S(2)}, u32[]{:S(2)}) collective-permute-start(bf16[2048,256]{1,0:T(8,128)(2,1)} %add_convert_fusion.1), channel_id=1, source_target_pairs={{0,8},{4,12},{24,16},{28,20},{1,9},{5,13},{25,17},{29,21},{2,10},{... | collective-permute-start | bytes 3145736 | tf_op jit(solution)/shard_map/ppermute | solution.py:199
  83.7 4.4 %collective-permute-start.17 = (bf16[1024,256]{1,0:T(8,128)(2,1)}, bf16[1024,256]{1,0:T(8,128)(2,1)S(1)}, u32[]{:S(2)}, u32[]{:S(2)}) collective-permute-start(bf16[1024,256]{1,0:T(8,128)(2,1)} %add_convert_fusion.5), channel_id=1, source_target_pairs={{8,16},{12,20},{16,8},{20,12},{9,17},{13,21},{17,9},{21,13},{10,18... | collective-permute-start | bytes 1572872 | tf_op jit(solution)/shard_map/ppermute | solution.py:199
  85.4 22.7 %collective-permute-start.20 = (bf16[1024,256]{1,0:T(8,128)(2,1)}, bf16[1024,256]{1,0:T(8,128)(2,1)}, u32[]{:S(2)}, u32[]{:S(2)}) collective-permute-start(bf16[1024,256]{1,0:T(8,128)(2,1)} %add_convert_fusion.4), channel_id=1, source_target_pairs={{8,16},{12,20},{16,8},{20,12},{9,17},{13,21},{17,9},{21,13},{10,18... | collective-permute-start | bytes 1572872 | tf_op jit(solution)/shard_map/ppermute | solution.py:199
  87.3 36.5 %collective-permute-start.14 = (bf16[2048,256]{1,0:T(8,128)(2,1)}, bf16[2048,256]{1,0:T(8,128)(2,1)S(1)}, u32[]{:S(2)}, u32[]{:S(2)}) collective-permute-start(bf16[2048,256]{1,0:T(8,128)(2,1)} %copy-done.7), channel_id=1, source_target_pairs={{0,4},{4,0},{8,12},{12,8},{16,20},{20,16},{24,28},{28,24},{1,5},{5... | collective-permute-start | bytes 3145736 | tf_op jit(solution)/shard_map/ppermute | solution.py:203
  100.1 15.8 %collective-permute-start.19 = (bf16[1024,256]{1,0:T(8,128)(2,1)S(1)}, bf16[1024,256]{1,0:T(8,128)(2,1)S(1)}, u32[]{:S(2)}, u32[]{:S(2)}) collective-permute-start(bf16[1024,256]{1,0:T(8,128)(2,1)S(1)} %add_convert_fusion.3), channel_id=1, source_target_pairs={{0,8},{4,12},{8,0},{12,4},{16,24},{20,28},{24,16},{28,20},{1,9},{5... | collective-permute-start | bytes 1572872 | tf_op jit(solution)/shard_map/ppermute | solution.py:199
  107.4 24.1 %collective-permute-start.18 = (bf16[2048,256]{1,0:T(8,128)(2,1)S(1)}, bf16[2048,256]{1,0:T(8,128)(2,1)S(1)}, u32[]{:S(2)}, u32[]{:S(2)}) collective-permute-start(bf16[2048,256]{1,0:T(8,128)(2,1)S(1)} %add_convert_fusion), channel_id=1, source_target_pairs={{8,16},{12,20},{16,8},{20,12},{9,17},{13,21},{17,9},{21,13},{10,18... | collective-permute-start | bytes 3145736 | tf_op jit(solution)/shard_map/ppermute | solution.py:199
  115.9 15.5 %copy-start.1 = (bf16[1024,256]{1,0:T(8,128)(2,1)}, bf16[1024,256]{1,0:T(8,128)(2,1)S(1)}, u32[]{:S(2)}) copy-start(bf16[1024,256]{1,0:T(8,128)(2,1)S(1)} %collective-permute-done.19.refs_3_) | copy-start | bytes 1572868
  117.6 13.8 %collective-permute-start.21 = (bf16[1024,256]{1,0:T(8,128)(2,1)S(1)}, bf16[1024,256]{1,0:T(8,128)(2,1)S(1)}, u32[]{:S(2)}, u32[]{:S(2)}) collective-permute-start(bf16[1024,256]{1,0:T(8,128)(2,1)S(1)} %add_convert_fusion.2), channel_id=1, source_target_pairs={{0,8},{4,12},{8,0},{12,4},{16,24},{20,28},{24,16},{28,20},{1,9},{5... | collective-permute-start | bytes 1572872 | tf_op jit(solution)/shard_map/ppermute | solution.py:199
  120.2 3.7 %collective-permute-start.13 = (f32[16,16]{1,0:T(8,128)S(1)}, f32[16,16]{1,0:T(8,128)S(1)}, u32[]{:S(2)}, u32[]{:S(2)}) collective-permute-start(f32[16,16]{1,0:T(8,128)S(1)} %select_reduce_fusion), channel_id=1, source_target_pairs={{0,4},{4,0},{8,12},{12,8},{16,20},{20,16},{24,28},{28,24},{1,5},{5... | collective-permute-start | bytes 3080 | tf_op jit(solution)/shard_map/ppermute | solution.py:203
  131.4 7.1 %copy-start.3 = (bf16[1024,256]{1,0:T(8,128)(2,1)}, bf16[1024,256]{1,0:T(8,128)(2,1)S(1)}, u32[]{:S(2)}) copy-start(bf16[1024,256]{1,0:T(8,128)(2,1)S(1)} %collective-permute-done.21.refs_4_) | copy-start | bytes 1572868
  138.5 12.7 %collective-permute-start.27 = (bf16[1024,256]{1,0:T(8,128)(2,1)}, bf16[1024,256]{1,0:T(8,128)(2,1)}, u32[]{:S(2)}, u32[]{:S(2)}) collective-permute-start(bf16[1024,256]{1,0:T(8,128)(2,1)} %get-tuple-element.139), channel_id=1, source_target_pairs={{0,4},{4,0},{8,12},{12,8},{16,20},{20,16},{24,28},{28,24},{1,5},{5... | collective-permute-start | bytes 1572872 | tf_op jit(solution)/shard_map/ppermute | solution.py:203
  139.0 17.8 %collective-permute-start.25 = (bf16[1024,256]{1,0:T(8,128)(2,1)}, bf16[1024,256]{1,0:T(8,128)(2,1)}, u32[]{:S(2)}, u32[]{:S(2)}) collective-permute-start(bf16[1024,256]{1,0:T(8,128)(2,1)} %get-tuple-element.139), channel_id=1, source_target_pairs={{0,8},{4,12},{8,0},{12,4},{16,24},{20,28},{24,16},{28,20},{1,9},{5... | collective-permute-start | bytes 1572872 | tf_op jit(solution)/shard_map/ppermute | solution.py:199
  143.6 13.2 %collective-permute-start.26 = (bf16[1024,256]{1,0:T(8,128)(2,1)}, bf16[1024,256]{1,0:T(8,128)(2,1)}, u32[]{:S(2)}, u32[]{:S(2)}) collective-permute-start(bf16[1024,256]{1,0:T(8,128)(2,1)} %get-tuple-element.139), channel_id=1, source_target_pairs={{8,16},{12,20},{16,8},{20,12},{9,17},{13,21},{17,9},{21,13},{10,18... | collective-permute-start | bytes 1572872 | tf_op jit(solution)/shard_map/ppermute | solution.py:199
  145.1 22.9 %collective-permute-start.22 = (bf16[1024,256]{1,0:T(8,128)(2,1)}, bf16[1024,256]{1,0:T(8,128)(2,1)}, u32[]{:S(2)}, u32[]{:S(2)}) collective-permute-start(bf16[1024,256]{1,0:T(8,128)(2,1)} %get-tuple-element.133), channel_id=1, source_target_pairs={{0,8},{4,12},{8,0},{12,4},{16,24},{20,28},{24,16},{28,20},{1,9},{5... | collective-permute-start | bytes 1572872 | tf_op jit(solution)/shard_map/ppermute | solution.py:199
  147.2 30.9 %collective-permute-start.23 = (bf16[1024,256]{1,0:T(8,128)(2,1)}, bf16[1024,256]{1,0:T(8,128)(2,1)}, u32[]{:S(2)}, u32[]{:S(2)}) collective-permute-start(bf16[1024,256]{1,0:T(8,128)(2,1)} %get-tuple-element.133), channel_id=1, source_target_pairs={{8,16},{12,20},{16,8},{20,12},{9,17},{13,21},{17,9},{21,13},{10,18... | collective-permute-start | bytes 1572872 | tf_op jit(solution)/shard_map/ppermute | solution.py:199
  151.2 26.9 %collective-permute-start.24 = (bf16[1024,256]{1,0:T(8,128)(2,1)}, bf16[1024,256]{1,0:T(8,128)(2,1)}, u32[]{:S(2)}, u32[]{:S(2)}) collective-permute-start(bf16[1024,256]{1,0:T(8,128)(2,1)} %get-tuple-element.133), channel_id=1, source_target_pairs={{0,4},{4,0},{8,12},{12,8},{16,20},{20,16},{24,28},{28,24},{1,5},{5... | collective-permute-start | bytes 1572872 | tf_op jit(solution)/shard_map/ppermute | solution.py:203
  156.8 22.6 %collective-permute-start.28 = (bf16[1024,256]{1,0:T(8,128)(2,1)}, bf16[1024,256]{1,0:T(8,128)(2,1)}, u32[]{:S(2)}, u32[]{:S(2)}) collective-permute-start(bf16[1024,256]{1,0:T(8,128)(2,1)} %collective-permute-done.25), channel_id=1, source_target_pairs={{8,16},{12,20},{16,8},{20,12},{9,17},{13,21},{17,9},{21,13},{10,18... | collective-permute-start | bytes 1572872 | tf_op jit(solution)/shard_map/ppermute | solution.py:199
  158.3 22.4 %collective-permute-start.29 = (bf16[1024,256]{1,0:T(8,128)(2,1)}, bf16[1024,256]{1,0:T(8,128)(2,1)}, u32[]{:S(2)}, u32[]{:S(2)}) collective-permute-start(bf16[1024,256]{1,0:T(8,128)(2,1)} %collective-permute-done.26), channel_id=1, source_target_pairs={{8,0},{12,4},{16,24},{20,28},{9,1},{13,5},{17,25},{21,29},{10,2},{... | collective-permute-start | bytes 1572872 | tf_op jit(solution)/shard_map/ppermute | solution.py:199
  168.1 12.6 %collective-permute-start.30 = (bf16[1024,256]{1,0:T(8,128)(2,1)}, bf16[1024,256]{1,0:T(8,128)(2,1)}, u32[]{:S(2)}, u32[]{:S(2)}) collective-permute-start(bf16[1024,256]{1,0:T(8,128)(2,1)} %collective-permute-done.25), channel_id=1, source_target_pairs={{0,4},{4,0},{8,12},{12,8},{16,20},{20,16},{24,28},{28,24},{1,5},{5... | collective-permute-start | bytes 1572872 | tf_op jit(solution)/shard_map/ppermute | solution.py:203
  169.5 1.0 copy-start.2
  170.6 1.0 copy-start.4
  178.1 10.9 %collective-permute-start.31 = (bf16[1024,256]{1,0:T(8,128)(2,1)}, bf16[1024,256]{1,0:T(8,128)(2,1)S(1)}, u32[]{:S(2)}, u32[]{:S(2)}) collective-permute-start(bf16[1024,256]{1,0:T(8,128)(2,1)} %collective-permute-done.22), channel_id=1, source_target_pairs={{8,16},{12,20},{16,8},{20,12},{9,17},{13,21},{17,9},{21,13},{10,18... | collective-permute-start | bytes 1572872 | tf_op jit(solution)/shard_map/ppermute | solution.py:199
  178.8 15.1 %collective-permute-start.33 = (bf16[1024,256]{1,0:T(8,128)(2,1)}, bf16[1024,256]{1,0:T(8,128)(2,1)S(1)}, u32[]{:S(2)}, u32[]{:S(2)}) collective-permute-start(bf16[1024,256]{1,0:T(8,128)(2,1)} %collective-permute-done.22), channel_id=1, source_target_pairs={{0,4},{4,0},{8,12},{12,8},{16,20},{20,16},{24,28},{28,24},{1,5},{5... | collective-permute-start | bytes 1572872 | tf_op jit(solution)/shard_map/ppermute | solution.py:203
  179.4 12.1 %collective-permute-start.32 = (bf16[1024,256]{1,0:T(8,128)(2,1)}, bf16[1024,256]{1,0:T(8,128)(2,1)S(1)}, u32[]{:S(2)}, u32[]{:S(2)}) collective-permute-start(bf16[1024,256]{1,0:T(8,128)(2,1)} %collective-permute-done.23), channel_id=1, source_target_pairs={{8,0},{12,4},{16,24},{20,28},{9,1},{13,5},{17,25},{21,29},{10,2},{... | collective-permute-start | bytes 1572872 | tf_op jit(solution)/shard_map/ppermute | solution.py:199
  181.8 42.0 %collective-permute-start.37 = (bf16[1024,256]{1,0:T(8,128)(2,1)S(1)}, bf16[1024,256]{1,0:T(8,128)(2,1)S(1)}, u32[]{:S(2)}, u32[]{:S(2)}) collective-permute-start(bf16[1024,256]{1,0:T(8,128)(2,1)S(1)} %broadcast_select_fusion.3), channel_id=1, source_target_pairs={{0,4},{4,0},{8,12},{12,8},{16,20},{20,16},{24,28},{28,24},{1,5},{5... | collective-permute-start | bytes 1572872 | tf_op jit(solution)/shard_map/ppermute | solution.py:203
  193.9 14.2 %collective-permute-start.34 = (bf16[1024,256]{1,0:T(8,128)(2,1)}, bf16[1024,256]{1,0:T(8,128)(2,1)S(1)}, u32[]{:S(2)}, u32[]{:S(2)}) collective-permute-start(bf16[1024,256]{1,0:T(8,128)(2,1)} %collective-permute-done.28), channel_id=1, source_target_pairs={{8,0},{12,4},{16,24},{20,28},{9,1},{13,5},{17,25},{21,29},{10,2},{... | collective-permute-start | bytes 1572872 | tf_op jit(solution)/shard_map/ppermute | solution.py:199
  195.3 18.4 %collective-permute-start.35 = (bf16[1024,256]{1,0:T(8,128)(2,1)S(1)}, bf16[1024,256]{1,0:T(8,128)(2,1)S(1)}, u32[]{:S(2)}, u32[]{:S(2)}) collective-permute-start(bf16[1024,256]{1,0:T(8,128)(2,1)S(1)} %collective-permute-done.31), channel_id=1, source_target_pairs={{8,0},{12,4},{16,24},{20,28},{9,1},{13,5},{17,25},{21,29},{10,2},{... | collective-permute-start | bytes 1572872 | tf_op jit(solution)/shard_map/ppermute | solution.py:199
  196.6 22.5 %collective-permute-start.36 = (bf16[1024,256]{1,0:T(8,128)(2,1)S(1)}, bf16[1024,256]{1,0:T(8,128)(2,1)S(1)}, u32[]{:S(2)}, u32[]{:S(2)}) collective-permute-start(bf16[1024,256]{1,0:T(8,128)(2,1)S(1)} %broadcast_select_fusion.1), channel_id=1, source_target_pairs={{0,4},{4,0},{8,12},{12,8},{16,20},{20,16},{24,28},{28,24},{1,5},{5... | collective-permute-start | bytes 1572872 | tf_op jit(solution)/shard_map/ppermute | solution.py:203
  208.1 26.3 %collective-permute-start.39 = (bf16[1024,256]{1,0:T(8,128)(2,1)S(1)}, bf16[1024,256]{1,0:T(8,128)(2,1)S(1)}, u32[]{:S(2)}, u32[]{:S(2)}) collective-permute-start(bf16[1024,256]{1,0:T(8,128)(2,1)S(1)} %broadcast_select_fusion.2), channel_id=1, source_target_pairs={{0,4},{4,0},{8,12},{12,8},{16,20},{20,16},{24,28},{28,24},{1,5},{5... | collective-permute-start | bytes 1572872 | tf_op jit(solution)/shard_map/ppermute | solution.py:203
  213.7 19.9 %collective-permute-start.38 = (bf16[1024,256]{1,0:T(8,128)(2,1)S(1)}, bf16[1024,256]{1,0:T(8,128)(2,1)S(1)}, u32[]{:S(2)}, u32[]{:S(2)}) collective-permute-start(bf16[1024,256]{1,0:T(8,128)(2,1)S(1)} %broadcast_select_fusion), channel_id=1, source_target_pairs={{0,4},{4,0},{8,12},{12,8},{16,20},{20,16},{24,28},{28,24},{1,5},{5... | collective-permute-start | bytes 1572872 | tf_op jit(solution)/shard_map/ppermute | solution.py:203
  219.1 3.7 %collective-permute-start.40 = (f32[16,16]{1,0:T(8,128)S(1)}, f32[16,16]{1,0:T(8,128)S(1)}, u32[]{:S(2)}, u32[]{:S(2)}) collective-permute-start(f32[16,16]{1,0:T(8,128)S(1)} %max.9), channel_id=1, source_target_pairs={{0,8},{4,12},{8,0},{12,4},{16,24},{20,28},{24,16},{28,20},{1,9},{5... | collective-permute-start | bytes 3080 | tf_op jit(solution)/shard_map/ppermute | solution.py:199
  222.7 4.5 %collective-permute-start.41 = (f32[16,16]{1,0:T(8,128)S(1)}, f32[16,16]{1,0:T(8,128)S(1)}, u32[]{:S(2)}, u32[]{:S(2)}) collective-permute-start(f32[16,16]{1,0:T(8,128)S(1)} %max.10), channel_id=1, source_target_pairs={{0,16},{4,20},{8,24},{12,28},{16,0},{20,4},{24,8},{28,12},{1,17},{... | collective-permute-start | bytes 3080 | tf_op jit(solution)/shard_map/ppermute | solution.py:199

commit v11 on v10

--- a/solution.py
+++ b/solution.py
@@ -297,13 +297,13 @@
         if h == 1:
             pairs[h], mid[h], weights = tie(pairs[h], mid[h], weights)
         else:
-            pairs[h], mid[h], new_master, *over[0][h] = tie(pairs[h], mid[h], new_master, *over[0][h])
+            pairs[h], mid[h], *over[0][h] = tie(pairs[h], mid[h], *over[0][h])
         over[1][h] = over_x(pairs[h])
         mid_far[h], outwards[h] = z_perm(pairs[h], MIDDLE), z_perm(mid[h], OUTWARDS)
     for h in (0, 1):
         mid_far[h], outwards[h], mid[h], *over[1][h] = tie(mid_far[h], outwards[h], mid[h], *over[1][h])
         far[h] = z_perm(mid_far[h], OUTWARDS)
-        (near[h],) = tie(jnp.where(between, mid[h], outwards[h]))
+        near[h], new_master = tie(jnp.where(between, mid[h], outwards[h]), new_master)
         over[2][h] = over_x(near[h])
     for h in (0, 1):
         (distant[h],) = tie(jnp.where(between, mid_far[h], far[h]))

time: 237 us -> 240 us (1.013)
    ppermute x20, waiting for transfers between devices: 47.2 us -> 54.8 us  [z_perm(): lax.ppermute(value, 'dp', [(a * n_x + i, b * n_x + i) for a, b in pairs f...]
    ppermute x13, waiting for transfers between devices: 27.4 us -> 21 us  [x_perm(): return lax.ppermute(value, 'dp', pairs)]
  transfers between devices with their start and end apart: 42 -> 42, of which waited for: 22 -> 22; matrix products, arithmetic and copies ran while one was open for 19% -> 18% of each run, Pallas kernels for 11% -> 11%
where the time goes in v11:
time: 240 us; the launch traced here: 239 us
  waiting for transfers between devices  94.7 us (39%)
  starting transfers between devices  54.4 us (23%)
  Pallas kernels  39.8 us (17%)
  local copies, waits for them, and re-layouts  33.5 us (14%)
  other arithmetic  15.7 us (7%)
    ppermute x20, waiting for transfers between devices, z_perm(): lax.ppermute(value, 'dp', [(a * n_x + i, b * n_x + i) for a, b in pairs f...  54.8 us
    ppermute x20, starting transfers between devices, z_perm(): lax.ppermute(value, 'dp', [(a * n_x + i, b * n_x + i) for a, b in pairs f...  37.1 us
    pallas_call x3, Pallas kernels, multiply(): pl.pallas_call(kernel, grid=(rows // step,), in_specs=[pl.BlockSpec((step...  23.7 us
    dynamic_update_slice x17, local copies, waits for them, and re-layouts, put(): return lax.dynamic_update_slice(weights, value[:count], (h * half, at))  21.8 us
    ppermute x13, waiting for transfers between devices, x_perm(): return lax.ppermute(value, 'dp', pairs)  21 us
    ppermute x9, waiting for transfers between devices, seat_perm(): lax.ppermute(value, 'tensor', [(i, i ^ flip) for i in range(n_tensor)])  18.9 us
    pallas_call x2, Pallas kernels, update(): pl.pallas_call(kernel, grid=(rows // step,), in_specs=specs + [whole] * 3...  13.3 us
    convert_element_type x8, other arithmetic, add(): return lax.optimization_barrier(total.astype(BF16))  12.2 us
  transfers between devices with their start and end apart: 42, of which 22 were waited for; matrix products, arithmetic and copies ran while one was open for 18% of the time, Pallas kernels for 11%

profile of v11, /device:TPU:0, one launch (start us, length us, event | category | flops | bytes accessed | tf_op | source)
XLA Modules:
  0.0 238.9 jit_solution(16898307646819302944)
XLA Ops:
  0.6 2.8 %arrange.1 = (bf16[384,256]{1,0:T(8,128)(2,1)}, bf16[384,512]{1,0:T(8,128)(2,1)}, bf16[384,1280]{1,0:T(8,128)(2,1)}) custom-call(bf16[384,2048]{1,0:T(8,128)(2,1)} %cot_ref.1), custom_call_target="tpu_custom_call" | custom-call | tf_op jit(solution)/shard_map/arrange/pallas_call | solution.py:55
  3.4 3.0 %collective-permute-start.1 = (bf16[384,256]{1,0:T(8,128)(2,1)}, bf16[384,256]{1,0:T(8,128)(2,1)S(1)}, u32[]{:S(2)}, u32[]{:S(2)}) collective-permute-start(bf16[384,256]{1,0:T(8,128)(2,1)} %get-tuple-element.90.refs_0_), channel_id=1, source_target_pairs={{0,2},{1,3},{2,0},{3,1},{4,6},{5,7},{6,4},{7,5},{8,10},{9,11},{10,... | collective-permute-start | bytes 589832 | tf_op jit(solution)/shard_map/ppermute | solution.py:206
  6.4 8.6 %copy.12 = bf16[1536,2048]{0,1:T(8,128)(2,1)} copy(bf16[1536,2048]{1,0:T(8,128)(2,1)} %param.5) | data formatting | bytes 12582912 | tf_op jit(solution)/shard_map/optimization_barrier | solution.py:180
  16.8 4.8 %partials.3 = (bf16[2048,256]{1,0:T(8,128)(2,1)S(1)}, f32[4,4,256]{2,1,0:T(4,128)S(1)}) custom-call(bf16[2048,1536]{1,0:T(8,128)(2,1)} %bitcast.17, bf16[384,256]{1,0:T(8,128)(2,1)S(1)} %copy-done.10, bf16[384,256]{1,0:T(8,128)(2,1)S(1)} %collective-permute-done.refs_1_, bf16[384,256]{1,0:T(8,128)(2,1)S(1)} %collective-permute-done.1.refs_2_, ...), custom_call_target="tpu_custom_call" | custom-call | flops 10000000000 | bytes 3145728 | tf_op jit(solution)/shard_map/partials/pallas_call | solution.py:79
  21.6 1.5 collective-permute-start.6
  23.6 1.5 collective-permute-start.8
  25.2 10.0 %collective-permute-done.4.refs_2_ = bf16[384,512]{1,0:T(8,128)(2,1)S(1)} collective-permute-done((bf16[384,512]{1,0:T(8,128)(2,1)S(1)}, bf16[384,512]{1,0:T(8,128)(2,1)S(1)}, u32[]{:S(2)}, u32[]{:S(2)}) %collective-permute-start.4) | collective-permute-done | bytes 393248 | tf_op jit(solution)/shard_map/ppermute | solution.py:206
  35.1 1.7 collective-permute-done.5.refs_3_
  36.8 6.8 %partials.4 = (bf16[2048,256]{1,0:T(8,128)(2,1)S(1)}, bf16[2048,256]{1,0:T(8,128)(2,1)}, f32[4,4,512]{2,1,0:T(4,128)S(1)}) custom-call(bf16[2048,1536]{1,0:T(8,128)(2,1)} %bitcast.18, bf16[384,512]{1,0:T(8,128)(2,1)S(1)} %copy-done.8, bf16[384,512]{1,0:T(8,128)(2,1)S(1)} %collective-permute-done.3.refs_1_, ...), custom_call_target="tpu_custom_call" | custom-call | tf_op jit(solution)/shard_map/partials/pallas_call | solution.py:79
  44.2 3.0 %collective-permute-done.6 = bf16[2048,256]{1,0:T(8,128)(2,1)S(1)} collective-permute-done((bf16[2048,256]{1,0:T(8,128)(2,1)S(1)}, bf16[2048,256]{1,0:T(8,128)(2,1)S(1)}, u32[]{:S(2)}, u32[]{:S(2)}) %collective-permute-start.6) | collective-permute-done | bytes 1048608 | tf_op jit(solution)/shard_map/ppermute | solution.py:203
  47.2 1.1 add_convert_fusion.7
  49.2 6.0 %collective-permute-done.8.refs_2_ = bf16[384,1280]{1,0:T(8,128)(2,1)S(1)} collective-permute-done((bf16[384,1280]{1,0:T(8,128)(2,1)S(1)}, bf16[384,1280]{1,0:T(8,128)(2,1)S(1)}, u32[]{:S(2)}, u32[]{:S(2)}) %collective-permute-start.8) | collective-permute-done | bytes 983072 | tf_op jit(solution)/shard_map/ppermute | solution.py:206
  55.3 3.6 %collective-permute-start.10 = (bf16[1024,256]{1,0:T(8,128)(2,1)}, bf16[1024,256]{1,0:T(8,128)(2,1)S(1)}, u32[]{:S(2)}, u32[]{:S(2)}) collective-permute-start(bf16[1024,256]{1,0:T(8,128)(2,1)} %add_convert_fusion.6), channel_id=1, source_target_pairs={{0,8},{4,12},{24,16},{28,20},{1,9},{5,13},{25,17},{29,21},{2,10},{... | collective-permute-start | bytes 1572872 | tf_op jit(solution)/shard_map/ppermute | solution.py:199
  58.9 1.3 collective-permute-start.11
  60.3 12.1 %partials.5 = (bf16[2048,256]{1,0:T(8,128)(2,1)}, bf16[2048,256]{1,0:T(8,128)(2,1)S(1)}, bf16[2048,256]{1,0:T(8,128)(2,1)}, bf16[2048,256]{1,0:T(8,128)(2,1)}, b...) custom-call(bf16[2048,1536]{1,0:T(8,128)(2,1)} %bitcast.19, bf16[384,1280]{1,0:T(8,128)(2,1)S(1)} %copy-done.5, ...), custom_call_target="tpu_custom_call" | custom-call | tf_op jit(solution)/shard_map/partials/pallas_call | solution.py:79
  73.0 2.9 %add_convert_fusion.1 = bf16[2048,256]{1,0:T(8,128)(2,1)} fusion(bf16[2048,256]{1,0:T(8,128)(2,1)} %collective-permute-done.12, bf16[2048,256]{1,0:T(8,128)(2,1)} %get-tuple-element.128), kind=kLoop, calls=%fused_computation.1 | loop fusion | flops 2097152 | bytes 3145728 | tf_op jit(solution)/shard_map/convert_element_type | solution.py:103
  75.8 2.3 collective-permute-start.15
  78.1 4.6 %collective-permute-done.11 = bf16[1024,256]{1,0:T(8,128)(2,1)S(1)} collective-permute-done((bf16[1024,256]{1,0:T(8,128)(2,1)}, bf16[1024,256]{1,0:T(8,128)(2,1)S(1)}, u32[]{:S(2)}, u32[]{:S(2)}) %collective-permute-start.11) | collective-permute-done | bytes 524320 | tf_op jit(solution)/shard_map/ppermute | solution.py:199
  85.4 1.5 collective-permute-start.20
  88.1 10.6 %collective-permute-done.16 = bf16[2048,256]{1,0:T(8,128)(2,1)} collective-permute-done((bf16[2048,256]{1,0:T(8,128)(2,1)}, bf16[2048,256]{1,0:T(8,128)(2,1)}, u32[]{:S(2)}, u32[]{:S(2)}) %collective-permute-start.16) | collective-permute-done | bytes 1048608 | tf_op jit(solution)/shard_map/ppermute | solution.py:203
  98.7 1.4 add_convert_fusion.3
  100.1 4.3 %collective-permute-start.19 = (bf16[1024,256]{1,0:T(8,128)(2,1)S(1)}, bf16[1024,256]{1,0:T(8,128)(2,1)S(1)}, u32[]{:S(2)}, u32[]{:S(2)}) collective-permute-start(bf16[1024,256]{1,0:T(8,128)(2,1)S(1)} %add_convert_fusion.3), channel_id=1, source_target_pairs={{0,8},{4,12},{8,0},{12,4},{16,24},{20,28},{24,16},{28,20},{1,9},{5... | collective-permute-start | bytes 1572872 | tf_op jit(solution)/shard_map/ppermute | solution.py:199
  105.1 2.2 add_convert_fusion
  108.1 7.8 %collective-permute-done.19.refs_3_ = bf16[1024,256]{1,0:T(8,128)(2,1)S(1)} collective-permute-done((bf16[1024,256]{1,0:T(8,128)(2,1)S(1)}, bf16[1024,256]{1,0:T(8,128)(2,1)S(1)}, u32[]{:S(2)}, u32[]{:S(2)}) %collective-permute-start.19) | collective-permute-done | bytes 524320 | tf_op jit(solution)/shard_map/ppermute | solution.py:199
  115.9 1.7 add_convert_fusion.2
  117.6 2.5 %collective-permute-start.21 = (bf16[1024,256]{1,0:T(8,128)(2,1)S(1)}, bf16[1024,256]{1,0:T(8,128)(2,1)S(1)}, u32[]{:S(2)}, u32[]{:S(2)}) collective-permute-start(bf16[1024,256]{1,0:T(8,128)(2,1)S(1)} %add_convert_fusion.2), channel_id=1, source_target_pairs={{0,8},{4,12},{8,0},{12,4},{16,24},{20,28},{24,16},{28,20},{1,9},{5... | collective-permute-start | bytes 1572872 | tf_op jit(solution)/shard_map/ppermute | solution.py:199
  120.7 3.1 %collective-permute-done.13 = f32[16,16]{1,0:T(8,128)S(1)} collective-permute-done((f32[16,16]{1,0:T(8,128)S(1)}, f32[16,16]{1,0:T(8,128)S(1)}, u32[]{:S(2)}, u32[]{:S(2)}) %collective-permute-start.13) | collective-permute-done | bytes 1056 | tf_op jit(solution)/shard_map/ppermute | solution.py:203
  123.8 7.6 %collective-permute-done.21.refs_4_ = bf16[1024,256]{1,0:T(8,128)(2,1)S(1)} collective-permute-done((bf16[1024,256]{1,0:T(8,128)(2,1)S(1)}, bf16[1024,256]{1,0:T(8,128)(2,1)S(1)}, u32[]{:S(2)}, u32[]{:S(2)}) %collective-permute-start.21) | collective-permute-done | bytes 524320 | tf_op jit(solution)/shard_map/ppermute | solution.py:199
  131.5 6.9 %weights.1 = (bf16[1024,256]{1,0:T(8,128)(2,1)S(1)}, bf16[1024,256]{1,0:T(8,128)(2,1)}) custom-call(bf16[2048,256]{1,0:T(8,128)(2,1)S(1)} %copy-done, bf16[2048,256]{1,0:T(8,128)(2,1)S(1)} %collective-permute-done.14.refs_1_, bf16[2048,256]{1,0:T(8,128)(2,1)S(1)} %collective-permute-done.18.refs_2_, bf16[1024,256]{1,0:T(8,128)(2,1)S(1)} %collective-permute-done.19.refs_3_, ...), custom_call_target="tpu_custom_call" | custom-call | tf_op jit(solution)/shard_map/weights/pallas_call | solution.py:155
  139.7 4.6 %collective-permute-start.22 = (bf16[1024,256]{1,0:T(8,128)(2,1)}, bf16[1024,256]{1,0:T(8,128)(2,1)}, u32[]{:S(2)}, u32[]{:S(2)}) collective-permute-start(bf16[1024,256]{1,0:T(8,128)(2,1)} %get-tuple-element.136), channel_id=1, source_target_pairs={{0,8},{4,12},{8,0},{12,4},{16,24},{20,28},{24,16},{28,20},{1,9},{5... | collective-permute-start | bytes 1572872 | tf_op jit(solution)/shard_map/ppermute | solution.py:199
  144.3 1.5 collective-permute-start.23
  145.8 2.1 collective-permute-start.28
  147.9 1.5 collective-permute-start.29
  149.3 2.5 %collective-permute-done.24 = bf16[1024,256]{1,0:T(8,128)(2,1)} collective-permute-done((bf16[1024,256]{1,0:T(8,128)(2,1)}, bf16[1024,256]{1,0:T(8,128)(2,1)}, u32[]{:S(2)}, u32[]{:S(2)}) %collective-permute-start.24) | collective-permute-done | bytes 524320 | tf_op jit(solution)/shard_map/ppermute | solution.py:203
  152.4 1.3 slice_dynamic-update-slice_fusion
  153.7 3.8 %collective-permute-done.22 = bf16[1024,256]{1,0:T(8,128)(2,1)} collective-permute-done((bf16[1024,256]{1,0:T(8,128)(2,1)}, bf16[1024,256]{1,0:T(8,128)(2,1)}, u32[]{:S(2)}, u32[]{:S(2)}) %collective-permute-start.22) | collective-permute-done | bytes 524320 | tf_op jit(solution)/shard_map/ppermute | solution.py:199
  157.5 1.5 collective-permute-start.25
  158.9 1.5 collective-permute-start.27
  160.4 5.7 %collective-permute-done.28 = bf16[1024,256]{1,0:T(8,128)(2,1)} collective-permute-done((bf16[1024,256]{1,0:T(8,128)(2,1)}, bf16[1024,256]{1,0:T(8,128)(2,1)}, u32[]{:S(2)}, u32[]{:S(2)}) %collective-permute-start.28) | collective-permute-done | bytes 524320 | tf_op jit(solution)/shard_map/ppermute | solution.py:199
  166.1 1.3 collective-permute-start.26
  167.4 1.5 collective-permute-start.31
  168.9 1.3 collective-permute-start.32
  170.2 1.5 collective-permute-start.33
  173.8 6.4 %states.1 = (f32[2048,256]{1,0:T(8,128)}, f32[2048,256]{1,0:T(8,128)}, f32[2048,256]{1,0:T(8,128)}) custom-call(bf16[2048,256]{1,0:T(8,128)(2,1)S(1)} %copy-done, bf16[2048,256]{1,0:T(8,128)(2,1)S(1)} %collective-permute-done.14.refs_1_, bf16[2048,256]{1,0:T(8,128)(2,1)S(1)} %collective-permute-done.18.refs_2_, bf16[1024,256]{1,0:T(8,128)(2,1)S(1)} %copy-done.2, ...), custom_call_target="tpu_custom_call" | custom-call | tf_op jit(solution)/shard_map/states/pallas_call | solution.py:155
  180.2 2.9 %collective-permute-done.26 = bf16[1024,256]{1,0:T(8,128)(2,1)} collective-permute-done((bf16[1024,256]{1,0:T(8,128)(2,1)}, bf16[1024,256]{1,0:T(8,128)(2,1)}, u32[]{:S(2)}, u32[]{:S(2)}) %collective-permute-start.26) | collective-permute-done | bytes 524320 | tf_op jit(solution)/shard_map/ppermute | solution.py:199
  183.2 7.7 %collective-permute-done.32 = bf16[1024,256]{1,0:T(8,128)(2,1)} collective-permute-done((bf16[1024,256]{1,0:T(8,128)(2,1)}, bf16[1024,256]{1,0:T(8,128)(2,1)}, u32[]{:S(2)}, u32[]{:S(2)}) %collective-permute-start.32) | collective-permute-done | bytes 524320 | tf_op jit(solution)/shard_map/ppermute | solution.py:199
  190.9 1.1 broadcast_select_fusion.2
  192.0 1.1 broadcast_select_fusion.3
  193.1 1.5 collective-permute-start.37
  195.5 1.9 constant_dynamic-update-slice_fusion.14
  197.3 1.9 constant_dynamic-update-slice_fusion.7
  199.2 1.3 collective-permute-start.34
  200.5 1.3 collective-permute-start.35
  202.4 1.9 constant_dynamic-update-slice_fusion.6
  204.3 1.9 constant_dynamic-update-slice_fusion.13
  206.1 1.9 constant_dynamic-update-slice_fusion.12
  208.0 1.9 constant_dynamic-update-slice_fusion.5
  209.9 1.9 constant_dynamic-update-slice_fusion.4
  211.7 4.4 %collective-permute-done.34 = bf16[1024,256]{1,0:T(8,128)(2,1)S(1)} collective-permute-done((bf16[1024,256]{1,0:T(8,128)(2,1)}, bf16[1024,256]{1,0:T(8,128)(2,1)S(1)}, u32[]{:S(2)}, u32[]{:S(2)}) %collective-permute-start.34) | collective-permute-done | bytes 524320 | tf_op jit(solution)/shard_map/ppermute | solution.py:199
  217.2 5.4 %collective-permute-done.35 = bf16[1024,256]{1,0:T(8,128)(2,1)S(1)} collective-permute-done((bf16[1024,256]{1,0:T(8,128)(2,1)}, bf16[1024,256]{1,0:T(8,128)(2,1)S(1)}, u32[]{:S(2)}, u32[]{:S(2)}) %collective-permute-start.35) | collective-permute-done | bytes 524320 | tf_op jit(solution)/shard_map/ppermute | solution.py:199
  228.1 2.1 collective-permute-done.40
  230.3 1.7 collective-permute-start.41
  232.8 2.0 collective-permute-done.41
  235.4 1.8 collective-permute-done.38
  (96 shorter events, 25.5 us)
Async XLA Ops:
  3.4 11.6 %copy-start.10 = (bf16[384,256]{1,0:T(8,128)(2,1)S(1)}, bf16[384,256]{1,0:T(8,128)(2,1)}, u32[]{:S(2)}) copy-start(bf16[384,256]{1,0:T(8,128)(2,1)} %get-tuple-element.90.refs_0_) | copy-start | bytes 589828
  3.4 11.7 %collective-permute-start.1 = (bf16[384,256]{1,0:T(8,128)(2,1)}, bf16[384,256]{1,0:T(8,128)(2,1)S(1)}, u32[]{:S(2)}, u32[]{:S(2)}) collective-permute-start(bf16[384,256]{1,0:T(8,128)(2,1)} %get-tuple-element.90.refs_0_), channel_id=1, source_target_pairs={{0,2},{1,3},{2,0},{3,1},{4,6},{5,7},{6,4},{7,5},{8,10},{9,11},{10,... | collective-permute-start | bytes 589832 | tf_op jit(solution)/shard_map/ppermute | solution.py:206
  15.0 8.1 %copy-start.8 = (bf16[384,512]{1,0:T(8,128)(2,1)S(1)}, bf16[384,512]{1,0:T(8,128)(2,1)}, u32[]{:S(2)}) copy-start(bf16[384,512]{1,0:T(8,128)(2,1)} %get-tuple-element.94.refs_0_) | copy-start | bytes 1179652
  15.0 8.7 %copy-start.5 = (bf16[384,1280]{1,0:T(8,128)(2,1)S(1)}, bf16[384,1280]{1,0:T(8,128)(2,1)}, u32[]{:S(2)}) copy-start(bf16[384,1280]{1,0:T(8,128)(2,1)} %get-tuple-element.102.refs_0_) | copy-start | bytes 2949124
  15.0 1.5 collective-permute-start
  15.1 1.7 collective-permute-start.2
  21.6 25.6 %collective-permute-start.6 = (bf16[2048,256]{1,0:T(8,128)(2,1)S(1)}, bf16[2048,256]{1,0:T(8,128)(2,1)S(1)}, u32[]{:S(2)}, u32[]{:S(2)}) collective-permute-start(bf16[2048,256]{1,0:T(8,128)(2,1)S(1)} %get-tuple-element.92), channel_id=1, source_target_pairs={{0,4},{4,0},{8,12},{12,8},{16,20},{20,16},{24,28},{28,24},{1,5},{5... | collective-permute-start | bytes 3145736 | tf_op jit(solution)/shard_map/ppermute | solution.py:203
  23.1 12.0 %collective-permute-start.4 = (bf16[384,512]{1,0:T(8,128)(2,1)S(1)}, bf16[384,512]{1,0:T(8,128)(2,1)S(1)}, u32[]{:S(2)}, u32[]{:S(2)}) collective-permute-start(bf16[384,512]{1,0:T(8,128)(2,1)S(1)} %copy-done.8), channel_id=1, source_target_pairs={{0,2},{1,3},{2,0},{3,1},{4,6},{5,7},{6,4},{7,5},{8,10},{9,11},{10,... | collective-permute-start | bytes 1179656 | tf_op jit(solution)/shard_map/ppermute | solution.py:206
  23.6 31.5 %collective-permute-start.8 = (bf16[384,1280]{1,0:T(8,128)(2,1)S(1)}, bf16[384,1280]{1,0:T(8,128)(2,1)S(1)}, u32[]{:S(2)}, u32[]{:S(2)}) collective-permute-start(bf16[384,1280]{1,0:T(8,128)(2,1)S(1)} %copy-done.5), channel_id=1, source_target_pairs={{0,2},{1,3},{2,0},{3,1},{4,6},{5,7},{6,4},{7,5},{8,10},{9,11},{10,... | collective-permute-start | bytes 2949128 | tf_op jit(solution)/shard_map/ppermute | solution.py:206
  25.2 10.0 %collective-permute-start.3 = (bf16[384,512]{1,0:T(8,128)(2,1)S(1)}, bf16[384,512]{1,0:T(8,128)(2,1)S(1)}, u32[]{:S(2)}, u32[]{:S(2)}) collective-permute-start(bf16[384,512]{1,0:T(8,128)(2,1)S(1)} %copy-done.8), channel_id=1, source_target_pairs={{0,1},{1,0},{2,3},{3,2},{4,5},{5,4},{6,7},{7,6},{8,9},{9,8},{10,11... | collective-permute-start | bytes 1179656 | tf_op jit(solution)/shard_map/ppermute | solution.py:206
  35.1 1.7 collective-permute-start.5
  43.7 29.3 %collective-permute-start.12 = (bf16[2048,256]{1,0:T(8,128)(2,1)}, bf16[2048,256]{1,0:T(8,128)(2,1)}, u32[]{:S(2)}, u32[]{:S(2)}) collective-permute-start(bf16[2048,256]{1,0:T(8,128)(2,1)} %get-tuple-element.107), channel_id=1, source_target_pairs={{0,4},{4,0},{8,12},{12,8},{16,20},{20,16},{24,28},{28,24},{1,5},{5... | collective-permute-start | bytes 3145736 | tf_op jit(solution)/shard_map/ppermute | solution.py:203
  47.2 8.0 %copy-start.11 = (bf16[2048,256]{1,0:T(8,128)(2,1)}, bf16[2048,256]{1,0:T(8,128)(2,1)S(1)}, u32[]{:S(2)}) copy-start(bf16[2048,256]{1,0:T(8,128)(2,1)S(1)} %collective-permute-done.6) | copy-start | bytes 3145732
  49.2 11.1 %collective-permute-start.7 = (bf16[384,1280]{1,0:T(8,128)(2,1)S(1)}, bf16[384,1280]{1,0:T(8,128)(2,1)}, u32[]{:S(2)}, u32[]{:S(2)}) collective-permute-start(bf16[384,1280]{1,0:T(8,128)(2,1)S(1)} %copy-done.5), channel_id=1, source_target_pairs={{0,1},{1,0},{2,3},{3,2},{4,5},{5,4},{6,7},{7,6},{8,9},{9,8},{10,11... | collective-permute-start | bytes 2949128 | tf_op jit(solution)/shard_map/ppermute | solution.py:206
  55.2 5.1 %collective-permute-start.9 = (bf16[384,1280]{1,0:T(8,128)(2,1)S(1)}, bf16[384,1280]{1,0:T(8,128)(2,1)}, u32[]{:S(2)}, u32[]{:S(2)}) collective-permute-start(bf16[384,1280]{1,0:T(8,128)(2,1)S(1)} %collective-permute-done.8.refs_2_), channel_id=1, source_target_pairs={{0,1},{1,0},{2,3},{3,2},{4,5},{5,4},{6,7},{7,6},{8,9},{9,8},{10,11... | collective-permute-start | bytes 2949128 | tf_op jit(solution)/shard_map/ppermute | solution.py:206
  55.3 27.4 %copy-start.12 = (bf16[2048,256]{1,0:T(8,128)(2,1)S(1)}, bf16[2048,256]{1,0:T(8,128)(2,1)}, u32[]{:S(2)}) copy-start(bf16[2048,256]{1,0:T(8,128)(2,1)} %copy-done.11) | copy-start | bytes 3145732
  55.3 29.1 %collective-permute-start.10 = (bf16[1024,256]{1,0:T(8,128)(2,1)}, bf16[1024,256]{1,0:T(8,128)(2,1)S(1)}, u32[]{:S(2)}, u32[]{:S(2)}) collective-permute-start(bf16[1024,256]{1,0:T(8,128)(2,1)} %add_convert_fusion.6), channel_id=1, source_target_pairs={{0,8},{4,12},{24,16},{28,20},{1,9},{5,13},{25,17},{29,21},{2,10},{... | collective-permute-start | bytes 1572872 | tf_op jit(solution)/shard_map/ppermute | solution.py:199
  58.9 23.7 %collective-permute-start.11 = (bf16[1024,256]{1,0:T(8,128)(2,1)}, bf16[1024,256]{1,0:T(8,128)(2,1)S(1)}, u32[]{:S(2)}, u32[]{:S(2)}) collective-permute-start(bf16[1024,256]{1,0:T(8,128)(2,1)} %add_convert_fusion.7), channel_id=1, source_target_pairs={{0,8},{4,12},{24,16},{28,20},{1,9},{5,13},{25,17},{29,21},{2,10},{... | collective-permute-start | bytes 1572872 | tf_op jit(solution)/shard_map/ppermute | solution.py:199
  72.3 13.1 %copy-start.9 = (bf16[2048,256]{1,0:T(8,128)(2,1)}, bf16[2048,256]{1,0:T(8,128)(2,1)S(1)}, u32[]{:S(2)}) copy-start(bf16[2048,256]{1,0:T(8,128)(2,1)S(1)} %get-tuple-element.123) | copy-start | bytes 3145732
  72.4 59.1 %copy-start = (bf16[2048,256]{1,0:T(8,128)(2,1)S(1)}, bf16[2048,256]{1,0:T(8,128)(2,1)}, u32[]{:S(2)}) copy-start(bf16[2048,256]{1,0:T(8,128)(2,1)} %get-tuple-element.146.refs_0_) | copy-start | bytes 3145732
  72.4 26.4 %collective-permute-start.16 = (bf16[2048,256]{1,0:T(8,128)(2,1)}, bf16[2048,256]{1,0:T(8,128)(2,1)}, u32[]{:S(2)}, u32[]{:S(2)}) collective-permute-start(bf16[2048,256]{1,0:T(8,128)(2,1)} %get-tuple-element.108), channel_id=1, source_target_pairs={{0,4},{4,0},{8,12},{12,8},{16,20},{20,16},{24,28},{28,24},{1,5},{5... | collective-permute-start | bytes 3145736 | tf_op jit(solution)/shard_map/ppermute | solution.py:203
  75.8 29.3 %collective-permute-start.15 = (bf16[2048,256]{1,0:T(8,128)(2,1)}, bf16[2048,256]{1,0:T(8,128)(2,1)}, u32[]{:S(2)}, u32[]{:S(2)}) collective-permute-start(bf16[2048,256]{1,0:T(8,128)(2,1)} %add_convert_fusion.1), channel_id=1, source_target_pairs={{0,8},{4,12},{24,16},{28,20},{1,9},{5,13},{25,17},{29,21},{2,10},{... | collective-permute-start | bytes 3145736 | tf_op jit(solution)/shard_map/ppermute | solution.py:199
  83.7 4.5 %collective-permute-start.17 = (bf16[1024,256]{1,0:T(8,128)(2,1)}, bf16[1024,256]{1,0:T(8,128)(2,1)S(1)}, u32[]{:S(2)}, u32[]{:S(2)}) collective-permute-start(bf16[1024,256]{1,0:T(8,128)(2,1)} %add_convert_fusion.5), channel_id=1, source_target_pairs={{8,16},{12,20},{16,8},{20,12},{9,17},{13,21},{17,9},{21,13},{10,18... | collective-permute-start | bytes 1572872 | tf_op jit(solution)/shard_map/ppermute | solution.py:199
  85.4 22.7 %collective-permute-start.20 = (bf16[1024,256]{1,0:T(8,128)(2,1)}, bf16[1024,256]{1,0:T(8,128)(2,1)}, u32[]{:S(2)}, u32[]{:S(2)}) collective-permute-start(bf16[1024,256]{1,0:T(8,128)(2,1)} %add_convert_fusion.4), channel_id=1, source_target_pairs={{8,16},{12,20},{16,8},{20,12},{9,17},{13,21},{17,9},{21,13},{10,18... | collective-permute-start | bytes 1572872 | tf_op jit(solution)/shard_map/ppermute | solution.py:199
  87.3 36.5 %collective-permute-start.14 = (bf16[2048,256]{1,0:T(8,128)(2,1)}, bf16[2048,256]{1,0:T(8,128)(2,1)S(1)}, u32[]{:S(2)}, u32[]{:S(2)}) collective-permute-start(bf16[2048,256]{1,0:T(8,128)(2,1)} %copy-done.9), channel_id=1, source_target_pairs={{0,4},{4,0},{8,12},{12,8},{16,20},{20,16},{24,28},{28,24},{1,5},{5... | collective-permute-start | bytes 3145736 | tf_op jit(solution)/shard_map/ppermute | solution.py:203
  100.1 15.8 %collective-permute-start.19 = (bf16[1024,256]{1,0:T(8,128)(2,1)S(1)}, bf16[1024,256]{1,0:T(8,128)(2,1)S(1)}, u32[]{:S(2)}, u32[]{:S(2)}) collective-permute-start(bf16[1024,256]{1,0:T(8,128)(2,1)S(1)} %add_convert_fusion.3), channel_id=1, source_target_pairs={{0,8},{4,12},{8,0},{12,4},{16,24},{20,28},{24,16},{28,20},{1,9},{5... | collective-permute-start | bytes 1572872 | tf_op jit(solution)/shard_map/ppermute | solution.py:199
  107.4 24.1 %collective-permute-start.18 = (bf16[2048,256]{1,0:T(8,128)(2,1)S(1)}, bf16[2048,256]{1,0:T(8,128)(2,1)S(1)}, u32[]{:S(2)}, u32[]{:S(2)}) collective-permute-start(bf16[2048,256]{1,0:T(8,128)(2,1)S(1)} %add_convert_fusion), channel_id=1, source_target_pairs={{8,16},{12,20},{16,8},{20,12},{9,17},{13,21},{17,9},{21,13},{10,18... | collective-permute-start | bytes 3145736 | tf_op jit(solution)/shard_map/ppermute | solution.py:199
  115.9 15.6 %copy-start.1 = (bf16[1024,256]{1,0:T(8,128)(2,1)}, bf16[1024,256]{1,0:T(8,128)(2,1)S(1)}, u32[]{:S(2)}) copy-start(bf16[1024,256]{1,0:T(8,128)(2,1)S(1)} %collective-permute-done.19.refs_3_) | copy-start | bytes 1572868
  117.6 13.8 %collective-permute-start.21 = (bf16[1024,256]{1,0:T(8,128)(2,1)S(1)}, bf16[1024,256]{1,0:T(8,128)(2,1)S(1)}, u32[]{:S(2)}, u32[]{:S(2)}) collective-permute-start(bf16[1024,256]{1,0:T(8,128)(2,1)S(1)} %add_convert_fusion.2), channel_id=1, source_target_pairs={{0,8},{4,12},{8,0},{12,4},{16,24},{20,28},{24,16},{28,20},{1,9},{5... | collective-permute-start | bytes 1572872 | tf_op jit(solution)/shard_map/ppermute | solution.py:199
  120.2 3.7 %collective-permute-start.13 = (f32[16,16]{1,0:T(8,128)S(1)}, f32[16,16]{1,0:T(8,128)S(1)}, u32[]{:S(2)}, u32[]{:S(2)}) collective-permute-start(f32[16,16]{1,0:T(8,128)S(1)} %select_reduce_fusion), channel_id=1, source_target_pairs={{0,4},{4,0},{8,12},{12,8},{16,20},{20,16},{24,28},{28,24},{1,5},{5... | collective-permute-start | bytes 3080 | tf_op jit(solution)/shard_map/ppermute | solution.py:203
  131.4 6.9 %copy-start.3 = (bf16[1024,256]{1,0:T(8,128)(2,1)}, bf16[1024,256]{1,0:T(8,128)(2,1)S(1)}, u32[]{:S(2)}) copy-start(bf16[1024,256]{1,0:T(8,128)(2,1)S(1)} %collective-permute-done.21.refs_4_) | copy-start | bytes 1572868
  138.3 0.8 copy-start.6
  139.2 12.7 %collective-permute-start.24 = (bf16[1024,256]{1,0:T(8,128)(2,1)}, bf16[1024,256]{1,0:T(8,128)(2,1)}, u32[]{:S(2)}, u32[]{:S(2)}) collective-permute-start(bf16[1024,256]{1,0:T(8,128)(2,1)} %get-tuple-element.136), channel_id=1, source_target_pairs={{0,4},{4,0},{8,12},{12,8},{16,20},{20,16},{24,28},{28,24},{1,5},{5... | collective-permute-start | bytes 1572872 | tf_op jit(solution)/shard_map/ppermute | solution.py:203
  139.7 17.8 %collective-permute-start.22 = (bf16[1024,256]{1,0:T(8,128)(2,1)}, bf16[1024,256]{1,0:T(8,128)(2,1)}, u32[]{:S(2)}, u32[]{:S(2)}) collective-permute-start(bf16[1024,256]{1,0:T(8,128)(2,1)} %get-tuple-element.136), channel_id=1, source_target_pairs={{0,8},{4,12},{8,0},{12,4},{16,24},{20,28},{24,16},{28,20},{1,9},{5... | collective-permute-start | bytes 1572872 | tf_op jit(solution)/shard_map/ppermute | solution.py:199
  144.3 13.2 %collective-permute-start.23 = (bf16[1024,256]{1,0:T(8,128)(2,1)}, bf16[1024,256]{1,0:T(8,128)(2,1)}, u32[]{:S(2)}, u32[]{:S(2)}) collective-permute-start(bf16[1024,256]{1,0:T(8,128)(2,1)} %get-tuple-element.136), channel_id=1, source_target_pairs={{8,16},{12,20},{16,8},{20,12},{9,17},{13,21},{17,9},{21,13},{10,18... | collective-permute-start | bytes 1572872 | tf_op jit(solution)/shard_map/ppermute | solution.py:199
  145.8 20.3 %collective-permute-start.28 = (bf16[1024,256]{1,0:T(8,128)(2,1)}, bf16[1024,256]{1,0:T(8,128)(2,1)}, u32[]{:S(2)}, u32[]{:S(2)}) collective-permute-start(bf16[1024,256]{1,0:T(8,128)(2,1)} %copy-done.6), channel_id=1, source_target_pairs={{0,8},{4,12},{8,0},{12,4},{16,24},{20,28},{24,16},{28,20},{1,9},{5... | collective-permute-start | bytes 1572872 | tf_op jit(solution)/shard_map/ppermute | solution.py:199
  147.9 19.5 %collective-permute-start.29 = (bf16[1024,256]{1,0:T(8,128)(2,1)}, bf16[1024,256]{1,0:T(8,128)(2,1)}, u32[]{:S(2)}, u32[]{:S(2)}) collective-permute-start(bf16[1024,256]{1,0:T(8,128)(2,1)} %copy-done.6), channel_id=1, source_target_pairs={{8,16},{12,20},{16,8},{20,12},{9,17},{13,21},{17,9},{21,13},{10,18... | collective-permute-start | bytes 1572872 | tf_op jit(solution)/shard_map/ppermute | solution.py:199
  151.8 15.6 %collective-permute-start.30 = (bf16[1024,256]{1,0:T(8,128)(2,1)}, bf16[1024,256]{1,0:T(8,128)(2,1)}, u32[]{:S(2)}, u32[]{:S(2)}) collective-permute-start(bf16[1024,256]{1,0:T(8,128)(2,1)} %copy-done.6), channel_id=1, source_target_pairs={{0,4},{4,0},{8,12},{12,8},{16,20},{20,16},{24,28},{28,24},{1,5},{5... | collective-permute-start | bytes 1572872 | tf_op jit(solution)/shard_map/ppermute | solution.py:203
  157.5 12.7 %collective-permute-start.25 = (bf16[1024,256]{1,0:T(8,128)(2,1)}, bf16[1024,256]{1,0:T(8,128)(2,1)}, u32[]{:S(2)}, u32[]{:S(2)}) collective-permute-start(bf16[1024,256]{1,0:T(8,128)(2,1)} %collective-permute-done.22), channel_id=1, source_target_pairs={{8,16},{12,20},{16,8},{20,12},{9,17},{13,21},{17,9},{21,13},{10,18... | collective-permute-start | bytes 1572872 | tf_op jit(solution)/shard_map/ppermute | solution.py:199
  158.9 24.2 %collective-permute-start.27 = (bf16[1024,256]{1,0:T(8,128)(2,1)}, bf16[1024,256]{1,0:T(8,128)(2,1)}, u32[]{:S(2)}, u32[]{:S(2)}) collective-permute-start(bf16[1024,256]{1,0:T(8,128)(2,1)} %collective-permute-done.22), channel_id=1, source_target_pairs={{0,4},{4,0},{8,12},{12,8},{16,20},{20,16},{24,28},{28,24},{1,5},{5... | collective-permute-start | bytes 1572872 | tf_op jit(solution)/shard_map/ppermute | solution.py:203
  166.1 17.1 %collective-permute-start.26 = (bf16[1024,256]{1,0:T(8,128)(2,1)}, bf16[1024,256]{1,0:T(8,128)(2,1)}, u32[]{:S(2)}, u32[]{:S(2)}) collective-permute-start(bf16[1024,256]{1,0:T(8,128)(2,1)} %collective-permute-done.23), channel_id=1, source_target_pairs={{8,0},{12,4},{16,24},{20,28},{9,1},{13,5},{17,25},{21,29},{10,2},{... | collective-permute-start | bytes 1572872 | tf_op jit(solution)/shard_map/ppermute | solution.py:199
  167.4 15.8 %collective-permute-start.31 = (bf16[1024,256]{1,0:T(8,128)(2,1)}, bf16[1024,256]{1,0:T(8,128)(2,1)}, u32[]{:S(2)}, u32[]{:S(2)}) collective-permute-start(bf16[1024,256]{1,0:T(8,128)(2,1)} %collective-permute-done.28), channel_id=1, source_target_pairs={{8,16},{12,20},{16,8},{20,12},{9,17},{13,21},{17,9},{21,13},{10,18... | collective-permute-start | bytes 1572872 | tf_op jit(solution)/shard_map/ppermute | solution.py:199
  168.9 22.0 %collective-permute-start.32 = (bf16[1024,256]{1,0:T(8,128)(2,1)}, bf16[1024,256]{1,0:T(8,128)(2,1)}, u32[]{:S(2)}, u32[]{:S(2)}) collective-permute-start(bf16[1024,256]{1,0:T(8,128)(2,1)} %collective-permute-done.29), channel_id=1, source_target_pairs={{8,0},{12,4},{16,24},{20,28},{9,1},{13,5},{17,25},{21,29},{10,2},{... | collective-permute-start | bytes 1572872 | tf_op jit(solution)/shard_map/ppermute | solution.py:199
  170.2 20.7 %collective-permute-start.33 = (bf16[1024,256]{1,0:T(8,128)(2,1)}, bf16[1024,256]{1,0:T(8,128)(2,1)}, u32[]{:S(2)}, u32[]{:S(2)}) collective-permute-start(bf16[1024,256]{1,0:T(8,128)(2,1)} %collective-permute-done.28), channel_id=1, source_target_pairs={{0,4},{4,0},{8,12},{12,8},{16,20},{20,16},{24,28},{28,24},{1,5},{5... | collective-permute-start | bytes 1572872 | tf_op jit(solution)/shard_map/ppermute | solution.py:203
  171.7 1.0 copy-start.2
  172.8 1.0 copy-start.4
  173.8 20.8 %copy-start.7 = (bf16[1024,256]{1,0:T(8,128)(2,1)S(1)}, bf16[1024,256]{1,0:T(8,128)(2,1)}, u32[]{:S(2)}) copy-start(bf16[1024,256]{1,0:T(8,128)(2,1)} %copy-done.6) | copy-start | bytes 1572868
  193.1 38.9 %collective-permute-start.37 = (bf16[1024,256]{1,0:T(8,128)(2,1)S(1)}, bf16[1024,256]{1,0:T(8,128)(2,1)S(1)}, u32[]{:S(2)}, u32[]{:S(2)}) collective-permute-start(bf16[1024,256]{1,0:T(8,128)(2,1)S(1)} %broadcast_select_fusion.3), channel_id=1, source_target_pairs={{0,4},{4,0},{8,12},{12,8},{16,20},{20,16},{24,28},{28,24},{1,5},{5... | collective-permute-start | bytes 1572872 | tf_op jit(solution)/shard_map/ppermute | solution.py:203
  199.2 17.0 %collective-permute-start.34 = (bf16[1024,256]{1,0:T(8,128)(2,1)}, bf16[1024,256]{1,0:T(8,128)(2,1)S(1)}, u32[]{:S(2)}, u32[]{:S(2)}) collective-permute-start(bf16[1024,256]{1,0:T(8,128)(2,1)} %collective-permute-done.25), channel_id=1, source_target_pairs={{8,0},{12,4},{16,24},{20,28},{9,1},{13,5},{17,25},{21,29},{10,2},{... | collective-permute-start | bytes 1572872 | tf_op jit(solution)/shard_map/ppermute | solution.py:199
  200.5 22.2 %collective-permute-start.35 = (bf16[1024,256]{1,0:T(8,128)(2,1)}, bf16[1024,256]{1,0:T(8,128)(2,1)S(1)}, u32[]{:S(2)}, u32[]{:S(2)}) collective-permute-start(bf16[1024,256]{1,0:T(8,128)(2,1)} %collective-permute-done.31), channel_id=1, source_target_pairs={{8,0},{12,4},{16,24},{20,28},{9,1},{13,5},{17,25},{21,29},{10,2},{... | collective-permute-start | bytes 1572872 | tf_op jit(solution)/shard_map/ppermute | solution.py:199
  201.8 25.5 %collective-permute-start.36 = (bf16[1024,256]{1,0:T(8,128)(2,1)S(1)}, bf16[1024,256]{1,0:T(8,128)(2,1)S(1)}, u32[]{:S(2)}, u32[]{:S(2)}) collective-permute-start(bf16[1024,256]{1,0:T(8,128)(2,1)S(1)} %broadcast_select_fusion.2), channel_id=1, source_target_pairs={{0,4},{4,0},{8,12},{12,8},{16,20},{20,16},{24,28},{28,24},{1,5},{5... | collective-permute-start | bytes 1572872 | tf_op jit(solution)/shard_map/ppermute | solution.py:203
  216.2 21.9 %collective-permute-start.39 = (bf16[1024,256]{1,0:T(8,128)(2,1)S(1)}, bf16[1024,256]{1,0:T(8,128)(2,1)S(1)}, u32[]{:S(2)}, u32[]{:S(2)}) collective-permute-start(bf16[1024,256]{1,0:T(8,128)(2,1)S(1)} %broadcast_select_fusion.1), channel_id=1, source_target_pairs={{0,4},{4,0},{8,12},{12,8},{16,20},{20,16},{24,28},{28,24},{1,5},{5... | collective-permute-start | bytes 1572872 | tf_op jit(solution)/shard_map/ppermute | solution.py:203
  222.7 14.5 %collective-permute-start.38 = (bf16[1024,256]{1,0:T(8,128)(2,1)S(1)}, bf16[1024,256]{1,0:T(8,128)(2,1)S(1)}, u32[]{:S(2)}, u32[]{:S(2)}) collective-permute-start(bf16[1024,256]{1,0:T(8,128)(2,1)S(1)} %broadcast_select_fusion), channel_id=1, source_target_pairs={{0,4},{4,0},{8,12},{12,8},{16,20},{20,16},{24,28},{28,24},{1,5},{5... | collective-permute-start | bytes 1572872 | tf_op jit(solution)/shard_map/ppermute | solution.py:203
  226.6 3.7 %collective-permute-start.40 = (f32[16,16]{1,0:T(8,128)S(1)}, f32[16,16]{1,0:T(8,128)S(1)}, u32[]{:S(2)}, u32[]{:S(2)}) collective-permute-start(f32[16,16]{1,0:T(8,128)S(1)} %max.9), channel_id=1, source_target_pairs={{0,8},{4,12},{8,0},{12,4},{16,24},{20,28},{24,16},{28,20},{1,9},{5... | collective-permute-start | bytes 3080 | tf_op jit(solution)/shard_map/ppermute | solution.py:199
  230.3 4.5 %collective-permute-start.41 = (f32[16,16]{1,0:T(8,128)S(1)}, f32[16,16]{1,0:T(8,128)S(1)}, u32[]{:S(2)}, u32[]{:S(2)}) collective-permute-start(f32[16,16]{1,0:T(8,128)S(1)} %max.10), channel_id=1, source_target_pairs={{0,16},{4,20},{8,24},{12,28},{16,0},{20,4},{24,8},{28,12},{1,17},{... | collective-permute-start | bytes 3080 | tf_op jit(solution)/shard_map/ppermute | solution.py:199
